TPU v7x, 256 devices: a whole 4x4x8 slice. The times are simulated.
256 devices in a mesh: dp: 4 (over x_hi, core), label: 64 (over x_lo, z, y).
Axes of the slice: x: 4 (x_hi: 2, x_lo: 2; x = x_hi * 2 + x_lo), y: 4, z: 8, core: 2. Of those that a mesh axis runs over, the one named last changes fastest.
Arguments:
- embeddings: bfloat16 [2048, 768], P(('dp', 'label')), may hold values from -16 to 16
- classifier: bfloat16 [262144, 768], P('label'), may hold values from -1 to 1
- positives: int32 [2048, 5], P(('dp', 'label')), may hold values from 0 to 262143
- counts: int32 [2048], P(('dp', 'label')), may hold values from 1 to 5
Outputs:
- loss: float32 [2048], P(('dp', 'label'))
- query_grad: bfloat16 [2048, 768], P(('dp', 'label'))
- class_grad: bfloat16 [262144, 768], P('label')
All inputs are finite; a program needn't handle non-finite values.
Results may differ from a plain program's by a relative error of at most 0.0095.
Values may be sent and summed in bfloat16 or wider, within the bound.
No kernel may reach another device: no remote copies, remote signals or barrier semaphores. Data moves between devices by JAX's collectives and lax.ppermute only.
A program may use at most 64 MiB of HBM per device.

v0:
```python
import jax
import jax.numpy as jnp
from jax import lax
from jax.sharding import PartitionSpec as P


def body(embeddings, classifier, positives, counts):
    lab_dev = classifier.shape[0]
    q_dev = embeddings.shape[0]
    rank = lax.axis_index("label")
    group = lax.all_gather(embeddings, "label", axis=0, tiled=True)
    ids, cnt = (
        lax.all_gather(positives, "label", axis=0, tiled=True),
        lax.all_gather(counts, "label", axis=0, tiled=True),
    )
    fcnt = cnt.astype(jnp.float32)
    scores = lax.dot_general(
        group, classifier, (((1,), (1,)), ((), ())), preferred_element_type=jnp.float32
    )
    local = ids - rank * lab_dev
    valid = (local >= 0) & (local < lab_dev) & (jnp.arange(ids.shape[1])[None, :] < cnt[:, None])
    picked = jnp.take_along_axis(scores, jnp.clip(local, 0, lab_dev - 1), 1)
    possum = jnp.sum(jnp.where(valid, picked, 0.0), 1)
    top = jnp.max(scores, 1)
    gmax = lax.pmax(top, "label")
    expsum = jnp.sum(jnp.exp(scores - gmax[:, None]), 1)
    total, pos_total = lax.psum((expsum, possum), "label")
    lse = gmax + jnp.log(total)
    loss_all = lse - pos_total / fcnt
    loss = lax.dynamic_slice_in_dim(loss_all, rank * q_dev, q_dev)
    cols = jnp.arange(lab_dev, dtype=jnp.int32)[None, :]
    target = jnp.zeros_like(scores)
    for slot in range(ids.shape[1]):
        hit = (cols == local[:, slot : slot + 1]) & valid[:, slot : slot + 1]
        target = target + jnp.where(hit, 1.0 / fcnt[:, None], 0.0)
    grad = (jnp.exp(scores - lse[:, None]) - target).astype(jnp.bfloat16)
    query_grad = lax.psum_scatter(
        jnp.dot(grad, classifier, preferred_element_type=jnp.float32),
        "label",
        scatter_dimension=0,
        tiled=True,
    ).astype(jnp.bfloat16)
    partial_rows = lax.dot_general(
        grad, group, (((0,), (0,)), ((), ())), preferred_element_type=jnp.float32
    )
    rounded = lax.optimization_barrier(partial_rows.astype(jnp.bfloat16))
    summed = lax.psum(rounded.astype(jnp.float32).astype(jnp.bfloat16), "dp")
    return (loss, query_grad, summed)


def solution(mesh):
    return jax.shard_map(
        body,
        mesh=mesh,
        in_specs=(
            P(("dp", "label"), None),
            P("label", None),
            P(("dp", "label"), None),
            P(("dp", "label")),
        ),
        out_specs=(P(("dp", "label")), P(("dp", "label"), None), P("label", None)),
        check_vma=False,
    )
```

profile of v0, /device:TPU:32, one launch (start us, length us, event | category | flops | bytes accessed | tf_op | source)
XLA Modules:
  0.0 1078.5 jit_solution(8235674720578872613)
XLA Ops:
  8.0 1.3 dynamic-slice
  10.0 0.9 dynamic-update-slice
  10.8 25.7 %all-reduce = s32[512]{0:T(512)S(1)} all-reduce(s32[512]{0:T(512)S(1)} %dynamic-update-slice), channel_id=1, replica_groups=mesh['dp'=4,'label'=64] {'label'}, use_global_device_ids=true, to_apply=%add | all-reduce | flops 512 | bytes 4096
  36.6 144.8 %all_gather.10 = s32[512,5]{1,0:T(8,128)S(1)} all-gather(s32[8,5]{1,0:T(8,128)} %param.6), channel_id=1, replica_groups=mesh['dp'=4,'label'=64] {'label'}, dimensions={0}, use_global_device_ids=true | all-gather | bytes 10400 | tf_op jit(solution)/shard_map/all_gather | solution.py:13
  181.6 0.7 slice_reduce_fusion.4
  182.3 155.6 %all_gather.9 = bf16[512,768]{1,0:T(8,128)(2,1)S(1)} all-gather(bf16[8,768]{1,0:T(8,128)(2,1)} %param.4), channel_id=1, replica_groups=mesh['dp'=4,'label'=64] {'label'}, dimensions={0}, use_global_device_ids=true | all-gather | bytes 798720 | tf_op jit(solution)/shard_map/all_gather | solution.py:11
  337.9 8.5 fusion.6
  346.4 152.9 %pmax.7 = f32[512]{0:T(512)S(1)} all-reduce(f32[512]{0:T(512)S(1)} %get-tuple-element.20), channel_id=1, replica_groups=mesh['dp'=4,'label'=64] {'label'}, use_global_device_ids=true, to_apply=%region_1.2 | all-reduce | flops 512 | bytes 4096 | tf_op jit(solution)/shard_map/pmax | solution.py:25
  499.3 0.2 reshape.21
  499.5 4.6 exponential_reduce_fusion
  504.2 63.2 %gather_fusion = f32[2560]{0:T(1024)S(1)} fusion(f32[512,4096]{1,0:T(8,128)} %get-tuple-element.21, s32[2560]{0:T(1024)S(1)} %reshape.21), kind=kCustom, calls=%fused_computation | custom fusion | bytes 40960 | tf_op jit(solution)/shard_map/jit(take_along_axis)/gather | solution.py:22
  567.3 0.2 reshape.24
  567.6 0.2 select_reduce_fusion
  567.8 0.7 slice_reduce_fusion.9
  568.5 159.2 %all-reduce.1 = (f32[512]{0:T(512)S(1)}, f32[512]{0:T(512)S(1)}) all-reduce(f32[512]{0:T(512)S(1)} %exponential_reduce_fusion, f32[512]{0:T(512)S(1)} %select_reduce_fusion), channel_id=1, replica_groups=mesh['dp'=4,'label'=64] {'label'}, use_global_device_ids=true, to_apply=%region_3.4 | all-reduce | flops 1024 | bytes 8192 | tf_op jit(solution)/shard_map/psum | solution.py:27
  727.7 16.0 %subtract_convert_fusion = bf16[512,4096]{1,0:T(8,128)(2,1)S(1)} fusion(f32[512,4096]{1,0:T(8,128)} %get-tuple-element.21, s32[512]{0:T(512)S(1)} %get-tuple-element.7, s32[512]{0:T(512)S(1)} %get-tuple-element.4, s32[512]{0:T(512)S(1)} %get-tuple-element.5, s32[512]{0:T(512)S(1)} %get-tuple-element.6, f32[512]{0:T(512)S(1)} %get-tuple-element.19, ...), kind=kLoop, calls=%fused_computation.1 | loop fusion | flops 46137344 | bytes 12599808 | tf_op jit(solution)/shard_map/convert_element_type | solution.py:36
  743.8 1.9 copy-done
  745.7 6.7 fusion.7
  752.4 0.2 all-reduce.4.cloned.1.call-start
  752.6 8.4 convolution_convert_fusion
  761.0 0.6 dynamic_slice.3
  761.6 302.3 %reduce-scatter.2.cloned.1.call-done = f32[8,768]{1,0:T(8,128)} async-done(((f32[512,768]{1,0:T(8,128)}), f32[8,768]{1,0:T(8,128)}) %reduce-scatter.2.cloned.1.call-update) | async-done | bytes 24592 | tf_op jit(solution)/shard_map/reduce_scatter | solution.py:37
  1063.9 1.3 convert_element_type.16
  1065.2 5.9 copy.9
  (9 shorter events, 0.3 us)
Async XLA Ops:
  8.0 1055.9 %reduce-scatter.2.cloned.1.call-start = ((), (), s32[]{:S(2)}) async-start(), calls=%async_computation.1 | async-start | bytes 1597440 | tf_op jit(solution)/shard_map/reduce_scatter | solution.py:37
  743.7 1.9 copy-start
  752.4 312.9 %all-reduce.4.cloned.1.call-start = ((), (), s32[]{:S(2)}) async-start(), calls=%async_computation.2 | async-start | bytes 12582912 | tf_op jit(solution)/shard_map/psum | solution.py:47
Sparse Core Ops, SparseCore 0:
  752.5 311.3 reduce-scatter.1
Sparse Core Ops, SparseCore 1:
  761.1 132.9 all-reduce.3
where the time goes:
time: 1090 us; the launch traced here: 1080 us
  blocking collectives  638 us (59%)
  waiting for transfers between devices  302 us (28%)
  local copies, waits for them, and re-layouts  75.5 us (7%)
  matrix products  23.5 us (2%)
  other arithmetic  22.5 us (2%)
  between operations  16.2 us (1%)
    reduce_scatter x1, waiting for transfers between devices, body(): lax.psum_scatter(jnp.dot(grad, classifier, preferred_element_type=jnp.flo...  302 us
    psum x1, blocking collectives, body(): total, pos_total = lax.psum((expsum, possum), 'label')  159 us
    all_gather x1, blocking collectives, body(): group = lax.all_gather(embeddings, 'label', axis=0, tiled=True)  156 us
    pmax x1, blocking collectives, body(): gmax = lax.pmax(top, 'label')  153 us
    all_gather x1, blocking collectives, body(): lax.all_gather(positives, 'label', axis=0, tiled=True)  145 us
    gather x3, local copies, waits for them, and re-layouts, body(): picked = jnp.take_along_axis(scores, jnp.clip(local, 0, lab_dev - 1), 1)  63.6 us
    unnamed x1, blocking collectives  25.7 us
  transfers between devices with their start and end apart: 2, of which 1 were waited for; matrix products, arithmetic and copies ran while one was open for 1% of the time, Pallas kernels for 0%

commit v1 on v0

v1 whole, which is shorter than its diff:
```python
import functools

import jax
import jax.numpy as jnp
from jax import lax
from jax.experimental import pallas as pl
from jax.experimental.pallas import tpu as pltpu
from jax.sharding import Mesh, PartitionSpec as P

AXES = ("xh", "core", "xl", "z", "y")
SIZES = {"xh": 2, "core": 2, "xl": 2, "z": 8, "y": 4}
EXTRA = 128
POS = 5
LO, MID, HI, CNT = 0, 8, 16, 24
VMEM = pl.BlockSpec(memory_space=pltpu.VMEM)
SMEM = pl.BlockSpec(memory_space=pltpu.SMEM)
NT = (((1,), (1,)), ((), ()))
TN = (((0,), (0,)), ((), ()))
LCH = 256


def shift(x, axis, step):
    n = SIZES[axis]
    return lax.ppermute(x, axis, [(i, (i + step) % n) for i in range(n)])


def scores_kernel(own_ref, oth_ref, w_ref, e_ref, m_ref, l_ref, s_ref):
    labels, width = w_ref.shape
    for part, q_ref in enumerate((own_ref, oth_ref)):
        rows = q_ref.shape[0]
        q = q_ref[:, :width]

        def product(i, top):
            at = pl.multiple_of(i * LCH, LCH)
            s = lax.dot_general(w_ref[pl.ds(at, LCH), :], q, NT, preferred_element_type=jnp.float32)
            s_ref[pl.ds(at, LCH), :] = s
            return jnp.maximum(top, jnp.max(s.reshape(LCH // 8, 8, rows), 0))

        top = lax.fori_loop(0, labels // LCH, product, jnp.full((8, rows), -1e30, jnp.float32))
        top = jnp.max(top, 0, keepdims=True)

        def expo(i, total):
            at = pl.multiple_of(i * LCH, LCH)
            e = jnp.exp(s_ref[pl.ds(at, LCH), :] - top)
            e_ref[pl.ds(at, LCH), part * rows:(part + 1) * rows] = e.astype(jnp.bfloat16)
            return total + jnp.sum(e.reshape(LCH // 8, 8, rows), 0)

        total = lax.fori_loop(0, labels // LCH, expo, jnp.zeros((8, rows), jnp.float32))
        m_ref[part:part + 1, :] = top
        l_ref[part:part + 1, :] = top + jnp.log(jnp.sum(total, 0, keepdims=True))


def scores_call(own, oth, w):
    rows = own.shape[0]
    labels = w.shape[0]
    return pl.pallas_call(
        scores_kernel,
        out_shape=(
            jax.ShapeDtypeStruct((labels, 2 * rows), jnp.bfloat16),
            jax.ShapeDtypeStruct((2, rows), jnp.float32),
            jax.ShapeDtypeStruct((2, rows), jnp.float32),
        ),
        in_specs=[VMEM] * 3,
        out_specs=(VMEM,) * 3,
        scratch_shapes=[pltpu.VMEM((labels, rows), jnp.float32)],
        compiler_params=pltpu.CompilerParams(vmem_limit_bytes=24 * 2**20),
        cost_estimate=pl.CostEstimate(flops=4 * rows * labels * w.shape[1], bytes_accessed=labels * rows * 4, transcendentals=2 * rows * labels),
        name="scores",
    )(own, oth, w)


def hits_kernel(base_ref, *refs):
    blocks = refs[:8]
    w_ref, n_ref, key_ref, s_ref, t_ref = refs[8:]
    labels, width = w_ref.shape
    base = base_ref[0].astype(jnp.float32)
    row = lax.broadcasted_iota(jnp.int32, (8, EXTRA), 0)
    col = lax.broadcasted_iota(jnp.int32, (8, EXTRA), 1)
    digits = jnp.where(col == row + LO, 1.0, jnp.where(col == row + MID, 128.0, jnp.where(col == row + HI, 16384.0, 0.0)))
    digits = jnp.where(row < POS, digits, 0.0).astype(jnp.bfloat16)
    counting = jnp.where(col == CNT, 1.0, 0.0).astype(jnp.bfloat16)
    big = 1e9
    for b, q_ref in enumerate(blocks):
        rows = q_ref.shape[0]
        extra = q_ref[:, width:]
        ids = lax.dot_general(digits, extra, NT, preferred_element_type=jnp.float32)
        cnt = lax.dot_general(counting, extra, NT, preferred_element_type=jnp.float32)
        slot = lax.broadcasted_iota(jnp.int32, (8, rows), 0)
        lane = lax.broadcasted_iota(jnp.int32, (8, rows), 1)
        valid = (slot.astype(jnp.float32) < cnt) & (slot < POS)
        ids = jnp.where(valid, ids, -1.0)
        same = jnp.zeros((8, rows), jnp.float32)
        again = jnp.zeros((8, rows), jnp.float32)
        for j in range(POS):
            eq = jnp.where(ids == ids[j:j + 1, :], 1.0, 0.0)
            same = same + eq
            again = again + jnp.where(slot > j, eq, 0.0)
        local = ids - base
        hit = valid & (local >= 0.0) & (local < float(labels)) & (again == 0.0)
        weight = same / cnt
        keys = jnp.where(hit, (lane * 8 + slot).astype(jnp.float32) * float(labels) + local, big)
        n = jnp.sum(jnp.where(hit, 1.0, 0.0)).astype(jnp.int32)
        n_ref[b] = n

        def step(i, keys):
            kf = jnp.min(keys)
            this = keys == kf
            k = kf.astype(jnp.int32)
            label = lax.rem(k, labels)
            query = lax.div(k, labels * 8)
            qat = pl.multiple_of(lax.div(query, 16) * 16, 16)
            lat = pl.multiple_of(lax.div(label, 16) * 16, 16)
            s16 = lax.dot_general(q_ref[pl.ds(qat, 16), :width], w_ref[pl.ds(lat, 16), :], NT, preferred_element_type=jnp.float32)
            r16 = lax.broadcasted_iota(jnp.int32, (16, 16), 0)
            c16 = lax.broadcasted_iota(jnp.int32, (16, 16), 1)
            at = b * rows * POS + i
            key_ref[at] = k
            s_ref[at] = jnp.sum(jnp.where((r16 == query - qat) & (c16 == label - lat), s16, 0.0))
            t_ref[at] = jnp.sum(jnp.where(this, weight, 0.0))
            return jnp.where(this, big, keys)

        lax.fori_loop(0, n, step, keys)


def hits_call(base, blocks, w):
    total = 8 * blocks[0].shape[0] * POS
    return pl.pallas_call(
        hits_kernel,
        out_shape=(
            jax.ShapeDtypeStruct((8,), jnp.int32),
            jax.ShapeDtypeStruct((total,), jnp.int32),
            jax.ShapeDtypeStruct((total,), jnp.float32),
            jax.ShapeDtypeStruct((total,), jnp.float32),
        ),
        in_specs=[SMEM] + [VMEM] * 9,
        out_specs=(SMEM,) * 4,
        compiler_params=pltpu.CompilerParams(vmem_limit_bytes=16 * 2**20),
        cost_estimate=pl.CostEstimate(flops=10**9, bytes_accessed=2**23, transcendentals=0),
        name="hits",
    )(base, *blocks, w)


def query_kernel(xh_ref, n_ref, key_ref, s_ref, t_ref, lse_ref, m_ref, e0, e1, e2, e3, w_ref, p0, p1, p2, p3, own_ref, oth_ref, pos_ref):
    labels, width = w_ref.shape
    rows = e0.shape[1] // 2
    xh = xh_ref[0]
    half = rows // 2
    pos_ref[...] = jnp.zeros_like(pos_ref)
    for d, (e_ref, p_ref) in enumerate(((e0, p0), (e1, p1), (e2, p2), (e3, p3))):
        scale = [jnp.exp(m_ref[2 * d + k:2 * d + k + 1, :] - lse_ref[2 * d + k:2 * d + k + 1, :]) for k in range(2)]

        def scaled(i, carry):
            at = pl.multiple_of(i * LCH, LCH)
            for k in range(2):
                cols = slice(k * rows, (k + 1) * rows)
                p_ref[pl.ds(at, LCH), cols] = (e_ref[pl.ds(at, LCH), cols].astype(jnp.float32) * scale[k]).astype(jnp.bfloat16)
            return carry

        lax.fori_loop(0, labels // LCH, scaled, 0)
        for k in range(2):
            b = 2 * d + k

            def patch(i, carry):
                at = b * rows * POS + i
                key = key_ref[at]
                s = s_ref[at]
                label = lax.rem(key, labels)
                rest = lax.div(key, labels)
                slot = lax.rem(rest, 8)
                query = lax.div(rest, 8)
                lat = pl.multiple_of(lax.div(label, 16) * 16, 16)
                qhi = lax.div(query, half)
                qlo = lax.rem(query, half)
                qat = pl.multiple_of(qhi * half, half)
                spot = (pl.ds(lat, 16), pl.ds(pl.multiple_of(k * rows + qhi * half, half), half))
                value = jnp.exp(s - lse_ref[b:b + 1, pl.ds(qat, half)]) - t_ref[at]
                r = lax.broadcasted_iota(jnp.int32, (16, half), 0)
                c = lax.broadcasted_iota(jnp.int32, (16, half), 1)
                old = p_ref[spot].astype(jnp.float32)
                p_ref[spot] = jnp.where((r == label - lat) & (c == qlo), value, old).astype(jnp.bfloat16)

                @pl.when(qhi == xh)
                def _():
                    c1 = lax.broadcasted_iota(jnp.int32, (1, EXTRA), 1)
                    times = t_ref[at] * 1.0
                    full = jnp.full((1, EXTRA), s * times, jnp.float32)
                    high = full.astype(jnp.bfloat16).astype(jnp.float32)
                    mid = (full - high).astype(jnp.bfloat16).astype(jnp.float32)
                    low = full - high - mid
                    put = jnp.where(c1 == slot, high, jnp.where(c1 == slot + 8, mid, jnp.where(c1 == slot + 16, low, 0.0)))
                    into = (k, pl.ds(d * half + qlo, 1), slice(None))
                    pos_ref[into] = pos_ref[into] + put

                return carry

            lax.fori_loop(0, n_ref[b], patch, 0)
        mine = pl.multiple_of(xh * half, half)
        both = jnp.concatenate([p_ref[:, pl.ds(mine, half)], p_ref[:, pl.ds(pl.multiple_of(rows + xh * half, half), half)]], 1)
        u = lax.dot_general(both, w_ref[...], TN, preferred_element_type=jnp.float32)
        for k, out in enumerate((own_ref, oth_ref)):
            out[d * half:(d + 1) * half, :width] = u[k * half:(k + 1) * half].astype(jnp.bfloat16)
            out[d * half:(d + 1) * half, width:] = pos_ref[k, d * half:(d + 1) * half, :].astype(jnp.bfloat16)


def query_call(xh, hits, lse, m, es, w):
    labels, width = w.shape
    rows = es[0].shape[1] // 2
    out = jax.ShapeDtypeStruct((4 * rows // 2, width + EXTRA), jnp.bfloat16)
    res = pl.pallas_call(
        query_kernel,
        out_shape=tuple(jax.ShapeDtypeStruct(e.shape, e.dtype) for e in es) + (out, out),
        in_specs=[SMEM] * 5 + [VMEM] * 7,
        out_specs=(VMEM,) * 6,
        scratch_shapes=[pltpu.VMEM((2, 4 * rows // 2, EXTRA), jnp.float32)],
        compiler_params=pltpu.CompilerParams(vmem_limit_bytes=40 * 2**20),
        cost_estimate=pl.CostEstimate(flops=8 * rows * labels * width, bytes_accessed=2**24, transcendentals=0),
        name="query_part",
    )(xh, *hits, lse, m, *es, w)
    return res[:4], res[4], res[5]


def class_kernel(core_ref, p0, p1, p2, p3, *refs):
    blocks = refs[:8]
    out_ref = refs[8]
    rows = blocks[0].shape[0]
    width = out_ref.shape[1]
    acc = None
    for d, p_ref in enumerate((p0, p1, p2, p3)):
        for k in range(2):
            term = jnp.dot(p_ref[:, k * rows:(k + 1) * rows], blocks[2 * d + k][:, :width], preferred_element_type=jnp.float32)
            acc = term if acc is None else acc + term
    out_ref[...] = acc.astype(jnp.bfloat16)


def class_call(core, ps, blocks, width):
    labels = ps[0].shape[0]
    steps = labels // LCH
    rows = blocks[0].shape[0]
    whole = lambda i, c: (0, 0)
    return pl.pallas_call(
        class_kernel,
        out_shape=jax.ShapeDtypeStruct((2 * labels, width), jnp.bfloat16),
        grid_spec=pltpu.PrefetchScalarGridSpec(
            num_scalar_prefetch=1,
            grid=(steps,),
            in_specs=[pl.BlockSpec((LCH, 2 * rows), lambda i, c: (i, 0))] * 4 + [pl.BlockSpec(blocks[0].shape, whole)] * 8,
            out_specs=pl.BlockSpec((LCH, width), lambda i, c: (c[0] * steps + i, 0)),
        ),
        compiler_params=pltpu.CompilerParams(vmem_limit_bytes=32 * 2**20),
        cost_estimate=pl.CostEstimate(flops=16 * rows * labels * width, bytes_accessed=2**24, transcendentals=0),
        name="class_part",
    )(core, *ps, *blocks)


def lse_of(parts, axis=None):
    if axis is None:
        top = functools.reduce(jnp.maximum, parts)
        return top + jnp.log(functools.reduce(jnp.add, [jnp.exp(p - top) for p in parts]))
    top = jnp.max(parts, axis)
    return top + jnp.log(jnp.sum(jnp.exp(parts - jnp.expand_dims(top, axis)), axis))


def body(embeddings, classifier, positives, counts):
    q_dev, width = embeddings.shape
    labels = classifier.shape[0] // 2
    xh, core, xl, z, y = (lax.axis_index(a) for a in AXES)
    rank = (xl * 8 + z) * 4 + y
    base = (rank * 2 + core) * labels

    blank = jnp.zeros((q_dev, 8 - POS), jnp.int32)
    extra = jnp.concatenate(
        [positives & 127, blank, (positives >> 7) & 127, blank, positives >> 14, blank, counts[:, None], jnp.zeros((q_dev, EXTRA - CNT - 1), jnp.int32)],
        1,
    ).astype(jnp.bfloat16)
    sent = jnp.concatenate([embeddings, extra], 1)
    copies = jnp.broadcast_to(sent[None], (32, q_dev, width + EXTRA)).reshape(32 * q_dev, width + EXTRA)
    mine = lax.all_to_all(copies, ("xh", "xl", "z"), 0, 0, tiled=True)
    own = [mine] + [shift(mine, "y", -d) for d in range(1, 4)]
    oth = [shift(b, "core", 1) for b in own]
    w = lax.dynamic_slice_in_dim(classifier, core * labels, labels)
    rows = mine.shape[0]

    es, ms, ls = zip(*[scores_call(a, b, w) for a, b in zip(own, oth)])
    blocks = [b for pair in zip(own, oth) for b in pair]
    hits = hits_call(base[None], blocks, w)
    m = jnp.concatenate(ms, 0)
    stat = jnp.concatenate(ls, 0)
    swapped = shift(stat, "core", 1).reshape(4, 2, rows)[:, ::-1].reshape(8, rows)
    stat = lse_of([stat, swapped])
    stat = lse_of([stat] + [jnp.roll(shift(stat, "y", -d), 2 * d, 0) for d in range(1, 4)])
    lse = lse_of(lax.all_to_all(jnp.broadcast_to(stat[None], (16, 8, rows)), ("xl", "z"), 0, 0, tiled=True), 0)

    ps, u_own, u_oth = query_call(xh[None], hits, lse, m, es, w)
    f32 = lambda a: a.astype(jnp.float32)
    u = (f32(u_own) + f32(shift(u_oth, "core", 1))).astype(jnp.bfloat16)
    part = u.shape[0] // 4
    u = [u[d * part:(d + 1) * part] for d in range(4)]
    total = f32(u[0])
    for d in range(1, 4):
        total = total + f32(shift(u[d], "y", d))
    got = lax.all_to_all(total.astype(jnp.bfloat16), ("xl", "z"), 0, 0, tiled=True)
    final = jnp.sum(f32(got).reshape(16, q_dev, width + EXTRA), 0)
    query_grad = final[:, :width].astype(jnp.bfloat16)
    pos_mean = jnp.sum(final[:, width:width + 24], 1)
    at = ((xh * 2 + xl) * 8 + z) * q_dev
    loss = lax.dynamic_slice(lse, (0, at), (1, q_dev))[0] - pos_mean

    halves = class_call(core[None], ps, blocks, width)
    mine_half = lax.dynamic_slice_in_dim(halves, core * labels, labels)
    class_grad = lax.dynamic_update_slice_in_dim(halves, shift(mine_half, "core", 1), (1 - core) * labels, 0)
    return loss, query_grad, class_grad


def solution(mesh):
    fine = Mesh(mesh.devices.reshape(tuple(SIZES[a] for a in AXES)), AXES)
    split = P(AXES, None)
    lab = P(("xl", "z", "y"), None)
    return jax.shard_map(
        body,
        mesh=fine,
        in_specs=(split, lab, split, P(AXES)),
        out_specs=(P(AXES), split, lab),
        check_vma=False,
    )
```

time: 1090 us -> 209 us (0.19); the launches traced: 1080 us -> 210 us
  blocking collectives: 638 us -> 27.3 us
  waiting for transfers between devices: 302 us -> 46.5 us
  Pallas kernels: 0 us -> 75.2 us
  local copies, waits for them, and re-layouts: 75.5 us -> 20.7 us
  starting transfers between devices: 0.26 us -> 36.4 us
  matrix products: 23.5 us -> 0 us
  other arithmetic: 22.5 us -> 3.26 us
  between operations: 16.2 us -> 0.9 us
    reduce_scatter x1 -> x0, waiting for transfers between devices: 302 us -> none  [body(): lax.psum_scatter(jnp.dot(grad, classifier, preferred_element_type=jnp.flo...]
    all_gather x2 -> x0, blocking collectives: 300 us -> none  [the longest x1 156 us: body(): group = lax.all_gather(embeddings, 'label', axis=0, tiled=True)]
    psum x1 -> x0, blocking collectives: 159 us -> none  [body(): total, pos_total = lax.psum((expsum, possum), 'label')]
    pmax x1 -> x0, blocking collectives: 153 us -> none  [body(): gmax = lax.pmax(top, 'label')]
    pallas_call x0 -> x7, Pallas kernels: none -> 75.2 us  [the longest x4 28.9 us: scores_call(): pl.pallas_call(scores_kernel, out_shape=(jax.ShapeDtypeStruct((labels, 2...]
    gather x3 -> x0, local copies, waits for them, and re-layouts: 63.6 us -> none  [body(): picked = jnp.take_along_axis(scores, jnp.clip(local, 0, lab_dev - 1), 1)]
    ppermute x0 -> x16, waiting for transfers between devices: none -> 37 us  [shift(): return lax.ppermute(x, axis, [(i, (i + step) % n) for i in range(n)])]
    all_to_all x0 -> x1, blocking collectives: none -> 27.3 us  [body(): mine = lax.all_to_all(copies, ('xh', 'xl', 'z'), 0, 0, tiled=True)]
  transfers between devices with their start and end apart: 2 -> 18, of which waited for: 1 -> 9; matrix products, arithmetic and copies ran while one was open for 1% -> 2% of each run, Pallas kernels for 0% -> 22%
where the time goes in v1:
time: 209 us; the launch traced here: 210 us
  Pallas kernels  75.2 us (36%)
  waiting for transfers between devices  46.5 us (22%)
  starting transfers between devices  36.4 us (17%)
  blocking collectives  27.3 us (13%)
  local copies, waits for them, and re-layouts  20.7 us (10%)
  other arithmetic  3.26 us (2%)
    ppermute x16, waiting for transfers between devices, shift(): return lax.ppermute(x, axis, [(i, (i + step) % n) for i in range(n)])  37 us
    pallas_call x4, Pallas kernels, scores_call(): pl.pallas_call(scores_kernel, out_shape=(jax.ShapeDtypeStruct((labels, 2...  28.9 us
    all_to_all x1, blocking collectives, body(): mine = lax.all_to_all(copies, ('xh', 'xl', 'z'), 0, 0, tiled=True)  27.3 us
    pallas_call x1, Pallas kernels, hits_call(): pl.pallas_call(hits_kernel, out_shape=(jax.ShapeDtypeStruct((8,), jnp.int...  24 us
    ppermute x16, starting transfers between devices, shift(): return lax.ppermute(x, axis, [(i, (i + step) % n) for i in range(n)])  21.4 us
    pallas_call x1, Pallas kernels, query_call(): pl.pallas_call(query_kernel, out_shape=tuple((jax.ShapeDtypeStruct(e.shap...  11.7 us
    unnamed x26, local copies, waits for them, and re-layouts  10.6 us
    pallas_call x1, Pallas kernels, class_call(): pl.pallas_call(class_kernel, out_shape=jax.ShapeDtypeStruct((2 * labels,...  10.6 us
  transfers between devices with their start and end apart: 18, of which 9 were waited for; matrix products, arithmetic and copies ran while one was open for 2% of the time, Pallas kernels for 22%

profile of v1, /device:TPU:32, one launch (start us, length us, event | category | flops | bytes accessed | tf_op | source)
XLA Modules:
  0.0 210.2 jit_solution(11404422743095586884)
XLA Ops:
  2.9 27.3 %all_to_all.22 = bf16[32,8,896]{2,1,0:T(8,128)(2,1)} all-to-all(bf16[32,8,896]{2,1,0:T(8,128)(2,1)S(1)} %broadcast_in_dim.31), channel_id=1, replica_groups=mesh['xh'=2,'core'=2,'xl'=2,'z'=8,'y'=4] {'xh','xl','z'}, dimensions={0} | all-to-all | bytes 917504 | tf_op jit(solution)/shard_map/all_to_all | solution.py:277
  31.8 2.9 %collective-permute-start.3 = (bf16[256,896]{1,0:T(8,128)(2,1)}, bf16[256,896]{1,0:T(8,128)(2,1)}, u32[]{:S(2)}, u32[]{:S(2)}) collective-permute-start(bf16[256,896]{1,0:T(8,128)(2,1)} %bitcast.1.own_ref.refs_0_), channel_id=1, source_target_pairs={{0,2},{1,3},{2,0},{3,1},{4,6},{5,7},{6,4},{7,5},{8,10},{9,11},{10,... | collective-permute-start | bytes 1376264 | tf_op jit(solution)/shard_map/ppermute | solution.py:24
  36.1 8.0 %collective-permute-done.5.own_ref.refs_6_ = bf16[256,896]{1,0:T(8,128)(2,1)} collective-permute-done((bf16[256,896]{1,0:T(8,128)(2,1)}, bf16[256,896]{1,0:T(8,128)(2,1)}, u32[]{:S(2)}, u32[]{:S(2)}) %collective-permute-start.5) | collective-permute-done | bytes 458784 | tf_op jit(solution)/shard_map/ppermute | solution.py:24
  44.1 9.0 %collective-permute-done.3.own_ref.refs_4_ = bf16[256,896]{1,0:T(8,128)(2,1)} collective-permute-done((bf16[256,896]{1,0:T(8,128)(2,1)}, bf16[256,896]{1,0:T(8,128)(2,1)}, u32[]{:S(2)}, u32[]{:S(2)}) %collective-permute-start.3) | collective-permute-done | bytes 458784 | tf_op jit(solution)/shard_map/ppermute | solution.py:24
  53.6 2.1 constant_dynamic-slice_fusion.2.w_ref.refs_8_
  55.7 7.7 %scores.4 = (bf16[2048,512]{1,0:T(8,128)(2,1)S(1)}, f32[2,256]{1,0:T(2,128)S(1)}, f32[2,256]{1,0:T(2,128)S(1)}) custom-call(bf16[256,896]{1,0:T(8,128)(2,1)} %bitcast.1.own_ref.refs_0_, bf16[256,896]{1,0:T(8,128)(2,1)} %collective-permute-done.oth_ref.refs_1_, bf16[2048,768]{1,0:T(8,128)(2,1)S(1)} %constant_dynamic-slice_fusion.2.w_ref.refs_8_), custom_call_target="tpu_custom_call" | custom-call | flops 1610612736 | bytes 2097152 | tf_op jit(solution)/shard_map/scores/pallas_call | solution.py:56
  64.7 7.0 %scores.7 = (bf16[2048,512]{1,0:T(8,128)(2,1)S(1)}, f32[2,256]{1,0:T(2,128)S(1)}, f32[2,256]{1,0:T(2,128)S(1)}) custom-call(bf16[256,896]{1,0:T(8,128)(2,1)} %collective-permute-done.5.own_ref.refs_6_, bf16[256,896]{1,0:T(8,128)(2,1)} %collective-permute-done.6.oth_ref.refs_7_, bf16[2048,768]{1,0:T(8,128)(2,1)S(1)} %constant_dynamic-slice_fusion.2.w_ref.refs_8_), custom_call_target="tpu_custom_call" | custom-call | flops 1610612736 | bytes 2097152 | tf_op jit(solution)/shard_map/scores/pallas_call | solution.py:56
  73.2 7.1 %scores.6 = (bf16[2048,512]{1,0:T(8,128)(2,1)S(1)}, f32[2,256]{1,0:T(2,128)S(1)}, f32[2,256]{1,0:T(2,128)S(1)}) custom-call(bf16[256,896]{1,0:T(8,128)(2,1)} %collective-permute-done.3.own_ref.refs_4_, bf16[256,896]{1,0:T(8,128)(2,1)S(1)} %collective-permute-done.4.oth_ref.refs_5_, bf16[2048,768]{1,0:T(8,128)(2,1)S(1)} %constant_dynamic-slice_fusion.2.w_ref.refs_8_), custom_call_target="tpu_custom_call" | custom-call | flops 1610612736 | bytes 2097152 | tf_op jit(solution)/shard_map/scores/pallas_call | solution.py:56
  81.6 7.1 %scores.5 = (bf16[2048,512]{1,0:T(8,128)(2,1)S(1)}, f32[2,256]{1,0:T(2,128)S(1)}, f32[2,256]{1,0:T(2,128)S(1)}) custom-call(bf16[256,896]{1,0:T(8,128)(2,1)} %collective-permute-done.1.own_ref.refs_2_, bf16[256,896]{1,0:T(8,128)(2,1)S(1)} %collective-permute-done.2.oth_ref.refs_3_, bf16[2048,768]{1,0:T(8,128)(2,1)S(1)} %constant_dynamic-slice_fusion.2.w_ref.refs_8_), custom_call_target="tpu_custom_call" | custom-call | flops 1610612736 | bytes 2097152 | tf_op jit(solution)/shard_map/scores/pallas_call | solution.py:56
  91.5 2.3 %collective-permute-start.9 = (f32[8,256]{1,0:T(8,128)S(1)}, f32[8,256]{1,0:T(8,128)S(1)}, u32[]{:S(2)}, u32[]{:S(2)}) collective-permute-start(f32[8,256]{1,0:T(8,128)S(1)} %log_add_fusion.2), channel_id=1, source_target_pairs={{0,2},{1,3},{2,0},{3,1},{4,6},{5,7},{6,4},{7,5},{8,10},{9,11},{10,... | collective-permute-start | bytes 24584 | tf_op jit(solution)/shard_map/ppermute | solution.py:24
  94.2 2.9 %collective-permute-start.8 = (f32[8,256]{1,0:T(8,128)S(1)}, f32[8,256]{1,0:T(8,128)S(1)}, u32[]{:S(2)}, u32[]{:S(2)}) collective-permute-start(f32[8,256]{1,0:T(8,128)S(1)} %log_add_fusion.2), channel_id=1, source_target_pairs={{0,3},{1,0},{2,1},{3,2},{4,7},{5,4},{6,5},{7,6},{8,11},{9,8},{10,9... | collective-permute-start | bytes 24584 | tf_op jit(solution)/shard_map/ppermute | solution.py:24
  99.4 5.3 %all-to-all-start.1 = ((f32[16,8,256]{2,1,0:T(8,128)}), f32[16,8,256]{2,1,0:T(8,128)S(1)}, u32[]{:S(2)}, u32[]{:S(2)}) async-start(f32[16,8,256]{2,1,0:T(8,128)} %broadcast_in_dim.32), calls=%async_computation.1 | async-start | bytes 262144 | tf_op jit(solution)/shard_map/all_to_all | solution.py:291
  106.7 24.0 %hits.1 = (s32[8]{0:T(128)S(1)}, s32[10240]{0:T(1024)S(1)}, f32[10240]{0:T(1024)S(1)}, f32[10240]{0:T(1024)S(1)}) custom-call(s32[1]{0:T(128)} %bitcast.4.base_ref, bf16[256,896]{1,0:T(8,128)(2,1)} %bitcast.1.own_ref.refs_0_, bf16[256,896]{1,0:T(8,128)(2,1)} %collective-permute-done.oth_ref.refs_1_, bf16[256,896]{1,0:T(8,128)(2,1)} %collective-permute-done.1.own_ref.refs_2_, ...), custom_call_target="tpu_custom_call" | custom-call | flops 1000000000 | bytes 8388608 | tf_op jit(solution)/shard_map/hits/pallas_call | solution.py:127
  134.0 11.7 %query_part.1 = (bf16[2048,512]{1,0:T(8,128)(2,1)S(1)}, bf16[2048,512]{1,0:T(8,128)(2,1)S(1)}, bf16[2048,512]{1,0:T(8,128)(2,1)S(1)}, bf16[2048,512]{1,0:T(8,128...) custom-call(s32[1]{0:T(128)} %bitcast.3.xh_ref, s32[8]{0:T(128)S(1)} %get-tuple-element.29.n_ref, ...), custom_call_target="tpu_custom_call" | custom-call | flops 3221225472 | bytes 16777216 | tf_op jit(solution)/shard_map/query_part/pallas_call | solution.py:209
  145.7 10.6 %class_part.1 = bf16[4096,768]{1,0:T(8,128)(2,1)} custom-call(s32[1]{0:T(128)} %bitcast.6.core_ref, bf16[2048,512]{1,0:T(8,128)(2,1)S(1)} %get-tuple-element.43.p0, bf16[2048,512]{1,0:T(8,128)(2,1)S(1)} %get-tuple-element.44.p1, bf16[2048,512]{1,0:T(8,128)(2,1)S(1)} %get-tuple-element.45.p2, bf16[2048,512]{1,0:T(8,128)(2,1)S(1)} %get-tuple-element.46.p3, ...), custom_call_target="tpu_custom_call" | custom-call | flops 6442450944 | bytes 16777216 | tf_op jit(solution)/shard_map/class_part/pallas_call | solution.py:240
  156.3 3.7 %constant_dynamic-slice_fusion = bf16[2048,768]{1,0:T(8,128)(2,1)} fusion(bf16[4096,768]{1,0:T(8,128)(2,1)} %class_part.1, s32[]{:T(128)S(6)} %select_n.10), kind=kLoop, calls=%fused_computation.21 | loop fusion | bytes 6291460 | tf_op jit(solution)/shard_map/dynamic_slice | solution.py:309
  161.6 6.5 %collective-permute-done.11 = bf16[512,896]{1,0:T(8,128)(2,1)S(1)} collective-permute-done((bf16[512,896]{1,0:T(8,128)(2,1)S(1)}, bf16[512,896]{1,0:T(8,128)(2,1)S(1)}, u32[]{:S(2)}, u32[]{:S(2)}) %collective-permute-start.11) | collective-permute-done | bytes 917536 | tf_op jit(solution)/shard_map/ppermute | solution.py:24
  169.1 5.7 %collective-permute-start.14 = (bf16[128,896]{1,0:T(8,128)(2,1)S(1)}, bf16[128,896]{1,0:T(8,128)(2,1)S(1)}, u32[]{:S(2)}, u32[]{:S(2)}) collective-permute-start(bf16[128,896]{1,0:T(8,128)(2,1)S(1)} %get-tuple-element.48), channel_id=1, source_target_pairs={{0,3},{1,0},{2,1},{3,2},{4,7},{5,4},{6,5},{7,6},{8,11},{9,8},{10,9... | collective-permute-start | bytes 688136 | tf_op jit(solution)/shard_map/ppermute | solution.py:24
  176.2 4.7 %collective-permute-done.12 = bf16[128,896]{1,0:T(8,128)(2,1)S(1)} collective-permute-done((bf16[128,896]{1,0:T(8,128)(2,1)S(1)}, bf16[128,896]{1,0:T(8,128)(2,1)S(1)}, u32[]{:S(2)}, u32[]{:S(2)}) %collective-permute-start.12) | collective-permute-done | bytes 229408 | tf_op jit(solution)/shard_map/ppermute | solution.py:24
  180.8 4.3 %collective-permute-done.14 = bf16[128,896]{1,0:T(8,128)(2,1)S(1)} collective-permute-done((bf16[128,896]{1,0:T(8,128)(2,1)S(1)}, bf16[128,896]{1,0:T(8,128)(2,1)S(1)}, u32[]{:S(2)}, u32[]{:S(2)}) %collective-permute-start.14) | collective-permute-done | bytes 229408 | tf_op jit(solution)/shard_map/ppermute | solution.py:24
  185.1 1.8 collective-permute-done.13
  187.8 9.8 %all-to-all-start.2 = ((bf16[16,8,896]{2,1,0:T(8,128)(2,1)}), bf16[16,8,896]{2,1,0:T(8,128)(2,1)S(1)}, u32[]{:S(2)}, u32[]{:S(2)}) async-start(bf16[16,8,896]{2,1,0:T(8,128)(2,1)} %fusion), calls=%async_computation.2 | async-start | bytes 458752 | tf_op jit(solution)/shard_map/all_to_all | solution.py:301
  197.5 9.5 %all-to-all-done.2 = bf16[16,8,896]{2,1,0:T(8,128)(2,1)S(1)} async-done(((bf16[16,8,896]{2,1,0:T(8,128)(2,1)}), bf16[16,8,896]{2,1,0:T(8,128)(2,1)S(1)}, u32[]{:S(2)}, u32[]{:S(2)}) %all-to-all-start.2) | async-done | bytes 229408 | tf_op jit(solution)/shard_map/all_to_all | solution.py:301
  208.3 1.9 constant_dynamic-update-slice_fusion
  (78 shorter events, 26.6 us)
Async XLA Ops:
  30.2 13.9 %collective-permute-start.5 = (bf16[256,896]{1,0:T(8,128)(2,1)}, bf16[256,896]{1,0:T(8,128)(2,1)}, u32[]{:S(2)}, u32[]{:S(2)}) collective-permute-start(bf16[256,896]{1,0:T(8,128)(2,1)} %bitcast.1.own_ref.refs_0_), channel_id=1, source_target_pairs={{0,1},{1,2},{2,3},{3,0},{4,5},{5,6},{6,7},{7,4},{8,9},{9,10},{10,1... | collective-permute-start | bytes 1376264 | tf_op jit(solution)/shard_map/ppermute | solution.py:24
  31.8 21.3 %collective-permute-start.3 = (bf16[256,896]{1,0:T(8,128)(2,1)}, bf16[256,896]{1,0:T(8,128)(2,1)}, u32[]{:S(2)}, u32[]{:S(2)}) collective-permute-start(bf16[256,896]{1,0:T(8,128)(2,1)} %bitcast.1.own_ref.refs_0_), channel_id=1, source_target_pairs={{0,2},{1,3},{2,0},{3,1},{4,6},{5,7},{6,4},{7,5},{8,10},{9,11},{10,... | collective-permute-start | bytes 1376264 | tf_op jit(solution)/shard_map/ppermute | solution.py:24
  34.7 18.4 %collective-permute-start.1 = (bf16[256,896]{1,0:T(8,128)(2,1)}, bf16[256,896]{1,0:T(8,128)(2,1)}, u32[]{:S(2)}, u32[]{:S(2)}) collective-permute-start(bf16[256,896]{1,0:T(8,128)(2,1)} %bitcast.1.own_ref.refs_0_), channel_id=1, source_target_pairs={{0,3},{1,0},{2,1},{3,2},{4,7},{5,4},{6,5},{7,6},{8,11},{9,8},{10,9... | collective-permute-start | bytes 1376264 | tf_op jit(solution)/shard_map/ppermute | solution.py:24
  36.0 19.6 %collective-permute-start = (bf16[256,896]{1,0:T(8,128)(2,1)}, bf16[256,896]{1,0:T(8,128)(2,1)}, u32[]{:S(2)}, u32[]{:S(2)}) collective-permute-start(bf16[256,896]{1,0:T(8,128)(2,1)} %bitcast.1.own_ref.refs_0_), channel_id=1, source_target_pairs={{0,64},{64,0},{1,65},{65,1},{2,66},{66,2},{3,67},{67,3},{4,68},{68... | collective-permute-start | bytes 1376264 | tf_op jit(solution)/shard_map/ppermute | solution.py:24
  44.1 20.7 %collective-permute-start.6 = (bf16[256,896]{1,0:T(8,128)(2,1)}, bf16[256,896]{1,0:T(8,128)(2,1)}, u32[]{:S(2)}, u32[]{:S(2)}) collective-permute-start(bf16[256,896]{1,0:T(8,128)(2,1)} %collective-permute-done.5.own_ref.refs_6_), channel_id=1, source_target_pairs={{0,64},{64,0},{1,65},{65,1},{2,66},{66,2},{3,67},{67,3},{4,68},{68... | collective-permute-start | bytes 1376264 | tf_op jit(solution)/shard_map/ppermute | solution.py:24
  53.1 20.1 %collective-permute-start.4 = (bf16[256,896]{1,0:T(8,128)(2,1)}, bf16[256,896]{1,0:T(8,128)(2,1)S(1)}, u32[]{:S(2)}, u32[]{:S(2)}) collective-permute-start(bf16[256,896]{1,0:T(8,128)(2,1)} %collective-permute-done.3.own_ref.refs_4_), channel_id=1, source_target_pairs={{0,64},{64,0},{1,65},{65,1},{2,66},{66,2},{3,67},{67,3},{4,68},{68... | collective-permute-start | bytes 1376264 | tf_op jit(solution)/shard_map/ppermute | solution.py:24
  53.1 28.5 %collective-permute-start.2 = (bf16[256,896]{1,0:T(8,128)(2,1)}, bf16[256,896]{1,0:T(8,128)(2,1)S(1)}, u32[]{:S(2)}, u32[]{:S(2)}) collective-permute-start(bf16[256,896]{1,0:T(8,128)(2,1)} %collective-permute-done.1.own_ref.refs_2_), channel_id=1, source_target_pairs={{0,64},{64,0},{1,65},{65,1},{2,66},{66,2},{3,67},{67,3},{4,68},{68... | collective-permute-start | bytes 1376264 | tf_op jit(solution)/shard_map/ppermute | solution.py:24
  55.7 49.0 %copy-start = (bf16[2048,768]{1,0:T(8,128)(2,1)}, bf16[2048,768]{1,0:T(8,128)(2,1)S(1)}, u32[]{:S(2)}) copy-start(bf16[2048,768]{1,0:T(8,128)(2,1)S(1)} %constant_dynamic-slice_fusion.2.w_ref.refs_8_) | copy-start | bytes 9437188
  73.1 15.5 %copy-start.1 = (bf16[256,896]{1,0:T(8,128)(2,1)}, bf16[256,896]{1,0:T(8,128)(2,1)S(1)}, u32[]{:S(2)}) copy-start(bf16[256,896]{1,0:T(8,128)(2,1)S(1)} %collective-permute-done.4.oth_ref.refs_5_) | copy-start | bytes 1376260
  81.6 8.5 %copy-start.4 = (bf16[256,896]{1,0:T(8,128)(2,1)}, bf16[256,896]{1,0:T(8,128)(2,1)S(1)}, u32[]{:S(2)}) copy-start(bf16[256,896]{1,0:T(8,128)(2,1)S(1)} %collective-permute-done.2.oth_ref.refs_3_) | copy-start | bytes 1376260
  90.1 1.3 collective-permute-start.7
  91.5 5.6 %collective-permute-start.9 = (f32[8,256]{1,0:T(8,128)S(1)}, f32[8,256]{1,0:T(8,128)S(1)}, u32[]{:S(2)}, u32[]{:S(2)}) collective-permute-start(f32[8,256]{1,0:T(8,128)S(1)} %log_add_fusion.2), channel_id=1, source_target_pairs={{0,2},{1,3},{2,0},{3,1},{4,6},{5,7},{6,4},{7,5},{8,10},{9,11},{10,... | collective-permute-start | bytes 24584 | tf_op jit(solution)/shard_map/ppermute | solution.py:24
  93.8 4.9 %collective-permute-start.10 = (f32[8,256]{1,0:T(8,128)S(1)}, f32[8,256]{1,0:T(8,128)S(1)}, u32[]{:S(2)}, u32[]{:S(2)}) collective-permute-start(f32[8,256]{1,0:T(8,128)S(1)} %log_add_fusion.2), channel_id=1, source_target_pairs={{0,1},{1,2},{2,3},{3,0},{4,5},{5,6},{6,7},{7,4},{8,9},{9,10},{10,1... | collective-permute-start | bytes 24584 | tf_op jit(solution)/shard_map/ppermute | solution.py:24
  94.2 4.5 %collective-permute-start.8 = (f32[8,256]{1,0:T(8,128)S(1)}, f32[8,256]{1,0:T(8,128)S(1)}, u32[]{:S(2)}, u32[]{:S(2)}) collective-permute-start(f32[8,256]{1,0:T(8,128)S(1)} %log_add_fusion.2), channel_id=1, source_target_pairs={{0,3},{1,0},{2,1},{3,2},{4,7},{5,4},{6,5},{7,6},{8,11},{9,8},{10,9... | collective-permute-start | bytes 24584 | tf_op jit(solution)/shard_map/ppermute | solution.py:24
  99.4 31.3 %all-to-all-start.1 = ((f32[16,8,256]{2,1,0:T(8,128)}), f32[16,8,256]{2,1,0:T(8,128)S(1)}, u32[]{:S(2)}, u32[]{:S(2)}) async-start(f32[16,8,256]{2,1,0:T(8,128)} %broadcast_in_dim.32), calls=%async_computation.1 | async-start | bytes 262144 | tf_op jit(solution)/shard_map/all_to_all | solution.py:291
  130.8 1.6 copy-start.8
  134.0 11.7 %copy-start.3 = (bf16[256,896]{1,0:T(8,128)(2,1)S(1)}, bf16[256,896]{1,0:T(8,128)(2,1)}, u32[]{:S(2)}) copy-start(bf16[256,896]{1,0:T(8,128)(2,1)} %copy-done.1) | copy-start | bytes 1376260
  134.0 11.7 %copy-start.6 = (bf16[256,896]{1,0:T(8,128)(2,1)S(1)}, bf16[256,896]{1,0:T(8,128)(2,1)}, u32[]{:S(2)}) copy-start(bf16[256,896]{1,0:T(8,128)(2,1)} %copy-done.4) | copy-start | bytes 1376260
  160.1 48.3 %collective-permute-start.15 = (bf16[2048,768]{1,0:T(8,128)(2,1)}, bf16[2048,768]{1,0:T(8,128)(2,1)S(1)}, u32[]{:S(2)}, u32[]{:S(2)}) collective-permute-start(bf16[2048,768]{1,0:T(8,128)(2,1)} %constant_dynamic-slice_fusion), channel_id=1, source_target_pairs={{0,64},{64,0},{1,65},{65,1},{2,66},{66,2},{3,67},{67,3},{4,68},{68... | collective-permute-start | bytes 9437192 | tf_op jit(solution)/shard_map/ppermute | solution.py:24
  161.6 6.5 %collective-permute-start.11 = (bf16[512,896]{1,0:T(8,128)(2,1)S(1)}, bf16[512,896]{1,0:T(8,128)(2,1)S(1)}, u32[]{:S(2)}, u32[]{:S(2)}) collective-permute-start(bf16[512,896]{1,0:T(8,128)(2,1)S(1)} %get-tuple-element.42), channel_id=1, source_target_pairs={{0,64},{64,0},{1,65},{65,1},{2,66},{66,2},{3,67},{67,3},{4,68},{68... | collective-permute-start | bytes 2752520 | tf_op jit(solution)/shard_map/ppermute | solution.py:24
  168.4 12.5 %collective-permute-start.12 = (bf16[128,896]{1,0:T(8,128)(2,1)S(1)}, bf16[128,896]{1,0:T(8,128)(2,1)S(1)}, u32[]{:S(2)}, u32[]{:S(2)}) collective-permute-start(bf16[128,896]{1,0:T(8,128)(2,1)S(1)} %get-tuple-element.47), channel_id=1, source_target_pairs={{0,1},{1,2},{2,3},{3,0},{4,5},{5,6},{6,7},{7,4},{8,9},{9,10},{10,1... | collective-permute-start | bytes 688136 | tf_op jit(solution)/shard_map/ppermute | solution.py:24
  169.1 16.0 %collective-permute-start.14 = (bf16[128,896]{1,0:T(8,128)(2,1)S(1)}, bf16[128,896]{1,0:T(8,128)(2,1)S(1)}, u32[]{:S(2)}, u32[]{:S(2)}) collective-permute-start(bf16[128,896]{1,0:T(8,128)(2,1)S(1)} %get-tuple-element.48), channel_id=1, source_target_pairs={{0,3},{1,0},{2,1},{3,2},{4,7},{5,4},{6,5},{7,6},{8,11},{9,8},{10,9... | collective-permute-start | bytes 688136 | tf_op jit(solution)/shard_map/ppermute | solution.py:24
  174.8 12.1 %collective-permute-start.13 = (bf16[128,896]{1,0:T(8,128)(2,1)S(1)}, bf16[128,896]{1,0:T(8,128)(2,1)S(1)}, u32[]{:S(2)}, u32[]{:S(2)}) collective-permute-start(bf16[128,896]{1,0:T(8,128)(2,1)S(1)} %get-tuple-element.49), channel_id=1, source_target_pairs={{0,2},{1,3},{2,0},{3,1},{4,6},{5,7},{6,4},{7,5},{8,10},{9,11},{10,... | collective-permute-start | bytes 688136 | tf_op jit(solution)/shard_map/ppermute | solution.py:24
  187.8 19.2 %all-to-all-start.2 = ((bf16[16,8,896]{2,1,0:T(8,128)(2,1)}), bf16[16,8,896]{2,1,0:T(8,128)(2,1)S(1)}, u32[]{:S(2)}, u32[]{:S(2)}) async-start(bf16[16,8,896]{2,1,0:T(8,128)(2,1)} %fusion), calls=%async_computation.2 | async-start | bytes 458752 | tf_op jit(solution)/shard_map/all_to_all | solution.py:301
  (7 other events, 9.0 us)

commit v2 on v1

v2 whole, which is shorter than its diff:
```python
import functools

import jax
import jax.numpy as jnp
from jax import lax
from jax.experimental import pallas as pl
from jax.experimental.pallas import tpu as pltpu
from jax.sharding import Mesh, PartitionSpec as P

AXES = ("xh", "core", "xl", "z", "y")
SIZES = {"xh": 2, "core": 2, "xl": 2, "z": 8, "y": 4}
EXTRA = 128
POS = 5
LO, MID, HI, CNT = 0, 8, 16, 24
VMEM = pl.BlockSpec(memory_space=pltpu.VMEM)
SMEM = pl.BlockSpec(memory_space=pltpu.SMEM)
NT = (((1,), (1,)), ((), ()))
TN = (((0,), (0,)), ((), ()))
LCH = 256
PROD = 1024
EXPO = 128


def shift(x, axis, step):
    n = SIZES[axis]
    return lax.ppermute(x, axis, [(i, (i + step) % n) for i in range(n)])


def scores_kernel(own_ref, oth_ref, w_ref, e_ref, m_ref, l_ref, s_ref, qt_ref):
    labels, width = w_ref.shape
    rows = own_ref.shape[0]
    both = 2 * rows
    qt_ref[:, :rows] = own_ref[:, :width].T
    qt_ref[:, rows:] = oth_ref[:, :width].T

    def product(i, top):
        at = pl.multiple_of(i * PROD, PROD)
        s = jnp.dot(w_ref[pl.ds(at, PROD), :], qt_ref[...], preferred_element_type=jnp.float32)
        s_ref[pl.ds(at, PROD), :] = s
        return jnp.maximum(top, jnp.max(s.reshape(PROD // 16, 16, both), 0))

    top = lax.fori_loop(0, labels // PROD, product, jnp.full((16, both), -1e30, jnp.float32))
    top = jnp.max(top, 0, keepdims=True)

    def expo(i, total):
        at = pl.multiple_of(i * EXPO, EXPO)
        e = jnp.exp(s_ref[pl.ds(at, EXPO), :] - top)
        e_ref[pl.ds(at, EXPO), :] = e.astype(jnp.bfloat16)
        return total + jnp.sum(e.reshape(EXPO // 16, 16, both), 0)

    total = lax.fori_loop(0, labels // EXPO, expo, jnp.zeros((16, both), jnp.float32))
    m_ref[...] = top
    l_ref[...] = top + jnp.log(jnp.sum(total, 0, keepdims=True))


def scores_call(own, oth, w):
    rows = own.shape[0]
    labels, width = w.shape
    line = jax.ShapeDtypeStruct((1, 2 * rows), jnp.float32)
    return pl.pallas_call(
        scores_kernel,
        out_shape=(jax.ShapeDtypeStruct((labels, 2 * rows), jnp.bfloat16), line, line),
        in_specs=[VMEM] * 3,
        out_specs=(VMEM,) * 3,
        scratch_shapes=[pltpu.VMEM((labels, 2 * rows), jnp.float32), pltpu.VMEM((width, 2 * rows), jnp.bfloat16)],
        compiler_params=pltpu.CompilerParams(vmem_limit_bytes=18 * 2**20),
        cost_estimate=pl.CostEstimate(flops=4 * rows * labels * width, bytes_accessed=labels * rows * 4, transcendentals=2 * rows * labels),
        name="scores",
    )(own, oth, w)


def hits_kernel(base_ref, *refs):
    blocks = refs[:8]
    w_ref, n_ref, key_ref, s_ref, t_ref = refs[8:]
    labels, width = w_ref.shape
    base = base_ref[0].astype(jnp.float32)
    row = lax.broadcasted_iota(jnp.int32, (8, EXTRA), 0)
    col = lax.broadcasted_iota(jnp.int32, (8, EXTRA), 1)
    digits = jnp.where(col == row + LO, 1.0, jnp.where(col == row + MID, 128.0, jnp.where(col == row + HI, 16384.0, 0.0)))
    digits = jnp.where(row < POS, digits, 0.0).astype(jnp.bfloat16)
    counting = jnp.where(col == CNT, 1.0, 0.0).astype(jnp.bfloat16)
    big = 1e9
    rows = blocks[0].shape[0]
    slot = lax.broadcasted_iota(jnp.int32, (8, rows), 0)
    lane = lax.broadcasted_iota(jnp.int32, (8, rows), 1)
    keys, weights, most = [], [], jnp.int32(0)
    for b, q_ref in enumerate(blocks):
        extra = q_ref[:, width:]
        ids = lax.dot_general(digits, extra, NT, preferred_element_type=jnp.float32)
        cnt = lax.dot_general(counting, extra, NT, preferred_element_type=jnp.float32)
        valid = (slot.astype(jnp.float32) < cnt) & (slot < POS)
        ids = jnp.where(valid, ids, -1.0)
        same = jnp.zeros((8, rows), jnp.float32)
        again = jnp.zeros((8, rows), jnp.float32)
        for j in range(POS):
            eq = jnp.where(ids == ids[j:j + 1, :], 1.0, 0.0)
            same = same + eq
            again = again + jnp.where(slot > j, eq, 0.0)
        local = ids - base
        hit = valid & (local >= 0.0) & (local < float(labels)) & (again == 0.0)
        weights.append(same / cnt)
        keys.append(jnp.where(hit, (lane * 8 + slot).astype(jnp.float32) * float(labels) + local, big))
        n = jnp.sum(jnp.where(hit, 1.0, 0.0)).astype(jnp.int32)
        n_ref[b] = n
        most = jnp.maximum(most, n)
    r16 = lax.broadcasted_iota(jnp.int32, (16, 16), 0)
    c16 = lax.broadcasted_iota(jnp.int32, (16, 16), 1)

    def step(i, keys):
        left = []
        for b in range(8):
            kf = jnp.min(keys[b])
            this = keys[b] == kf
            k = jnp.where(kf < big, kf, 0.0).astype(jnp.int32)
            label = k & (labels - 1)
            query = lax.div(k, 8 * labels)
            qat = pl.multiple_of((query >> 4) << 4, 16)
            lat = pl.multiple_of((label >> 4) << 4, 16)
            s16 = lax.dot_general(blocks[b][pl.ds(qat, 16), :width], w_ref[pl.ds(lat, 16), :], NT, preferred_element_type=jnp.float32)
            at = b * rows * POS + i
            key_ref[at] = k
            s_ref[at] = jnp.sum(jnp.where((r16 == query - qat) & (c16 == label - lat), s16, 0.0))
            t_ref[at] = jnp.sum(jnp.where(this, weights[b], 0.0))
            left.append(jnp.where(this, big, keys[b]))
        return tuple(left)

    lax.fori_loop(0, most, step, tuple(keys))


def hits_call(base, blocks, w):
    total = 8 * blocks[0].shape[0] * POS
    return pl.pallas_call(
        hits_kernel,
        out_shape=(
            jax.ShapeDtypeStruct((8,), jnp.int32),
            jax.ShapeDtypeStruct((total,), jnp.int32),
            jax.ShapeDtypeStruct((total,), jnp.float32),
            jax.ShapeDtypeStruct((total,), jnp.float32),
        ),
        in_specs=[SMEM] + [VMEM] * 9,
        out_specs=(SMEM,) * 4,
        compiler_params=pltpu.CompilerParams(vmem_limit_bytes=16 * 2**20),
        cost_estimate=pl.CostEstimate(flops=10**9, bytes_accessed=2**23, transcendentals=0),
        name="hits",
    )(base, *blocks, w)


def query_kernel(at_ref, n_ref, key_ref, s_ref, t_ref, lse_ref, m_ref, e0, e1, e2, e3, w_ref, p0, p1, p2, p3, own_ref, oth_ref, pos_ref):
    labels, width = w_ref.shape
    rows = e0.shape[1] // 2
    xh, y = at_ref[0], at_ref[1]
    half = rows // 2
    ps = (p0, p1, p2, p3)
    pos_ref[...] = jnp.zeros_like(pos_ref)
    for d, (e_ref, p_ref) in enumerate(zip((e0, e1, e2, e3), ps)):
        scale = jnp.exp(m_ref[d:d + 1, :] - lse_ref[d:d + 1, :])

        def scaled(i, carry):
            at = pl.multiple_of(i * 64, 64)
            p_ref[pl.ds(at, 64), :] = (e_ref[pl.ds(at, 64), :].astype(jnp.float32) * scale).astype(jnp.bfloat16)
            return carry

        lax.fori_loop(0, labels // 64, scaled, 0)

    r = lax.broadcasted_iota(jnp.int32, (16, half), 0)
    c = lax.broadcasted_iota(jnp.int32, (16, half), 1)
    c1 = lax.broadcasted_iota(jnp.int32, (1, EXTRA), 1)
    most = n_ref[0]
    for b in range(1, 8):
        most = jnp.maximum(most, n_ref[b])

    def patch(i, carry):
        todo = []
        for b in range(8):
            d, k = b // 2, b % 2
            at = b * rows * POS + i
            live = i < n_ref[b]
            key, s, weight = key_ref[at], s_ref[at], t_ref[at]
            label = key & (labels - 1)
            rest = lax.div(key, labels)
            slot = rest & 7
            query = rest >> 3
            lat = pl.multiple_of((label >> 4) << 4, 16)
            qhi = lax.div(query, half)
            qlo = query & (half - 1)
            qat = pl.multiple_of(k * rows + qhi * half, half)
            spot = (pl.ds(lat, 16), pl.ds(qat, half))
            value = jnp.exp(s - lse_ref[d:d + 1, pl.ds(qat, half)]) - weight
            row = jnp.where(live, label - lat, -1)
            old = ps[d][spot].astype(jnp.float32)
            new = jnp.where((r == row) & (c == qlo), value, old).astype(jnp.bfloat16)
            full = jnp.full((1, EXTRA), s * weight, jnp.float32)
            high = full.astype(jnp.bfloat16).astype(jnp.float32)
            mid = (full - high).astype(jnp.bfloat16).astype(jnp.float32)
            low = full - high - mid
            put = jnp.where(c1 == slot, high, jnp.where(c1 == slot + 8, mid, jnp.where(c1 == slot + 16, low, 0.0)))
            put = jnp.where(jnp.logical_and(live, qhi == xh), put, 0.0)
            into = (k, pl.ds(d * half + qlo, 1), slice(None))
            todo.append((d, spot, new, into, pos_ref[into] + put))
        for d, spot, new, into, pos in todo:
            ps[d][spot] = new
            pos_ref[into] = pos
        return carry

    lax.fori_loop(0, most, patch, 0)
    for d, p_ref in enumerate(ps):
        both = jnp.concatenate([p_ref[:, pl.ds(pl.multiple_of(k * rows + xh * half, half), half)] for k in range(2)], 1)
        u = lax.dot_general(both, w_ref[...], TN, preferred_element_type=jnp.float32)
        to = pl.ds(pl.multiple_of(((y + d) & 3) * half, half), half)
        for k, out in enumerate((own_ref, oth_ref)):
            out[to, :width] = u[k * half:(k + 1) * half].astype(jnp.bfloat16)
            out[to, width:] = pos_ref[k, d * half:(d + 1) * half, :].astype(jnp.bfloat16)


def query_call(at, hits, lse, m, es, w):
    labels, width = w.shape
    rows = es[0].shape[1] // 2
    out = jax.ShapeDtypeStruct((2 * rows, width + EXTRA), jnp.bfloat16)
    res = pl.pallas_call(
        query_kernel,
        out_shape=tuple(jax.ShapeDtypeStruct(e.shape, e.dtype) for e in es) + (out, out),
        in_specs=[SMEM] * 5 + [VMEM] * 7,
        out_specs=(VMEM,) * 6,
        scratch_shapes=[pltpu.VMEM((2, 2 * rows, EXTRA), jnp.float32)],
        input_output_aliases={7 + d: d for d in range(4)},
        compiler_params=pltpu.CompilerParams(vmem_limit_bytes=28 * 2**20),
        cost_estimate=pl.CostEstimate(flops=8 * rows * labels * width, bytes_accessed=2**24, transcendentals=0),
        name="query_part",
    )(at, *hits, lse, m, *es, w)
    return res[:4], res[4], res[5]


def class_kernel(core_ref, p0, p1, p2, p3, *refs):
    blocks = refs[:8]
    out_ref, mine_ref = refs[8:]
    rows = blocks[0].shape[0]
    width = out_ref.shape[1]
    acc = None
    for d, p_ref in enumerate((p0, p1, p2, p3)):
        for k in range(2):
            term = jnp.dot(p_ref[:, k * rows:(k + 1) * rows], blocks[2 * d + k][:, :width], preferred_element_type=jnp.float32)
            acc = term if acc is None else acc + term
    done = acc.astype(jnp.bfloat16)
    out_ref[...] = done
    mine_ref[...] = done


def class_call(core, ps, blocks, width):
    labels = ps[0].shape[0]
    steps = labels // LCH
    rows = blocks[0].shape[0]
    whole = lambda i, c: (0, 0)
    return pl.pallas_call(
        class_kernel,
        out_shape=tuple(jax.ShapeDtypeStruct((n * labels, width), jnp.bfloat16) for n in (2, 1)),
        grid_spec=pltpu.PrefetchScalarGridSpec(
            num_scalar_prefetch=1,
            grid=(steps,),
            in_specs=[pl.BlockSpec((LCH, 2 * rows), lambda i, c: (i, 0))] * 4 + [pl.BlockSpec(blocks[0].shape, whole)] * 8,
            out_specs=(pl.BlockSpec((LCH, width), lambda i, c: (c[0] * steps + i, 0)), pl.BlockSpec((LCH, width), lambda i, c: (i, 0))),
        ),
        compiler_params=pltpu.CompilerParams(vmem_limit_bytes=18 * 2**20),
        cost_estimate=pl.CostEstimate(flops=16 * rows * labels * width, bytes_accessed=2**24, transcendentals=0),
        name="class_part",
    )(core, *ps, *blocks)


def lse_of(parts, axis=None):
    if axis is None:
        top = functools.reduce(jnp.maximum, parts)
        return top + jnp.log(functools.reduce(jnp.add, [jnp.exp(p - top) for p in parts]))
    top = jnp.max(parts, axis)
    return top + jnp.log(jnp.sum(jnp.exp(parts - jnp.expand_dims(top, axis)), axis))


def body(embeddings, classifier, positives, counts):
    q_dev, width = embeddings.shape
    labels = classifier.shape[0] // 2
    xh, core, xl, z, y = (lax.axis_index(a) for a in AXES)
    rank = (xl * 8 + z) * 4 + y
    base = (rank * 2 + core) * labels

    blank = jnp.zeros((q_dev, 8 - POS), jnp.int32)
    extra = jnp.concatenate(
        [positives & 127, blank, (positives >> 7) & 127, blank, positives >> 14, blank, counts[:, None], jnp.zeros((q_dev, EXTRA - CNT - 1), jnp.int32)],
        1,
    ).astype(jnp.bfloat16)
    sent = jnp.concatenate([embeddings, extra], 1)
    copies = jnp.broadcast_to(sent[None], (32, q_dev, width + EXTRA)).reshape(32 * q_dev, width + EXTRA)
    mine = lax.all_to_all(copies, ("xh", "xl", "z"), 0, 0, tiled=True)
    own = [mine] + [shift(mine, "y", -d) for d in range(1, 4)]
    oth = [shift(b, "core", 1) for b in own]
    w = lax.dynamic_slice_in_dim(classifier, core * labels, labels)
    rows = mine.shape[0]

    oth, parts, after = [None] * 4, [None] * 4, None
    for turn in ((0,), (3,), (1, 2)):
        for d in turn:
            if after is not None:
                own[d], _ = lax.optimization_barrier((own[d], after))
            oth[d] = shift(own[d], "core", 1)
        for d in turn:
            parts[d] = scores_call(own[d], oth[d], w)
        after = parts[turn[-1]][1]
    es, ms, ls = zip(*parts)
    blocks = [b for pair in zip(own, oth) for b in pair]
    hits = hits_call(base[None], blocks, w)
    m = jnp.concatenate(ms, 0)
    stat = jnp.concatenate(ls, 0)
    stat = lse_of([stat, jnp.roll(shift(stat, "core", 1), rows, 1)])
    stat = lse_of([stat] + [jnp.roll(shift(stat, "y", -d), d, 0) for d in range(1, 4)])
    stat = stat.reshape(8, rows)
    lse = lse_of(lax.all_to_all(jnp.broadcast_to(stat[None], (16, 8, rows)), ("xl", "z"), 0, 0, tiled=True), 0)

    ps, u_own, u_oth = query_call(jnp.stack([xh, y]), hits, lse.reshape(4, 2 * rows), m, es, w)
    f32 = lambda a: a.astype(jnp.float32)
    u = (f32(u_own) + f32(shift(u_oth, "core", 1))).astype(jnp.bfloat16)
    first, u = lax.optimization_barrier((ps[0], u))
    got = lax.all_to_all(u, ("y", "xl", "z"), 0, 0, tiled=True)
    halves, mine_half = class_call(core[None], (first,) + tuple(ps[1:]), blocks, width)

    final = jnp.sum(f32(got).reshape(64, q_dev, width + EXTRA), 0)
    query_grad = final[:, :width].astype(jnp.bfloat16)
    pos_mean = jnp.sum(final[:, width:width + 24], 1)
    at = ((xh * 2 + xl) * 8 + z) * q_dev
    loss = lax.dynamic_slice(lse, (0, at), (1, q_dev))[0] - pos_mean
    class_grad = lax.dynamic_update_slice_in_dim(halves, shift(mine_half, "core", 1), (1 - core) * labels, 0)
    return loss, query_grad, class_grad


def solution(mesh):
    fine = Mesh(mesh.devices.reshape(tuple(SIZES[a] for a in AXES)), AXES)
    split = P(AXES, None)
    lab = P(("xl", "z", "y"), None)
    return jax.shard_map(
        body,
        mesh=fine,
        in_specs=(split, lab, split, P(AXES)),
        out_specs=(P(AXES), split, lab),
        check_vma=False,
    )
```

time: 209 us -> 204 us (0.976); the launches traced: 210 us -> 202 us
  starting transfers between devices: 36.4 us -> 23.8 us
  Pallas kernels: 75.2 us -> 64.8 us
  waiting for transfers between devices: 46.5 us -> 53.6 us
  local copies, waits for them, and re-layouts: 20.7 us -> 26.6 us
    all_to_all x1, waiting for transfers between devices: 9.46 us -> 26.6 us  [body(): got = lax.all_to_all(u, ('y', 'xl', 'z'), 0, 0, tiled=True)]
    pallas_call x4, Pallas kernels: 28.9 us -> 14.2 us  [scores_call(): pl.pallas_call(scores_kernel, out_shape=(jax.ShapeDtypeStruct((labels, 2...]
    ppermute x16 -> x13, starting transfers between devices: 21.4 us -> 9.92 us  [shift(): return lax.ppermute(x, axis, [(i, (i + step) % n) for i in range(n)])]
    ppermute x16 -> x13, waiting for transfers between devices: 37 us -> 27 us  [shift(): return lax.ppermute(x, axis, [(i, (i + step) % n) for i in range(n)])]
    unnamed x26 -> x50, local copies, waits for them, and re-layouts: 10.6 us -> 18.4 us
    pallas_call x1, Pallas kernels: 24 us -> 30.8 us  [hits_call(): pl.pallas_call(hits_kernel, out_shape=(jax.ShapeDtypeStruct((8,), jnp.int...]
    dynamic_slice x1 -> x0, local copies, waits for them, and re-layouts: 3.72 us -> none  [body(): mine_half = lax.dynamic_slice_in_dim(halves, core * labels, labels)]
  transfers between devices with their start and end apart: 18 -> 15, of which waited for: 9 -> 9; matrix products, arithmetic and copies ran while one was open for 2% -> 2% of each run, Pallas kernels for 22% -> 21%
where the time goes in v2:
time: 204 us; the launch traced here: 202 us
  Pallas kernels  64.8 us (32%)
  waiting for transfers between devices  53.6 us (26%)
  blocking collectives  27.3 us (13%)
  local copies, waits for them, and re-layouts  26.6 us (13%)
  starting transfers between devices  23.8 us (12%)
  other arithmetic  4.85 us (2%)
    pallas_call x1, Pallas kernels, hits_call(): pl.pallas_call(hits_kernel, out_shape=(jax.ShapeDtypeStruct((8,), jnp.int...  30.8 us
    all_to_all x1, blocking collectives, body(): mine = lax.all_to_all(copies, ('xh', 'xl', 'z'), 0, 0, tiled=True)  27.3 us
    ppermute x13, waiting for transfers between devices, shift(): return lax.ppermute(x, axis, [(i, (i + step) % n) for i in range(n)])  27 us
    all_to_all x1, waiting for transfers between devices, body(): got = lax.all_to_all(u, ('y', 'xl', 'z'), 0, 0, tiled=True)  26.6 us
    unnamed x50, local copies, waits for them, and re-layouts  18.4 us
    pallas_call x4, Pallas kernels, scores_call(): pl.pallas_call(scores_kernel, out_shape=(jax.ShapeDtypeStruct((labels, 2...  14.2 us
    pallas_call x1, Pallas kernels, class_call(): pl.pallas_call(class_kernel, out_shape=tuple((jax.ShapeDtypeStruct((n * l...  10.1 us
    ppermute x13, starting transfers between devices, shift(): return lax.ppermute(x, axis, [(i, (i + step) % n) for i in range(n)])  9.92 us
  transfers between devices with their start and end apart: 15, of which 9 were waited for; matrix products, arithmetic and copies ran while one was open for 2% of the time, Pallas kernels for 21%

profile of v2, /device:TPU:32, one launch (start us, length us, event | category | flops | bytes accessed | tf_op | source)
XLA Modules:
  0.0 201.9 jit_solution(8774151251558973043)
XLA Ops:
  2.9 27.3 %all_to_all.22 = bf16[32,8,896]{2,1,0:T(8,128)(2,1)} all-to-all(bf16[32,8,896]{2,1,0:T(8,128)(2,1)S(1)} %broadcast_in_dim.27), channel_id=1, replica_groups=mesh['xh'=2,'core'=2,'xl'=2,'z'=8,'y'=4] {'xh','xl','z'}, dimensions={0} | all-to-all | bytes 917504 | tf_op jit(solution)/shard_map/all_to_all | solution.py:290
  31.8 2.1 %constant_dynamic-slice_fusion.1.w_ref.refs_8_ = bf16[2048,768]{1,0:T(8,128)(2,1)S(1)} fusion(bf16[4096,768]{1,0:T(8,128)(2,1)} %param.5, s32[]{:T(128)S(6)} %select_n.9), kind=kLoop, calls=%fused_computation.23 | loop fusion | bytes 6291460 | tf_op jit(solution)/shard_map/dynamic_slice | solution.py:293
  33.9 4.1 %scores.4 = (bf16[2048,512]{1,0:T(8,128)(2,1)S(1)}, f32[1,512]{1,0:T(1,128)S(1)}, f32[1,512]{1,0:T(1,128)S(1)}) custom-call(bf16[256,896]{1,0:T(8,128)(2,1)} %bitcast.1.own_ref.refs_0_, bf16[256,896]{1,0:T(8,128)(2,1)} %collective-permute-done.oth_ref.refs_1_, bf16[2048,768]{1,0:T(8,128)(2,1)S(1)} %constant_dynamic-slice_fusion.1.w_ref.refs_8_), custom_call_target="tpu_custom_call" | custom-call | flops 1610612736 | bytes 2097152 | tf_op jit(solution)/shard_map/scores/pallas_call | solution.py:60
  39.4 5.4 %collective-permute-done.2.own_ref.refs_6_ = bf16[256,896]{1,0:T(8,128)(2,1)} collective-permute-done((bf16[256,896]{1,0:T(8,128)(2,1)}, bf16[256,896]{1,0:T(8,128)(2,1)}, u32[]{:S(2)}, u32[]{:S(2)}) %collective-permute-start.2) | collective-permute-done | bytes 458784 | tf_op jit(solution)/shard_map/ppermute | solution.py:26
  44.7 1.9 collective-permute-start.5
  47.7 4.1 %scores.5 = (bf16[2048,512]{1,0:T(8,128)(2,1)S(1)}, f32[1,512]{1,0:T(1,128)S(1)}, f32[1,512]{1,0:T(1,128)S(1)}) custom-call(bf16[256,896]{1,0:T(8,128)(2,1)} %collective-permute-done.2.own_ref.refs_6_, bf16[256,896]{1,0:T(8,128)(2,1)S(1)} %collective-permute-done.3.oth_ref.refs_7_, bf16[2048,768]{1,0:T(8,128)(2,1)S(1)} %constant_dynamic-slice_fusion.1.w_ref.refs_8_), custom_call_target="tpu_custom_call" | custom-call | flops 1610612736 | bytes 2097152 | tf_op jit(solution)/shard_map/scores/pallas_call | solution.py:60
  53.2 6.1 %collective-permute-done.5.own_ref.refs_4_ = bf16[256,896]{1,0:T(8,128)(2,1)S(1)} collective-permute-done((bf16[256,896]{1,0:T(8,128)(2,1)}, bf16[256,896]{1,0:T(8,128)(2,1)S(1)}, u32[]{:S(2)}, u32[]{:S(2)}) %collective-permute-start.5) | collective-permute-done | bytes 458784 | tf_op jit(solution)/shard_map/ppermute | solution.py:26
  59.4 8.9 %collective-permute-done.1.own_ref.refs_2_ = bf16[256,896]{1,0:T(8,128)(2,1)S(1)} collective-permute-done((bf16[256,896]{1,0:T(8,128)(2,1)}, bf16[256,896]{1,0:T(8,128)(2,1)S(1)}, u32[]{:S(2)}, u32[]{:S(2)}) %collective-permute-start.1) | collective-permute-done | bytes 458784 | tf_op jit(solution)/shard_map/ppermute | solution.py:26
  68.4 3.0 %scores.7 = (bf16[2048,512]{1,0:T(8,128)(2,1)S(1)}, f32[1,512]{1,0:T(1,128)S(1)}, f32[1,512]{1,0:T(1,128)S(1)}) custom-call(bf16[256,896]{1,0:T(8,128)(2,1)S(1)} %collective-permute-done.5.own_ref.refs_4_, bf16[256,896]{1,0:T(8,128)(2,1)S(1)} %collective-permute-done.6.oth_ref.refs_5_, bf16[2048,768]{1,0:T(8,128)(2,1)S(1)} %constant_dynamic-slice_fusion.1.w_ref.refs_8_), custom_call_target="tpu_custom_call" | custom-call | flops 1610612736 | bytes 2097152 | tf_op jit(solution)/shard_map/scores/pallas_call | solution.py:60
  72.7 3.0 %scores.6 = (bf16[2048,512]{1,0:T(8,128)(2,1)S(1)}, f32[1,512]{1,0:T(1,128)S(1)}, f32[1,512]{1,0:T(1,128)S(1)}) custom-call(bf16[256,896]{1,0:T(8,128)(2,1)S(1)} %collective-permute-done.1.own_ref.refs_2_, bf16[256,896]{1,0:T(8,128)(2,1)S(1)} %collective-permute-done.4.oth_ref.refs_3_, bf16[2048,768]{1,0:T(8,128)(2,1)S(1)} %constant_dynamic-slice_fusion.1.w_ref.refs_8_), custom_call_target="tpu_custom_call" | custom-call | flops 1610612736 | bytes 2097152 | tf_op jit(solution)/shard_map/scores/pallas_call | solution.py:60
  79.8 2.9 %collective-permute-start.9 = (f32[4,512]{1,0:T(4,128)S(1)}, f32[4,512]{1,0:T(4,128)S(1)}, u32[]{:S(2)}, u32[]{:S(2)}) collective-permute-start(f32[4,512]{1,0:T(4,128)S(1)} %get-tuple-element.62), channel_id=1, source_target_pairs={{0,2},{1,3},{2,0},{3,1},{4,6},{5,7},{6,4},{7,5},{8,10},{9,11},{10,... | collective-permute-start | bytes 24584 | tf_op jit(solution)/shard_map/ppermute | solution.py:26
  87.1 3.9 %all-to-all-start.1 = ((f32[16,8,256]{2,1,0:T(8,128)}), f32[16,8,256]{2,1,0:T(8,128)S(1)}, u32[]{:S(2)}, u32[]{:S(2)}) async-start(f32[16,8,256]{2,1,0:T(8,128)} %broadcast_in_dim.28), calls=%async_computation.1 | async-start | bytes 262144 | tf_op jit(solution)/shard_map/all_to_all | solution.py:313
  96.2 30.8 %hits.1 = (s32[8]{0:T(128)S(1)}, s32[10240]{0:T(1024)S(1)}, f32[10240]{0:T(1024)S(1)}, f32[10240]{0:T(1024)S(1)}) custom-call(s32[1]{0:T(128)} %bitcast.5.base_ref, bf16[256,896]{1,0:T(8,128)(2,1)} %bitcast.1.own_ref.refs_0_, bf16[256,896]{1,0:T(8,128)(2,1)} %collective-permute-done.oth_ref.refs_1_, bf16[256,896]{1,0:T(8,128)(2,1)S(1)} %copy-done.7, ...), custom_call_target="tpu_custom_call" | custom-call | flops 1000000000 | bytes 8388608 | tf_op jit(solution)/shard_map/hits/pallas_call | solution.py:132
  127.2 1.6 copy-done.16
  128.8 1.6 copy-done.18
  130.4 1.6 copy-done.22
  131.9 1.6 copy-done.24
  133.5 9.7 %query_part.1 = (bf16[2048,512]{1,0:T(8,128)(2,1)S(1)}, bf16[2048,512]{1,0:T(8,128)(2,1)S(1)}, bf16[2048,512]{1,0:T(8,128)(2,1)S(1)}, bf16[2048,512]{1,0:T(8,128...) custom-call(s32[2]{0:T(128)S(1)} %pad_add_fusion.at_ref, ...), custom_call_target="tpu_custom_call", output_to_operand_aliasing={{0}: (7, {}), {1}: (8, {}), {2}: (9, {}), {3}: (10, {})} | custom-call | flops 3221225472 | bytes 16777216 | tf_op jit(solution)/shard_map/query_part/pallas_call | solution.py:219
  143.4 2.5 %collective-permute-done.11 = bf16[512,896]{1,0:T(8,128)(2,1)S(1)} collective-permute-done((bf16[512,896]{1,0:T(8,128)(2,1)S(1)}, bf16[512,896]{1,0:T(8,128)(2,1)S(1)}, u32[]{:S(2)}, u32[]{:S(2)}) %collective-permute-start.11) | collective-permute-done | bytes 917536 | tf_op jit(solution)/shard_map/ppermute | solution.py:26
  147.1 1.6 copy-done.20
  148.7 10.1 %class_part.1 = (bf16[4096,768]{1,0:T(8,128)(2,1)}, bf16[2048,768]{1,0:T(8,128)(2,1)S(1)}) custom-call(s32[1]{0:T(128)} %bitcast.7.core_ref, bf16[2048,512]{1,0:T(8,128)(2,1)S(1)} %get-tuple-element.55.p0, bf16[2048,512]{1,0:T(8,128)(2,1)S(1)} %get-tuple-element.56.p1, bf16[2048,512]{1,0:T(8,128)(2,1)S(1)} %get-tuple-element.57.p2, ...), custom_call_target="tpu_custom_call" | custom-call | flops 6442450944 | bytes 16777216 | tf_op jit(solution)/shard_map/class_part/pallas_call | solution.py:253
  158.9 9.9 %all-to-all-start.2 = ((bf16[64,8,896]{2,1,0:T(8,128)(2,1)}), bf16[64,8,896]{2,1,0:T(8,128)(2,1)}, u32[]{:S(2)}, u32[]{:S(2)}) async-start(bf16[64,8,896]{2,1,0:T(8,128)(2,1)} %bitcast.13), calls=%async_computation.2 | async-start | bytes 1835008 | tf_op jit(solution)/shard_map/all_to_all | solution.py:319
  168.8 26.6 %all-to-all-done.2 = bf16[64,8,896]{2,1,0:T(8,128)(2,1)} async-done(((bf16[64,8,896]{2,1,0:T(8,128)(2,1)}), bf16[64,8,896]{2,1,0:T(8,128)(2,1)}, u32[]{:S(2)}, u32[]{:S(2)}) %all-to-all-start.2) | async-done | bytes 917536 | tf_op jit(solution)/shard_map/all_to_all | solution.py:319
  198.1 3.8 %constant_dynamic-update-slice_fusion = bf16[4096,768]{1,0:T(8,128)(2,1)} fusion(bf16[4096,768]{1,0:T(8,128)(2,1)} %get-tuple-element.59, bf16[2048,768]{1,0:T(8,128)(2,1)} %collective-permute-done.12, s32[]{:T(128)S(6)} %select_n.11), kind=kLoop, calls=%fused_computation.21 | loop fusion | bytes 6291460 | tf_op jit(solution)/shard_map/dynamic_update_slice | solution.py:327
  (101 shorter events, 26.8 us)
Async XLA Ops:
  30.2 3.7 %collective-permute-start = (bf16[256,896]{1,0:T(8,128)(2,1)}, bf16[256,896]{1,0:T(8,128)(2,1)}, u32[]{:S(2)}, u32[]{:S(2)}) collective-permute-start(bf16[256,896]{1,0:T(8,128)(2,1)} %bitcast.1.own_ref.refs_0_), channel_id=1, source_target_pairs={{0,64},{64,0},{1,65},{65,1},{2,66},{66,2},{3,67},{67,3},{4,68},{68... | collective-permute-start | bytes 1376264 | tf_op jit(solution)/shard_map/ppermute | solution.py:26
  30.2 14.5 %collective-permute-start.2 = (bf16[256,896]{1,0:T(8,128)(2,1)}, bf16[256,896]{1,0:T(8,128)(2,1)}, u32[]{:S(2)}, u32[]{:S(2)}) collective-permute-start(bf16[256,896]{1,0:T(8,128)(2,1)} %bitcast.1.own_ref.refs_0_), channel_id=1, source_target_pairs={{0,1},{1,2},{2,3},{3,0},{4,5},{5,6},{6,7},{7,4},{8,9},{9,10},{10,1... | collective-permute-start | bytes 1376264 | tf_op jit(solution)/shard_map/ppermute | solution.py:26
  44.7 3.0 %collective-permute-start.3 = (bf16[256,896]{1,0:T(8,128)(2,1)}, bf16[256,896]{1,0:T(8,128)(2,1)S(1)}, u32[]{:S(2)}, u32[]{:S(2)}) collective-permute-start(bf16[256,896]{1,0:T(8,128)(2,1)} %collective-permute-done.2.own_ref.refs_6_), channel_id=1, source_target_pairs={{0,64},{64,0},{1,65},{65,1},{2,66},{66,2},{3,67},{67,3},{4,68},{68... | collective-permute-start | bytes 1376264 | tf_op jit(solution)/shard_map/ppermute | solution.py:26
  44.7 14.6 %collective-permute-start.5 = (bf16[256,896]{1,0:T(8,128)(2,1)}, bf16[256,896]{1,0:T(8,128)(2,1)S(1)}, u32[]{:S(2)}, u32[]{:S(2)}) collective-permute-start(bf16[256,896]{1,0:T(8,128)(2,1)} %bitcast.1.own_ref.refs_0_), channel_id=1, source_target_pairs={{0,2},{1,3},{2,0},{3,1},{4,6},{5,7},{6,4},{7,5},{8,10},{9,11},{10,... | collective-permute-start | bytes 1376264 | tf_op jit(solution)/shard_map/ppermute | solution.py:26
  46.7 21.7 %collective-permute-start.1 = (bf16[256,896]{1,0:T(8,128)(2,1)}, bf16[256,896]{1,0:T(8,128)(2,1)S(1)}, u32[]{:S(2)}, u32[]{:S(2)}) collective-permute-start(bf16[256,896]{1,0:T(8,128)(2,1)} %bitcast.1.own_ref.refs_0_), channel_id=1, source_target_pairs={{0,3},{1,0},{2,1},{3,2},{4,7},{5,4},{6,5},{7,6},{8,11},{9,8},{10,9... | collective-permute-start | bytes 1376264 | tf_op jit(solution)/shard_map/ppermute | solution.py:26
  47.7 4.2 %copy-start = (bf16[256,896]{1,0:T(8,128)(2,1)}, bf16[256,896]{1,0:T(8,128)(2,1)S(1)}, u32[]{:S(2)}) copy-start(bf16[256,896]{1,0:T(8,128)(2,1)S(1)} %collective-permute-done.3.oth_ref.refs_7_) | copy-start | bytes 1376260
  59.4 11.9 %copy-start.3 = (bf16[256,896]{1,0:T(8,128)(2,1)}, bf16[256,896]{1,0:T(8,128)(2,1)S(1)}, u32[]{:S(2)}) copy-start(bf16[256,896]{1,0:T(8,128)(2,1)S(1)} %collective-permute-done.5.own_ref.refs_4_) | copy-start | bytes 1376260
  59.4 9.0 %collective-permute-start.6 = (bf16[256,896]{1,0:T(8,128)(2,1)S(1)}, bf16[256,896]{1,0:T(8,128)(2,1)S(1)}, u32[]{:S(2)}, u32[]{:S(2)}) collective-permute-start(bf16[256,896]{1,0:T(8,128)(2,1)S(1)} %collective-permute-done.5.own_ref.refs_4_), channel_id=1, source_target_pairs={{0,64},{64,0},{1,65},{65,1},{2,66},{66,2},{3,67},{67,3},{4,68},{68... | collective-permute-start | bytes 1376264 | tf_op jit(solution)/shard_map/ppermute | solution.py:26
  68.3 4.4 %copy-start.6 = (bf16[256,896]{1,0:T(8,128)(2,1)}, bf16[256,896]{1,0:T(8,128)(2,1)S(1)}, u32[]{:S(2)}) copy-start(bf16[256,896]{1,0:T(8,128)(2,1)S(1)} %collective-permute-done.1.own_ref.refs_2_) | copy-start | bytes 1376260
  68.3 4.4 %collective-permute-start.4 = (bf16[256,896]{1,0:T(8,128)(2,1)S(1)}, bf16[256,896]{1,0:T(8,128)(2,1)S(1)}, u32[]{:S(2)}, u32[]{:S(2)}) collective-permute-start(bf16[256,896]{1,0:T(8,128)(2,1)S(1)} %collective-permute-done.1.own_ref.refs_2_), channel_id=1, source_target_pairs={{0,64},{64,0},{1,65},{65,1},{2,66},{66,2},{3,67},{67,3},{4,68},{68... | collective-permute-start | bytes 1376264 | tf_op jit(solution)/shard_map/ppermute | solution.py:26
  77.1 1.4 collective-permute-start.7
  78.5 4.9 %collective-permute-start.10 = (f32[4,512]{1,0:T(4,128)S(1)}, f32[4,512]{1,0:T(4,128)S(1)}, u32[]{:S(2)}, u32[]{:S(2)}) collective-permute-start(f32[4,512]{1,0:T(4,128)S(1)} %get-tuple-element.62), channel_id=1, source_target_pairs={{0,1},{1,2},{2,3},{3,0},{4,5},{5,6},{6,7},{7,4},{8,9},{9,10},{10,1... | collective-permute-start | bytes 24584 | tf_op jit(solution)/shard_map/ppermute | solution.py:26
  79.8 5.2 %collective-permute-start.9 = (f32[4,512]{1,0:T(4,128)S(1)}, f32[4,512]{1,0:T(4,128)S(1)}, u32[]{:S(2)}, u32[]{:S(2)}) collective-permute-start(f32[4,512]{1,0:T(4,128)S(1)} %get-tuple-element.62), channel_id=1, source_target_pairs={{0,2},{1,3},{2,0},{3,1},{4,6},{5,7},{6,4},{7,5},{8,10},{9,11},{10,... | collective-permute-start | bytes 24584 | tf_op jit(solution)/shard_map/ppermute | solution.py:26
  82.7 3.7 %collective-permute-start.8 = (f32[4,512]{1,0:T(4,128)S(1)}, f32[4,512]{1,0:T(4,128)S(1)}, u32[]{:S(2)}, u32[]{:S(2)}) collective-permute-start(f32[4,512]{1,0:T(4,128)S(1)} %get-tuple-element.62), channel_id=1, source_target_pairs={{0,3},{1,0},{2,1},{3,2},{4,7},{5,4},{6,5},{7,6},{8,11},{9,8},{10,9... | collective-permute-start | bytes 24584 | tf_op jit(solution)/shard_map/ppermute | solution.py:26
  87.1 40.0 %all-to-all-start.1 = ((f32[16,8,256]{2,1,0:T(8,128)}), f32[16,8,256]{2,1,0:T(8,128)S(1)}, u32[]{:S(2)}, u32[]{:S(2)}) async-start(f32[16,8,256]{2,1,0:T(8,128)} %broadcast_in_dim.28), calls=%async_computation.1 | async-start | bytes 262144 | tf_op jit(solution)/shard_map/all_to_all | solution.py:313
  143.3 3.8 %copy-start.19 = (bf16[2048,512]{1,0:T(8,128)(2,1)}, bf16[2048,512]{1,0:T(8,128)(2,1)S(1)}, u32[]{:S(2)}) copy-start(bf16[2048,512]{1,0:T(8,128)(2,1)S(1)} %get-tuple-element.58.p3) | copy-start | bytes 6291460
  143.3 3.8 %copy-start.2 = (bf16[256,896]{1,0:T(8,128)(2,1)S(1)}, bf16[256,896]{1,0:T(8,128)(2,1)}, u32[]{:S(2)}) copy-start(bf16[256,896]{1,0:T(8,128)(2,1)} %copy-done) | copy-start | bytes 1376260
  143.3 3.8 %copy-start.5 = (bf16[256,896]{1,0:T(8,128)(2,1)S(1)}, bf16[256,896]{1,0:T(8,128)(2,1)}, u32[]{:S(2)}) copy-start(bf16[256,896]{1,0:T(8,128)(2,1)} %copy-done.3) | copy-start | bytes 1376260
  143.3 3.8 %copy-start.8 = (bf16[256,896]{1,0:T(8,128)(2,1)S(1)}, bf16[256,896]{1,0:T(8,128)(2,1)}, u32[]{:S(2)}) copy-start(bf16[256,896]{1,0:T(8,128)(2,1)} %copy-done.6) | copy-start | bytes 1376260
  143.3 3.8 %copy-start.11 = (bf16[256,896]{1,0:T(8,128)(2,1)S(1)}, bf16[256,896]{1,0:T(8,128)(2,1)}, u32[]{:S(2)}) copy-start(bf16[256,896]{1,0:T(8,128)(2,1)} %copy-done.9) | copy-start | bytes 1376260
  143.3 3.8 %copy-start.14 = (bf16[256,896]{1,0:T(8,128)(2,1)S(1)}, bf16[256,896]{1,0:T(8,128)(2,1)}, u32[]{:S(2)}) copy-start(bf16[256,896]{1,0:T(8,128)(2,1)} %copy-done.12) | copy-start | bytes 1376260
  143.3 2.6 %collective-permute-start.11 = (bf16[512,896]{1,0:T(8,128)(2,1)S(1)}, bf16[512,896]{1,0:T(8,128)(2,1)S(1)}, u32[]{:S(2)}, u32[]{:S(2)}) collective-permute-start(bf16[512,896]{1,0:T(8,128)(2,1)S(1)} %get-tuple-element.53), channel_id=1, source_target_pairs={{0,64},{64,0},{1,65},{65,1},{2,66},{66,2},{3,67},{67,3},{4,68},{68... | collective-permute-start | bytes 2752520 | tf_op jit(solution)/shard_map/ppermute | solution.py:26
  158.8 39.3 %collective-permute-start.12 = (bf16[2048,768]{1,0:T(8,128)(2,1)S(1)}, bf16[2048,768]{1,0:T(8,128)(2,1)}, u32[]{:S(2)}, u32[]{:S(2)}) collective-permute-start(bf16[2048,768]{1,0:T(8,128)(2,1)S(1)} %get-tuple-element.60), channel_id=1, source_target_pairs={{0,64},{64,0},{1,65},{65,1},{2,66},{66,2},{3,67},{67,3},{4,68},{68... | collective-permute-start | bytes 9437192 | tf_op jit(solution)/shard_map/ppermute | solution.py:26
  158.9 36.6 %all-to-all-start.2 = ((bf16[64,8,896]{2,1,0:T(8,128)(2,1)}), bf16[64,8,896]{2,1,0:T(8,128)(2,1)}, u32[]{:S(2)}, u32[]{:S(2)}) async-start(bf16[64,8,896]{2,1,0:T(8,128)(2,1)} %bitcast.13), calls=%async_computation.2 | async-start | bytes 1835008 | tf_op jit(solution)/shard_map/all_to_all | solution.py:319
  (16 other events, 24.4 us)

commit v3 on v2

--- a/solution.py
+++ b/solution.py
@@ -14,11 +14,13 @@
 LO, MID, HI, CNT = 0, 8, 16, 24
 VMEM = pl.BlockSpec(memory_space=pltpu.VMEM)
 SMEM = pl.BlockSpec(memory_space=pltpu.SMEM)
+HBM = pl.BlockSpec(memory_space=pltpu.HBM)
 NT = (((1,), (1,)), ((), ()))
 TN = (((0,), (0,)), ((), ()))
 LCH = 256
 PROD = 1024
 EXPO = 128
+PARTS = 4
 
 
 def shift(x, axis, step):
@@ -26,7 +28,7 @@
     return lax.ppermute(x, axis, [(i, (i + step) % n) for i in range(n)])
 
 
-def scores_kernel(own_ref, oth_ref, w_ref, e_ref, m_ref, l_ref, s_ref, qt_ref):
+def scores_kernel(own_ref, oth_ref, w_ref, e_ref, m_ref, l_ref, s_ref, qt_ref, held_ref, sem):
     labels, width = w_ref.shape
     rows = own_ref.shape[0]
     both = 2 * rows
@@ -42,15 +44,26 @@
     top = lax.fori_loop(0, labels // PROD, product, jnp.full((16, both), -1e30, jnp.float32))
     top = jnp.max(top, 0, keepdims=True)
 
+    def leave(i):
+        part = pl.ds(pl.multiple_of(i * EXPO, EXPO), EXPO)
+        return pltpu.make_async_copy(held_ref.at[part, :], e_ref.at[part, :], sem.at[i])
+
     def expo(i, total):
         at = pl.multiple_of(i * EXPO, EXPO)
         e = jnp.exp(s_ref[pl.ds(at, EXPO), :] - top)
-        e_ref[pl.ds(at, EXPO), :] = e.astype(jnp.bfloat16)
+        held_ref[pl.ds(at, EXPO), :] = e.astype(jnp.bfloat16)
+        leave(i).start()
         return total + jnp.sum(e.reshape(EXPO // 16, 16, both), 0)
 
     total = lax.fori_loop(0, labels // EXPO, expo, jnp.zeros((16, both), jnp.float32))
     m_ref[...] = top
     l_ref[...] = top + jnp.log(jnp.sum(total, 0, keepdims=True))
+
+    def gone(i, carry):
+        leave(i).wait()
+        return carry
+
+    lax.fori_loop(0, labels // EXPO, gone, 0)
 
 
 def scores_call(own, oth, w):
@@ -59,19 +72,27 @@
     line = jax.ShapeDtypeStruct((1, 2 * rows), jnp.float32)
     return pl.pallas_call(
         scores_kernel,
-        out_shape=(jax.ShapeDtypeStruct((labels, 2 * rows), jnp.bfloat16), line, line),
+        out_shape=(pltpu.HBM((labels, 2 * rows), jnp.bfloat16), line, line),
         in_specs=[VMEM] * 3,
-        out_specs=(VMEM,) * 3,
-        scratch_shapes=[pltpu.VMEM((labels, 2 * rows), jnp.float32), pltpu.VMEM((width, 2 * rows), jnp.bfloat16)],
+        out_specs=(HBM, VMEM, VMEM),
+        scratch_shapes=[
+            pltpu.VMEM((labels, 2 * rows), jnp.float32),
+            pltpu.VMEM((width, 2 * rows), jnp.bfloat16),
+            pltpu.VMEM((labels, 2 * rows), jnp.bfloat16),
+            pltpu.SemaphoreType.DMA((labels // EXPO,)),
+        ],
         compiler_params=pltpu.CompilerParams(vmem_limit_bytes=18 * 2**20),
-        cost_estimate=pl.CostEstimate(flops=4 * rows * labels * width, bytes_accessed=labels * rows * 4, transcendentals=2 * rows * labels),
+        cost_estimate=pl.CostEstimate(flops=1000, bytes_accessed=1000, transcendentals=0),
         name="scores",
     )(own, oth, w)
 
 
 def hits_kernel(base_ref, *refs):
-    blocks = refs[:8]
-    w_ref, n_ref, key_ref, s_ref, t_ref = refs[8:]
+    sources = refs[:4]
+    w_ref, n_ref, key_ref, s_ref, t_ref, blocks, sem = refs[4:]
+    copies = [pltpu.make_async_copy(q, blocks.at[b], sem.at[b]) for b, q in enumerate(sources)]
+    for copy in copies:
+        copy.start()
     labels, width = w_ref.shape
     base = base_ref[0].astype(jnp.float32)
     row = lax.broadcasted_iota(jnp.int32, (8, EXTRA), 0)
@@ -80,12 +101,13 @@
     digits = jnp.where(row < POS, digits, 0.0).astype(jnp.bfloat16)
     counting = jnp.where(col == CNT, 1.0, 0.0).astype(jnp.bfloat16)
     big = 1e9
-    rows = blocks[0].shape[0]
+    rows = blocks.shape[1]
     slot = lax.broadcasted_iota(jnp.int32, (8, rows), 0)
     lane = lax.broadcasted_iota(jnp.int32, (8, rows), 1)
     keys, weights, most = [], [], jnp.int32(0)
-    for b, q_ref in enumerate(blocks):
-        extra = q_ref[:, width:]
+    for b in range(4):
+        copies[b].wait()
+        extra = blocks[b, :, width:]
         ids = lax.dot_general(digits, extra, NT, preferred_element_type=jnp.float32)
         cnt = lax.dot_general(counting, extra, NT, preferred_element_type=jnp.float32)
         valid = (slot.astype(jnp.float32) < cnt) & (slot < POS)
@@ -103,61 +125,70 @@
         n = jnp.sum(jnp.where(hit, 1.0, 0.0)).astype(jnp.int32)
         n_ref[b] = n
         most = jnp.maximum(most, n)
-    r16 = lax.broadcasted_iota(jnp.int32, (16, 16), 0)
-    c16 = lax.broadcasted_iota(jnp.int32, (16, 16), 1)
+    r16 = lax.broadcasted_iota(jnp.int32, (16, width), 0)
 
     def step(i, keys):
-        left = []
-        for b in range(8):
-            kf = jnp.min(keys[b])
-            this = keys[b] == kf
-            k = jnp.where(kf < big, kf, 0.0).astype(jnp.int32)
+        least = [jnp.min(k) for k in keys]
+        found = [jnp.where(k < big, k, 0.0).astype(jnp.int32) for k in least]
+        same = [k == kf for k, kf in zip(keys, least)]
+        score, weight = [], []
+        for b, k in enumerate(found):
             label = k & (labels - 1)
             query = lax.div(k, 8 * labels)
             qat = pl.multiple_of((query >> 4) << 4, 16)
             lat = pl.multiple_of((label >> 4) << 4, 16)
-            s16 = lax.dot_general(blocks[b][pl.ds(qat, 16), :width], w_ref[pl.ds(lat, 16), :], NT, preferred_element_type=jnp.float32)
+            row_q = jnp.where(r16 == query - qat, blocks[b, pl.ds(qat, 16), :width].astype(jnp.float32), 0.0)
+            row_w = jnp.where(r16 == label - lat, w_ref[pl.ds(lat, 16), :].astype(jnp.float32), 0.0)
+            score.append(jnp.sum(row_w * jnp.sum(row_q, 0, keepdims=True)))
+            weight.append(jnp.sum(jnp.where(same[b], weights[b], 0.0)))
+        for b in range(4):
             at = b * rows * POS + i
-            key_ref[at] = k
-            s_ref[at] = jnp.sum(jnp.where((r16 == query - qat) & (c16 == label - lat), s16, 0.0))
-            t_ref[at] = jnp.sum(jnp.where(this, weights[b], 0.0))
-            left.append(jnp.where(this, big, keys[b]))
-        return tuple(left)
+            key_ref[at] = found[b]
+            s_ref[at] = score[b]
+            t_ref[at] = weight[b]
+        return tuple(jnp.where(t, big, k) for t, k in zip(same, keys))
 
     lax.fori_loop(0, most, step, tuple(keys))
 
 
 def hits_call(base, blocks, w):
-    total = 8 * blocks[0].shape[0] * POS
+    total = 4 * blocks[0].shape[0] * POS
     return pl.pallas_call(
         hits_kernel,
         out_shape=(
-            jax.ShapeDtypeStruct((8,), jnp.int32),
+            jax.ShapeDtypeStruct((4,), jnp.int32),
             jax.ShapeDtypeStruct((total,), jnp.int32),
             jax.ShapeDtypeStruct((total,), jnp.float32),
             jax.ShapeDtypeStruct((total,), jnp.float32),
         ),
-        in_specs=[SMEM] + [VMEM] * 9,
+        in_specs=[SMEM] + [HBM] * 4 + [VMEM],
         out_specs=(SMEM,) * 4,
-        compiler_params=pltpu.CompilerParams(vmem_limit_bytes=16 * 2**20),
-        cost_estimate=pl.CostEstimate(flops=10**9, bytes_accessed=2**23, transcendentals=0),
+        scratch_shapes=[pltpu.VMEM((4,) + blocks[0].shape, jnp.bfloat16), pltpu.SemaphoreType.DMA((4,))],
+        compiler_params=pltpu.CompilerParams(vmem_limit_bytes=12 * 2**20),
+        cost_estimate=pl.CostEstimate(flops=1000, bytes_accessed=1000, transcendentals=0),
         name="hits",
     )(base, *blocks, w)
 
 
-def query_kernel(at_ref, n_ref, key_ref, s_ref, t_ref, lse_ref, m_ref, e0, e1, e2, e3, w_ref, p0, p1, p2, p3, own_ref, oth_ref, pos_ref):
+def query_kernel(at_ref, na, ka, sa, ta, nb, kb, sb, tb, lse_ref, m_ref, e0, e1, e2, e3, w_ref, *outs):
+    own_ref, oth_ref, pos_ref, held, sem = outs[4:]
+    ps = [held.at[d] for d in range(4)]
+    copies = [pltpu.make_async_copy(e, p, sem.at[d]) for d, (e, p) in enumerate(zip((e0, e1, e2, e3), ps))]
+    for copy in copies:
+        copy.start()
     labels, width = w_ref.shape
+    lists = ((na, ka, sa, ta, 0), (na, ka, sa, ta, 2), (nb, kb, sb, tb, 0), (nb, kb, sb, tb, 2))
     rows = e0.shape[1] // 2
     xh, y = at_ref[0], at_ref[1]
     half = rows // 2
-    ps = (p0, p1, p2, p3)
     pos_ref[...] = jnp.zeros_like(pos_ref)
-    for d, (e_ref, p_ref) in enumerate(zip((e0, e1, e2, e3), ps)):
+    for d, p_ref in enumerate(ps):
+        copies[d].wait()
         scale = jnp.exp(m_ref[d:d + 1, :] - lse_ref[d:d + 1, :])
 
         def scaled(i, carry):
             at = pl.multiple_of(i * 64, 64)
-            p_ref[pl.ds(at, 64), :] = (e_ref[pl.ds(at, 64), :].astype(jnp.float32) * scale).astype(jnp.bfloat16)
+            p_ref[pl.ds(at, 64), :] = (p_ref[pl.ds(at, 64), :].astype(jnp.float32) * scale).astype(jnp.bfloat16)
             return carry
 
         lax.fori_loop(0, labels // 64, scaled, 0)
@@ -165,17 +196,18 @@
     r = lax.broadcasted_iota(jnp.int32, (16, half), 0)
     c = lax.broadcasted_iota(jnp.int32, (16, half), 1)
     c1 = lax.broadcasted_iota(jnp.int32, (1, EXTRA), 1)
-    most = n_ref[0]
-    for b in range(1, 8):
-        most = jnp.maximum(most, n_ref[b])
+    most = jnp.int32(0)
+    for b in range(4):
+        most = jnp.maximum(most, jnp.maximum(na[b], nb[b]))
 
     def patch(i, carry):
         todo = []
         for b in range(8):
             d, k = b // 2, b % 2
-            at = b * rows * POS + i
-            live = i < n_ref[b]
-            key, s, weight = key_ref[at], s_ref[at], t_ref[at]
+            n_ref, key_ref, s_ref, t_ref, first = lists[d]
+            at = (first + k) * rows * POS + i
+            live = i < n_ref[first + k]
+            key, s, weight = jnp.where(live, key_ref[at], 0), s_ref[at], t_ref[at]
             label = key & (labels - 1)
             rest = lax.div(key, labels)
             slot = rest & 7
@@ -203,6 +235,9 @@
         return carry
 
     lax.fori_loop(0, most, patch, 0)
+    copies = [pltpu.make_async_copy(p, out, sem.at[d]) for d, (p, out) in enumerate(zip(ps, outs))]
+    for copy in copies:
+        copy.start()
     for d, p_ref in enumerate(ps):
         both = jnp.concatenate([p_ref[:, pl.ds(pl.multiple_of(k * rows + xh * half, half), half)] for k in range(2)], 1)
         u = lax.dot_general(both, w_ref[...], TN, preferred_element_type=jnp.float32)
@@ -210,6 +245,8 @@
         for k, out in enumerate((own_ref, oth_ref)):
             out[to, :width] = u[k * half:(k + 1) * half].astype(jnp.bfloat16)
             out[to, width:] = pos_ref[k, d * half:(d + 1) * half, :].astype(jnp.bfloat16)
+    for copy in copies:
+        copy.wait()
 
 
 def query_call(at, hits, lse, m, es, w):
@@ -218,21 +255,20 @@
     out = jax.ShapeDtypeStruct((2 * rows, width + EXTRA), jnp.bfloat16)
     res = pl.pallas_call(
         query_kernel,
-        out_shape=tuple(jax.ShapeDtypeStruct(e.shape, e.dtype) for e in es) + (out, out),
-        in_specs=[SMEM] * 5 + [VMEM] * 7,
-        out_specs=(VMEM,) * 6,
-        scratch_shapes=[pltpu.VMEM((2, 2 * rows, EXTRA), jnp.float32)],
-        input_output_aliases={7 + d: d for d in range(4)},
+        out_shape=tuple(pltpu.HBM(e.shape, e.dtype) for e in es) + (out, out),
+        in_specs=[SMEM] * 9 + [VMEM] * 2 + [HBM] * 4 + [VMEM],
+        out_specs=(HBM,) * 4 + (VMEM,) * 2,
+        scratch_shapes=[pltpu.VMEM((2, 2 * rows, EXTRA), jnp.float32), pltpu.VMEM((4,) + es[0].shape, jnp.bfloat16), pltpu.SemaphoreType.DMA((4,))],
         compiler_params=pltpu.CompilerParams(vmem_limit_bytes=28 * 2**20),
         cost_estimate=pl.CostEstimate(flops=8 * rows * labels * width, bytes_accessed=2**24, transcendentals=0),
         name="query_part",
-    )(at, *hits, lse, m, *es, w)
+    )(at, *hits[0], *hits[1], lse, m, *[pltpu.with_memory_space_constraint(e, pltpu.HBM) for e in es], w)
     return res[:4], res[4], res[5]
 
 
 def class_kernel(core_ref, p0, p1, p2, p3, *refs):
     blocks = refs[:8]
-    out_ref, mine_ref = refs[8:]
+    out_ref, parts = refs[8], refs[9:]
     rows = blocks[0].shape[0]
     width = out_ref.shape[1]
     acc = None
@@ -242,27 +278,33 @@
             acc = term if acc is None else acc + term
     done = acc.astype(jnp.bfloat16)
     out_ref[...] = done
-    mine_ref[...] = done
+    each = pl.num_programs(0) // len(parts)
+    for j, part in enumerate(parts):
+        @pl.when(pl.program_id(0) // each == j)
+        def _():
+            part[...] = done
 
 
 def class_call(core, ps, blocks, width):
     labels = ps[0].shape[0]
     steps = labels // LCH
+    each = steps // PARTS
     rows = blocks[0].shape[0]
     whole = lambda i, c: (0, 0)
     return pl.pallas_call(
         class_kernel,
-        out_shape=tuple(jax.ShapeDtypeStruct((n * labels, width), jnp.bfloat16) for n in (2, 1)),
+        out_shape=(jax.ShapeDtypeStruct((2 * labels, width), jnp.bfloat16),) + (jax.ShapeDtypeStruct((labels // PARTS, width), jnp.bfloat16),) * PARTS,
         grid_spec=pltpu.PrefetchScalarGridSpec(
             num_scalar_prefetch=1,
             grid=(steps,),
             in_specs=[pl.BlockSpec((LCH, 2 * rows), lambda i, c: (i, 0))] * 4 + [pl.BlockSpec(blocks[0].shape, whole)] * 8,
-            out_specs=(pl.BlockSpec((LCH, width), lambda i, c: (c[0] * steps + i, 0)), pl.BlockSpec((LCH, width), lambda i, c: (i, 0))),
+            out_specs=(pl.BlockSpec((LCH, width), lambda i, c: (c[0] * steps + i, 0)),)
+            + tuple(pl.BlockSpec((LCH, width), lambda i, c, j=j: (jnp.clip(i - j * each, 0, each - 1), 0)) for j in range(PARTS)),
         ),
-        compiler_params=pltpu.CompilerParams(vmem_limit_bytes=18 * 2**20),
+        compiler_params=pltpu.CompilerParams(vmem_limit_bytes=20 * 2**20),
         cost_estimate=pl.CostEstimate(flops=16 * rows * labels * width, bytes_accessed=2**24, transcendentals=0),
         name="class_part",
-    )(core, *ps, *blocks)
+    )(core, *[pltpu.with_memory_space_constraint(p, pltpu.HBM) for p in ps], *blocks)
 
 
 def lse_of(parts, axis=None):
@@ -293,18 +335,20 @@
     w = lax.dynamic_slice_in_dim(classifier, core * labels, labels)
     rows = mine.shape[0]
 
-    oth, parts, after = [None] * 4, [None] * 4, None
-    for turn in ((0,), (3,), (1, 2)):
-        for d in turn:
-            if after is not None:
-                own[d], _ = lax.optimization_barrier((own[d], after))
-            oth[d] = shift(own[d], "core", 1)
-        for d in turn:
-            parts[d] = scores_call(own[d], oth[d], w)
-        after = parts[turn[-1]][1]
+    oth, parts, ready = [None] * 4, [None] * 4, list(own)
+    for d in range(4):
+        if d:
+            own[d], _ = lax.optimization_barrier((own[d], parts[0][1]))
+        oth[d] = shift(own[d], "core", 1)
+        ready[d] = own[d]
+        if d >= 2:
+            ready[d], _ = lax.optimization_barrier((own[d], hits[0][0]))
+        parts[d] = scores_call(ready[d], oth[d], w)
+        if d == 1:
+            hits = [hits_call(base[None], (own[0], oth[0], own[1], oth[1]), w)]
     es, ms, ls = zip(*parts)
     blocks = [b for pair in zip(own, oth) for b in pair]
-    hits = hits_call(base[None], blocks, w)
+    hits.append(hits_call(base[None], blocks[4:], w))
     m = jnp.concatenate(ms, 0)
     stat = jnp.concatenate(ls, 0)
     stat = lse_of([stat, jnp.roll(shift(stat, "core", 1), rows, 1)])
@@ -317,14 +361,15 @@
     u = (f32(u_own) + f32(shift(u_oth, "core", 1))).astype(jnp.bfloat16)
     first, u = lax.optimization_barrier((ps[0], u))
     got = lax.all_to_all(u, ("y", "xl", "z"), 0, 0, tiled=True)
-    halves, mine_half = class_call(core[None], (first,) + tuple(ps[1:]), blocks, width)
+    class_grad, *mine_parts = class_call(core[None], (first,) + tuple(ps[1:]), blocks, width)
 
     final = jnp.sum(f32(got).reshape(64, q_dev, width + EXTRA), 0)
     query_grad = final[:, :width].astype(jnp.bfloat16)
     pos_mean = jnp.sum(final[:, width:width + 24], 1)
     at = ((xh * 2 + xl) * 8 + z) * q_dev
     loss = lax.dynamic_slice(lse, (0, at), (1, q_dev))[0] - pos_mean
-    class_grad = lax.dynamic_update_slice_in_dim(halves, shift(mine_half, "core", 1), (1 - core) * labels, 0)
+    for j, part in enumerate(mine_parts):
+        class_grad = lax.dynamic_update_slice_in_dim(class_grad, shift(part, "core", 1), (1 - core) * labels + j * part.shape[0], 0)
     return loss, query_grad, class_grad
 
 

time: 204 us -> 156 us (0.76)
  waiting for transfers between devices: 53.6 us -> 28 us
  local copies, waits for them, and re-layouts: 26.6 us -> 12.6 us
  Pallas kernels: 64.8 us -> 56.9 us
    all_to_all x1, waiting for transfers between devices: 26.6 us -> 3.65 us  [body(): got = lax.all_to_all(u, ('y', 'xl', 'z'), 0, 0, tiled=True)]
    unnamed x50 -> x0, local copies, waits for them, and re-layouts: 18.4 us -> none
    pallas_call x7 -> x8, Pallas kernels: 64.8 us -> 56.9 us  [the longest x4 19.7 us: scores_call(): pl.pallas_call(scores_kernel, out_shape=(pltpu.HBM((labels, 2 * rows), jn...]
    dynamic_update_slice x1 -> x4, local copies, waits for them, and re-layouts: 3.76 us -> 8.25 us  [body(): lax.dynamic_update_slice_in_dim(class_grad, shift(part, 'core', 1), (1 -...]
    ppermute x13 -> x16, waiting for transfers between devices: 27 us -> 23.8 us  [shift(): return lax.ppermute(x, axis, [(i, (i + step) % n) for i in range(n)])]
    ppermute x13 -> x16, starting transfers between devices: 9.92 us -> 11 us  [shift(): return lax.ppermute(x, axis, [(i, (i + step) % n) for i in range(n)])]
  transfers between devices with their start and end apart: 15 -> 18, of which waited for: 9 -> 8; matrix products, arithmetic and copies ran while one was open for 2% -> 7% of each run, Pallas kernels for 21% -> 26%
where the time goes in v3:
time: 156 us; the launch traced here: 155 us
  Pallas kernels  56.9 us (36%)
  waiting for transfers between devices  28 us (18%)
  blocking collectives  27.3 us (18%)
  starting transfers between devices  24.8 us (16%)
  local copies, waits for them, and re-layouts  12.6 us (8%)
  other arithmetic  4.83 us (3%)
    all_to_all x1, blocking collectives, body(): mine = lax.all_to_all(copies, ('xh', 'xl', 'z'), 0, 0, tiled=True)  27.3 us
    ppermute x16, waiting for transfers between devices, shift(): return lax.ppermute(x, axis, [(i, (i + step) % n) for i in range(n)])  23.8 us
    pallas_call x4, Pallas kernels, scores_call(): pl.pallas_call(scores_kernel, out_shape=(pltpu.HBM((labels, 2 * rows), jn...  19.7 us
    pallas_call x2, Pallas kernels, hits_call(): pl.pallas_call(hits_kernel, out_shape=(jax.ShapeDtypeStruct((4,), jnp.int...  13.2 us
    pallas_call x1, Pallas kernels, class_call(): pl.pallas_call(class_kernel, out_shape=(jax.ShapeDtypeStruct((2 * labels,...  12.5 us
    pallas_call x1, Pallas kernels, query_call(): pl.pallas_call(query_kernel, out_shape=tuple((pltpu.HBM(e.shape, e.dtype)...  11.4 us
    ppermute x16, starting transfers between devices, shift(): return lax.ppermute(x, axis, [(i, (i + step) % n) for i in range(n)])  11 us
    all_to_all x1, starting transfers between devices, body(): got = lax.all_to_all(u, ('y', 'xl', 'z'), 0, 0, tiled=True)  9.22 us
  transfers between devices with their start and end apart: 18, of which 8 were waited for; matrix products, arithmetic and copies ran while one was open for 7% of the time, Pallas kernels for 26%

profile of v3, /device:TPU:32, one launch (start us, length us, event | category | flops | bytes accessed | tf_op | source)
XLA Modules:
  0.0 155.3 jit_solution(16618887497872136060)
XLA Ops:
  2.9 27.3 %all_to_all.22 = bf16[32,8,896]{2,1,0:T(8,128)(2,1)} all-to-all(bf16[32,8,896]{2,1,0:T(8,128)(2,1)S(1)} %broadcast_in_dim.28), channel_id=1, replica_groups=mesh['xh'=2,'core'=2,'xl'=2,'z'=8,'y'=4] {'xh','xl','z'}, dimensions={0} | all-to-all | bytes 917504 | tf_op jit(solution)/shard_map/all_to_all | solution.py:332
  30.2 3.0 %collective-permute-start.1 = (bf16[256,896]{1,0:T(8,128)(2,1)}, bf16[256,896]{1,0:T(8,128)(2,1)}, u32[]{:S(2)}, u32[]{:S(2)}) collective-permute-start(bf16[256,896]{1,0:T(8,128)(2,1)} %bitcast.1.own_ref.refs_0_), channel_id=1, source_target_pairs={{0,3},{1,0},{2,1},{3,2},{4,7},{5,4},{6,5},{7,6},{8,11},{9,8},{10,9... | collective-permute-start | bytes 1376264 | tf_op jit(solution)/shard_map/ppermute | solution.py:28
  34.8 2.1 %constant_dynamic-slice_fusion.1.w_ref.refs_4_ = bf16[2048,768]{1,0:T(8,128)(2,1)S(1)} fusion(bf16[4096,768]{1,0:T(8,128)(2,1)} %param.5, s32[]{:T(128)S(6)} %select_n.18), kind=kLoop, calls=%fused_computation.26 | loop fusion | bytes 6291460 | tf_op jit(solution)/shard_map/dynamic_slice | solution.py:335
  36.9 4.9 %scores.4 = (bf16[2048,512]{1,0:T(8,128)(2,1)}, f32[1,512]{1,0:T(1,128)S(1)}, f32[1,512]{1,0:T(1,128)S(1)}) custom-call(bf16[256,896]{1,0:T(8,128)(2,1)} %bitcast.1.own_ref.refs_0_, bf16[256,896]{1,0:T(8,128)(2,1)} %collective-permute-done.oth_ref.refs_1_, bf16[2048,768]{1,0:T(8,128)(2,1)S(1)} %constant_dynamic-slice_fusion.1.w_ref.refs_4_), custom_call_target="tpu_custom_call" | custom-call | flops 1000 | bytes 1000 | tf_op jit(solution)/shard_map/scores/pallas_call | solution.py:73
  41.9 11.9 %collective-permute-done.1.own_ref.refs_2_ = bf16[256,896]{1,0:T(8,128)(2,1)} collective-permute-done((bf16[256,896]{1,0:T(8,128)(2,1)}, bf16[256,896]{1,0:T(8,128)(2,1)}, u32[]{:S(2)}, u32[]{:S(2)}) %collective-permute-start.1) | collective-permute-done | bytes 458784 | tf_op jit(solution)/shard_map/ppermute | solution.py:28
  54.3 3.2 %collective-permute-done.5.own_ref.refs_2_.refs_6_ = bf16[256,896]{1,0:T(8,128)(2,1)} collective-permute-done((bf16[256,896]{1,0:T(8,128)(2,1)}, bf16[256,896]{1,0:T(8,128)(2,1)}, u32[]{:S(2)}, u32[]{:S(2)}) %collective-permute-start.5) | collective-permute-done | bytes 458784 | tf_op jit(solution)/shard_map/ppermute | solution.py:28
  57.6 4.9 %scores.5 = (bf16[2048,512]{1,0:T(8,128)(2,1)}, f32[1,512]{1,0:T(1,128)S(1)}, f32[1,512]{1,0:T(1,128)S(1)}) custom-call(bf16[256,896]{1,0:T(8,128)(2,1)} %collective-permute-done.1.own_ref.refs_2_, bf16[256,896]{1,0:T(8,128)(2,1)} %collective-permute-done.2.oth_ref.refs_3_, bf16[2048,768]{1,0:T(8,128)(2,1)S(1)} %constant_dynamic-slice_fusion.1.w_ref.refs_4_), custom_call_target="tpu_custom_call" | custom-call | flops 1000 | bytes 1000 | tf_op jit(solution)/shard_map/scores/pallas_call | solution.py:73
  62.5 6.0 %hits.2 = (s32[4]{0:T(128)S(1)}, s32[5120]{0:T(1024)S(1)}, f32[5120]{0:T(1024)S(1)}, f32[5120]{0:T(1024)S(1)}) custom-call(s32[1]{0:T(128)} %bitcast.2.base_ref, bf16[256,896]{1,0:T(8,128)(2,1)} %bitcast.1.own_ref.refs_0_, bf16[256,896]{1,0:T(8,128)(2,1)} %collective-permute-done.oth_ref.refs_1_, bf16[256,896]{1,0:T(8,128)(2,1)} %collective-permute-done.1.own_ref.refs_2_, ...), custom_call_target="tpu_custom_call" | custom-call | flops 1000 | bytes 1000 | tf_op jit(solution)/shard_map/hits/pallas_call | solution.py:156
  68.6 4.9 %scores.6 = (bf16[2048,512]{1,0:T(8,128)(2,1)}, f32[1,512]{1,0:T(1,128)S(1)}, f32[1,512]{1,0:T(1,128)S(1)}) custom-call(bf16[256,896]{1,0:T(8,128)(2,1)} %collective-permute-done.3.own_ref.refs_0_.refs_4_, bf16[256,896]{1,0:T(8,128)(2,1)} %collective-permute-done.4.oth_ref.refs_1_.refs_5_, bf16[2048,768]{1,0:T(8,128)(2,1)S(1)} %constant_dynamic-slice_fusion.1.w_ref.refs_4_), custom_call_target="tpu_custom_call" | custom-call | flops 1000 | bytes 1000 | tf_op jit(solution)/shard_map/scores/pallas_call | solution.py:73
  73.5 4.9 %scores.7 = (bf16[2048,512]{1,0:T(8,128)(2,1)}, f32[1,512]{1,0:T(1,128)S(1)}, f32[1,512]{1,0:T(1,128)S(1)}) custom-call(bf16[256,896]{1,0:T(8,128)(2,1)} %collective-permute-done.5.own_ref.refs_2_.refs_6_, bf16[256,896]{1,0:T(8,128)(2,1)} %collective-permute-done.6.oth_ref.refs_3_.refs_7_, bf16[2048,768]{1,0:T(8,128)(2,1)S(1)} %constant_dynamic-slice_fusion.1.w_ref.refs_4_), custom_call_target="tpu_custom_call" | custom-call | flops 1000 | bytes 1000 | tf_op jit(solution)/shard_map/scores/pallas_call | solution.py:73
  79.8 3.2 %collective-permute-start.8 = (f32[4,512]{1,0:T(4,128)S(1)}, f32[4,512]{1,0:T(4,128)S(1)}, u32[]{:S(2)}, u32[]{:S(2)}) collective-permute-start(f32[4,512]{1,0:T(4,128)S(1)} %get-tuple-element.80), channel_id=1, source_target_pairs={{0,3},{1,0},{2,1},{3,2},{4,7},{5,4},{6,5},{7,6},{8,11},{9,8},{10,9... | collective-permute-start | bytes 24584 | tf_op jit(solution)/shard_map/ppermute | solution.py:28
  84.3 3.7 %collective-permute-done.9 = f32[4,512]{1,0:T(4,128)S(1)} collective-permute-done((f32[4,512]{1,0:T(4,128)S(1)}, f32[4,512]{1,0:T(4,128)S(1)}, u32[]{:S(2)}, u32[]{:S(2)}) %collective-permute-start.9) | collective-permute-done | bytes 8224 | tf_op jit(solution)/shard_map/ppermute | solution.py:28
  88.9 4.5 %all-to-all-start.1 = ((f32[16,8,256]{2,1,0:T(8,128)}), f32[16,8,256]{2,1,0:T(8,128)S(1)}, u32[]{:S(2)}, u32[]{:S(2)}) async-start(f32[16,8,256]{2,1,0:T(8,128)} %broadcast_in_dim.30), calls=%async_computation.1 | async-start | bytes 262144 | tf_op jit(solution)/shard_map/all_to_all | solution.py:357
  93.5 7.2 %hits.3 = (s32[4]{0:T(128)S(1)}, s32[5120]{0:T(1024)S(1)}, f32[5120]{0:T(1024)S(1)}, f32[5120]{0:T(1024)S(1)}) custom-call(s32[1]{0:T(128)} %bitcast.2.base_ref, bf16[256,896]{1,0:T(8,128)(2,1)} %collective-permute-done.3.own_ref.refs_0_.refs_4_, bf16[256,896]{1,0:T(8,128)(2,1)} %collective-permute-done.4.oth_ref.refs_1_.refs_5_, ...), custom_call_target="tpu_custom_call" | custom-call | flops 1000 | bytes 1000 | tf_op jit(solution)/shard_map/hits/pallas_call | solution.py:156
  101.4 11.4 %query_part.1 = (bf16[2048,512]{1,0:T(8,128)(2,1)}, bf16[2048,512]{1,0:T(8,128)(2,1)}, bf16[2048,512]{1,0:T(8,128)(2,1)}, bf16[2048,512]{1,0:T(8,128)(2,1)}, bf1...) custom-call(s32[2]{0:T(128)S(1)} %pad_add_fusion.at_ref, s32[4]{0:T(128)S(1)} %get-tuple-element.46.na, ...), custom_call_target="tpu_custom_call" | custom-call | flops 3221225472 | bytes 16777216 | tf_op jit(solution)/shard_map/query_part/pallas_call | solution.py:256
  112.9 2.5 %collective-permute-done.11 = bf16[512,896]{1,0:T(8,128)(2,1)S(1)} collective-permute-done((bf16[512,896]{1,0:T(8,128)(2,1)S(1)}, bf16[512,896]{1,0:T(8,128)(2,1)S(1)}, u32[]{:S(2)}, u32[]{:S(2)}) %collective-permute-start.11) | collective-permute-done | bytes 917536 | tf_op jit(solution)/shard_map/ppermute | solution.py:28
  116.6 9.2 %all-to-all-start.2 = ((bf16[64,8,896]{2,1,0:T(8,128)(2,1)}), bf16[64,8,896]{2,1,0:T(8,128)(2,1)}, u32[]{:S(2)}, u32[]{:S(2)}) async-start(bf16[64,8,896]{2,1,0:T(8,128)(2,1)} %bitcast.6), calls=%async_computation.2 | async-start | bytes 1835008 | tf_op jit(solution)/shard_map/all_to_all | solution.py:363
  125.8 12.5 %class_part.1 = (bf16[4096,768]{1,0:T(8,128)(2,1)}, bf16[512,768]{1,0:T(8,128)(2,1)S(1)}, bf16[512,768]{1,0:T(8,128)(2,1)S(1)}, bf16[512,768]{1,0:T(8,128)(2,1)S(1)}, bf16[512,768]{1,0:T(8,128)(2,1)S(1)}) custom-call(s32[1]{0:T(128)} %bitcast.7.core_ref, bf16[2048,512]{1,0:T(8,128)(2,1)} %get-tuple-element.70.p0, bf16[2048,512]{1,0:T(8,128)(2,1)} %get-tuple-element.71.p1, ...), custom_call_target="tpu_custom_call" | custom-call | flops 6442450944 | bytes 16777216 | tf_op jit(solution)/shard_map/class_part/pallas_call | solution.py:294
  139.3 1.4 collective-permute-done.12
  140.7 2.1 %constant_dynamic-update-slice_fusion.3 = bf16[4096,768]{1,0:T(8,128)(2,1)} fusion(bf16[4096,768]{1,0:T(8,128)(2,1)} %get-tuple-element.74, bf16[512,768]{1,0:T(8,128)(2,1)} %collective-permute-done.12, s32[]{:T(128)S(6)} %select_n.20), kind=kLoop, calls=%fused_computation.24 | loop fusion | bytes 1572868 | tf_op jit(solution)/shard_map/dynamic_update_slice | solution.py:372
  142.8 2.1 %constant_dynamic-update-slice_fusion.2 = bf16[4096,768]{1,0:T(8,128)(2,1)} fusion(bf16[4096,768]{1,0:T(8,128)(2,1)} %constant_dynamic-update-slice_fusion.3, bf16[512,768]{1,0:T(8,128)(2,1)} %collective-permute-done.13, s32[]{:T(128)S(6)} %select_n.21), kind=kLoop, calls=%fused_computation.23 | loop fusion | bytes 1572868 | tf_op jit(solution)/shard_map/dynamic_update_slice | solution.py:372
  144.8 2.1 %constant_dynamic-update-slice_fusion.1 = bf16[4096,768]{1,0:T(8,128)(2,1)} fusion(bf16[4096,768]{1,0:T(8,128)(2,1)} %constant_dynamic-update-slice_fusion.2, bf16[512,768]{1,0:T(8,128)(2,1)} %collective-permute-done.14, s32[]{:T(128)S(6)} %select_n.22), kind=kLoop, calls=%fused_computation.22 | loop fusion | bytes 1572868 | tf_op jit(solution)/shard_map/dynamic_update_slice | solution.py:372
  146.9 2.1 %constant_dynamic-update-slice_fusion = bf16[4096,768]{1,0:T(8,128)(2,1)} fusion(bf16[4096,768]{1,0:T(8,128)(2,1)} %constant_dynamic-update-slice_fusion.1, bf16[512,768]{1,0:T(8,128)(2,1)} %collective-permute-done.15, s32[]{:T(128)S(6)} %select_n.23), kind=kLoop, calls=%fused_computation.21 | loop fusion | bytes 1572868 | tf_op jit(solution)/shard_map/dynamic_update_slice | solution.py:372
  149.0 3.6 %all-to-all-done.2 = bf16[64,8,896]{2,1,0:T(8,128)(2,1)} async-done(((bf16[64,8,896]{2,1,0:T(8,128)(2,1)}), bf16[64,8,896]{2,1,0:T(8,128)(2,1)}, u32[]{:S(2)}, u32[]{:S(2)}) %all-to-all-start.2) | async-done | bytes 917536 | tf_op jit(solution)/shard_map/all_to_all | solution.py:363
  (61 shorter events, 13.6 us)
Async XLA Ops:
  30.2 6.7 %collective-permute-start = (bf16[256,896]{1,0:T(8,128)(2,1)}, bf16[256,896]{1,0:T(8,128)(2,1)}, u32[]{:S(2)}, u32[]{:S(2)}) collective-permute-start(bf16[256,896]{1,0:T(8,128)(2,1)} %bitcast.1.own_ref.refs_0_), channel_id=1, source_target_pairs={{0,64},{64,0},{1,65},{65,1},{2,66},{66,2},{3,67},{67,3},{4,68},{68... | collective-permute-start | bytes 1376264 | tf_op jit(solution)/shard_map/ppermute | solution.py:28
  30.2 23.6 %collective-permute-start.1 = (bf16[256,896]{1,0:T(8,128)(2,1)}, bf16[256,896]{1,0:T(8,128)(2,1)}, u32[]{:S(2)}, u32[]{:S(2)}) collective-permute-start(bf16[256,896]{1,0:T(8,128)(2,1)} %bitcast.1.own_ref.refs_0_), channel_id=1, source_target_pairs={{0,3},{1,0},{2,1},{3,2},{4,7},{5,4},{6,5},{7,6},{8,11},{9,8},{10,9... | collective-permute-start | bytes 1376264 | tf_op jit(solution)/shard_map/ppermute | solution.py:28
  33.2 20.6 %collective-permute-start.3 = (bf16[256,896]{1,0:T(8,128)(2,1)}, bf16[256,896]{1,0:T(8,128)(2,1)}, u32[]{:S(2)}, u32[]{:S(2)}) collective-permute-start(bf16[256,896]{1,0:T(8,128)(2,1)} %bitcast.1.own_ref.refs_0_), channel_id=1, source_target_pairs={{0,2},{1,3},{2,0},{3,1},{4,6},{5,7},{6,4},{7,5},{8,10},{9,11},{10,... | collective-permute-start | bytes 1376264 | tf_op jit(solution)/shard_map/ppermute | solution.py:28
  33.9 23.7 %collective-permute-start.5 = (bf16[256,896]{1,0:T(8,128)(2,1)}, bf16[256,896]{1,0:T(8,128)(2,1)}, u32[]{:S(2)}, u32[]{:S(2)}) collective-permute-start(bf16[256,896]{1,0:T(8,128)(2,1)} %bitcast.1.own_ref.refs_0_), channel_id=1, source_target_pairs={{0,1},{1,2},{2,3},{3,0},{4,5},{5,6},{6,7},{7,4},{8,9},{9,10},{10,1... | collective-permute-start | bytes 1376264 | tf_op jit(solution)/shard_map/ppermute | solution.py:28
  53.8 3.7 %collective-permute-start.2 = (bf16[256,896]{1,0:T(8,128)(2,1)}, bf16[256,896]{1,0:T(8,128)(2,1)}, u32[]{:S(2)}, u32[]{:S(2)}) collective-permute-start(bf16[256,896]{1,0:T(8,128)(2,1)} %collective-permute-done.1.own_ref.refs_2_), channel_id=1, source_target_pairs={{0,64},{64,0},{1,65},{65,1},{2,66},{66,2},{3,67},{67,3},{4,68},{68... | collective-permute-start | bytes 1376264 | tf_op jit(solution)/shard_map/ppermute | solution.py:28
  53.8 14.7 %collective-permute-start.4 = (bf16[256,896]{1,0:T(8,128)(2,1)}, bf16[256,896]{1,0:T(8,128)(2,1)}, u32[]{:S(2)}, u32[]{:S(2)}) collective-permute-start(bf16[256,896]{1,0:T(8,128)(2,1)} %collective-permute-done.3.own_ref.refs_0_.refs_4_), channel_id=1, source_target_pairs={{0,64},{64,0},{1,65},{65,1},{2,66},{66,2},{3,67},{67,3},{4,68},{68... | collective-permute-start | bytes 1376264 | tf_op jit(solution)/shard_map/ppermute | solution.py:28
  57.5 16.0 %collective-permute-start.6 = (bf16[256,896]{1,0:T(8,128)(2,1)}, bf16[256,896]{1,0:T(8,128)(2,1)}, u32[]{:S(2)}, u32[]{:S(2)}) collective-permute-start(bf16[256,896]{1,0:T(8,128)(2,1)} %collective-permute-done.5.own_ref.refs_2_.refs_6_), channel_id=1, source_target_pairs={{0,64},{64,0},{1,65},{65,1},{2,66},{66,2},{3,67},{67,3},{4,68},{68... | collective-permute-start | bytes 1376264 | tf_op jit(solution)/shard_map/ppermute | solution.py:28
  78.5 1.3 collective-permute-start.7
  79.8 4.6 %collective-permute-start.8 = (f32[4,512]{1,0:T(4,128)S(1)}, f32[4,512]{1,0:T(4,128)S(1)}, u32[]{:S(2)}, u32[]{:S(2)}) collective-permute-start(f32[4,512]{1,0:T(4,128)S(1)} %get-tuple-element.80), channel_id=1, source_target_pairs={{0,3},{1,0},{2,1},{3,2},{4,7},{5,4},{6,5},{7,6},{8,11},{9,8},{10,9... | collective-permute-start | bytes 24584 | tf_op jit(solution)/shard_map/ppermute | solution.py:28
  82.9 5.2 %collective-permute-start.9 = (f32[4,512]{1,0:T(4,128)S(1)}, f32[4,512]{1,0:T(4,128)S(1)}, u32[]{:S(2)}, u32[]{:S(2)}) collective-permute-start(f32[4,512]{1,0:T(4,128)S(1)} %get-tuple-element.80), channel_id=1, source_target_pairs={{0,2},{1,3},{2,0},{3,1},{4,6},{5,7},{6,4},{7,5},{8,10},{9,11},{10,... | collective-permute-start | bytes 24584 | tf_op jit(solution)/shard_map/ppermute | solution.py:28
  83.0 5.1 %collective-permute-start.10 = (f32[4,512]{1,0:T(4,128)S(1)}, f32[4,512]{1,0:T(4,128)S(1)}, u32[]{:S(2)}, u32[]{:S(2)}) collective-permute-start(f32[4,512]{1,0:T(4,128)S(1)} %get-tuple-element.80), channel_id=1, source_target_pairs={{0,1},{1,2},{2,3},{3,0},{4,5},{5,6},{6,7},{7,4},{8,9},{9,10},{10,1... | collective-permute-start | bytes 24584 | tf_op jit(solution)/shard_map/ppermute | solution.py:28
  88.9 12.4 %all-to-all-start.1 = ((f32[16,8,256]{2,1,0:T(8,128)}), f32[16,8,256]{2,1,0:T(8,128)S(1)}, u32[]{:S(2)}, u32[]{:S(2)}) async-start(f32[16,8,256]{2,1,0:T(8,128)} %broadcast_in_dim.30), calls=%async_computation.1 | async-start | bytes 262144 | tf_op jit(solution)/shard_map/all_to_all | solution.py:357
  112.8 2.6 %collective-permute-start.11 = (bf16[512,896]{1,0:T(8,128)(2,1)S(1)}, bf16[512,896]{1,0:T(8,128)(2,1)S(1)}, u32[]{:S(2)}, u32[]{:S(2)}) collective-permute-start(bf16[512,896]{1,0:T(8,128)(2,1)S(1)} %get-tuple-element.68), channel_id=1, source_target_pairs={{0,64},{64,0},{1,65},{65,1},{2,66},{66,2},{3,67},{67,3},{4,68},{68... | collective-permute-start | bytes 2752520 | tf_op jit(solution)/shard_map/ppermute | solution.py:28
  116.6 36.1 %all-to-all-start.2 = ((bf16[64,8,896]{2,1,0:T(8,128)(2,1)}), bf16[64,8,896]{2,1,0:T(8,128)(2,1)}, u32[]{:S(2)}, u32[]{:S(2)}) async-start(bf16[64,8,896]{2,1,0:T(8,128)(2,1)} %bitcast.6), calls=%async_computation.2 | async-start | bytes 1835008 | tf_op jit(solution)/shard_map/all_to_all | solution.py:363
  138.3 2.4 %collective-permute-start.12 = (bf16[512,768]{1,0:T(8,128)(2,1)S(1)}, bf16[512,768]{1,0:T(8,128)(2,1)}, u32[]{:S(2)}, u32[]{:S(2)}) collective-permute-start(bf16[512,768]{1,0:T(8,128)(2,1)S(1)} %get-tuple-element.75), channel_id=1, source_target_pairs={{0,64},{64,0},{1,65},{65,1},{2,66},{66,2},{3,67},{67,3},{4,68},{68... | collective-permute-start | bytes 2359304 | tf_op jit(solution)/shard_map/ppermute | solution.py:28
  138.3 4.5 %collective-permute-start.13 = (bf16[512,768]{1,0:T(8,128)(2,1)S(1)}, bf16[512,768]{1,0:T(8,128)(2,1)}, u32[]{:S(2)}, u32[]{:S(2)}) collective-permute-start(bf16[512,768]{1,0:T(8,128)(2,1)S(1)} %get-tuple-element.76), channel_id=1, source_target_pairs={{0,64},{64,0},{1,65},{65,1},{2,66},{66,2},{3,67},{67,3},{4,68},{68... | collective-permute-start | bytes 2359304 | tf_op jit(solution)/shard_map/ppermute | solution.py:28
  138.8 6.0 %collective-permute-start.14 = (bf16[512,768]{1,0:T(8,128)(2,1)S(1)}, bf16[512,768]{1,0:T(8,128)(2,1)}, u32[]{:S(2)}, u32[]{:S(2)}) collective-permute-start(bf16[512,768]{1,0:T(8,128)(2,1)S(1)} %get-tuple-element.77), channel_id=1, source_target_pairs={{0,64},{64,0},{1,65},{65,1},{2,66},{66,2},{3,67},{67,3},{4,68},{68... | collective-permute-start | bytes 2359304 | tf_op jit(solution)/shard_map/ppermute | solution.py:28
  138.9 8.0 %collective-permute-start.15 = (bf16[512,768]{1,0:T(8,128)(2,1)S(1)}, bf16[512,768]{1,0:T(8,128)(2,1)}, u32[]{:S(2)}, u32[]{:S(2)}) collective-permute-start(bf16[512,768]{1,0:T(8,128)(2,1)S(1)} %get-tuple-element.78), channel_id=1, source_target_pairs={{0,64},{64,0},{1,65},{65,1},{2,66},{66,2},{3,67},{67,3},{4,68},{68... | collective-permute-start | bytes 2359304 | tf_op jit(solution)/shard_map/ppermute | solution.py:28

commit v4 on v3

--- a/solution.py
+++ b/solution.py
@@ -14,13 +14,15 @@
 LO, MID, HI, CNT = 0, 8, 16, 24
 VMEM = pl.BlockSpec(memory_space=pltpu.VMEM)
 SMEM = pl.BlockSpec(memory_space=pltpu.SMEM)
+ANY = pl.BlockSpec(memory_space=pl.ANY)
 HBM = pl.BlockSpec(memory_space=pltpu.HBM)
 NT = (((1,), (1,)), ((), ()))
 TN = (((0,), (0,)), ((), ()))
 LCH = 256
 PROD = 1024
 EXPO = 128
-PARTS = 4
+PARTS = 2
+CLASS = 512
 
 
 def shift(x, axis, step):
@@ -28,12 +30,20 @@
     return lax.ppermute(x, axis, [(i, (i + step) % n) for i in range(n)])
 
 
-def scores_kernel(own_ref, oth_ref, w_ref, e_ref, m_ref, l_ref, s_ref, qt_ref, held_ref, sem):
+def in_hbm(arrays):
+    return [pltpu.with_memory_space_constraint(a, pltpu.HBM) for a in arrays]
+
+
+def scores_kernel(own_ref, oth_ref, w_ref, e_ref, m_ref, l_ref, q_ref, s_ref, qt_ref, held_ref, sem):
     labels, width = w_ref.shape
     rows = own_ref.shape[0]
     both = 2 * rows
-    qt_ref[:, :rows] = own_ref[:, :width].T
-    qt_ref[:, rows:] = oth_ref[:, :width].T
+    copies = [pltpu.make_async_copy(a, q_ref.at[k], sem.at[k]) for k, a in enumerate((own_ref, oth_ref))]
+    for copy in copies:
+        copy.start()
+    for k, copy in enumerate(copies):
+        copy.wait()
+        qt_ref[:, k * rows:(k + 1) * rows] = q_ref[k, :, :width].T
 
     def product(i, top):
         at = pl.multiple_of(i * PROD, PROD)
@@ -73,9 +83,10 @@
     return pl.pallas_call(
         scores_kernel,
         out_shape=(pltpu.HBM((labels, 2 * rows), jnp.bfloat16), line, line),
-        in_specs=[VMEM] * 3,
+        in_specs=[ANY, ANY, VMEM],
         out_specs=(HBM, VMEM, VMEM),
         scratch_shapes=[
+            pltpu.VMEM((2,) + own.shape, jnp.bfloat16),
             pltpu.VMEM((labels, 2 * rows), jnp.float32),
             pltpu.VMEM((width, 2 * rows), jnp.bfloat16),
             pltpu.VMEM((labels, 2 * rows), jnp.bfloat16),
@@ -88,8 +99,8 @@
 
 
 def hits_kernel(base_ref, *refs):
-    sources = refs[:4]
-    w_ref, n_ref, key_ref, s_ref, t_ref, blocks, sem = refs[4:]
+    sources = refs[:8]
+    w_ref, n_ref, key_ref, s_ref, t_ref, blocks, sem = refs[8:]
     copies = [pltpu.make_async_copy(q, blocks.at[b], sem.at[b]) for b, q in enumerate(sources)]
     for copy in copies:
         copy.start()
@@ -105,7 +116,7 @@
     slot = lax.broadcasted_iota(jnp.int32, (8, rows), 0)
     lane = lax.broadcasted_iota(jnp.int32, (8, rows), 1)
     keys, weights, most = [], [], jnp.int32(0)
-    for b in range(4):
+    for b in range(8):
         copies[b].wait()
         extra = blocks[b, :, width:]
         ids = lax.dot_general(digits, extra, NT, preferred_element_type=jnp.float32)
@@ -141,7 +152,7 @@
             row_w = jnp.where(r16 == label - lat, w_ref[pl.ds(lat, 16), :].astype(jnp.float32), 0.0)
             score.append(jnp.sum(row_w * jnp.sum(row_q, 0, keepdims=True)))
             weight.append(jnp.sum(jnp.where(same[b], weights[b], 0.0)))
-        for b in range(4):
+        for b in range(8):
             at = b * rows * POS + i
             key_ref[at] = found[b]
             s_ref[at] = score[b]
@@ -152,32 +163,31 @@
 
 
 def hits_call(base, blocks, w):
-    total = 4 * blocks[0].shape[0] * POS
+    total = 8 * blocks[0].shape[0] * POS
     return pl.pallas_call(
         hits_kernel,
         out_shape=(
-            jax.ShapeDtypeStruct((4,), jnp.int32),
+            jax.ShapeDtypeStruct((8,), jnp.int32),
             jax.ShapeDtypeStruct((total,), jnp.int32),
             jax.ShapeDtypeStruct((total,), jnp.float32),
             jax.ShapeDtypeStruct((total,), jnp.float32),
         ),
-        in_specs=[SMEM] + [HBM] * 4 + [VMEM],
+        in_specs=[SMEM] + [HBM] * 8 + [VMEM],
         out_specs=(SMEM,) * 4,
-        scratch_shapes=[pltpu.VMEM((4,) + blocks[0].shape, jnp.bfloat16), pltpu.SemaphoreType.DMA((4,))],
-        compiler_params=pltpu.CompilerParams(vmem_limit_bytes=12 * 2**20),
+        scratch_shapes=[pltpu.VMEM((8,) + blocks[0].shape, jnp.bfloat16), pltpu.SemaphoreType.DMA((8,))],
+        compiler_params=pltpu.CompilerParams(vmem_limit_bytes=16 * 2**20),
         cost_estimate=pl.CostEstimate(flops=1000, bytes_accessed=1000, transcendentals=0),
         name="hits",
-    )(base, *blocks, w)
-
-
-def query_kernel(at_ref, na, ka, sa, ta, nb, kb, sb, tb, lse_ref, m_ref, e0, e1, e2, e3, w_ref, *outs):
+    )(base, *in_hbm(blocks), w)
+
+
+def query_kernel(at_ref, n_ref, key_ref, s_ref, t_ref, lse_ref, m_ref, e0, e1, e2, e3, w_ref, *outs):
     own_ref, oth_ref, pos_ref, held, sem = outs[4:]
     ps = [held.at[d] for d in range(4)]
     copies = [pltpu.make_async_copy(e, p, sem.at[d]) for d, (e, p) in enumerate(zip((e0, e1, e2, e3), ps))]
     for copy in copies:
         copy.start()
     labels, width = w_ref.shape
-    lists = ((na, ka, sa, ta, 0), (na, ka, sa, ta, 2), (nb, kb, sb, tb, 0), (nb, kb, sb, tb, 2))
     rows = e0.shape[1] // 2
     xh, y = at_ref[0], at_ref[1]
     half = rows // 2
@@ -197,16 +207,15 @@
     c = lax.broadcasted_iota(jnp.int32, (16, half), 1)
     c1 = lax.broadcasted_iota(jnp.int32, (1, EXTRA), 1)
     most = jnp.int32(0)
-    for b in range(4):
-        most = jnp.maximum(most, jnp.maximum(na[b], nb[b]))
+    for b in range(8):
+        most = jnp.maximum(most, n_ref[b])
 
     def patch(i, carry):
         todo = []
         for b in range(8):
             d, k = b // 2, b % 2
-            n_ref, key_ref, s_ref, t_ref, first = lists[d]
-            at = (first + k) * rows * POS + i
-            live = i < n_ref[first + k]
+            at = b * rows * POS + i
+            live = i < n_ref[b]
             key, s, weight = jnp.where(live, key_ref[at], 0), s_ref[at], t_ref[at]
             label = key & (labels - 1)
             rest = lax.div(key, labels)
@@ -256,19 +265,19 @@
     res = pl.pallas_call(
         query_kernel,
         out_shape=tuple(pltpu.HBM(e.shape, e.dtype) for e in es) + (out, out),
-        in_specs=[SMEM] * 9 + [VMEM] * 2 + [HBM] * 4 + [VMEM],
+        in_specs=[SMEM] * 5 + [VMEM] * 2 + [HBM] * 4 + [VMEM],
         out_specs=(HBM,) * 4 + (VMEM,) * 2,
         scratch_shapes=[pltpu.VMEM((2, 2 * rows, EXTRA), jnp.float32), pltpu.VMEM((4,) + es[0].shape, jnp.bfloat16), pltpu.SemaphoreType.DMA((4,))],
         compiler_params=pltpu.CompilerParams(vmem_limit_bytes=28 * 2**20),
         cost_estimate=pl.CostEstimate(flops=8 * rows * labels * width, bytes_accessed=2**24, transcendentals=0),
         name="query_part",
-    )(at, *hits[0], *hits[1], lse, m, *[pltpu.with_memory_space_constraint(e, pltpu.HBM) for e in es], w)
+    )(at, *hits, lse, m, *in_hbm(es), w)
     return res[:4], res[4], res[5]
 
 
 def class_kernel(core_ref, p0, p1, p2, p3, *refs):
     blocks = refs[:8]
-    out_ref, parts = refs[8], refs[9:]
+    out_ref, mine_ref = refs[-2:]
     rows = blocks[0].shape[0]
     width = out_ref.shape[1]
     acc = None
@@ -278,33 +287,61 @@
             acc = term if acc is None else acc + term
     done = acc.astype(jnp.bfloat16)
     out_ref[...] = done
-    each = pl.num_programs(0) // len(parts)
-    for j, part in enumerate(parts):
-        @pl.when(pl.program_id(0) // each == j)
-        def _():
-            part[...] = done
-
-
-def class_call(core, ps, blocks, width):
+    mine_ref[...] = done
+
+
+def class_call(core, ps, blocks, width, part, before):
     labels = ps[0].shape[0]
-    steps = labels // LCH
+    steps = labels // CLASS
     each = steps // PARTS
     rows = blocks[0].shape[0]
     whole = lambda i, c: (0, 0)
+    kept = () if before is None else (before,)
     return pl.pallas_call(
         class_kernel,
-        out_shape=(jax.ShapeDtypeStruct((2 * labels, width), jnp.bfloat16),) + (jax.ShapeDtypeStruct((labels // PARTS, width), jnp.bfloat16),) * PARTS,
+        out_shape=tuple(jax.ShapeDtypeStruct((n, width), jnp.bfloat16) for n in (2 * labels, labels // PARTS)),
         grid_spec=pltpu.PrefetchScalarGridSpec(
             num_scalar_prefetch=1,
-            grid=(steps,),
-            in_specs=[pl.BlockSpec((LCH, 2 * rows), lambda i, c: (i, 0))] * 4 + [pl.BlockSpec(blocks[0].shape, whole)] * 8,
-            out_specs=(pl.BlockSpec((LCH, width), lambda i, c: (c[0] * steps + i, 0)),)
-            + tuple(pl.BlockSpec((LCH, width), lambda i, c, j=j: (jnp.clip(i - j * each, 0, each - 1), 0)) for j in range(PARTS)),
+            grid=(each,),
+            in_specs=[pl.BlockSpec((CLASS, 2 * rows), lambda i, c: (part * each + i, 0))] * 4
+            + [pl.BlockSpec(blocks[0].shape, whole)] * 8
+            + [HBM] * len(kept),
+            out_specs=(
+                pl.BlockSpec((CLASS, width), lambda i, c: (c[0] * steps + part * each + i, 0)),
+                pl.BlockSpec((CLASS, width), lambda i, c: (i, 0)),
+            ),
         ),
-        compiler_params=pltpu.CompilerParams(vmem_limit_bytes=20 * 2**20),
-        cost_estimate=pl.CostEstimate(flops=16 * rows * labels * width, bytes_accessed=2**24, transcendentals=0),
+        input_output_aliases={13: 0} if kept else {},
+        compiler_params=pltpu.CompilerParams(vmem_limit_bytes=24 * 2**20),
+        cost_estimate=pl.CostEstimate(flops=16 * rows * labels * width // PARTS, bytes_accessed=2**23, transcendentals=0),
         name="class_part",
-    )(core, *[pltpu.with_memory_space_constraint(p, pltpu.HBM) for p in ps], *blocks)
+    )(core, *in_hbm(ps), *in_hbm(blocks), *kept)
+
+
+def place_kernel(core_ref, *refs):
+    parts, out_ref, sem = refs[:PARTS], refs[-2], refs[-1]
+    rows = parts[0].shape[0]
+    first = (1 - core_ref[0]) * (PARTS * rows)
+    copies = [
+        pltpu.make_async_copy(p, out_ref.at[pl.ds(pl.multiple_of(first + j * rows, rows), rows), :], sem.at[j]) for j, p in enumerate(parts)
+    ]
+    for copy in copies:
+        copy.start()
+    for copy in copies:
+        copy.wait()
+
+
+def place_call(core, parts, into):
+    return pl.pallas_call(
+        place_kernel,
+        out_shape=jax.ShapeDtypeStruct(into.shape, into.dtype),
+        in_specs=[SMEM] + [ANY] * PARTS + [HBM],
+        out_specs=HBM,
+        scratch_shapes=[pltpu.SemaphoreType.DMA((PARTS,))],
+        input_output_aliases={1 + PARTS: 0},
+        cost_estimate=pl.CostEstimate(flops=1000, bytes_accessed=1000, transcendentals=0),
+        name="place",
+    )(core, *parts, into)
 
 
 def lse_of(parts, axis=None):
@@ -328,27 +365,25 @@
         1,
     ).astype(jnp.bfloat16)
     sent = jnp.concatenate([embeddings, extra], 1)
-    copies = jnp.broadcast_to(sent[None], (32, q_dev, width + EXTRA)).reshape(32 * q_dev, width + EXTRA)
-    mine = lax.all_to_all(copies, ("xh", "xl", "z"), 0, 0, tiled=True)
-    own = [mine] + [shift(mine, "y", -d) for d in range(1, 4)]
-    oth = [shift(b, "core", 1) for b in own]
+    spread = lambda x, n: jnp.broadcast_to(x[None], (n,) + x.shape).reshape((n * x.shape[0],) + x.shape[1:])
+    column = lax.all_to_all(spread(sent, SIZES["z"]), "z", 0, 0, tiled=True)
+    mine = lax.all_to_all(spread(column, 4), ("xh", "xl"), 0, 0, tiled=True)
+    own = [mine, shift(mine, "y", -1), None, shift(mine, "y", 1)]
+    relay = [(c * 4 + i, c * 4 + (i + 2 * c - 1) % 4) for c in range(2) for i in range(4)]
+    own[2] = lax.ppermute(jnp.where(core == 0, own[1], own[3]), ("core", "y"), relay)
     w = lax.dynamic_slice_in_dim(classifier, core * labels, labels)
     rows = mine.shape[0]
 
-    oth, parts, ready = [None] * 4, [None] * 4, list(own)
-    for d in range(4):
+    oth, parts = [None] * 4, [None] * 4
+    for d in (0, 1, 3, 2):
         if d:
-            own[d], _ = lax.optimization_barrier((own[d], parts[0][1]))
+            done = (parts[1][1], parts[3][1]) if d == 2 else (parts[0][1],)
+            own[d] = lax.optimization_barrier((own[d],) + done)[0]
         oth[d] = shift(own[d], "core", 1)
-        ready[d] = own[d]
-        if d >= 2:
-            ready[d], _ = lax.optimization_barrier((own[d], hits[0][0]))
-        parts[d] = scores_call(ready[d], oth[d], w)
-        if d == 1:
-            hits = [hits_call(base[None], (own[0], oth[0], own[1], oth[1]), w)]
+        parts[d] = scores_call(own[d], oth[d], w)
     es, ms, ls = zip(*parts)
     blocks = [b for pair in zip(own, oth) for b in pair]
-    hits.append(hits_call(base[None], blocks[4:], w))
+    hits = hits_call(base[None], blocks, w)
     m = jnp.concatenate(ms, 0)
     stat = jnp.concatenate(ls, 0)
     stat = lse_of([stat, jnp.roll(shift(stat, "core", 1), rows, 1)])
@@ -361,15 +396,17 @@
     u = (f32(u_own) + f32(shift(u_oth, "core", 1))).astype(jnp.bfloat16)
     first, u = lax.optimization_barrier((ps[0], u))
     got = lax.all_to_all(u, ("y", "xl", "z"), 0, 0, tiled=True)
-    class_grad, *mine_parts = class_call(core[None], (first,) + tuple(ps[1:]), blocks, width)
+    class_grad, sent_parts = None, []
+    for j in range(PARTS):
+        class_grad, mine_part = class_call(core[None], (first,) + tuple(ps[1:]), blocks, width, j, class_grad)
+        sent_parts.append(shift(mine_part, "core", 1))
+    class_grad = place_call(core[None], sent_parts, class_grad)
 
     final = jnp.sum(f32(got).reshape(64, q_dev, width + EXTRA), 0)
     query_grad = final[:, :width].astype(jnp.bfloat16)
     pos_mean = jnp.sum(final[:, width:width + 24], 1)
     at = ((xh * 2 + xl) * 8 + z) * q_dev
     loss = lax.dynamic_slice(lse, (0, at), (1, q_dev))[0] - pos_mean
-    for j, part in enumerate(mine_parts):
-        class_grad = lax.dynamic_update_slice_in_dim(class_grad, shift(part, "core", 1), (1 - core) * labels + j * part.shape[0], 0)
     return loss, query_grad, class_grad
 
 

time: 156 us -> 236 us (1.51)
  Pallas kernels: 56.9 us -> 152 us
  waiting for transfers between devices: 28 us -> 19 us
  local copies, waits for them, and re-layouts: 12.6 us -> 4.39 us
    pallas_call x3 -> x4, Pallas kernels: 25.7 us -> 121 us  [the longest x1 96.4 us: place_call(): pl.pallas_call(place_kernel, out_shape=jax.ShapeDtypeStruct(into.shape, i...]
    dynamic_update_slice x4 -> x0, local copies, waits for them, and re-layouts: 8.25 us -> none  [body(): lax.dynamic_update_slice_in_dim(class_grad, shift(part, 'core', 1), (1 -...]
    ppermute x16 -> x13, waiting for transfers between devices: 23.8 us -> 19 us  [shift(): return lax.ppermute(x, axis, [(i, (i + step) % n) for i in range(n)])]
    all_to_all x1, waiting for transfers between devices: 3.65 us -> 0.01 us  [body(): got = lax.all_to_all(u, ('y', 'xl', 'z'), 0, 0, tiled=True)]
    ppermute x16 -> x13, starting transfers between devices: 11 us -> 8.01 us  [shift(): return lax.ppermute(x, axis, [(i, (i + step) % n) for i in range(n)])]
    all_to_all x1 -> x2, blocking collectives: 27.3 us -> 27.6 us  [the longest x1 15.7 us: body(): column = lax.all_to_all(spread(sent, SIZES['z']), 'z', 0, 0, tiled=True)]
  transfers between devices with their start and end apart: 18 -> 16, of which waited for: 8 -> 9; matrix products, arithmetic and copies ran while one was open for 7% -> 1% of each run, Pallas kernels for 26% -> 58%
where the time goes in v4:
time: 236 us; the launch traced here: 234 us
  Pallas kernels  152 us (64%)
  blocking collectives  27.6 us (12%)
  starting transfers between devices  24.1 us (10%)
  waiting for transfers between devices  19 us (8%)
  other arithmetic  5.9 us (2%)
  local copies, waits for them, and re-layouts  4.39 us (2%)
    pallas_call x1, Pallas kernels, place_call(): pl.pallas_call(place_kernel, out_shape=jax.ShapeDtypeStruct(into.shape, i...  96.4 us
    pallas_call x4, Pallas kernels, scores_call(): pl.pallas_call(scores_kernel, out_shape=(pltpu.HBM((labels, 2 * rows), jn...  19.2 us
    ppermute x13, waiting for transfers between devices, shift(): return lax.ppermute(x, axis, [(i, (i + step) % n) for i in range(n)])  19 us
    all_to_all x1, blocking collectives, body(): column = lax.all_to_all(spread(sent, SIZES['z']), 'z', 0, 0, tiled=True)  15.7 us
    pallas_call x2, Pallas kernels, class_call(): pl.pallas_call(class_kernel, out_shape=tuple((jax.ShapeDtypeStruct((n, wi...  14.7 us
    all_to_all x1, blocking collectives, body(): mine = lax.all_to_all(spread(column, 4), ('xh', 'xl'), 0, 0, tiled=True)  11.9 us
    pallas_call x1, Pallas kernels, query_call(): pl.pallas_call(query_kernel, out_shape=tuple((pltpu.HBM(e.shape, e.dtype)...  11.6 us
    pallas_call x1, Pallas kernels, hits_call(): pl.pallas_call(hits_kernel, out_shape=(jax.ShapeDtypeStruct((8,), jnp.int...  10.3 us
  transfers between devices with their start and end apart: 16, of which 9 were waited for; matrix products, arithmetic and copies ran while one was open for 1% of the time, Pallas kernels for 58%

profile of v4, /device:TPU:32, one launch (start us, length us, event | category | flops | bytes accessed | tf_op | source)
XLA Modules:
  0.0 234.1 jit_solution(506234889899964337)
XLA Ops:
  2.9 15.7 %all_to_all.28 = bf16[8,8,896]{2,1,0:T(8,128)(2,1)S(1)} all-to-all(bf16[8,8,896]{2,1,0:T(8,128)(2,1)S(1)} %broadcast_in_dim.37), channel_id=1, replica_groups=mesh['xh'=2,'core'=2,'xl'=2,'z'=8,'y'=4] {'z'}, dimensions={0} | all-to-all | bytes 229376 | tf_op jit(solution)/shard_map/all_to_all | solution.py:369
  18.6 11.9 %all_to_all.29 = bf16[4,64,896]{2,1,0:T(8,128)(2,1)} all-to-all(bf16[4,64,896]{2,1,0:T(8,128)(2,1)S(1)} %broadcast_in_dim.39), channel_id=1, replica_groups=mesh['xh'=2,'core'=2,'xl'=2,'z'=8,'y'=4] {'xh','xl'}, dimensions={0} | all-to-all | bytes 917504 | tf_op jit(solution)/shard_map/all_to_all | solution.py:370
  30.5 3.0 %collective-permute-start.1 = (bf16[256,896]{1,0:T(8,128)(2,1)}, bf16[256,896]{1,0:T(8,128)(2,1)}, u32[]{:S(2)}, u32[]{:S(2)}) collective-permute-start(bf16[256,896]{1,0:T(8,128)(2,1)} %bitcast.2.own_ref.refs_0_), channel_id=1, source_target_pairs={{0,3},{1,0},{2,1},{3,2},{4,7},{5,4},{6,5},{7,6},{8,11},{9,8},{10,9... | collective-permute-start | bytes 1376264 | tf_op jit(solution)/shard_map/ppermute | solution.py:30
  33.6 2.1 constant_dynamic-slice_fusion.w_ref.refs_8_
  35.7 4.9 %scores.4 = (bf16[2048,512]{1,0:T(8,128)(2,1)}, f32[1,512]{1,0:T(1,128)S(1)}, f32[1,512]{1,0:T(1,128)S(1)}) custom-call(bf16[256,896]{1,0:T(8,128)(2,1)} %bitcast.2.own_ref.refs_0_, bf16[256,896]{1,0:T(8,128)(2,1)} %collective-permute-done.oth_ref.refs_1_, bf16[2048,768]{1,0:T(8,128)(2,1)S(1)} %constant_dynamic-slice_fusion.w_ref.refs_8_), custom_call_target="tpu_custom_call" | custom-call | flops 1000 | bytes 1000 | tf_op jit(solution)/shard_map/scores/pallas_call | solution.py:83
  40.5 3.8 %collective-permute-done.1.own_ref.refs_2_ = bf16[256,896]{1,0:T(8,128)(2,1)} collective-permute-done((bf16[256,896]{1,0:T(8,128)(2,1)}, bf16[256,896]{1,0:T(8,128)(2,1)}, u32[]{:S(2)}, u32[]{:S(2)}) %collective-permute-start.1) | collective-permute-done | bytes 458784 | tf_op jit(solution)/shard_map/ppermute | solution.py:30
  44.3 3.4 %collective-permute-done.3.own_ref.refs_6_ = bf16[256,896]{1,0:T(8,128)(2,1)} collective-permute-done((bf16[256,896]{1,0:T(8,128)(2,1)}, bf16[256,896]{1,0:T(8,128)(2,1)}, u32[]{:S(2)}, u32[]{:S(2)}) %collective-permute-start.3) | collective-permute-done | bytes 458784 | tf_op jit(solution)/shard_map/ppermute | solution.py:30
  49.7 5.0 %scores.5 = (bf16[2048,512]{1,0:T(8,128)(2,1)}, f32[1,512]{1,0:T(1,128)S(1)}, f32[1,512]{1,0:T(1,128)S(1)}) custom-call(bf16[256,896]{1,0:T(8,128)(2,1)} %collective-permute-done.1.own_ref.refs_2_, bf16[256,896]{1,0:T(8,128)(2,1)S(1)} %collective-permute-done.2.oth_ref.refs_3_, bf16[2048,768]{1,0:T(8,128)(2,1)S(1)} %constant_dynamic-slice_fusion.w_ref.refs_8_), custom_call_target="tpu_custom_call" | custom-call | flops 1000 | bytes 1000 | tf_op jit(solution)/shard_map/scores/pallas_call | solution.py:83
  54.7 5.0 %scores.6 = (bf16[2048,512]{1,0:T(8,128)(2,1)}, f32[1,512]{1,0:T(1,128)S(1)}, f32[1,512]{1,0:T(1,128)S(1)}) custom-call(bf16[256,896]{1,0:T(8,128)(2,1)} %collective-permute-done.3.own_ref.refs_6_, bf16[256,896]{1,0:T(8,128)(2,1)S(1)} %collective-permute-done.5.oth_ref.refs_7_, bf16[2048,768]{1,0:T(8,128)(2,1)S(1)} %constant_dynamic-slice_fusion.w_ref.refs_8_), custom_call_target="tpu_custom_call" | custom-call | flops 1000 | bytes 1000 | tf_op jit(solution)/shard_map/scores/pallas_call | solution.py:83
  59.9 1.8 collective-permute-done.6.oth_ref.refs_5_
  61.7 4.4 %scores.7 = (bf16[2048,512]{1,0:T(8,128)(2,1)}, f32[1,512]{1,0:T(1,128)S(1)}, f32[1,512]{1,0:T(1,128)S(1)}) custom-call(bf16[256,896]{1,0:T(8,128)(2,1)S(1)} %collective-permute-done.4.own_ref.refs_4_, bf16[256,896]{1,0:T(8,128)(2,1)S(1)} %collective-permute-done.6.oth_ref.refs_5_, bf16[2048,768]{1,0:T(8,128)(2,1)S(1)} %constant_dynamic-slice_fusion.w_ref.refs_8_), custom_call_target="tpu_custom_call" | custom-call | flops 1000 | bytes 1000 | tf_op jit(solution)/shard_map/scores/pallas_call | solution.py:83
  67.4 1.3 collective-permute-start.10
  68.7 2.6 %collective-permute-start.9 = (f32[4,512]{1,0:T(4,128)S(1)}, f32[4,512]{1,0:T(4,128)S(1)}, u32[]{:S(2)}, u32[]{:S(2)}) collective-permute-start(f32[4,512]{1,0:T(4,128)S(1)} %get-tuple-element.66), channel_id=1, source_target_pairs={{0,2},{1,3},{2,0},{3,1},{4,6},{5,7},{6,4},{7,5},{8,10},{9,11},{10,... | collective-permute-start | bytes 24584 | tf_op jit(solution)/shard_map/ppermute | solution.py:30
  72.3 1.5 collective-permute-done.9
  75.7 4.9 %all-to-all-start.2 = ((f32[16,8,256]{2,1,0:T(8,128)}), f32[16,8,256]{2,1,0:T(8,128)S(1)}, u32[]{:S(2)}, u32[]{:S(2)}) async-start(f32[16,8,256]{2,1,0:T(8,128)} %broadcast_in_dim.40), calls=%async_computation.2 | async-start | bytes 262144 | tf_op jit(solution)/shard_map/all_to_all | solution.py:392
  80.7 10.3 %hits.1 = (s32[8]{0:T(128)S(1)}, s32[10240]{0:T(1024)S(1)}, f32[10240]{0:T(1024)S(1)}, f32[10240]{0:T(1024)S(1)}) custom-call(s32[1]{0:T(128)} %bitcast.6.base_ref, bf16[256,896]{1,0:T(8,128)(2,1)} %bitcast.2.own_ref.refs_0_, bf16[256,896]{1,0:T(8,128)(2,1)} %collective-permute-done.oth_ref.refs_1_, bf16[256,896]{1,0:T(8,128)(2,1)} %collective-permute-done.1.own_ref.refs_2_, ...), custom_call_target="tpu_custom_call" | custom-call | flops 1000 | bytes 1000 | tf_op jit(solution)/shard_map/hits/pallas_call | solution.py:167
  91.1 11.6 %query_part.1 = (bf16[2048,512]{1,0:T(8,128)(2,1)}, bf16[2048,512]{1,0:T(8,128)(2,1)}, bf16[2048,512]{1,0:T(8,128)(2,1)}, bf16[2048,512]{1,0:T(8,128)(2,1)}, bf1...) custom-call(s32[2]{0:T(128)S(1)} %pad_add_fusion.at_ref, s32[8]{0:T(128)S(1)} %get-tuple-element.44.n_ref, ...), custom_call_target="tpu_custom_call" | custom-call | flops 3221225472 | bytes 16777216 | tf_op jit(solution)/shard_map/query_part/pallas_call | solution.py:265
  102.8 2.5 %collective-permute-done.11 = bf16[512,896]{1,0:T(8,128)(2,1)S(1)} collective-permute-done((bf16[512,896]{1,0:T(8,128)(2,1)S(1)}, bf16[512,896]{1,0:T(8,128)(2,1)S(1)}, u32[]{:S(2)}, u32[]{:S(2)}) %collective-permute-start.11) | collective-permute-done | bytes 917536 | tf_op jit(solution)/shard_map/ppermute | solution.py:30
  106.4 10.3 %all-to-all-start.3 = ((bf16[64,8,896]{2,1,0:T(8,128)(2,1)}), bf16[64,8,896]{2,1,0:T(8,128)(2,1)}, u32[]{:S(2)}, u32[]{:S(2)}) async-start(bf16[64,8,896]{2,1,0:T(8,128)(2,1)} %bitcast.7), calls=%async_computation.3 | async-start | bytes 1835008 | tf_op jit(solution)/shard_map/all_to_all | solution.py:398
  116.7 7.4 %class_part.2 = (bf16[4096,768]{1,0:T(8,128)(2,1)}, bf16[1024,768]{1,0:T(8,128)(2,1)S(1)}) custom-call(s32[1]{0:T(128)} %bitcast.8.core_ref, bf16[2048,512]{1,0:T(8,128)(2,1)} %get-tuple-element.57.p0, bf16[2048,512]{1,0:T(8,128)(2,1)} %get-tuple-element.58.p1, bf16[2048,512]{1,0:T(8,128)(2,1)} %get-tuple-element.59.p2, ...), custom_call_target="tpu_custom_call" | custom-call | flops 3221225472 | bytes 8388608 | tf_op jit(solution)/shard_map/class_part/pallas_call | solution.py:300
  124.1 7.4 %class_part.3 = (bf16[4096,768]{1,0:T(8,128)(2,1)}, bf16[1024,768]{1,0:T(8,128)(2,1)S(1)}) custom-call(s32[1]{0:T(128)} %bitcast.8.core_ref, bf16[2048,512]{1,0:T(8,128)(2,1)} %get-tuple-element.57.p0, bf16[2048,512]{1,0:T(8,128)(2,1)} %get-tuple-element.58.p1, bf16[2048,512]{1,0:T(8,128)(2,1)} %get-tuple-element.59.p2, ...), custom_call_target="tpu_custom_call", output_to_operand_aliasing={{0}: (13, {})} | custom-call | flops 3221225472 | bytes 8388608 | tf_op jit(solution)/shard_map/class_part/pallas_call | solution.py:300
  131.9 3.2 %collective-permute-done.13.refs_1_ = bf16[1024,768]{1,0:T(8,128)(2,1)} collective-permute-done((bf16[1024,768]{1,0:T(8,128)(2,1)S(1)}, bf16[1024,768]{1,0:T(8,128)(2,1)}, u32[]{:S(2)}, u32[]{:S(2)}) %collective-permute-start.13) | collective-permute-done | bytes 1572896 | tf_op jit(solution)/shard_map/ppermute | solution.py:30
  135.1 96.4 %place.1 = bf16[4096,768]{1,0:T(8,128)(2,1)} custom-call(s32[1]{0:T(128)} %bitcast.8.core_ref, bf16[1024,768]{1,0:T(8,128)(2,1)} %collective-permute-done.12.refs_0_, bf16[1024,768]{1,0:T(8,128)(2,1)} %collective-permute-done.13.refs_1_, bf16[4096,768]{1,0:T(8,128)(2,1)} %get-tuple-element.64.refs_2_), custom_call_target="tpu_custom_call", output_to_operand_aliasing={{}: (3, {})} | custom-call | flops 1000 | bytes 1000 | tf_op jit(solution)/shard_map/place/pallas_call | solution.py:335
  231.5 1.3 convert_reduce_fusion
  (65 shorter events, 11.7 us)
Async XLA Ops:
  30.5 5.1 %collective-permute-start = (bf16[256,896]{1,0:T(8,128)(2,1)}, bf16[256,896]{1,0:T(8,128)(2,1)}, u32[]{:S(2)}, u32[]{:S(2)}) collective-permute-start(bf16[256,896]{1,0:T(8,128)(2,1)} %bitcast.2.own_ref.refs_0_), channel_id=1, source_target_pairs={{0,64},{64,0},{1,65},{65,1},{2,66},{66,2},{3,67},{67,3},{4,68},{68... | collective-permute-start | bytes 1376264 | tf_op jit(solution)/shard_map/ppermute | solution.py:30
  30.5 13.8 %collective-permute-start.1 = (bf16[256,896]{1,0:T(8,128)(2,1)}, bf16[256,896]{1,0:T(8,128)(2,1)}, u32[]{:S(2)}, u32[]{:S(2)}) collective-permute-start(bf16[256,896]{1,0:T(8,128)(2,1)} %bitcast.2.own_ref.refs_0_), channel_id=1, source_target_pairs={{0,3},{1,0},{2,1},{3,2},{4,7},{5,4},{6,5},{7,6},{8,11},{9,8},{10,9... | collective-permute-start | bytes 1376264 | tf_op jit(solution)/shard_map/ppermute | solution.py:30
  33.5 14.2 %collective-permute-start.3 = (bf16[256,896]{1,0:T(8,128)(2,1)}, bf16[256,896]{1,0:T(8,128)(2,1)}, u32[]{:S(2)}, u32[]{:S(2)}) collective-permute-start(bf16[256,896]{1,0:T(8,128)(2,1)} %bitcast.2.own_ref.refs_0_), channel_id=1, source_target_pairs={{0,1},{1,2},{2,3},{3,0},{4,5},{5,6},{6,7},{7,4},{8,9},{9,10},{10,1... | collective-permute-start | bytes 1376264 | tf_op jit(solution)/shard_map/ppermute | solution.py:30
  44.3 5.4 %collective-permute-start.2 = (bf16[256,896]{1,0:T(8,128)(2,1)}, bf16[256,896]{1,0:T(8,128)(2,1)S(1)}, u32[]{:S(2)}, u32[]{:S(2)}) collective-permute-start(bf16[256,896]{1,0:T(8,128)(2,1)} %collective-permute-done.1.own_ref.refs_2_), channel_id=1, source_target_pairs={{0,64},{64,0},{1,65},{65,1},{2,66},{66,2},{3,67},{67,3},{4,68},{68... | collective-permute-start | bytes 1376264 | tf_op jit(solution)/shard_map/ppermute | solution.py:30
  47.7 7.0 %collective-permute-start.5 = (bf16[256,896]{1,0:T(8,128)(2,1)}, bf16[256,896]{1,0:T(8,128)(2,1)S(1)}, u32[]{:S(2)}, u32[]{:S(2)}) collective-permute-start(bf16[256,896]{1,0:T(8,128)(2,1)} %collective-permute-done.3.own_ref.refs_6_), channel_id=1, source_target_pairs={{0,64},{64,0},{1,65},{65,1},{2,66},{66,2},{3,67},{67,3},{4,68},{68... | collective-permute-start | bytes 1376264 | tf_op jit(solution)/shard_map/ppermute | solution.py:30
  48.8 10.9 %collective-permute-start.4 = (bf16[256,896]{1,0:T(8,128)(2,1)S(1)}, bf16[256,896]{1,0:T(8,128)(2,1)S(1)}, u32[]{:S(2)}, u32[]{:S(2)}) collective-permute-start(bf16[256,896]{1,0:T(8,128)(2,1)S(1)} %broadcast_select_fusion), channel_id=1, source_target_pairs={{0,3},{1,0},{2,1},{3,2},{64,65},{65,66},{66,67},{67,64},{4,7},{5,4... | collective-permute-start | bytes 1376264 | tf_op jit(solution)/shard_map/ppermute | solution.py:373
  49.7 10.1 %copy-start = (bf16[256,896]{1,0:T(8,128)(2,1)}, bf16[256,896]{1,0:T(8,128)(2,1)S(1)}, u32[]{:S(2)}) copy-start(bf16[256,896]{1,0:T(8,128)(2,1)S(1)} %collective-permute-done.2.oth_ref.refs_3_) | copy-start | bytes 1376260
  54.7 11.3 %copy-start.1 = (bf16[256,896]{1,0:T(8,128)(2,1)}, bf16[256,896]{1,0:T(8,128)(2,1)S(1)}, u32[]{:S(2)}) copy-start(bf16[256,896]{1,0:T(8,128)(2,1)S(1)} %collective-permute-done.5.oth_ref.refs_7_) | copy-start | bytes 1376260
  59.7 6.3 %copy-start.2 = (bf16[256,896]{1,0:T(8,128)(2,1)}, bf16[256,896]{1,0:T(8,128)(2,1)S(1)}, u32[]{:S(2)}) copy-start(bf16[256,896]{1,0:T(8,128)(2,1)S(1)} %collective-permute-done.4.own_ref.refs_4_) | copy-start | bytes 1376260
  59.8 1.9 collective-permute-start.6
  61.7 4.4 %copy-start.3 = (bf16[256,896]{1,0:T(8,128)(2,1)}, bf16[256,896]{1,0:T(8,128)(2,1)S(1)}, u32[]{:S(2)}) copy-start(bf16[256,896]{1,0:T(8,128)(2,1)S(1)} %collective-permute-done.6.oth_ref.refs_5_) | copy-start | bytes 1376260
  66.1 1.3 collective-permute-start.7
  67.4 4.9 %collective-permute-start.10 = (f32[4,512]{1,0:T(4,128)S(1)}, f32[4,512]{1,0:T(4,128)S(1)}, u32[]{:S(2)}, u32[]{:S(2)}) collective-permute-start(f32[4,512]{1,0:T(4,128)S(1)} %get-tuple-element.66), channel_id=1, source_target_pairs={{0,1},{1,2},{2,3},{3,0},{4,5},{5,6},{6,7},{7,4},{8,9},{9,10},{10,1... | collective-permute-start | bytes 24584 | tf_op jit(solution)/shard_map/ppermute | solution.py:30
  68.7 5.2 %collective-permute-start.9 = (f32[4,512]{1,0:T(4,128)S(1)}, f32[4,512]{1,0:T(4,128)S(1)}, u32[]{:S(2)}, u32[]{:S(2)}) collective-permute-start(f32[4,512]{1,0:T(4,128)S(1)} %get-tuple-element.66), channel_id=1, source_target_pairs={{0,2},{1,3},{2,0},{3,1},{4,6},{5,7},{6,4},{7,5},{8,10},{9,11},{10,... | collective-permute-start | bytes 24584 | tf_op jit(solution)/shard_map/ppermute | solution.py:30
  71.3 3.7 %collective-permute-start.8 = (f32[4,512]{1,0:T(4,128)S(1)}, f32[4,512]{1,0:T(4,128)S(1)}, u32[]{:S(2)}, u32[]{:S(2)}) collective-permute-start(f32[4,512]{1,0:T(4,128)S(1)} %get-tuple-element.66), channel_id=1, source_target_pairs={{0,3},{1,0},{2,1},{3,2},{4,7},{5,4},{6,5},{7,6},{8,11},{9,8},{10,9... | collective-permute-start | bytes 24584 | tf_op jit(solution)/shard_map/ppermute | solution.py:30
  75.7 15.3 %all-to-all-start.2 = ((f32[16,8,256]{2,1,0:T(8,128)}), f32[16,8,256]{2,1,0:T(8,128)S(1)}, u32[]{:S(2)}, u32[]{:S(2)}) async-start(f32[16,8,256]{2,1,0:T(8,128)} %broadcast_in_dim.40), calls=%async_computation.2 | async-start | bytes 262144 | tf_op jit(solution)/shard_map/all_to_all | solution.py:392
  102.7 2.6 %collective-permute-start.11 = (bf16[512,896]{1,0:T(8,128)(2,1)S(1)}, bf16[512,896]{1,0:T(8,128)(2,1)S(1)}, u32[]{:S(2)}, u32[]{:S(2)}) collective-permute-start(bf16[512,896]{1,0:T(8,128)(2,1)S(1)} %get-tuple-element.55), channel_id=1, source_target_pairs={{0,64},{64,0},{1,65},{65,1},{2,66},{66,2},{3,67},{67,3},{4,68},{68... | collective-permute-start | bytes 2752520 | tf_op jit(solution)/shard_map/ppermute | solution.py:30
  106.4 125.1 %all-to-all-start.3 = ((bf16[64,8,896]{2,1,0:T(8,128)(2,1)}), bf16[64,8,896]{2,1,0:T(8,128)(2,1)}, u32[]{:S(2)}, u32[]{:S(2)}) async-start(bf16[64,8,896]{2,1,0:T(8,128)(2,1)} %bitcast.7), calls=%async_computation.3 | async-start | bytes 1835008 | tf_op jit(solution)/shard_map/all_to_all | solution.py:398
  124.1 7.8 %collective-permute-start.12 = (bf16[1024,768]{1,0:T(8,128)(2,1)S(1)}, bf16[1024,768]{1,0:T(8,128)(2,1)}, u32[]{:S(2)}, u32[]{:S(2)}) collective-permute-start(bf16[1024,768]{1,0:T(8,128)(2,1)S(1)} %get-tuple-element.61), channel_id=1, source_target_pairs={{0,64},{64,0},{1,65},{65,1},{2,66},{66,2},{3,67},{67,3},{4,68},{68... | collective-permute-start | bytes 4718600 | tf_op jit(solution)/shard_map/ppermute | solution.py:30
  131.4 3.6 %collective-permute-start.13 = (bf16[1024,768]{1,0:T(8,128)(2,1)S(1)}, bf16[1024,768]{1,0:T(8,128)(2,1)}, u32[]{:S(2)}, u32[]{:S(2)}) collective-permute-start(bf16[1024,768]{1,0:T(8,128)(2,1)S(1)} %get-tuple-element.63), channel_id=1, source_target_pairs={{0,64},{64,0},{1,65},{65,1},{2,66},{66,2},{3,67},{67,3},{4,68},{68... | collective-permute-start | bytes 4718600 | tf_op jit(solution)/shard_map/ppermute | solution.py:30

commit v5 on v4

--- a/solution.py
+++ b/solution.py
@@ -22,6 +22,7 @@
 PROD = 1024
 EXPO = 128
 PARTS = 2
+EARLY = 2
 CLASS = 512
 
 
@@ -99,8 +100,9 @@
 
 
 def hits_kernel(base_ref, *refs):
-    sources = refs[:8]
-    w_ref, n_ref, key_ref, s_ref, t_ref, blocks, sem = refs[8:]
+    count = len(refs) - 7
+    sources = refs[:count]
+    w_ref, n_ref, key_ref, s_ref, t_ref, blocks, sem = refs[count:]
     copies = [pltpu.make_async_copy(q, blocks.at[b], sem.at[b]) for b, q in enumerate(sources)]
     for copy in copies:
         copy.start()
@@ -116,7 +118,7 @@
     slot = lax.broadcasted_iota(jnp.int32, (8, rows), 0)
     lane = lax.broadcasted_iota(jnp.int32, (8, rows), 1)
     keys, weights, most = [], [], jnp.int32(0)
-    for b in range(8):
+    for b in range(count):
         copies[b].wait()
         extra = blocks[b, :, width:]
         ids = lax.dot_general(digits, extra, NT, preferred_element_type=jnp.float32)
@@ -152,7 +154,7 @@
             row_w = jnp.where(r16 == label - lat, w_ref[pl.ds(lat, 16), :].astype(jnp.float32), 0.0)
             score.append(jnp.sum(row_w * jnp.sum(row_q, 0, keepdims=True)))
             weight.append(jnp.sum(jnp.where(same[b], weights[b], 0.0)))
-        for b in range(8):
+        for b in range(count):
             at = b * rows * POS + i
             key_ref[at] = found[b]
             s_ref[at] = score[b]
@@ -163,25 +165,26 @@
 
 
 def hits_call(base, blocks, w):
-    total = 8 * blocks[0].shape[0] * POS
+    count = len(blocks)
+    total = count * blocks[0].shape[0] * POS
     return pl.pallas_call(
         hits_kernel,
         out_shape=(
-            jax.ShapeDtypeStruct((8,), jnp.int32),
+            jax.ShapeDtypeStruct((count,), jnp.int32),
             jax.ShapeDtypeStruct((total,), jnp.int32),
             jax.ShapeDtypeStruct((total,), jnp.float32),
             jax.ShapeDtypeStruct((total,), jnp.float32),
         ),
-        in_specs=[SMEM] + [HBM] * 8 + [VMEM],
+        in_specs=[SMEM] + [HBM] * count + [VMEM],
         out_specs=(SMEM,) * 4,
-        scratch_shapes=[pltpu.VMEM((8,) + blocks[0].shape, jnp.bfloat16), pltpu.SemaphoreType.DMA((8,))],
+        scratch_shapes=[pltpu.VMEM((count,) + blocks[0].shape, jnp.bfloat16), pltpu.SemaphoreType.DMA((count,))],
         compiler_params=pltpu.CompilerParams(vmem_limit_bytes=16 * 2**20),
         cost_estimate=pl.CostEstimate(flops=1000, bytes_accessed=1000, transcendentals=0),
         name="hits",
     )(base, *in_hbm(blocks), w)
 
 
-def query_kernel(at_ref, n_ref, key_ref, s_ref, t_ref, lse_ref, m_ref, e0, e1, e2, e3, w_ref, *outs):
+def query_kernel(at_ref, na, ka, sa, ta, nb, kb, sb, tb, lse_ref, m_ref, e0, e1, e2, e3, w_ref, *outs):
     own_ref, oth_ref, pos_ref, held, sem = outs[4:]
     ps = [held.at[d] for d in range(4)]
     copies = [pltpu.make_async_copy(e, p, sem.at[d]) for d, (e, p) in enumerate(zip((e0, e1, e2, e3), ps))]
@@ -208,14 +211,16 @@
     c1 = lax.broadcasted_iota(jnp.int32, (1, EXTRA), 1)
     most = jnp.int32(0)
     for b in range(8):
-        most = jnp.maximum(most, n_ref[b])
+        most = jnp.maximum(most, na[b] if b < EARLY else nb[b - EARLY])
 
     def patch(i, carry):
         todo = []
         for b in range(8):
             d, k = b // 2, b % 2
-            at = b * rows * POS + i
-            live = i < n_ref[b]
+            n_ref, key_ref, s_ref, t_ref = (na, ka, sa, ta) if b < EARLY else (nb, kb, sb, tb)
+            spot = b if b < EARLY else b - EARLY
+            at = spot * rows * POS + i
+            live = i < n_ref[spot]
             key, s, weight = jnp.where(live, key_ref[at], 0), s_ref[at], t_ref[at]
             label = key & (labels - 1)
             rest = lax.div(key, labels)
@@ -265,13 +270,13 @@
     res = pl.pallas_call(
         query_kernel,
         out_shape=tuple(pltpu.HBM(e.shape, e.dtype) for e in es) + (out, out),
-        in_specs=[SMEM] * 5 + [VMEM] * 2 + [HBM] * 4 + [VMEM],
+        in_specs=[SMEM] * 9 + [VMEM] * 2 + [HBM] * 4 + [VMEM],
         out_specs=(HBM,) * 4 + (VMEM,) * 2,
         scratch_shapes=[pltpu.VMEM((2, 2 * rows, EXTRA), jnp.float32), pltpu.VMEM((4,) + es[0].shape, jnp.bfloat16), pltpu.SemaphoreType.DMA((4,))],
         compiler_params=pltpu.CompilerParams(vmem_limit_bytes=28 * 2**20),
         cost_estimate=pl.CostEstimate(flops=8 * rows * labels * width, bytes_accessed=2**24, transcendentals=0),
         name="query_part",
-    )(at, *hits, lse, m, *in_hbm(es), w)
+    )(at, *hits[0], *hits[1], lse, m, *in_hbm(es), w)
     return res[:4], res[4], res[5]
 
 
@@ -315,7 +320,7 @@
         compiler_params=pltpu.CompilerParams(vmem_limit_bytes=24 * 2**20),
         cost_estimate=pl.CostEstimate(flops=16 * rows * labels * width // PARTS, bytes_accessed=2**23, transcendentals=0),
         name="class_part",
-    )(core, *in_hbm(ps), *in_hbm(blocks), *kept)
+    )(core, *in_hbm(ps), *blocks, *kept)
 
 
 def place_kernel(core_ref, *refs):
@@ -335,10 +340,11 @@
     return pl.pallas_call(
         place_kernel,
         out_shape=jax.ShapeDtypeStruct(into.shape, into.dtype),
-        in_specs=[SMEM] + [ANY] * PARTS + [HBM],
+        in_specs=[SMEM] + [VMEM] * PARTS + [HBM],
         out_specs=HBM,
         scratch_shapes=[pltpu.SemaphoreType.DMA((PARTS,))],
         input_output_aliases={1 + PARTS: 0},
+        compiler_params=pltpu.CompilerParams(vmem_limit_bytes=8 * 2**20),
         cost_estimate=pl.CostEstimate(flops=1000, bytes_accessed=1000, transcendentals=0),
         name="place",
     )(core, *parts, into)
@@ -377,13 +383,16 @@
     oth, parts = [None] * 4, [None] * 4
     for d in (0, 1, 3, 2):
         if d:
-            done = (parts[1][1], parts[3][1]) if d == 2 else (parts[0][1],)
+            done = (parts[1][1], parts[3][1]) if d == 2 else (hits[0][0],)
             own[d] = lax.optimization_barrier((own[d],) + done)[0]
         oth[d] = shift(own[d], "core", 1)
         parts[d] = scores_call(own[d], oth[d], w)
+        if d == 0:
+            first = lax.optimization_barrier((own[0], parts[0][1]))[0]
+            hits = [hits_call(base[None], (first, oth[0]), w)]
     es, ms, ls = zip(*parts)
     blocks = [b for pair in zip(own, oth) for b in pair]
-    hits = hits_call(base[None], blocks, w)
+    hits.append(hits_call(base[None], blocks[EARLY:], w))
     m = jnp.concatenate(ms, 0)
     stat = jnp.concatenate(ls, 0)
     stat = lse_of([stat, jnp.roll(shift(stat, "core", 1), rows, 1)])

time: 236 us -> 146 us (0.62)
  Pallas kernels: 152 us -> 58.8 us
    pallas_call x1, Pallas kernels: 96.4 us -> 1.68 us  [place_call(): pl.pallas_call(place_kernel, out_shape=jax.ShapeDtypeStruct(into.shape, i...]
    all_to_all x1, waiting for transfers between devices: 0.01 us -> 7.25 us  [body(): got = lax.all_to_all(u, ('y', 'xl', 'z'), 0, 0, tiled=True)]
    ppermute x13, waiting for transfers between devices: 19 us -> 13.5 us  [shift(): return lax.ppermute(x, axis, [(i, (i + step) % n) for i in range(n)])]
    pallas_call x1 -> x2, Pallas kernels: 10.3 us -> 12.5 us  [hits_call(): pl.pallas_call(hits_kernel, out_shape=(jax.ShapeDtypeStruct((count,), jnp...]
  transfers between devices with their start and end apart: 16 -> 16, of which waited for: 9 -> 9; matrix products, arithmetic and copies ran while one was open for 1% -> 2% of each run, Pallas kernels for 58% -> 30%
where the time goes in v5:
time: 146 us; the launch traced here: 145 us
  Pallas kernels  58.8 us (40%)
  blocking collectives  27.6 us (19%)
  starting transfers between devices  26.1 us (18%)
  waiting for transfers between devices  20.8 us (14%)
  other arithmetic  6 us (4%)
  local copies, waits for them, and re-layouts  4.41 us (3%)
    pallas_call x4, Pallas kernels, scores_call(): pl.pallas_call(scores_kernel, out_shape=(pltpu.HBM((labels, 2 * rows), jn...  19.2 us
    all_to_all x1, blocking collectives, body(): column = lax.all_to_all(spread(sent, SIZES['z']), 'z', 0, 0, tiled=True)  15.7 us
    pallas_call x2, Pallas kernels, class_call(): pl.pallas_call(class_kernel, out_shape=tuple((jax.ShapeDtypeStruct((n, wi...  14.1 us
    ppermute x13, waiting for transfers between devices, shift(): return lax.ppermute(x, axis, [(i, (i + step) % n) for i in range(n)])  13.5 us
    pallas_call x2, Pallas kernels, hits_call(): pl.pallas_call(hits_kernel, out_shape=(jax.ShapeDtypeStruct((count,), jnp...  12.5 us
    all_to_all x1, blocking collectives, body(): mine = lax.all_to_all(spread(column, 4), ('xh', 'xl'), 0, 0, tiled=True)  11.9 us
    pallas_call x1, Pallas kernels, query_call(): pl.pallas_call(query_kernel, out_shape=tuple((pltpu.HBM(e.shape, e.dtype)...  11.3 us
    all_to_all x1, starting transfers between devices, body(): got = lax.all_to_all(u, ('y', 'xl', 'z'), 0, 0, tiled=True)  11 us
  transfers between devices with their start and end apart: 16, of which 9 were waited for; matrix products, arithmetic and copies ran while one was open for 2% of the time, Pallas kernels for 30%

profile of v5, /device:TPU:32, one launch (start us, length us, event | category | flops | bytes accessed | tf_op | source)
XLA Modules:
  0.0 144.6 jit_solution(3619140595606920796)
XLA Ops:
  2.9 15.7 %all_to_all.28 = bf16[8,8,896]{2,1,0:T(8,128)(2,1)S(1)} all-to-all(bf16[8,8,896]{2,1,0:T(8,128)(2,1)S(1)} %broadcast_in_dim.38), channel_id=1, replica_groups=mesh['xh'=2,'core'=2,'xl'=2,'z'=8,'y'=4] {'z'}, dimensions={0} | all-to-all | bytes 229376 | tf_op jit(solution)/shard_map/all_to_all | solution.py:375
  18.6 11.9 %all_to_all.29 = bf16[4,64,896]{2,1,0:T(8,128)(2,1)} all-to-all(bf16[4,64,896]{2,1,0:T(8,128)(2,1)S(1)} %broadcast_in_dim.40), channel_id=1, replica_groups=mesh['xh'=2,'core'=2,'xl'=2,'z'=8,'y'=4] {'xh','xl'}, dimensions={0} | all-to-all | bytes 917504 | tf_op jit(solution)/shard_map/all_to_all | solution.py:376
  30.5 3.0 %collective-permute-start.1 = (bf16[256,896]{1,0:T(8,128)(2,1)}, bf16[256,896]{1,0:T(8,128)(2,1)}, u32[]{:S(2)}, u32[]{:S(2)}) collective-permute-start(bf16[256,896]{1,0:T(8,128)(2,1)} %bitcast.2.own_ref.refs_0_), channel_id=1, source_target_pairs={{0,3},{1,0},{2,1},{3,2},{4,7},{5,4},{6,5},{7,6},{8,11},{9,8},{10,9... | collective-permute-start | bytes 1376264 | tf_op jit(solution)/shard_map/ppermute | solution.py:31
  33.6 2.1 %constant_dynamic-slice_fusion.w_ref.refs_2_.refs_6_ = bf16[2048,768]{1,0:T(8,128)(2,1)S(1)} fusion(bf16[4096,768]{1,0:T(8,128)(2,1)} %param.5, s32[]{:T(128)S(6)} %select_n.14), kind=kLoop, calls=%fused_computation.24 | loop fusion | bytes 6291460 | tf_op jit(solution)/shard_map/dynamic_slice | solution.py:380
  35.7 4.9 %scores.4 = (bf16[2048,512]{1,0:T(8,128)(2,1)}, f32[1,512]{1,0:T(1,128)S(1)}, f32[1,512]{1,0:T(1,128)S(1)}) custom-call(bf16[256,896]{1,0:T(8,128)(2,1)} %bitcast.2.own_ref.refs_0_, bf16[256,896]{1,0:T(8,128)(2,1)} %collective-permute-done.oth_ref.refs_1_, bf16[2048,768]{1,0:T(8,128)(2,1)S(1)} %constant_dynamic-slice_fusion.w_ref.refs_2_.refs_6_), custom_call_target="tpu_custom_call" | custom-call | flops 1000 | bytes 1000 | tf_op jit(solution)/shard_map/scores/pallas_call | solution.py:84
  40.5 4.4 %hits.2 = (s32[2]{0:T(128)S(1)}, s32[2560]{0:T(1024)S(1)}, f32[2560]{0:T(1024)S(1)}, f32[2560]{0:T(1024)S(1)}) custom-call(s32[1]{0:T(128)} %bitcast.3.base_ref, bf16[256,896]{1,0:T(8,128)(2,1)} %bitcast.2.own_ref.refs_0_, bf16[256,896]{1,0:T(8,128)(2,1)} %collective-permute-done.oth_ref.refs_1_, ...), custom_call_target="tpu_custom_call" | custom-call | flops 1000 | bytes 1000 | tf_op jit(solution)/shard_map/hits/pallas_call | solution.py:170
  45.8 1.9 %collective-permute-done.3.own_ref.refs_4_.refs_6_ = bf16[256,896]{1,0:T(8,128)(2,1)} collective-permute-done((bf16[256,896]{1,0:T(8,128)(2,1)}, bf16[256,896]{1,0:T(8,128)(2,1)}, u32[]{:S(2)}, u32[]{:S(2)}) %collective-permute-start.3) | collective-permute-done | bytes 458784 | tf_op jit(solution)/shard_map/ppermute | solution.py:31
  48.8 1.4 collective-permute-start.4
  50.2 5.0 %scores.5 = (bf16[2048,512]{1,0:T(8,128)(2,1)}, f32[1,512]{1,0:T(1,128)S(1)}, f32[1,512]{1,0:T(1,128)S(1)}) custom-call(bf16[256,896]{1,0:T(8,128)(2,1)} %collective-permute-done.1.own_ref.refs_0_.refs_2_, bf16[256,896]{1,0:T(8,128)(2,1)S(1)} %collective-permute-done.2.oth_ref.refs_1_.refs_3_, ...), custom_call_target="tpu_custom_call" | custom-call | flops 1000 | bytes 1000 | tf_op jit(solution)/shard_map/scores/pallas_call | solution.py:84
  55.3 5.0 %scores.6 = (bf16[2048,512]{1,0:T(8,128)(2,1)}, f32[1,512]{1,0:T(1,128)S(1)}, f32[1,512]{1,0:T(1,128)S(1)}) custom-call(bf16[256,896]{1,0:T(8,128)(2,1)} %collective-permute-done.3.own_ref.refs_4_.refs_6_, bf16[256,896]{1,0:T(8,128)(2,1)S(1)} %collective-permute-done.5.oth_ref.refs_5_.refs_7_, ...), custom_call_target="tpu_custom_call" | custom-call | flops 1000 | bytes 1000 | tf_op jit(solution)/shard_map/scores/pallas_call | solution.py:84
  60.4 1.8 %collective-permute-done.6.oth_ref.refs_3_.refs_5_ = bf16[256,896]{1,0:T(8,128)(2,1)S(1)} collective-permute-done((bf16[256,896]{1,0:T(8,128)(2,1)S(1)}, bf16[256,896]{1,0:T(8,128)(2,1)S(1)}, u32[]{:S(2)}, u32[]{:S(2)}) %collective-permute-start.6) | collective-permute-done | bytes 458784 | tf_op jit(solution)/shard_map/ppermute | solution.py:31
  62.2 4.4 %scores.7 = (bf16[2048,512]{1,0:T(8,128)(2,1)}, f32[1,512]{1,0:T(1,128)S(1)}, f32[1,512]{1,0:T(1,128)S(1)}) custom-call(bf16[256,896]{1,0:T(8,128)(2,1)S(1)} %collective-permute-done.4.own_ref.refs_2_.refs_4_, bf16[256,896]{1,0:T(8,128)(2,1)S(1)} %collective-permute-done.6.oth_ref.refs_3_.refs_5_, ...), custom_call_target="tpu_custom_call" | custom-call | flops 1000 | bytes 1000 | tf_op jit(solution)/shard_map/scores/pallas_call | solution.py:84
  68.7 2.6 %collective-permute-start.9 = (f32[4,512]{1,0:T(4,128)S(1)}, f32[4,512]{1,0:T(4,128)S(1)}, u32[]{:S(2)}, u32[]{:S(2)}) collective-permute-start(f32[4,512]{1,0:T(4,128)S(1)} %get-tuple-element.76), channel_id=1, source_target_pairs={{0,2},{1,3},{2,0},{3,1},{4,6},{5,7},{6,4},{7,5},{8,10},{9,11},{10,... | collective-permute-start | bytes 24584 | tf_op jit(solution)/shard_map/ppermute | solution.py:31
  75.7 5.1 %all-to-all-start.2 = ((f32[16,8,256]{2,1,0:T(8,128)}), f32[16,8,256]{2,1,0:T(8,128)S(1)}, u32[]{:S(2)}, u32[]{:S(2)}) async-start(f32[16,8,256]{2,1,0:T(8,128)} %broadcast_in_dim.42), calls=%async_computation.2 | async-start | bytes 262144 | tf_op jit(solution)/shard_map/all_to_all | solution.py:401
  80.8 8.1 %hits.3 = (s32[6]{0:T(128)S(1)}, s32[7680]{0:T(1024)S(1)}, f32[7680]{0:T(1024)S(1)}, f32[7680]{0:T(1024)S(1)}) custom-call(s32[1]{0:T(128)} %bitcast.3.base_ref, bf16[256,896]{1,0:T(8,128)(2,1)} %collective-permute-done.1.own_ref.refs_0_.refs_2_, bf16[256,896]{1,0:T(8,128)(2,1)} %copy-done, bf16[256,896]{1,0:T(8,128)(2,1)} %copy-done.4, ...), custom_call_target="tpu_custom_call" | custom-call | flops 1000 | bytes 1000 | tf_op jit(solution)/shard_map/hits/pallas_call | solution.py:170
  89.1 11.3 %query_part.1 = (bf16[2048,512]{1,0:T(8,128)(2,1)}, bf16[2048,512]{1,0:T(8,128)(2,1)}, bf16[2048,512]{1,0:T(8,128)(2,1)}, bf16[2048,512]{1,0:T(8,128)(2,1)}, bf1...) custom-call(s32[2]{0:T(128)S(1)} %pad_add_fusion.at_ref, s32[2]{0:T(128)S(1)} %get-tuple-element.42.na, ...), custom_call_target="tpu_custom_call" | custom-call | flops 3221225472 | bytes 16777216 | tf_op jit(solution)/shard_map/query_part/pallas_call | solution.py:270
  100.7 2.3 %collective-permute-done.11 = bf16[512,896]{1,0:T(8,128)(2,1)S(1)} collective-permute-done((bf16[512,896]{1,0:T(8,128)(2,1)S(1)}, bf16[512,896]{1,0:T(8,128)(2,1)S(1)}, u32[]{:S(2)}, u32[]{:S(2)}) %collective-permute-start.11) | collective-permute-done | bytes 917536 | tf_op jit(solution)/shard_map/ppermute | solution.py:31
  104.2 11.0 %all-to-all-start.3 = ((bf16[64,8,896]{2,1,0:T(8,128)(2,1)}), bf16[64,8,896]{2,1,0:T(8,128)(2,1)}, u32[]{:S(2)}, u32[]{:S(2)}) async-start(bf16[64,8,896]{2,1,0:T(8,128)(2,1)} %bitcast.7), calls=%async_computation.3 | async-start | bytes 1835008 | tf_op jit(solution)/shard_map/all_to_all | solution.py:407
  115.2 7.1 %class_part.2 = (bf16[4096,768]{1,0:T(8,128)(2,1)}, bf16[1024,768]{1,0:T(8,128)(2,1)}) custom-call(s32[1]{0:T(128)} %bitcast.8.core_ref, bf16[2048,512]{1,0:T(8,128)(2,1)} %get-tuple-element.67.p0, bf16[2048,512]{1,0:T(8,128)(2,1)} %get-tuple-element.68.p1, bf16[2048,512]{1,0:T(8,128)(2,1)} %get-tuple-element.69.p2, bf16[2048,512]{1,0:T(8,128)(2,1)} %get-tuple-element.70.p3, ...), custom_call_target="tpu_custom_call" | custom-call | flops 3221225472 | bytes 8388608 | tf_op jit(solution)/shard_map/class_part/pallas_call | solution.py:305
  122.3 7.1 %class_part.3 = (bf16[4096,768]{1,0:T(8,128)(2,1)}, bf16[1024,768]{1,0:T(8,128)(2,1)}) custom-call(s32[1]{0:T(128)} %bitcast.8.core_ref, bf16[2048,512]{1,0:T(8,128)(2,1)} %get-tuple-element.67.p0, bf16[2048,512]{1,0:T(8,128)(2,1)} %get-tuple-element.68.p1, bf16[2048,512]{1,0:T(8,128)(2,1)} %get-tuple-element.69.p2, ...), custom_call_target="tpu_custom_call", output_to_operand_aliasing={{0}: (13, {})} | custom-call | flops 3221225472 | bytes 8388608 | tf_op jit(solution)/shard_map/class_part/pallas_call | solution.py:305
  129.8 3.2 %collective-permute-done.13.refs_1_ = bf16[1024,768]{1,0:T(8,128)(2,1)S(1)} collective-permute-done((bf16[1024,768]{1,0:T(8,128)(2,1)}, bf16[1024,768]{1,0:T(8,128)(2,1)S(1)}, u32[]{:S(2)}, u32[]{:S(2)}) %collective-permute-start.13) | collective-permute-done | bytes 1572896 | tf_op jit(solution)/shard_map/ppermute | solution.py:31
  133.1 1.7 %place.1 = bf16[4096,768]{1,0:T(8,128)(2,1)} custom-call(s32[1]{0:T(128)} %bitcast.8.core_ref, bf16[1024,768]{1,0:T(8,128)(2,1)S(1)} %collective-permute-done.12.refs_0_, bf16[1024,768]{1,0:T(8,128)(2,1)S(1)} %collective-permute-done.13.refs_1_, bf16[4096,768]{1,0:T(8,128)(2,1)} %get-tuple-element.74.refs_2_), custom_call_target="tpu_custom_call", output_to_operand_aliasing={{}: (3, {})} | custom-call | flops 1000 | bytes 1000 | tf_op jit(solution)/shard_map/place/pallas_call | solution.py:340
  134.7 7.3 %all-to-all-done.3 = bf16[64,8,896]{2,1,0:T(8,128)(2,1)} async-done(((bf16[64,8,896]{2,1,0:T(8,128)(2,1)}), bf16[64,8,896]{2,1,0:T(8,128)(2,1)}, u32[]{:S(2)}, u32[]{:S(2)}) %all-to-all-start.3) | async-done | bytes 917536 | tf_op jit(solution)/shard_map/all_to_all | solution.py:407
  142.0 1.3 convert_reduce_fusion
  (74 shorter events, 14.4 us)
Async XLA Ops:
  30.5 5.1 %collective-permute-start = (bf16[256,896]{1,0:T(8,128)(2,1)}, bf16[256,896]{1,0:T(8,128)(2,1)}, u32[]{:S(2)}, u32[]{:S(2)}) collective-permute-start(bf16[256,896]{1,0:T(8,128)(2,1)} %bitcast.2.own_ref.refs_0_), channel_id=1, source_target_pairs={{0,64},{64,0},{1,65},{65,1},{2,66},{66,2},{3,67},{67,3},{4,68},{68... | collective-permute-start | bytes 1376264 | tf_op jit(solution)/shard_map/ppermute | solution.py:31
  30.5 14.4 %collective-permute-start.1 = (bf16[256,896]{1,0:T(8,128)(2,1)}, bf16[256,896]{1,0:T(8,128)(2,1)}, u32[]{:S(2)}, u32[]{:S(2)}) collective-permute-start(bf16[256,896]{1,0:T(8,128)(2,1)} %bitcast.2.own_ref.refs_0_), channel_id=1, source_target_pairs={{0,3},{1,0},{2,1},{3,2},{4,7},{5,4},{6,5},{7,6},{8,11},{9,8},{10,9... | collective-permute-start | bytes 1376264 | tf_op jit(solution)/shard_map/ppermute | solution.py:31
  33.5 14.2 %collective-permute-start.3 = (bf16[256,896]{1,0:T(8,128)(2,1)}, bf16[256,896]{1,0:T(8,128)(2,1)}, u32[]{:S(2)}, u32[]{:S(2)}) collective-permute-start(bf16[256,896]{1,0:T(8,128)(2,1)} %bitcast.2.own_ref.refs_0_), channel_id=1, source_target_pairs={{0,1},{1,2},{2,3},{3,0},{4,5},{5,6},{6,7},{7,4},{8,9},{9,10},{10,1... | collective-permute-start | bytes 1376264 | tf_op jit(solution)/shard_map/ppermute | solution.py:31
  44.9 5.3 %collective-permute-start.2 = (bf16[256,896]{1,0:T(8,128)(2,1)}, bf16[256,896]{1,0:T(8,128)(2,1)S(1)}, u32[]{:S(2)}, u32[]{:S(2)}) collective-permute-start(bf16[256,896]{1,0:T(8,128)(2,1)} %collective-permute-done.1.own_ref.refs_0_.refs_2_), channel_id=1, source_target_pairs={{0,64},{64,0},{1,65},{65,1},{2,66},{66,2},{3,67},{67,3},{4,68},{68... | collective-permute-start | bytes 1376264 | tf_op jit(solution)/shard_map/ppermute | solution.py:31
  47.7 7.5 %collective-permute-start.5 = (bf16[256,896]{1,0:T(8,128)(2,1)}, bf16[256,896]{1,0:T(8,128)(2,1)S(1)}, u32[]{:S(2)}, u32[]{:S(2)}) collective-permute-start(bf16[256,896]{1,0:T(8,128)(2,1)} %collective-permute-done.3.own_ref.refs_4_.refs_6_), channel_id=1, source_target_pairs={{0,64},{64,0},{1,65},{65,1},{2,66},{66,2},{3,67},{67,3},{4,68},{68... | collective-permute-start | bytes 1376264 | tf_op jit(solution)/shard_map/ppermute | solution.py:31
  48.8 11.5 %collective-permute-start.4 = (bf16[256,896]{1,0:T(8,128)(2,1)S(1)}, bf16[256,896]{1,0:T(8,128)(2,1)S(1)}, u32[]{:S(2)}, u32[]{:S(2)}) collective-permute-start(bf16[256,896]{1,0:T(8,128)(2,1)S(1)} %broadcast_select_fusion), channel_id=1, source_target_pairs={{0,3},{1,0},{2,1},{3,2},{64,65},{65,66},{66,67},{67,64},{4,7},{5,4... | collective-permute-start | bytes 1376264 | tf_op jit(solution)/shard_map/ppermute | solution.py:379
  50.2 10.0 %copy-start = (bf16[256,896]{1,0:T(8,128)(2,1)}, bf16[256,896]{1,0:T(8,128)(2,1)S(1)}, u32[]{:S(2)}) copy-start(bf16[256,896]{1,0:T(8,128)(2,1)S(1)} %collective-permute-done.2.oth_ref.refs_1_.refs_3_) | copy-start | bytes 1376260
  55.2 11.3 %copy-start.2 = (bf16[256,896]{1,0:T(8,128)(2,1)}, bf16[256,896]{1,0:T(8,128)(2,1)S(1)}, u32[]{:S(2)}) copy-start(bf16[256,896]{1,0:T(8,128)(2,1)S(1)} %collective-permute-done.5.oth_ref.refs_5_.refs_7_) | copy-start | bytes 1376260
  60.3 6.3 %copy-start.4 = (bf16[256,896]{1,0:T(8,128)(2,1)}, bf16[256,896]{1,0:T(8,128)(2,1)S(1)}, u32[]{:S(2)}) copy-start(bf16[256,896]{1,0:T(8,128)(2,1)S(1)} %collective-permute-done.4.own_ref.refs_2_.refs_4_) | copy-start | bytes 1376260
  60.3 1.9 %collective-permute-start.6 = (bf16[256,896]{1,0:T(8,128)(2,1)S(1)}, bf16[256,896]{1,0:T(8,128)(2,1)S(1)}, u32[]{:S(2)}, u32[]{:S(2)}) collective-permute-start(bf16[256,896]{1,0:T(8,128)(2,1)S(1)} %collective-permute-done.4.own_ref.refs_2_.refs_4_), channel_id=1, source_target_pairs={{0,64},{64,0},{1,65},{65,1},{2,66},{66,2},{3,67},{67,3},{4,68},{68... | collective-permute-start | bytes 1376264 | tf_op jit(solution)/shard_map/ppermute | solution.py:31
  62.2 4.4 %copy-start.6 = (bf16[256,896]{1,0:T(8,128)(2,1)}, bf16[256,896]{1,0:T(8,128)(2,1)S(1)}, u32[]{:S(2)}) copy-start(bf16[256,896]{1,0:T(8,128)(2,1)S(1)} %collective-permute-done.6.oth_ref.refs_3_.refs_5_) | copy-start | bytes 1376260
  66.6 1.3 collective-permute-start.7
  67.9 5.0 %collective-permute-start.10 = (f32[4,512]{1,0:T(4,128)S(1)}, f32[4,512]{1,0:T(4,128)S(1)}, u32[]{:S(2)}, u32[]{:S(2)}) collective-permute-start(f32[4,512]{1,0:T(4,128)S(1)} %get-tuple-element.76), channel_id=1, source_target_pairs={{0,1},{1,2},{2,3},{3,0},{4,5},{5,6},{6,7},{7,4},{8,9},{9,10},{10,1... | collective-permute-start | bytes 24584 | tf_op jit(solution)/shard_map/ppermute | solution.py:31
  68.7 5.2 %collective-permute-start.9 = (f32[4,512]{1,0:T(4,128)S(1)}, f32[4,512]{1,0:T(4,128)S(1)}, u32[]{:S(2)}, u32[]{:S(2)}) collective-permute-start(f32[4,512]{1,0:T(4,128)S(1)} %get-tuple-element.76), channel_id=1, source_target_pairs={{0,2},{1,3},{2,0},{3,1},{4,6},{5,7},{6,4},{7,5},{8,10},{9,11},{10,... | collective-permute-start | bytes 24584 | tf_op jit(solution)/shard_map/ppermute | solution.py:31
  71.3 3.7 %collective-permute-start.8 = (f32[4,512]{1,0:T(4,128)S(1)}, f32[4,512]{1,0:T(4,128)S(1)}, u32[]{:S(2)}, u32[]{:S(2)}) collective-permute-start(f32[4,512]{1,0:T(4,128)S(1)} %get-tuple-element.76), channel_id=1, source_target_pairs={{0,3},{1,0},{2,1},{3,2},{4,7},{5,4},{6,5},{7,6},{8,11},{9,8},{10,9... | collective-permute-start | bytes 24584 | tf_op jit(solution)/shard_map/ppermute | solution.py:31
  75.7 13.3 %all-to-all-start.2 = ((f32[16,8,256]{2,1,0:T(8,128)}), f32[16,8,256]{2,1,0:T(8,128)S(1)}, u32[]{:S(2)}, u32[]{:S(2)}) async-start(f32[16,8,256]{2,1,0:T(8,128)} %broadcast_in_dim.42), calls=%async_computation.2 | async-start | bytes 262144 | tf_op jit(solution)/shard_map/all_to_all | solution.py:401
  100.4 2.6 %collective-permute-start.11 = (bf16[512,896]{1,0:T(8,128)(2,1)S(1)}, bf16[512,896]{1,0:T(8,128)(2,1)S(1)}, u32[]{:S(2)}, u32[]{:S(2)}) collective-permute-start(bf16[512,896]{1,0:T(8,128)(2,1)S(1)} %get-tuple-element.65), channel_id=1, source_target_pairs={{0,64},{64,0},{1,65},{65,1},{2,66},{66,2},{3,67},{67,3},{4,68},{68... | collective-permute-start | bytes 2752520 | tf_op jit(solution)/shard_map/ppermute | solution.py:31
  102.9 12.2 %copy-start.1 = (bf16[256,896]{1,0:T(8,128)(2,1)S(1)}, bf16[256,896]{1,0:T(8,128)(2,1)}, u32[]{:S(2)}) copy-start(bf16[256,896]{1,0:T(8,128)(2,1)} %copy-done) | copy-start | bytes 1376260
  102.9 12.2 %copy-start.3 = (bf16[256,896]{1,0:T(8,128)(2,1)S(1)}, bf16[256,896]{1,0:T(8,128)(2,1)}, u32[]{:S(2)}) copy-start(bf16[256,896]{1,0:T(8,128)(2,1)} %copy-done.2) | copy-start | bytes 1376260
  102.9 12.2 %copy-start.5 = (bf16[256,896]{1,0:T(8,128)(2,1)S(1)}, bf16[256,896]{1,0:T(8,128)(2,1)}, u32[]{:S(2)}) copy-start(bf16[256,896]{1,0:T(8,128)(2,1)} %copy-done.4) | copy-start | bytes 1376260
  102.9 12.3 %copy-start.7 = (bf16[256,896]{1,0:T(8,128)(2,1)S(1)}, bf16[256,896]{1,0:T(8,128)(2,1)}, u32[]{:S(2)}) copy-start(bf16[256,896]{1,0:T(8,128)(2,1)} %copy-done.6) | copy-start | bytes 1376260
  104.2 37.8 %all-to-all-start.3 = ((bf16[64,8,896]{2,1,0:T(8,128)(2,1)}), bf16[64,8,896]{2,1,0:T(8,128)(2,1)}, u32[]{:S(2)}, u32[]{:S(2)}) async-start(bf16[64,8,896]{2,1,0:T(8,128)(2,1)} %bitcast.7), calls=%async_computation.3 | async-start | bytes 1835008 | tf_op jit(solution)/shard_map/all_to_all | solution.py:407
  122.3 7.5 %collective-permute-start.12 = (bf16[1024,768]{1,0:T(8,128)(2,1)}, bf16[1024,768]{1,0:T(8,128)(2,1)S(1)}, u32[]{:S(2)}, u32[]{:S(2)}) collective-permute-start(bf16[1024,768]{1,0:T(8,128)(2,1)} %get-tuple-element.71), channel_id=1, source_target_pairs={{0,64},{64,0},{1,65},{65,1},{2,66},{66,2},{3,67},{67,3},{4,68},{68... | collective-permute-start | bytes 4718600 | tf_op jit(solution)/shard_map/ppermute | solution.py:31
  129.3 3.7 %collective-permute-start.13 = (bf16[1024,768]{1,0:T(8,128)(2,1)}, bf16[1024,768]{1,0:T(8,128)(2,1)S(1)}, u32[]{:S(2)}, u32[]{:S(2)}) collective-permute-start(bf16[1024,768]{1,0:T(8,128)(2,1)} %get-tuple-element.73), channel_id=1, source_target_pairs={{0,64},{64,0},{1,65},{65,1},{2,66},{66,2},{3,67},{67,3},{4,68},{68... | collective-permute-start | bytes 4718600 | tf_op jit(solution)/shard_map/ppermute | solution.py:31

commit v6 on v5

--- a/solution.py
+++ b/solution.py
@@ -21,7 +21,8 @@
 LCH = 256
 PROD = 1024
 EXPO = 128
-PARTS = 2
+SPLIT = (2, 2)
+PARTS = len(SPLIT)
 EARLY = 2
 CLASS = 512
 
@@ -298,37 +299,37 @@
 def class_call(core, ps, blocks, width, part, before):
     labels = ps[0].shape[0]
     steps = labels // CLASS
-    each = steps // PARTS
+    start, each = sum(SPLIT[:part]), SPLIT[part]
     rows = blocks[0].shape[0]
     whole = lambda i, c: (0, 0)
     kept = () if before is None else (before,)
     return pl.pallas_call(
         class_kernel,
-        out_shape=tuple(jax.ShapeDtypeStruct((n, width), jnp.bfloat16) for n in (2 * labels, labels // PARTS)),
+        out_shape=tuple(jax.ShapeDtypeStruct((n, width), jnp.bfloat16) for n in (2 * labels, each * CLASS)),
         grid_spec=pltpu.PrefetchScalarGridSpec(
             num_scalar_prefetch=1,
             grid=(each,),
-            in_specs=[pl.BlockSpec((CLASS, 2 * rows), lambda i, c: (part * each + i, 0))] * 4
+            in_specs=[pl.BlockSpec((CLASS, 2 * rows), lambda i, c: (start + i, 0))] * 4
             + [pl.BlockSpec(blocks[0].shape, whole)] * 8
             + [HBM] * len(kept),
             out_specs=(
-                pl.BlockSpec((CLASS, width), lambda i, c: (c[0] * steps + part * each + i, 0)),
+                pl.BlockSpec((CLASS, width), lambda i, c: (c[0] * steps + start + i, 0)),
                 pl.BlockSpec((CLASS, width), lambda i, c: (i, 0)),
             ),
         ),
         input_output_aliases={13: 0} if kept else {},
         compiler_params=pltpu.CompilerParams(vmem_limit_bytes=24 * 2**20),
-        cost_estimate=pl.CostEstimate(flops=16 * rows * labels * width // PARTS, bytes_accessed=2**23, transcendentals=0),
+        cost_estimate=pl.CostEstimate(flops=16 * rows * each * CLASS * width, bytes_accessed=2**23, transcendentals=0),
         name="class_part",
     )(core, *in_hbm(ps), *blocks, *kept)
 
 
 def place_kernel(core_ref, *refs):
     parts, out_ref, sem = refs[:PARTS], refs[-2], refs[-1]
-    rows = parts[0].shape[0]
-    first = (1 - core_ref[0]) * (PARTS * rows)
+    first = (1 - core_ref[0]) * (out_ref.shape[0] // 2)
     copies = [
-        pltpu.make_async_copy(p, out_ref.at[pl.ds(pl.multiple_of(first + j * rows, rows), rows), :], sem.at[j]) for j, p in enumerate(parts)
+        pltpu.make_async_copy(p, out_ref.at[pl.ds(pl.multiple_of(first + sum(SPLIT[:j]) * CLASS, CLASS), p.shape[0]), :], sem.at[j])
+        for j, p in enumerate(parts)
     ]
     for copy in copies:
         copy.start()
@@ -350,6 +351,55 @@
     )(core, *parts, into)
 
 
+def pack_kernel(counts_ref, emb_ref, pos_ref, out_ref):
+    q_dev = emb_ref.shape[0]
+    row = lax.broadcasted_iota(jnp.int32, (q_dev, EXTRA), 0)
+    lane = lax.broadcasted_iota(jnp.int32, (q_dev, EXTRA), 1)
+    extra = jnp.zeros((q_dev, EXTRA), jnp.int32)
+    for j in range(POS):
+        ids = pos_ref[:, j:j + 1]
+        for first, digit in ((LO, ids & 127), (MID, (ids >> 7) & 127), (HI, ids >> 14)):
+            extra = jnp.where(lane == first + j, digit, extra)
+    for i in range(q_dev):
+        extra = jnp.where((row == i) & (lane == CNT), counts_ref[i], extra)
+    one = jnp.concatenate([emb_ref[...].astype(jnp.float32), extra.astype(jnp.float32)], 1)
+    two = jnp.concatenate([one, one], 0).astype(jnp.bfloat16)
+    for i in range(out_ref.shape[0] // two.shape[0]):
+        out_ref[i * two.shape[0]:(i + 1) * two.shape[0], :] = two
+
+
+def pack_call(embeddings, positives, counts):
+    q_dev, width = embeddings.shape
+    return pl.pallas_call(
+        pack_kernel,
+        out_shape=jax.ShapeDtypeStruct((SIZES["z"] * q_dev, width + EXTRA), jnp.bfloat16),
+        in_specs=[SMEM, VMEM, VMEM],
+        out_specs=VMEM,
+        name="pack",
+    )(counts, embeddings, positives)
+
+
+def close_kernel(got_ref, grad_ref, tail_ref):
+    q_dev, width = grad_ref.shape
+    step = 2 * q_dev
+    total = got_ref[:step, :].astype(jnp.float32)
+    for i in range(1, got_ref.shape[0] // step):
+        total = total + got_ref[i * step:(i + 1) * step, :].astype(jnp.float32)
+    total = total[:q_dev] + total[q_dev:]
+    grad_ref[...] = total[:, :width].astype(jnp.bfloat16)
+    tail_ref[...] = total[:, width:]
+
+
+def close_call(got, q_dev, width):
+    return pl.pallas_call(
+        close_kernel,
+        out_shape=(jax.ShapeDtypeStruct((q_dev, width), jnp.bfloat16), jax.ShapeDtypeStruct((q_dev, EXTRA), jnp.float32)),
+        in_specs=[VMEM],
+        out_specs=(VMEM, VMEM),
+        name="close",
+    )(got)
+
+
 def lse_of(parts, axis=None):
     if axis is None:
         top = functools.reduce(jnp.maximum, parts)
@@ -365,14 +415,8 @@
     rank = (xl * 8 + z) * 4 + y
     base = (rank * 2 + core) * labels
 
-    blank = jnp.zeros((q_dev, 8 - POS), jnp.int32)
-    extra = jnp.concatenate(
-        [positives & 127, blank, (positives >> 7) & 127, blank, positives >> 14, blank, counts[:, None], jnp.zeros((q_dev, EXTRA - CNT - 1), jnp.int32)],
-        1,
-    ).astype(jnp.bfloat16)
-    sent = jnp.concatenate([embeddings, extra], 1)
     spread = lambda x, n: jnp.broadcast_to(x[None], (n,) + x.shape).reshape((n * x.shape[0],) + x.shape[1:])
-    column = lax.all_to_all(spread(sent, SIZES["z"]), "z", 0, 0, tiled=True)
+    column = lax.all_to_all(pack_call(embeddings, positives, counts), "z", 0, 0, tiled=True)
     mine = lax.all_to_all(spread(column, 4), ("xh", "xl"), 0, 0, tiled=True)
     own = [mine, shift(mine, "y", -1), None, shift(mine, "y", 1)]
     relay = [(c * 4 + i, c * 4 + (i + 2 * c - 1) % 4) for c in range(2) for i in range(4)]
@@ -404,16 +448,18 @@
     f32 = lambda a: a.astype(jnp.float32)
     u = (f32(u_own) + f32(shift(u_oth, "core", 1))).astype(jnp.bfloat16)
     first, u = lax.optimization_barrier((ps[0], u))
-    got = lax.all_to_all(u, ("y", "xl", "z"), 0, 0, tiled=True)
-    class_grad, sent_parts = None, []
-    for j in range(PARTS):
-        class_grad, mine_part = class_call(core[None], (first,) + tuple(ps[1:]), blocks, width, j, class_grad)
-        sent_parts.append(shift(mine_part, "core", 1))
+    by_y = lax.all_to_all(u, "y", 0, 0, tiled=True)
+    v = jnp.sum(f32(by_y).reshape((4, -1) + by_y.shape[1:]), 0).astype(jnp.bfloat16)
+    class_grad, one = class_call(core[None], (first,) + tuple(ps[1:]), blocks, width, 0, None)
+    second, v, one = lax.optimization_barrier((ps[0], v, one))
+    got = lax.all_to_all(v, ("xl", "z"), 0, 0, tiled=True)
+    class_grad, two = class_call(core[None], (second,) + tuple(ps[1:]), blocks, width, 1, class_grad)
+    two, got = lax.optimization_barrier((two, got))
+    sent_parts = [shift(one, "core", 1), shift(two, "core", 1)]
     class_grad = place_call(core[None], sent_parts, class_grad)
 
-    final = jnp.sum(f32(got).reshape(64, q_dev, width + EXTRA), 0)
-    query_grad = final[:, :width].astype(jnp.bfloat16)
-    pos_mean = jnp.sum(final[:, width:width + 24], 1)
+    query_grad, tail = close_call(got, q_dev, width)
+    pos_mean = jnp.sum(tail, 1)
     at = ((xh * 2 + xl) * 8 + z) * q_dev
     loss = lax.dynamic_slice(lse, (0, at), (1, q_dev))[0] - pos_mean
     return loss, query_grad, class_grad

time: 146 us -> 147 us (level)
  waiting for transfers between devices: 20.8 us -> 15.2 us
  starting transfers between devices: 26.1 us -> 30.2 us
  Pallas kernels: 58.8 us -> 61.3 us
    ppermute x13, waiting for transfers between devices: 13.5 us -> 7.9 us  [shift(): return lax.ppermute(x, axis, [(i, (i + step) % n) for i in range(n)])]
    pallas_call x0 -> x2, Pallas kernels: none -> 3.03 us  [the longest x1 1.57 us: close_call(): pl.pallas_call(close_kernel, out_shape=(jax.ShapeDtypeStruct((q_dev, widt...]
    all_to_all x1 -> x2, starting transfers between devices: 11 us -> 14 us  [the longest x1 10.2 us: body(): got = lax.all_to_all(v, ('xl', 'z'), 0, 0, tiled=True)]
    unnamed x16 -> x20, local copies, waits for them, and re-layouts: 0.03 us -> 2.41 us
    all_to_all x1 -> x2, waiting for transfers between devices: 7.25 us -> 7.29 us  [the longest x1 5.98 us: body(): by_y = lax.all_to_all(u, 'y', 0, 0, tiled=True)]
  transfers between devices with their start and end apart: 16 -> 17, of which waited for: 9 -> 8; matrix products, arithmetic and copies ran while one was open for 2% -> 3% of each run, Pallas kernels for 30% -> 29%
where the time goes in v6:
time: 147 us; the launch traced here: 146 us
  Pallas kernels  61.3 us (42%)
  starting transfers between devices  30.2 us (21%)
  blocking collectives  27.8 us (19%)
  waiting for transfers between devices  15.2 us (10%)
  local copies, waits for them, and re-layouts  5.28 us (4%)
  other arithmetic  4.77 us (3%)
    pallas_call x4, Pallas kernels, scores_call(): pl.pallas_call(scores_kernel, out_shape=(pltpu.HBM((labels, 2 * rows), jn...  19.3 us
    all_to_all x1, blocking collectives, body(): lax.all_to_all(pack_call(embeddings, positives, counts), 'z', 0, 0, tiled...  15.9 us
    pallas_call x2, Pallas kernels, class_call(): pl.pallas_call(class_kernel, out_shape=tuple((jax.ShapeDtypeStruct((n, wi...  13.6 us
    pallas_call x2, Pallas kernels, hits_call(): pl.pallas_call(hits_kernel, out_shape=(jax.ShapeDtypeStruct((count,), jnp...  12.5 us
    all_to_all x1, blocking collectives, body(): mine = lax.all_to_all(spread(column, 4), ('xh', 'xl'), 0, 0, tiled=True)  11.9 us
    pallas_call x1, Pallas kernels, query_call(): pl.pallas_call(query_kernel, out_shape=tuple((pltpu.HBM(e.shape, e.dtype)...  11.3 us
    all_to_all x1, starting transfers between devices, body(): got = lax.all_to_all(v, ('xl', 'z'), 0, 0, tiled=True)  10.2 us
    ppermute x13, starting transfers between devices, shift(): return lax.ppermute(x, axis, [(i, (i + step) % n) for i in range(n)])  9.44 us
  transfers between devices with their start and end apart: 17, of which 8 were waited for; matrix products, arithmetic and copies ran while one was open for 3% of the time, Pallas kernels for 29%

profile of v6, /device:TPU:32, one launch (start us, length us, event | category | flops | bytes accessed | tf_op | source)
XLA Modules:
  0.0 145.6 jit_solution(9043123765097348501)
XLA Ops:
  2.1 15.9 %all_to_all.43 = bf16[8,8,896]{2,1,0:T(8,128)(2,1)S(1)} all-to-all(bf16[8,8,896]{2,1,0:T(8,128)(2,1)} %bitcast.14), channel_id=1, replica_groups=mesh['xh'=2,'core'=2,'xl'=2,'z'=8,'y'=4] {'z'}, dimensions={0} | all-to-all | bytes 229376 | tf_op jit(solution)/shard_map/all_to_all | solution.py:419
  18.0 11.9 %all_to_all.44 = bf16[4,64,896]{2,1,0:T(8,128)(2,1)} all-to-all(bf16[4,64,896]{2,1,0:T(8,128)(2,1)S(1)} %broadcast_in_dim.11), channel_id=1, replica_groups=mesh['xh'=2,'core'=2,'xl'=2,'z'=8,'y'=4] {'xh','xl'}, dimensions={0} | all-to-all | bytes 917504 | tf_op jit(solution)/shard_map/all_to_all | solution.py:420
  29.9 1.6 %collective-permute-start.3 = (bf16[256,896]{1,0:T(8,128)(2,1)}, bf16[256,896]{1,0:T(8,128)(2,1)}, u32[]{:S(2)}, u32[]{:S(2)}) collective-permute-start(bf16[256,896]{1,0:T(8,128)(2,1)} %bitcast.2.own_ref.refs_0_), channel_id=1, source_target_pairs={{0,1},{1,2},{2,3},{3,0},{4,5},{5,6},{6,7},{7,4},{8,9},{9,10},{10,1... | collective-permute-start | bytes 1376264 | tf_op jit(solution)/shard_map/ppermute | solution.py:32
  31.5 1.7 %collective-permute-start.1 = (bf16[256,896]{1,0:T(8,128)(2,1)}, bf16[256,896]{1,0:T(8,128)(2,1)}, u32[]{:S(2)}, u32[]{:S(2)}) collective-permute-start(bf16[256,896]{1,0:T(8,128)(2,1)} %bitcast.2.own_ref.refs_0_), channel_id=1, source_target_pairs={{0,3},{1,0},{2,1},{3,2},{4,7},{5,4},{6,5},{7,6},{8,11},{9,8},{10,9... | collective-permute-start | bytes 1376264 | tf_op jit(solution)/shard_map/ppermute | solution.py:32
  33.2 2.1 %constant_dynamic-slice_fusion.w_ref.refs_2_.refs_6_ = bf16[2048,768]{1,0:T(8,128)(2,1)S(1)} fusion(bf16[4096,768]{1,0:T(8,128)(2,1)} %param.5, s32[]{:T(128)S(6)} %select_n.14), kind=kLoop, calls=%fused_computation.18 | loop fusion | bytes 6291460 | tf_op jit(solution)/shard_map/dynamic_slice | solution.py:424
  35.3 4.9 %scores.4 = (bf16[2048,512]{1,0:T(8,128)(2,1)}, f32[1,512]{1,0:T(1,128)S(1)}, f32[1,512]{1,0:T(1,128)S(1)}) custom-call(bf16[256,896]{1,0:T(8,128)(2,1)} %bitcast.2.own_ref.refs_0_, bf16[256,896]{1,0:T(8,128)(2,1)} %collective-permute-done.oth_ref.refs_1_, bf16[2048,768]{1,0:T(8,128)(2,1)S(1)} %constant_dynamic-slice_fusion.w_ref.refs_2_.refs_6_), custom_call_target="tpu_custom_call" | custom-call | flops 1000 | bytes 1000 | tf_op jit(solution)/shard_map/scores/pallas_call | solution.py:85
  40.1 4.4 %hits.2 = (s32[2]{0:T(128)S(1)}, s32[2560]{0:T(1024)S(1)}, f32[2560]{0:T(1024)S(1)}, f32[2560]{0:T(1024)S(1)}) custom-call(s32[1]{0:T(128)} %bitcast.3.base_ref, bf16[256,896]{1,0:T(8,128)(2,1)} %bitcast.2.own_ref.refs_0_, bf16[256,896]{1,0:T(8,128)(2,1)} %collective-permute-done.oth_ref.refs_1_, ...), custom_call_target="tpu_custom_call" | custom-call | flops 1000 | bytes 1000 | tf_op jit(solution)/shard_map/hits/pallas_call | solution.py:171
  46.2 2.8 %collective-permute-start.4 = (bf16[256,896]{1,0:T(8,128)(2,1)S(1)}, bf16[256,896]{1,0:T(8,128)(2,1)S(1)}, u32[]{:S(2)}, u32[]{:S(2)}) collective-permute-start(bf16[256,896]{1,0:T(8,128)(2,1)S(1)} %broadcast_select_fusion), channel_id=1, source_target_pairs={{0,3},{1,0},{2,1},{3,2},{64,65},{65,66},{66,67},{67,64},{4,7},{5,4... | collective-permute-start | bytes 1376264 | tf_op jit(solution)/shard_map/ppermute | solution.py:423
  49.1 5.0 %scores.6 = (bf16[2048,512]{1,0:T(8,128)(2,1)}, f32[1,512]{1,0:T(1,128)S(1)}, f32[1,512]{1,0:T(1,128)S(1)}) custom-call(bf16[256,896]{1,0:T(8,128)(2,1)} %collective-permute-done.3.own_ref.refs_4_.refs_6_, bf16[256,896]{1,0:T(8,128)(2,1)S(1)} %collective-permute-done.5.oth_ref.refs_5_.refs_7_, ...), custom_call_target="tpu_custom_call" | custom-call | flops 1000 | bytes 1000 | tf_op jit(solution)/shard_map/scores/pallas_call | solution.py:85
  54.1 5.0 %scores.5 = (bf16[2048,512]{1,0:T(8,128)(2,1)}, f32[1,512]{1,0:T(1,128)S(1)}, f32[1,512]{1,0:T(1,128)S(1)}) custom-call(bf16[256,896]{1,0:T(8,128)(2,1)} %collective-permute-done.1.own_ref.refs_0_.refs_2_, bf16[256,896]{1,0:T(8,128)(2,1)S(1)} %collective-permute-done.2.oth_ref.refs_1_.refs_3_, ...), custom_call_target="tpu_custom_call" | custom-call | flops 1000 | bytes 1000 | tf_op jit(solution)/shard_map/scores/pallas_call | solution.py:85
  59.3 1.8 %collective-permute-done.6.oth_ref.refs_3_.refs_5_ = bf16[256,896]{1,0:T(8,128)(2,1)S(1)} collective-permute-done((bf16[256,896]{1,0:T(8,128)(2,1)S(1)}, bf16[256,896]{1,0:T(8,128)(2,1)S(1)}, u32[]{:S(2)}, u32[]{:S(2)}) %collective-permute-start.6) | collective-permute-done | bytes 458784 | tf_op jit(solution)/shard_map/ppermute | solution.py:32
  61.1 4.4 %scores.7 = (bf16[2048,512]{1,0:T(8,128)(2,1)}, f32[1,512]{1,0:T(1,128)S(1)}, f32[1,512]{1,0:T(1,128)S(1)}) custom-call(bf16[256,896]{1,0:T(8,128)(2,1)S(1)} %collective-permute-done.4.own_ref.refs_2_.refs_4_, bf16[256,896]{1,0:T(8,128)(2,1)S(1)} %collective-permute-done.6.oth_ref.refs_3_.refs_5_, ...), custom_call_target="tpu_custom_call" | custom-call | flops 1000 | bytes 1000 | tf_op jit(solution)/shard_map/scores/pallas_call | solution.py:85
  67.8 2.6 %collective-permute-start.9 = (f32[4,512]{1,0:T(4,128)S(1)}, f32[4,512]{1,0:T(4,128)S(1)}, u32[]{:S(2)}, u32[]{:S(2)}) collective-permute-start(f32[4,512]{1,0:T(4,128)S(1)} %get-tuple-element.90), channel_id=1, source_target_pairs={{0,2},{1,3},{2,0},{3,1},{4,6},{5,7},{6,4},{7,5},{8,10},{9,11},{10,... | collective-permute-start | bytes 24584 | tf_op jit(solution)/shard_map/ppermute | solution.py:32
  70.4 1.6 %collective-permute-start.8 = (f32[4,512]{1,0:T(4,128)S(1)}, f32[4,512]{1,0:T(4,128)S(1)}, u32[]{:S(2)}, u32[]{:S(2)}) collective-permute-start(f32[4,512]{1,0:T(4,128)S(1)} %get-tuple-element.90), channel_id=1, source_target_pairs={{0,3},{1,0},{2,1},{3,2},{4,7},{5,4},{6,5},{7,6},{8,11},{9,8},{10,9... | collective-permute-start | bytes 24584 | tf_op jit(solution)/shard_map/ppermute | solution.py:32
  74.8 3.9 %all-to-all-start.2 = ((f32[16,8,256]{2,1,0:T(8,128)}), f32[16,8,256]{2,1,0:T(8,128)S(1)}, u32[]{:S(2)}, u32[]{:S(2)}) async-start(f32[16,8,256]{2,1,0:T(8,128)} %broadcast_in_dim.26), calls=%async_computation.2 | async-start | bytes 262144 | tf_op jit(solution)/shard_map/all_to_all | solution.py:445
  78.8 8.1 %hits.3 = (s32[6]{0:T(128)S(1)}, s32[7680]{0:T(1024)S(1)}, f32[7680]{0:T(1024)S(1)}, f32[7680]{0:T(1024)S(1)}) custom-call(s32[1]{0:T(128)} %bitcast.3.base_ref, bf16[256,896]{1,0:T(8,128)(2,1)} %collective-permute-done.1.own_ref.refs_0_.refs_2_, bf16[256,896]{1,0:T(8,128)(2,1)} %copy-done, bf16[256,896]{1,0:T(8,128)(2,1)} %copy-done.4, ...), custom_call_target="tpu_custom_call" | custom-call | flops 1000 | bytes 1000 | tf_op jit(solution)/shard_map/hits/pallas_call | solution.py:171
  87.0 11.3 %query_part.1 = (bf16[2048,512]{1,0:T(8,128)(2,1)}, bf16[2048,512]{1,0:T(8,128)(2,1)}, bf16[2048,512]{1,0:T(8,128)(2,1)}, bf16[2048,512]{1,0:T(8,128)(2,1)}, bf1...) custom-call(s32[2]{0:T(128)S(1)} %pad_add_fusion.at_ref, s32[2]{0:T(128)S(1)} %get-tuple-element.49.na, ...), custom_call_target="tpu_custom_call" | custom-call | flops 3221225472 | bytes 16777216 | tf_op jit(solution)/shard_map/query_part/pallas_call | solution.py:271
  98.4 2.5 %collective-permute-done.11 = bf16[512,896]{1,0:T(8,128)(2,1)S(1)} collective-permute-done((bf16[512,896]{1,0:T(8,128)(2,1)S(1)}, bf16[512,896]{1,0:T(8,128)(2,1)S(1)}, u32[]{:S(2)}, u32[]{:S(2)}) %collective-permute-start.11) | collective-permute-done | bytes 917536 | tf_op jit(solution)/shard_map/ppermute | solution.py:32
  102.0 3.8 %all-to-all-start.3 = ((bf16[4,128,896]{2,1,0:T(8,128)(2,1)}), bf16[4,128,896]{2,1,0:T(8,128)(2,1)S(1)}, u32[]{:S(2)}, u32[]{:S(2)}) async-start(bf16[4,128,896]{2,1,0:T(8,128)(2,1)} %bitcast.13), calls=%async_computation.3 | async-start | bytes 1835008 | tf_op jit(solution)/shard_map/all_to_all | solution.py:451
  105.9 6.8 %class_part.2 = (bf16[4096,768]{1,0:T(8,128)(2,1)}, bf16[1024,768]{1,0:T(8,128)(2,1)S(1)}) custom-call(s32[1]{0:T(128)} %bitcast.5.core_ref, bf16[2048,512]{1,0:T(8,128)(2,1)} %get-tuple-element.79.p0, bf16[2048,512]{1,0:T(8,128)(2,1)} %get-tuple-element.75.p1, bf16[2048,512]{1,0:T(8,128)(2,1)} %get-tuple-element.76.p2, ...), custom_call_target="tpu_custom_call" | custom-call | flops 3221225472 | bytes 8388608 | tf_op jit(solution)/shard_map/class_part/pallas_call | solution.py:306
  113.8 6.0 %all-to-all-done.3 = bf16[4,128,896]{2,1,0:T(8,128)(2,1)S(1)} async-done(((bf16[4,128,896]{2,1,0:T(8,128)(2,1)}), bf16[4,128,896]{2,1,0:T(8,128)(2,1)S(1)}, u32[]{:S(2)}, u32[]{:S(2)}) %all-to-all-start.3) | async-done | bytes 917536 | tf_op jit(solution)/shard_map/all_to_all | solution.py:451
  120.7 10.2 %all-to-all-start.4 = ((bf16[16,8,896]{2,1,0:T(8,128)(2,1)}), bf16[16,8,896]{2,1,0:T(8,128)(2,1)}, u32[]{:S(2)}, u32[]{:S(2)}) async-start(bf16[16,8,896]{2,1,0:T(8,128)(2,1)} %bitcast.9), calls=%async_computation.4 | async-start | bytes 458752 | tf_op jit(solution)/shard_map/all_to_all | solution.py:455
  130.9 6.8 %class_part.3 = (bf16[4096,768]{1,0:T(8,128)(2,1)}, bf16[1024,768]{1,0:T(8,128)(2,1)S(1)}) custom-call(s32[1]{0:T(128)} %bitcast.5.core_ref, bf16[2048,512]{1,0:T(8,128)(2,1)} %get-tuple-element.79.p0, bf16[2048,512]{1,0:T(8,128)(2,1)} %get-tuple-element.75.p1, bf16[2048,512]{1,0:T(8,128)(2,1)} %get-tuple-element.76.p2, ...), custom_call_target="tpu_custom_call", output_to_operand_aliasing={{0}: (13, {})} | custom-call | flops 3221225472 | bytes 8388608 | tf_op jit(solution)/shard_map/class_part/pallas_call | solution.py:306
  143.8 1.7 %place.1 = bf16[4096,768]{1,0:T(8,128)(2,1)} custom-call(s32[1]{0:T(128)} %bitcast.5.core_ref, bf16[1024,768]{1,0:T(8,128)(2,1)S(1)} %collective-permute-done.12.refs_0_, bf16[1024,768]{1,0:T(8,128)(2,1)S(1)} %collective-permute-done.13.refs_1_, bf16[4096,768]{1,0:T(8,128)(2,1)} %get-tuple-element.88.refs_2_), custom_call_target="tpu_custom_call", output_to_operand_aliasing={{}: (3, {})} | custom-call | flops 1000 | bytes 1000 | tf_op jit(solution)/shard_map/place/pallas_call | solution.py:341
  (74 shorter events, 17.9 us)
Async XLA Ops:
  29.9 5.3 %collective-permute-start = (bf16[256,896]{1,0:T(8,128)(2,1)}, bf16[256,896]{1,0:T(8,128)(2,1)}, u32[]{:S(2)}, u32[]{:S(2)}) collective-permute-start(bf16[256,896]{1,0:T(8,128)(2,1)} %bitcast.2.own_ref.refs_0_), channel_id=1, source_target_pairs={{0,64},{64,0},{1,65},{65,1},{2,66},{66,2},{3,67},{67,3},{4,68},{68... | collective-permute-start | bytes 1376264 | tf_op jit(solution)/shard_map/ppermute | solution.py:32
  29.9 14.6 %collective-permute-start.3 = (bf16[256,896]{1,0:T(8,128)(2,1)}, bf16[256,896]{1,0:T(8,128)(2,1)}, u32[]{:S(2)}, u32[]{:S(2)}) collective-permute-start(bf16[256,896]{1,0:T(8,128)(2,1)} %bitcast.2.own_ref.refs_0_), channel_id=1, source_target_pairs={{0,1},{1,2},{2,3},{3,0},{4,5},{5,6},{6,7},{7,4},{8,9},{9,10},{10,1... | collective-permute-start | bytes 1376264 | tf_op jit(solution)/shard_map/ppermute | solution.py:32
  31.5 13.0 %collective-permute-start.1 = (bf16[256,896]{1,0:T(8,128)(2,1)}, bf16[256,896]{1,0:T(8,128)(2,1)}, u32[]{:S(2)}, u32[]{:S(2)}) collective-permute-start(bf16[256,896]{1,0:T(8,128)(2,1)} %bitcast.2.own_ref.refs_0_), channel_id=1, source_target_pairs={{0,3},{1,0},{2,1},{3,2},{4,7},{5,4},{6,5},{7,6},{8,11},{9,8},{10,9... | collective-permute-start | bytes 1376264 | tf_op jit(solution)/shard_map/ppermute | solution.py:32
  44.6 9.5 %collective-permute-start.2 = (bf16[256,896]{1,0:T(8,128)(2,1)}, bf16[256,896]{1,0:T(8,128)(2,1)S(1)}, u32[]{:S(2)}, u32[]{:S(2)}) collective-permute-start(bf16[256,896]{1,0:T(8,128)(2,1)} %collective-permute-done.1.own_ref.refs_0_.refs_2_), channel_id=1, source_target_pairs={{0,64},{64,0},{1,65},{65,1},{2,66},{66,2},{3,67},{67,3},{4,68},{68... | collective-permute-start | bytes 1376264 | tf_op jit(solution)/shard_map/ppermute | solution.py:32
  44.7 4.4 %collective-permute-start.5 = (bf16[256,896]{1,0:T(8,128)(2,1)}, bf16[256,896]{1,0:T(8,128)(2,1)S(1)}, u32[]{:S(2)}, u32[]{:S(2)}) collective-permute-start(bf16[256,896]{1,0:T(8,128)(2,1)} %collective-permute-done.3.own_ref.refs_4_.refs_6_), channel_id=1, source_target_pairs={{0,64},{64,0},{1,65},{65,1},{2,66},{66,2},{3,67},{67,3},{4,68},{68... | collective-permute-start | bytes 1376264 | tf_op jit(solution)/shard_map/ppermute | solution.py:32
  46.2 12.9 %collective-permute-start.4 = (bf16[256,896]{1,0:T(8,128)(2,1)S(1)}, bf16[256,896]{1,0:T(8,128)(2,1)S(1)}, u32[]{:S(2)}, u32[]{:S(2)}) collective-permute-start(bf16[256,896]{1,0:T(8,128)(2,1)S(1)} %broadcast_select_fusion), channel_id=1, source_target_pairs={{0,3},{1,0},{2,1},{3,2},{64,65},{65,66},{66,67},{67,64},{4,7},{5,4... | collective-permute-start | bytes 1376264 | tf_op jit(solution)/shard_map/ppermute | solution.py:423
  49.1 10.1 %copy-start.2 = (bf16[256,896]{1,0:T(8,128)(2,1)}, bf16[256,896]{1,0:T(8,128)(2,1)S(1)}, u32[]{:S(2)}) copy-start(bf16[256,896]{1,0:T(8,128)(2,1)S(1)} %collective-permute-done.5.oth_ref.refs_5_.refs_7_) | copy-start | bytes 1376260
  54.1 11.4 %copy-start = (bf16[256,896]{1,0:T(8,128)(2,1)}, bf16[256,896]{1,0:T(8,128)(2,1)S(1)}, u32[]{:S(2)}) copy-start(bf16[256,896]{1,0:T(8,128)(2,1)S(1)} %collective-permute-done.2.oth_ref.refs_1_.refs_3_) | copy-start | bytes 1376260
  59.2 6.3 %copy-start.4 = (bf16[256,896]{1,0:T(8,128)(2,1)}, bf16[256,896]{1,0:T(8,128)(2,1)S(1)}, u32[]{:S(2)}) copy-start(bf16[256,896]{1,0:T(8,128)(2,1)S(1)} %collective-permute-done.4.own_ref.refs_2_.refs_4_) | copy-start | bytes 1376260
  59.2 1.9 %collective-permute-start.6 = (bf16[256,896]{1,0:T(8,128)(2,1)S(1)}, bf16[256,896]{1,0:T(8,128)(2,1)S(1)}, u32[]{:S(2)}, u32[]{:S(2)}) collective-permute-start(bf16[256,896]{1,0:T(8,128)(2,1)S(1)} %collective-permute-done.4.own_ref.refs_2_.refs_4_), channel_id=1, source_target_pairs={{0,64},{64,0},{1,65},{65,1},{2,66},{66,2},{3,67},{67,3},{4,68},{68... | collective-permute-start | bytes 1376264 | tf_op jit(solution)/shard_map/ppermute | solution.py:32
  65.5 1.3 collective-permute-start.7
  66.8 5.2 %collective-permute-start.10 = (f32[4,512]{1,0:T(4,128)S(1)}, f32[4,512]{1,0:T(4,128)S(1)}, u32[]{:S(2)}, u32[]{:S(2)}) collective-permute-start(f32[4,512]{1,0:T(4,128)S(1)} %get-tuple-element.90), channel_id=1, source_target_pairs={{0,1},{1,2},{2,3},{3,0},{4,5},{5,6},{6,7},{7,4},{8,9},{9,10},{10,1... | collective-permute-start | bytes 24584 | tf_op jit(solution)/shard_map/ppermute | solution.py:32
  67.8 5.2 %collective-permute-start.9 = (f32[4,512]{1,0:T(4,128)S(1)}, f32[4,512]{1,0:T(4,128)S(1)}, u32[]{:S(2)}, u32[]{:S(2)}) collective-permute-start(f32[4,512]{1,0:T(4,128)S(1)} %get-tuple-element.90), channel_id=1, source_target_pairs={{0,2},{1,3},{2,0},{3,1},{4,6},{5,7},{6,4},{7,5},{8,10},{9,11},{10,... | collective-permute-start | bytes 24584 | tf_op jit(solution)/shard_map/ppermute | solution.py:32
  70.4 3.7 %collective-permute-start.8 = (f32[4,512]{1,0:T(4,128)S(1)}, f32[4,512]{1,0:T(4,128)S(1)}, u32[]{:S(2)}, u32[]{:S(2)}) collective-permute-start(f32[4,512]{1,0:T(4,128)S(1)} %get-tuple-element.90), channel_id=1, source_target_pairs={{0,3},{1,0},{2,1},{3,2},{4,7},{5,4},{6,5},{7,6},{8,11},{9,8},{10,9... | collective-permute-start | bytes 24584 | tf_op jit(solution)/shard_map/ppermute | solution.py:32
  74.8 12.1 %all-to-all-start.2 = ((f32[16,8,256]{2,1,0:T(8,128)}), f32[16,8,256]{2,1,0:T(8,128)S(1)}, u32[]{:S(2)}, u32[]{:S(2)}) async-start(f32[16,8,256]{2,1,0:T(8,128)} %broadcast_in_dim.26), calls=%async_computation.2 | async-start | bytes 262144 | tf_op jit(solution)/shard_map/all_to_all | solution.py:445
  98.3 2.6 %collective-permute-start.11 = (bf16[512,896]{1,0:T(8,128)(2,1)S(1)}, bf16[512,896]{1,0:T(8,128)(2,1)S(1)}, u32[]{:S(2)}, u32[]{:S(2)}) collective-permute-start(bf16[512,896]{1,0:T(8,128)(2,1)S(1)} %get-tuple-element.72), channel_id=1, source_target_pairs={{0,64},{64,0},{1,65},{65,1},{2,66},{66,2},{3,67},{67,3},{4,68},{68... | collective-permute-start | bytes 2752520 | tf_op jit(solution)/shard_map/ppermute | solution.py:32
  100.9 5.0 %copy-start.1 = (bf16[256,896]{1,0:T(8,128)(2,1)S(1)}, bf16[256,896]{1,0:T(8,128)(2,1)}, u32[]{:S(2)}) copy-start(bf16[256,896]{1,0:T(8,128)(2,1)} %copy-done) | copy-start | bytes 1376260
  100.9 5.0 %copy-start.3 = (bf16[256,896]{1,0:T(8,128)(2,1)S(1)}, bf16[256,896]{1,0:T(8,128)(2,1)}, u32[]{:S(2)}) copy-start(bf16[256,896]{1,0:T(8,128)(2,1)} %copy-done.2) | copy-start | bytes 1376260
  100.9 5.0 %copy-start.5 = (bf16[256,896]{1,0:T(8,128)(2,1)S(1)}, bf16[256,896]{1,0:T(8,128)(2,1)}, u32[]{:S(2)}) copy-start(bf16[256,896]{1,0:T(8,128)(2,1)} %copy-done.4) | copy-start | bytes 1376260
  100.9 5.0 %copy-start.7 = (bf16[256,896]{1,0:T(8,128)(2,1)S(1)}, bf16[256,896]{1,0:T(8,128)(2,1)}, u32[]{:S(2)}) copy-start(bf16[256,896]{1,0:T(8,128)(2,1)} %copy-done.6) | copy-start | bytes 1376260
  102.0 17.8 %all-to-all-start.3 = ((bf16[4,128,896]{2,1,0:T(8,128)(2,1)}), bf16[4,128,896]{2,1,0:T(8,128)(2,1)S(1)}, u32[]{:S(2)}, u32[]{:S(2)}) async-start(bf16[4,128,896]{2,1,0:T(8,128)(2,1)} %bitcast.13), calls=%async_computation.3 | async-start | bytes 1835008 | tf_op jit(solution)/shard_map/all_to_all | solution.py:451
  120.7 19.5 %all-to-all-start.4 = ((bf16[16,8,896]{2,1,0:T(8,128)(2,1)}), bf16[16,8,896]{2,1,0:T(8,128)(2,1)}, u32[]{:S(2)}, u32[]{:S(2)}) async-start(bf16[16,8,896]{2,1,0:T(8,128)(2,1)} %bitcast.9), calls=%async_computation.4 | async-start | bytes 458752 | tf_op jit(solution)/shard_map/all_to_all | solution.py:455
  130.9 12.3 %collective-permute-start.12 = (bf16[1024,768]{1,0:T(8,128)(2,1)}, bf16[1024,768]{1,0:T(8,128)(2,1)S(1)}, u32[]{:S(2)}, u32[]{:S(2)}) collective-permute-start(bf16[1024,768]{1,0:T(8,128)(2,1)} %copy-done.8), channel_id=1, source_target_pairs={{0,64},{64,0},{1,65},{65,1},{2,66},{66,2},{3,67},{67,3},{4,68},{68... | collective-permute-start | bytes 4718600 | tf_op jit(solution)/shard_map/ppermute | solution.py:32
  140.2 3.6 %collective-permute-start.13 = (bf16[1024,768]{1,0:T(8,128)(2,1)}, bf16[1024,768]{1,0:T(8,128)(2,1)S(1)}, u32[]{:S(2)}, u32[]{:S(2)}) collective-permute-start(bf16[1024,768]{1,0:T(8,128)(2,1)} %copy-done.9), channel_id=1, source_target_pairs={{0,64},{64,0},{1,65},{65,1},{2,66},{66,2},{3,67},{67,3},{4,68},{68... | collective-permute-start | bytes 4718600 | tf_op jit(solution)/shard_map/ppermute | solution.py:32
  (3 other events, 6.8 us)

commit v7 on v6

--- a/solution.py
+++ b/solution.py
@@ -36,16 +36,23 @@
     return [pltpu.with_memory_space_constraint(a, pltpu.HBM) for a in arrays]
 
 
-def scores_kernel(own_ref, oth_ref, w_ref, e_ref, m_ref, l_ref, q_ref, s_ref, qt_ref, held_ref, sem):
+def scores_kernel(xh_ref, own_ref, oth_ref, w_ref, e_ref, m_ref, l_ref, kept_ref, q_ref, s_ref, qt_ref, held_ref, sem, keep_sem):
     labels, width = w_ref.shape
     rows = own_ref.shape[0]
     both = 2 * rows
     copies = [pltpu.make_async_copy(a, q_ref.at[k], sem.at[k]) for k, a in enumerate((own_ref, oth_ref))]
     for copy in copies:
         copy.start()
+    half = rows // 2
+    keep = []
     for k, copy in enumerate(copies):
         copy.wait()
-        qt_ref[:, k * rows:(k + 1) * rows] = q_ref[k, :, :width].T
+        for x in range(2):
+            rowsx = pl.ds(pl.multiple_of((xh_ref[0] ^ x) * half, half), half)
+            at = x * rows + k * half
+            keep.append(pltpu.make_async_copy(q_ref.at[k, rowsx, pl.ds(0, width)], kept_ref.at[pl.ds(at, half), :], keep_sem.at[2 * k + x]))
+            keep[-1].start()
+            qt_ref[:, at:at + half] = q_ref[k, rowsx, :width].T
 
     def product(i, top):
         at = pl.multiple_of(i * PROD, PROD)
@@ -76,28 +83,31 @@
         return carry
 
     lax.fori_loop(0, labels // EXPO, gone, 0)
-
-
-def scores_call(own, oth, w):
+    for copy in keep:
+        copy.wait()
+
+
+def scores_call(xh, own, oth, w):
     rows = own.shape[0]
     labels, width = w.shape
     line = jax.ShapeDtypeStruct((1, 2 * rows), jnp.float32)
     return pl.pallas_call(
         scores_kernel,
-        out_shape=(pltpu.HBM((labels, 2 * rows), jnp.bfloat16), line, line),
-        in_specs=[ANY, ANY, VMEM],
-        out_specs=(HBM, VMEM, VMEM),
+        out_shape=(pltpu.HBM((labels, 2 * rows), jnp.bfloat16), line, line, pltpu.HBM((2 * rows, width), jnp.bfloat16)),
+        in_specs=[SMEM, ANY, ANY, VMEM],
+        out_specs=(HBM, VMEM, VMEM, HBM),
         scratch_shapes=[
             pltpu.VMEM((2,) + own.shape, jnp.bfloat16),
             pltpu.VMEM((labels, 2 * rows), jnp.float32),
             pltpu.VMEM((width, 2 * rows), jnp.bfloat16),
             pltpu.VMEM((labels, 2 * rows), jnp.bfloat16),
             pltpu.SemaphoreType.DMA((labels // EXPO,)),
+            pltpu.SemaphoreType.DMA((4,)),
         ],
         compiler_params=pltpu.CompilerParams(vmem_limit_bytes=18 * 2**20),
         cost_estimate=pl.CostEstimate(flops=1000, bytes_accessed=1000, transcendentals=0),
         name="scores",
-    )(own, oth, w)
+    )(xh, own, oth, w)
 
 
 def hits_kernel(base_ref, *refs):
@@ -109,19 +119,23 @@
         copy.start()
     labels, width = w_ref.shape
     base = base_ref[0].astype(jnp.float32)
+    half = sources[0].shape[0] // 2
+    starts = [pl.multiple_of((base_ref[1] ^ x) * half, half) for x in range(2)]
     row = lax.broadcasted_iota(jnp.int32, (8, EXTRA), 0)
     col = lax.broadcasted_iota(jnp.int32, (8, EXTRA), 1)
     digits = jnp.where(col == row + LO, 1.0, jnp.where(col == row + MID, 128.0, jnp.where(col == row + HI, 16384.0, 0.0)))
     digits = jnp.where(row < POS, digits, 0.0).astype(jnp.bfloat16)
     counting = jnp.where(col == CNT, 1.0, 0.0).astype(jnp.bfloat16)
     big = 1e9
-    rows = blocks.shape[1]
+    rows = half
     slot = lax.broadcasted_iota(jnp.int32, (8, rows), 0)
     lane = lax.broadcasted_iota(jnp.int32, (8, rows), 1)
     keys, weights, most = [], [], jnp.int32(0)
-    for b in range(count):
-        copies[b].wait()
-        extra = blocks[b, :, width:]
+    for part in range(2 * count):
+        b = part // 2
+        if part % 2 == 0:
+            copies[b].wait()
+        extra = blocks[b, pl.ds(starts[part % 2], half), width:]
         ids = lax.dot_general(digits, extra, NT, preferred_element_type=jnp.float32)
         cnt = lax.dot_general(counting, extra, NT, preferred_element_type=jnp.float32)
         valid = (slot.astype(jnp.float32) < cnt) & (slot < POS)
@@ -137,7 +151,7 @@
         weights.append(same / cnt)
         keys.append(jnp.where(hit, (lane * 8 + slot).astype(jnp.float32) * float(labels) + local, big))
         n = jnp.sum(jnp.where(hit, 1.0, 0.0)).astype(jnp.int32)
-        n_ref[b] = n
+        n_ref[part] = n
         most = jnp.maximum(most, n)
     r16 = lax.broadcasted_iota(jnp.int32, (16, width), 0)
 
@@ -146,20 +160,22 @@
         found = [jnp.where(k < big, k, 0.0).astype(jnp.int32) for k in least]
         same = [k == kf for k, kf in zip(keys, least)]
         score, weight = [], []
-        for b, k in enumerate(found):
+        for part, k in enumerate(found):
+            b = part // 2
             label = k & (labels - 1)
             query = lax.div(k, 8 * labels)
             qat = pl.multiple_of((query >> 4) << 4, 16)
+            brow = pl.multiple_of(starts[part % 2] + qat, 16)
             lat = pl.multiple_of((label >> 4) << 4, 16)
-            row_q = jnp.where(r16 == query - qat, blocks[b, pl.ds(qat, 16), :width].astype(jnp.float32), 0.0)
+            row_q = jnp.where(r16 == query - qat, blocks[b, pl.ds(brow, 16), :width].astype(jnp.float32), 0.0)
             row_w = jnp.where(r16 == label - lat, w_ref[pl.ds(lat, 16), :].astype(jnp.float32), 0.0)
             score.append(jnp.sum(row_w * jnp.sum(row_q, 0, keepdims=True)))
-            weight.append(jnp.sum(jnp.where(same[b], weights[b], 0.0)))
-        for b in range(count):
-            at = b * rows * POS + i
-            key_ref[at] = found[b]
-            s_ref[at] = score[b]
-            t_ref[at] = weight[b]
+            weight.append(jnp.sum(jnp.where(same[part], weights[part], 0.0)))
+        for part in range(2 * count):
+            at = part * rows * POS + i
+            key_ref[at] = found[part]
+            s_ref[at] = score[part]
+            t_ref[at] = weight[part]
         return tuple(jnp.where(t, big, k) for t, k in zip(same, keys))
 
     lax.fori_loop(0, most, step, tuple(keys))
@@ -171,7 +187,7 @@
     return pl.pallas_call(
         hits_kernel,
         out_shape=(
-            jax.ShapeDtypeStruct((count,), jnp.int32),
+            jax.ShapeDtypeStruct((2 * count,), jnp.int32),
             jax.ShapeDtypeStruct((total,), jnp.int32),
             jax.ShapeDtypeStruct((total,), jnp.float32),
             jax.ShapeDtypeStruct((total,), jnp.float32),
@@ -185,111 +201,124 @@
     )(base, *in_hbm(blocks), w)
 
 
-def query_kernel(at_ref, na, ka, sa, ta, nb, kb, sb, tb, lse_ref, m_ref, e0, e1, e2, e3, w_ref, *outs):
-    own_ref, oth_ref, pos_ref, held, sem = outs[4:]
+def grad_kernel(x, at_ref, na, ka, sa, ta, nb, kb, sb, tb, lse_ref, m_ref, e0, e1, e2, e3, *refs):
+    labels, rows = e0.shape[0], e0.shape[1] // 2
+    half = rows // 2
+    if x == 0:
+        w_ref, outs = refs[0], refs[1:5]
+        own_ref, oth_ref, pos_ref = refs[5:8]
+        width = w_ref.shape[1]
+        pos_ref[...] = jnp.zeros_like(pos_ref)
+    else:
+        outs = refs[:4]
+    held, sem = refs[-2:]
+    lanes = slice(x * rows, (x + 1) * rows)
     ps = [held.at[d] for d in range(4)]
-    copies = [pltpu.make_async_copy(e, p, sem.at[d]) for d, (e, p) in enumerate(zip((e0, e1, e2, e3), ps))]
+    copies = [pltpu.make_async_copy(e.at[:, lanes], p, sem.at[d]) for d, (e, p) in enumerate(zip((e0, e1, e2, e3), ps))]
     for copy in copies:
         copy.start()
-    labels, width = w_ref.shape
-    rows = e0.shape[1] // 2
-    xh, y = at_ref[0], at_ref[1]
-    half = rows // 2
-    pos_ref[...] = jnp.zeros_like(pos_ref)
     for d, p_ref in enumerate(ps):
         copies[d].wait()
-        scale = jnp.exp(m_ref[d:d + 1, :] - lse_ref[d:d + 1, :])
+        scale = jnp.exp(m_ref[d:d + 1, lanes] - lse_ref[d:d + 1, lanes])
 
         def scaled(i, carry):
-            at = pl.multiple_of(i * 64, 64)
-            p_ref[pl.ds(at, 64), :] = (p_ref[pl.ds(at, 64), :].astype(jnp.float32) * scale).astype(jnp.bfloat16)
+            at = pl.multiple_of(i * 128, 128)
+            p_ref[pl.ds(at, 128), :] = (p_ref[pl.ds(at, 128), :].astype(jnp.float32) * scale).astype(jnp.bfloat16)
             return carry
 
-        lax.fori_loop(0, labels // 64, scaled, 0)
+        lax.fori_loop(0, labels // 128, scaled, 0)
 
     r = lax.broadcasted_iota(jnp.int32, (16, half), 0)
     c = lax.broadcasted_iota(jnp.int32, (16, half), 1)
     c1 = lax.broadcasted_iota(jnp.int32, (1, EXTRA), 1)
+    lists = []
+    for b in range(8):
+        group, spot = ((na, ka, sa, ta), b) if b < EARLY else ((nb, kb, sb, tb), b - EARLY)
+        lists.append(group + (2 * spot + x,))
     most = jnp.int32(0)
-    for b in range(8):
-        most = jnp.maximum(most, na[b] if b < EARLY else nb[b - EARLY])
+    for n_ref, _, _, _, part in lists:
+        most = jnp.maximum(most, n_ref[part])
 
     def patch(i, carry):
         todo = []
-        for b in range(8):
+        for b, (n_ref, key_ref, s_ref, t_ref, part) in enumerate(lists):
             d, k = b // 2, b % 2
-            n_ref, key_ref, s_ref, t_ref = (na, ka, sa, ta) if b < EARLY else (nb, kb, sb, tb)
-            spot = b if b < EARLY else b - EARLY
-            at = spot * rows * POS + i
-            live = i < n_ref[spot]
+            at = part * half * POS + i
+            live = i < n_ref[part]
             key, s, weight = jnp.where(live, key_ref[at], 0), s_ref[at], t_ref[at]
             label = key & (labels - 1)
             rest = lax.div(key, labels)
             slot = rest & 7
             query = rest >> 3
             lat = pl.multiple_of((label >> 4) << 4, 16)
-            qhi = lax.div(query, half)
-            qlo = query & (half - 1)
-            qat = pl.multiple_of(k * rows + qhi * half, half)
-            spot = (pl.ds(lat, 16), pl.ds(qat, half))
-            value = jnp.exp(s - lse_ref[d:d + 1, pl.ds(qat, half)]) - weight
+            spot = (pl.ds(lat, 16), slice(k * half, (k + 1) * half))
+            first = x * rows + k * half
+            value = jnp.exp(s - lse_ref[d:d + 1, first:first + half]) - weight
             row = jnp.where(live, label - lat, -1)
             old = ps[d][spot].astype(jnp.float32)
-            new = jnp.where((r == row) & (c == qlo), value, old).astype(jnp.bfloat16)
-            full = jnp.full((1, EXTRA), s * weight, jnp.float32)
-            high = full.astype(jnp.bfloat16).astype(jnp.float32)
-            mid = (full - high).astype(jnp.bfloat16).astype(jnp.float32)
-            low = full - high - mid
-            put = jnp.where(c1 == slot, high, jnp.where(c1 == slot + 8, mid, jnp.where(c1 == slot + 16, low, 0.0)))
-            put = jnp.where(jnp.logical_and(live, qhi == xh), put, 0.0)
-            into = (k, pl.ds(d * half + qlo, 1), slice(None))
-            todo.append((d, spot, new, into, pos_ref[into] + put))
+            new = jnp.where((r == row) & (c == query), value, old).astype(jnp.bfloat16)
+            into = pos = None
+            if x == 0:
+                full = jnp.full((1, EXTRA), s * weight, jnp.float32)
+                high = full.astype(jnp.bfloat16).astype(jnp.float32)
+                mid = (full - high).astype(jnp.bfloat16).astype(jnp.float32)
+                low = full - high - mid
+                put = jnp.where(c1 == slot, high, jnp.where(c1 == slot + 8, mid, jnp.where(c1 == slot + 16, low, 0.0)))
+                into = (k, pl.ds(d * half + query, 1), slice(None))
+                pos = pos_ref[into] + jnp.where(live, put, 0.0)
+            todo.append((d, spot, new, into, pos))
         for d, spot, new, into, pos in todo:
             ps[d][spot] = new
-            pos_ref[into] = pos
+            if x == 0:
+                pos_ref[into] = pos
         return carry
 
     lax.fori_loop(0, most, patch, 0)
     copies = [pltpu.make_async_copy(p, out, sem.at[d]) for d, (p, out) in enumerate(zip(ps, outs))]
     for copy in copies:
         copy.start()
-    for d, p_ref in enumerate(ps):
-        both = jnp.concatenate([p_ref[:, pl.ds(pl.multiple_of(k * rows + xh * half, half), half)] for k in range(2)], 1)
-        u = lax.dot_general(both, w_ref[...], TN, preferred_element_type=jnp.float32)
-        to = pl.ds(pl.multiple_of(((y + d) & 3) * half, half), half)
-        for k, out in enumerate((own_ref, oth_ref)):
-            out[to, :width] = u[k * half:(k + 1) * half].astype(jnp.bfloat16)
-            out[to, width:] = pos_ref[k, d * half:(d + 1) * half, :].astype(jnp.bfloat16)
+    if x == 0:
+        for d, p_ref in enumerate(ps):
+            u = lax.dot_general(p_ref[...], w_ref[...], TN, preferred_element_type=jnp.float32)
+            to = pl.ds(pl.multiple_of(((at_ref[0] + d) & 3) * half, half), half)
+            for k, out in enumerate((own_ref, oth_ref)):
+                out[to, :width] = u[k * half:(k + 1) * half].astype(jnp.bfloat16)
+                out[to, width:] = pos_ref[k, d * half:(d + 1) * half, :].astype(jnp.bfloat16)
     for copy in copies:
         copy.wait()
 
 
-def query_call(at, hits, lse, m, es, w):
-    labels, width = w.shape
-    rows = es[0].shape[1] // 2
-    out = jax.ShapeDtypeStruct((2 * rows, width + EXTRA), jnp.bfloat16)
+def grad_call(x, at, hits, lse, m, es, w=None):
+    labels, rows = es[0].shape[0], es[0].shape[1] // 2
+    p = (pltpu.HBM((labels, rows), jnp.bfloat16),) * 4
+    held = [pltpu.VMEM((4, labels, rows), jnp.bfloat16), pltpu.SemaphoreType.DMA((4,))]
+    more, specs, u, pos = (), [], (), []
+    if x == 0:
+        more, specs = (w,), [VMEM]
+        u = (jax.ShapeDtypeStruct((2 * rows, w.shape[1] + EXTRA), jnp.bfloat16),) * 2
+        pos = [pltpu.VMEM((2, 2 * rows, EXTRA), jnp.float32)]
     res = pl.pallas_call(
-        query_kernel,
-        out_shape=tuple(pltpu.HBM(e.shape, e.dtype) for e in es) + (out, out),
-        in_specs=[SMEM] * 9 + [VMEM] * 2 + [HBM] * 4 + [VMEM],
-        out_specs=(HBM,) * 4 + (VMEM,) * 2,
-        scratch_shapes=[pltpu.VMEM((2, 2 * rows, EXTRA), jnp.float32), pltpu.VMEM((4,) + es[0].shape, jnp.bfloat16), pltpu.SemaphoreType.DMA((4,))],
-        compiler_params=pltpu.CompilerParams(vmem_limit_bytes=28 * 2**20),
-        cost_estimate=pl.CostEstimate(flops=8 * rows * labels * width, bytes_accessed=2**24, transcendentals=0),
-        name="query_part",
-    )(at, *hits[0], *hits[1], lse, m, *in_hbm(es), w)
-    return res[:4], res[4], res[5]
-
-
-def class_kernel(core_ref, p0, p1, p2, p3, *refs):
-    blocks = refs[:8]
+        functools.partial(grad_kernel, x),
+        out_shape=p + u,
+        in_specs=[SMEM] * 9 + [VMEM] * 2 + [HBM] * 4 + specs,
+        out_specs=(HBM,) * 4 + (VMEM,) * len(u),
+        scratch_shapes=pos + held,
+        compiler_params=pltpu.CompilerParams(vmem_limit_bytes=20 * 2**20),
+        cost_estimate=pl.CostEstimate(flops=4 * labels * rows * 4096 if x == 0 else 1000, bytes_accessed=2**23, transcendentals=0),
+        name="rest_part" if x else "query_part",
+    )(at, *hits[0], *hits[1], lse, m, *in_hbm(es), *more)
+    return res[:4], res[4:]
+
+
+def class_kernel(core_ref, *refs):
+    ps, blocks = refs[:8], refs[8:12]
     out_ref, mine_ref = refs[-2:]
-    rows = blocks[0].shape[0]
+    rows = ps[0].shape[1]
     width = out_ref.shape[1]
     acc = None
-    for d, p_ref in enumerate((p0, p1, p2, p3)):
-        for k in range(2):
-            term = jnp.dot(p_ref[:, k * rows:(k + 1) * rows], blocks[2 * d + k][:, :width], preferred_element_type=jnp.float32)
+    for d in range(4):
+        for x in range(2):
+            term = jnp.dot(ps[4 * x + d][...], blocks[d][x * rows:(x + 1) * rows, :], preferred_element_type=jnp.float32)
             acc = term if acc is None else acc + term
     done = acc.astype(jnp.bfloat16)
     out_ref[...] = done
@@ -300,7 +329,7 @@
     labels = ps[0].shape[0]
     steps = labels // CLASS
     start, each = sum(SPLIT[:part]), SPLIT[part]
-    rows = blocks[0].shape[0]
+    rows = ps[0].shape[1]
     whole = lambda i, c: (0, 0)
     kept = () if before is None else (before,)
     return pl.pallas_call(
@@ -309,8 +338,8 @@
         grid_spec=pltpu.PrefetchScalarGridSpec(
             num_scalar_prefetch=1,
             grid=(each,),
-            in_specs=[pl.BlockSpec((CLASS, 2 * rows), lambda i, c: (start + i, 0))] * 4
-            + [pl.BlockSpec(blocks[0].shape, whole)] * 8
+            in_specs=[pl.BlockSpec((CLASS, rows), lambda i, c: (start + i, 0))] * 8
+            + [pl.BlockSpec(blocks[0].shape, whole)] * 4
             + [HBM] * len(kept),
             out_specs=(
                 pl.BlockSpec((CLASS, width), lambda i, c: (c[0] * steps + start + i, 0)),
@@ -379,6 +408,34 @@
     )(counts, embeddings, positives)
 
 
+def take_kernel(core_ref, all_ref, out_ref, sem):
+    rows = out_ref.shape[0]
+    part = rows // 4
+    first = core_ref[0] * rows
+    copies = [
+        pltpu.make_async_copy(all_ref.at[pl.ds(pl.multiple_of(first + i * part, part), part), :], out_ref.at[pl.ds(i * part, part), :], sem.at[i])
+        for i in range(4)
+    ]
+    for copy in copies:
+        copy.start()
+    for copy in copies:
+        copy.wait()
+
+
+def take_call(core, everything):
+    rows, width = everything.shape
+    return pl.pallas_call(
+        take_kernel,
+        out_shape=jax.ShapeDtypeStruct((rows // 2, width), everything.dtype),
+        in_specs=[SMEM, HBM],
+        out_specs=VMEM,
+        scratch_shapes=[pltpu.SemaphoreType.DMA((4,))],
+        compiler_params=pltpu.CompilerParams(vmem_limit_bytes=8 * 2**20),
+        cost_estimate=pl.CostEstimate(flops=1000, bytes_accessed=1000, transcendentals=0),
+        name="take",
+    )(core, *in_hbm([everything]))
+
+
 def close_kernel(got_ref, grad_ref, tail_ref):
     q_dev, width = grad_ref.shape
     step = 2 * q_dev
@@ -421,7 +478,7 @@
     own = [mine, shift(mine, "y", -1), None, shift(mine, "y", 1)]
     relay = [(c * 4 + i, c * 4 + (i + 2 * c - 1) % 4) for c in range(2) for i in range(4)]
     own[2] = lax.ppermute(jnp.where(core == 0, own[1], own[3]), ("core", "y"), relay)
-    w = lax.dynamic_slice_in_dim(classifier, core * labels, labels)
+    w = take_call(core[None], classifier)
     rows = mine.shape[0]
 
     oth, parts = [None] * 4, [None] * 4
@@ -430,37 +487,41 @@
             done = (parts[1][1], parts[3][1]) if d == 2 else (hits[0][0],)
             own[d] = lax.optimization_barrier((own[d],) + done)[0]
         oth[d] = shift(own[d], "core", 1)
-        parts[d] = scores_call(own[d], oth[d], w)
+        parts[d] = scores_call(xh[None], own[d], oth[d], w)
         if d == 0:
             first = lax.optimization_barrier((own[0], parts[0][1]))[0]
-            hits = [hits_call(base[None], (first, oth[0]), w)]
-    es, ms, ls = zip(*parts)
+            hits = [hits_call(jnp.stack([base, xh]), (first, oth[0]), w)]
+    es, ms, ls, kept = zip(*parts)
     blocks = [b for pair in zip(own, oth) for b in pair]
-    hits.append(hits_call(base[None], blocks[EARLY:], w))
+    hits.append(hits_call(jnp.stack([base, xh]), blocks[EARLY:], w))
     m = jnp.concatenate(ms, 0)
     stat = jnp.concatenate(ls, 0)
-    stat = lse_of([stat, jnp.roll(shift(stat, "core", 1), rows, 1)])
+    their, n = shift(stat, "core", 1), rows // 2
+    their = jnp.concatenate([their[:, n:2 * n], their[:, :n], their[:, 3 * n:], their[:, 2 * n:3 * n]], 1)
+    stat = lse_of([stat, their])
     stat = lse_of([stat] + [jnp.roll(shift(stat, "y", -d), d, 0) for d in range(1, 4)])
     stat = stat.reshape(8, rows)
     lse = lse_of(lax.all_to_all(jnp.broadcast_to(stat[None], (16, 8, rows)), ("xl", "z"), 0, 0, tiled=True), 0)
 
-    ps, u_own, u_oth = query_call(jnp.stack([xh, y]), hits, lse.reshape(4, 2 * rows), m, es, w)
+    lines = lse.reshape(4, 2 * rows)
+    ps, (u_own, u_oth) = grad_call(0, y[None], hits, lines, m, es, w)
     f32 = lambda a: a.astype(jnp.float32)
     u = (f32(u_own) + f32(shift(u_oth, "core", 1))).astype(jnp.bfloat16)
-    first, u = lax.optimization_barrier((ps[0], u))
+    lines, u = lax.optimization_barrier((lines, u))
+    ps += grad_call(1, y[None], hits, lines, m, es)[0]
     by_y = lax.all_to_all(u, "y", 0, 0, tiled=True)
     v = jnp.sum(f32(by_y).reshape((4, -1) + by_y.shape[1:]), 0).astype(jnp.bfloat16)
-    class_grad, one = class_call(core[None], (first,) + tuple(ps[1:]), blocks, width, 0, None)
+    class_grad, one = class_call(core[None], ps, kept, width, 0, None)
     second, v, one = lax.optimization_barrier((ps[0], v, one))
     got = lax.all_to_all(v, ("xl", "z"), 0, 0, tiled=True)
-    class_grad, two = class_call(core[None], (second,) + tuple(ps[1:]), blocks, width, 1, class_grad)
+    class_grad, two = class_call(core[None], (second,) + tuple(ps[1:]), kept, width, 1, class_grad)
     two, got = lax.optimization_barrier((two, got))
     sent_parts = [shift(one, "core", 1), shift(two, "core", 1)]
     class_grad = place_call(core[None], sent_parts, class_grad)
 
     query_grad, tail = close_call(got, q_dev, width)
     pos_mean = jnp.sum(tail, 1)
-    at = ((xh * 2 + xl) * 8 + z) * q_dev
+    at = (xl * 8 + z) * q_dev
     loss = lax.dynamic_slice(lse, (0, at), (1, q_dev))[0] - pos_mean
     return loss, query_grad, class_grad
 

time: 147 us -> 148 us (level)
  waiting for transfers between devices: 15.2 us -> 7.89 us
  Pallas kernels: 61.3 us -> 67.5 us
    pallas_call x3 -> x5, Pallas kernels: 23.8 us -> 31.2 us  [the longest x2 16.3 us: grad_call(): pl.pallas_call(functools.partial(grad_kernel, x), out_shape=p + u, in_spe...]
    all_to_all x1, waiting for transfers between devices: 5.98 us -> 0.01 us  [body(): by_y = lax.all_to_all(u, 'y', 0, 0, tiled=True)]
    unnamed x20 -> x26, local copies, waits for them, and re-layouts: 2.41 us -> 4.78 us
    dynamic_slice x1 -> x0, local copies, waits for them, and re-layouts: 2.09 us -> none  [body(): w = lax.dynamic_slice_in_dim(classifier, core * labels, labels)]
    pallas_call x2, Pallas kernels: 13.6 us -> 12.1 us  [class_call(): pl.pallas_call(class_kernel, out_shape=tuple((jax.ShapeDtypeStruct((n, wi...]
  transfers between devices with their start and end apart: 17 -> 17, of which waited for: 8 -> 7; matrix products, arithmetic and copies ran while one was open for 3% -> 2% of each run, Pallas kernels for 29% -> 35%
where the time goes in v7:
time: 148 us; the launch traced here: 146 us
  Pallas kernels  67.5 us (46%)
  starting transfers between devices  30.4 us (21%)
  blocking collectives  27.8 us (19%)
  waiting for transfers between devices  7.89 us (5%)
  other arithmetic  5.96 us (4%)
  local copies, waits for them, and re-layouts  5.55 us (4%)
    pallas_call x4, Pallas kernels, scores_call(): pl.pallas_call(scores_kernel, out_shape=(pltpu.HBM((labels, 2 * rows), jn...  19.4 us
    pallas_call x2, Pallas kernels, grad_call(): pl.pallas_call(functools.partial(grad_kernel, x), out_shape=p + u, in_spe...  16.3 us
    all_to_all x1, blocking collectives, body(): lax.all_to_all(pack_call(embeddings, positives, counts), 'z', 0, 0, tiled...  15.9 us
    pallas_call x2, Pallas kernels, hits_call(): pl.pallas_call(hits_kernel, out_shape=(jax.ShapeDtypeStruct((2 * count,),...  13.1 us
    pallas_call x2, Pallas kernels, class_call(): pl.pallas_call(class_kernel, out_shape=tuple((jax.ShapeDtypeStruct((n, wi...  12.1 us
    all_to_all x1, blocking collectives, body(): mine = lax.all_to_all(spread(column, 4), ('xh', 'xl'), 0, 0, tiled=True)  11.9 us
    all_to_all x1, starting transfers between devices, body(): got = lax.all_to_all(v, ('xl', 'z'), 0, 0, tiled=True)  9.92 us
    ppermute x13, starting transfers between devices, shift(): return lax.ppermute(x, axis, [(i, (i + step) % n) for i in range(n)])  8.43 us
  transfers between devices with their start and end apart: 17, of which 7 were waited for; matrix products, arithmetic and copies ran while one was open for 2% of the time, Pallas kernels for 35%

profile of v7, /device:TPU:32, one launch (start us, length us, event | category | flops | bytes accessed | tf_op | source)
XLA Modules:
  0.0 146.2 jit_solution(5366121112043451588)
XLA Ops:
  2.1 15.9 %all_to_all.43 = bf16[8,8,896]{2,1,0:T(8,128)(2,1)S(1)} all-to-all(bf16[8,8,896]{2,1,0:T(8,128)(2,1)} %bitcast.14), channel_id=1, replica_groups=mesh['xh'=2,'core'=2,'xl'=2,'z'=8,'y'=4] {'z'}, dimensions={0} | all-to-all | bytes 229376 | tf_op jit(solution)/shard_map/all_to_all | solution.py:476
  18.0 11.9 %all_to_all.44 = bf16[4,64,896]{2,1,0:T(8,128)(2,1)} all-to-all(bf16[4,64,896]{2,1,0:T(8,128)(2,1)S(1)} %broadcast_in_dim.14), channel_id=1, replica_groups=mesh['xh'=2,'core'=2,'xl'=2,'z'=8,'y'=4] {'xh','xl'}, dimensions={0} | all-to-all | bytes 917504 | tf_op jit(solution)/shard_map/all_to_all | solution.py:477
  29.9 1.6 %collective-permute-start.3 = (bf16[256,896]{1,0:T(8,128)(2,1)}, bf16[256,896]{1,0:T(8,128)(2,1)}, u32[]{:S(2)}, u32[]{:S(2)}) collective-permute-start(bf16[256,896]{1,0:T(8,128)(2,1)} %bitcast.3.own_ref.refs_0_), channel_id=1, source_target_pairs={{0,1},{1,2},{2,3},{3,0},{4,5},{5,6},{6,7},{7,4},{8,9},{9,10},{10,1... | collective-permute-start | bytes 1376264 | tf_op jit(solution)/shard_map/ppermute | solution.py:32
  31.5 1.7 %collective-permute-start.1 = (bf16[256,896]{1,0:T(8,128)(2,1)}, bf16[256,896]{1,0:T(8,128)(2,1)}, u32[]{:S(2)}, u32[]{:S(2)}) collective-permute-start(bf16[256,896]{1,0:T(8,128)(2,1)} %bitcast.3.own_ref.refs_0_), channel_id=1, source_target_pairs={{0,3},{1,0},{2,1},{3,2},{4,7},{5,4},{6,5},{7,6},{8,11},{9,8},{10,9... | collective-permute-start | bytes 1376264 | tf_op jit(solution)/shard_map/ppermute | solution.py:32
  33.2 1.9 %take.1.w_ref.refs_2_.refs_6_.refs_0_ = bf16[2048,768]{1,0:T(8,128)(2,1)S(1)} custom-call(s32[1]{0:T(128)} %bitcast.4.core_ref, bf16[4096,768]{1,0:T(8,128)(2,1)} %all_ref.1), custom_call_target="tpu_custom_call" | custom-call | flops 1000 | bytes 1000 | tf_op jit(solution)/shard_map/take/pallas_call | solution.py:427
  35.2 4.9 %scores.4 = (bf16[2048,512]{1,0:T(8,128)(2,1)}, f32[1,512]{1,0:T(1,128)S(1)}, f32[1,512]{1,0:T(1,128)S(1)}, bf16[512,768]{1,0:T(8,128)(2,1)}) custom-call(s32[1]{0:T(128)} %bitcast.xh_ref, bf16[256,896]{1,0:T(8,128)(2,1)} %bitcast.3.own_ref.refs_0_, bf16[256,896]{1,0:T(8,128)(2,1)} %collective-permute-done.oth_ref.refs_1_, ...), custom_call_target="tpu_custom_call" | custom-call | flops 1000 | bytes 1000 | tf_op jit(solution)/shard_map/scores/pallas_call | solution.py:94
  40.0 4.6 %hits.2 = (s32[4]{0:T(128)S(1)}, s32[2560]{0:T(1024)S(1)}, f32[2560]{0:T(1024)S(1)}, f32[2560]{0:T(1024)S(1)}) custom-call(s32[2]{0:T(128)S(1)} %pad_add_fusion.base_ref, bf16[256,896]{1,0:T(8,128)(2,1)} %bitcast.3.own_ref.refs_0_, bf16[256,896]{1,0:T(8,128)(2,1)} %collective-permute-done.oth_ref.refs_1_, bf16[2048,768]{1,0:T(8,128)(2,1)S(1)} %take.1.w_ref.refs_2_.refs_6_.refs_0_), custom_call_target="tpu_custom_call" | custom-call | flops 1000 | bytes 1000 | tf_op jit(solution)/shard_map/hits/pallas_call | solution.py:187
  46.3 2.7 %collective-permute-start.4 = (bf16[256,896]{1,0:T(8,128)(2,1)S(1)}, bf16[256,896]{1,0:T(8,128)(2,1)S(1)}, u32[]{:S(2)}, u32[]{:S(2)}) collective-permute-start(bf16[256,896]{1,0:T(8,128)(2,1)S(1)} %broadcast_select_fusion), channel_id=1, source_target_pairs={{0,3},{1,0},{2,1},{3,2},{64,65},{65,66},{66,67},{67,64},{4,7},{5,4... | collective-permute-start | bytes 1376264 | tf_op jit(solution)/shard_map/ppermute | solution.py:480
  49.1 5.0 %scores.6 = (bf16[2048,512]{1,0:T(8,128)(2,1)}, f32[1,512]{1,0:T(1,128)S(1)}, f32[1,512]{1,0:T(1,128)S(1)}, bf16[512,768]{1,0:T(8,128)(2,1)}) custom-call(s32[1]{0:T(128)} %bitcast.xh_ref, bf16[256,896]{1,0:T(8,128)(2,1)} %collective-permute-done.3.own_ref.refs_4_, bf16[256,896]{1,0:T(8,128)(2,1)S(1)} %collective-permute-done.5.oth_ref.refs_5_, ...), custom_call_target="tpu_custom_call" | custom-call | flops 1000 | bytes 1000 | tf_op jit(solution)/shard_map/scores/pallas_call | solution.py:94
  54.1 5.1 %scores.5 = (bf16[2048,512]{1,0:T(8,128)(2,1)}, f32[1,512]{1,0:T(1,128)S(1)}, f32[1,512]{1,0:T(1,128)S(1)}, bf16[512,768]{1,0:T(8,128)(2,1)}) custom-call(s32[1]{0:T(128)} %bitcast.xh_ref, bf16[256,896]{1,0:T(8,128)(2,1)} %collective-permute-done.1.own_ref.refs_0_, bf16[256,896]{1,0:T(8,128)(2,1)S(1)} %collective-permute-done.2.oth_ref.refs_1_, ...), custom_call_target="tpu_custom_call" | custom-call | flops 1000 | bytes 1000 | tf_op jit(solution)/shard_map/scores/pallas_call | solution.py:94
  59.3 1.8 %collective-permute-done.6.oth_ref.refs_3_ = bf16[256,896]{1,0:T(8,128)(2,1)S(1)} collective-permute-done((bf16[256,896]{1,0:T(8,128)(2,1)S(1)}, bf16[256,896]{1,0:T(8,128)(2,1)S(1)}, u32[]{:S(2)}, u32[]{:S(2)}) %collective-permute-start.6) | collective-permute-done | bytes 458784 | tf_op jit(solution)/shard_map/ppermute | solution.py:32
  61.1 4.4 %scores.7 = (bf16[2048,512]{1,0:T(8,128)(2,1)}, f32[1,512]{1,0:T(1,128)S(1)}, f32[1,512]{1,0:T(1,128)S(1)}, bf16[512,768]{1,0:T(8,128)(2,1)}) custom-call(s32[1]{0:T(128)} %bitcast.xh_ref, bf16[256,896]{1,0:T(8,128)(2,1)S(1)} %collective-permute-done.4.own_ref.refs_2_, bf16[256,896]{1,0:T(8,128)(2,1)S(1)} %collective-permute-done.6.oth_ref.refs_3_, ...), custom_call_target="tpu_custom_call" | custom-call | flops 1000 | bytes 1000 | tf_op jit(solution)/shard_map/scores/pallas_call | solution.py:94
  67.0 2.5 %collective-permute-start.9 = (f32[4,512]{1,0:T(4,128)S(1)}, f32[4,512]{1,0:T(4,128)S(1)}, u32[]{:S(2)}, u32[]{:S(2)}) collective-permute-start(f32[4,512]{1,0:T(4,128)S(1)} %get-tuple-element.106), channel_id=1, source_target_pairs={{0,2},{1,3},{2,0},{3,1},{4,6},{5,7},{6,4},{7,5},{8,10},{9,11},{10,... | collective-permute-start | bytes 24584 | tf_op jit(solution)/shard_map/ppermute | solution.py:32
  73.9 5.1 %all-to-all-start.2 = ((f32[16,8,256]{2,1,0:T(8,128)}), f32[16,8,256]{2,1,0:T(8,128)S(1)}, u32[]{:S(2)}, u32[]{:S(2)}) async-start(f32[16,8,256]{2,1,0:T(8,128)} %broadcast_in_dim.16), calls=%async_computation.2 | async-start | bytes 262144 | tf_op jit(solution)/shard_map/all_to_all | solution.py:504
  79.0 8.5 %hits.3 = (s32[12]{0:T(128)S(1)}, s32[7680]{0:T(1024)S(1)}, f32[7680]{0:T(1024)S(1)}, f32[7680]{0:T(1024)S(1)}) custom-call(s32[2]{0:T(128)S(1)} %pad_add_fusion.base_ref, bf16[256,896]{1,0:T(8,128)(2,1)} %collective-permute-done.1.own_ref.refs_0_, bf16[256,896]{1,0:T(8,128)(2,1)} %copy-done, bf16[256,896]{1,0:T(8,128)(2,1)} %copy-done.2, ...), custom_call_target="tpu_custom_call" | custom-call | flops 1000 | bytes 1000 | tf_op jit(solution)/shard_map/hits/pallas_call | solution.py:187
  87.6 8.8 %query_part.1 = (bf16[2048,256]{1,0:T(8,128)(2,1)}, bf16[2048,256]{1,0:T(8,128)(2,1)}, bf16[2048,256]{1,0:T(8,128)(2,1)}, bf16[2048,256]{1,0:T(8,128)(2,1)}, bf1...) custom-call(s32[1]{0:T(128)} %bitcast.7.at_ref, s32[4]{0:T(128)S(1)} %get-tuple-element.57.na, ...), custom_call_target="tpu_custom_call" | custom-call | flops 8589934592 | bytes 8388608 | tf_op jit(solution)/shard_map/query_part/pallas_call | solution.py:300
  96.6 2.5 %collective-permute-done.11 = bf16[512,896]{1,0:T(8,128)(2,1)S(1)} collective-permute-done((bf16[512,896]{1,0:T(8,128)(2,1)S(1)}, bf16[512,896]{1,0:T(8,128)(2,1)S(1)}, u32[]{:S(2)}, u32[]{:S(2)}) %collective-permute-start.11) | collective-permute-done | bytes 917536 | tf_op jit(solution)/shard_map/ppermute | solution.py:32
  100.2 4.2 %all-to-all-start.3 = ((bf16[4,128,896]{2,1,0:T(8,128)(2,1)}), bf16[4,128,896]{2,1,0:T(8,128)(2,1)}, u32[]{:S(2)}, u32[]{:S(2)}) async-start(bf16[4,128,896]{2,1,0:T(8,128)(2,1)} %bitcast.8), calls=%async_computation.3 | async-start | bytes 1835008 | tf_op jit(solution)/shard_map/all_to_all | solution.py:512
  104.5 7.4 %rest_part.1 = (bf16[2048,256]{1,0:T(8,128)(2,1)}, bf16[2048,256]{1,0:T(8,128)(2,1)}, bf16[2048,256]{1,0:T(8,128)(2,1)}, bf16[2048,256]{1,0:T(8,128)(2,1)}) custom-call(s32[1]{0:T(128)} %bitcast.7.at_ref, s32[4]{0:T(128)S(1)} %get-tuple-element.57.na, s32[2560]{0:T(1024)S(1)} %get-tuple-element.66.ka, f32[2560]{0:T(1024)S(1)} %get-tuple-element.67.sa, ...), custom_call_target="tpu_custom_call" | custom-call | flops 1000 | bytes 8388608 | tf_op jit(solution)/shard_map/rest_part/pallas_call | solution.py:300
  112.0 6.1 %class_part.2 = (bf16[4096,768]{1,0:T(8,128)(2,1)}, bf16[1024,768]{1,0:T(8,128)(2,1)S(1)}) custom-call(s32[1]{0:T(128)} %bitcast.4.core_ref, bf16[2048,256]{1,0:T(8,128)(2,1)} %get-tuple-element.95.refs_0_, bf16[2048,256]{1,0:T(8,128)(2,1)} %get-tuple-element.82.refs_1_, bf16[2048,256]{1,0:T(8,128)(2,1)} %get-tuple-element.83.refs_2_, ...), custom_call_target="tpu_custom_call" | custom-call | flops 3221225472 | bytes 8388608 | tf_op jit(solution)/shard_map/class_part/pallas_call | solution.py:335
  119.2 2.1 %reduce_sum.31 = bf16[128,896]{1,0:T(8,128)(2,1)} reduce(bf16[4,128,896]{2,1,0:T(8,128)(2,1)} %all-to-all-done.3, bf16[]{:T(256)} %constant.39.clone.1), dimensions={0}, to_apply=%region_2.3 | reduce | flops 344064 | bytes 1146882 | tf_op jit(solution)/shard_map/reduce_sum | solution.py:513
  121.3 9.9 %all-to-all-start.4 = ((bf16[16,8,896]{2,1,0:T(8,128)(2,1)}), bf16[16,8,896]{2,1,0:T(8,128)(2,1)S(1)}, u32[]{:S(2)}, u32[]{:S(2)}) async-start(bf16[16,8,896]{2,1,0:T(8,128)(2,1)} %bitcast.9), calls=%async_computation.4 | async-start | bytes 458752 | tf_op jit(solution)/shard_map/all_to_all | solution.py:516
  133.5 6.0 %class_part.3 = (bf16[4096,768]{1,0:T(8,128)(2,1)}, bf16[1024,768]{1,0:T(8,128)(2,1)S(1)}) custom-call(s32[1]{0:T(128)} %bitcast.4.core_ref, bf16[2048,256]{1,0:T(8,128)(2,1)} %get-tuple-element.95.refs_0_, bf16[2048,256]{1,0:T(8,128)(2,1)} %get-tuple-element.82.refs_1_, ...), custom_call_target="tpu_custom_call", output_to_operand_aliasing={{0}: (13, {})} | custom-call | flops 3221225472 | bytes 8388608 | tf_op jit(solution)/shard_map/class_part/pallas_call | solution.py:335
  144.4 1.7 %place.1 = bf16[4096,768]{1,0:T(8,128)(2,1)} custom-call(s32[1]{0:T(128)} %bitcast.4.core_ref, bf16[1024,768]{1,0:T(8,128)(2,1)S(1)} %collective-permute-done.12.refs_0_, bf16[1024,768]{1,0:T(8,128)(2,1)S(1)} %collective-permute-done.13.refs_1_, bf16[4096,768]{1,0:T(8,128)(2,1)} %get-tuple-element.104.refs_2_), custom_call_target="tpu_custom_call", output_to_operand_aliasing={{}: (3, {})} | custom-call | flops 1000 | bytes 1000 | tf_op jit(solution)/shard_map/place/pallas_call | solution.py:370
  (81 shorter events, 18.8 us)
Async XLA Ops:
  29.9 5.2 %collective-permute-start = (bf16[256,896]{1,0:T(8,128)(2,1)}, bf16[256,896]{1,0:T(8,128)(2,1)}, u32[]{:S(2)}, u32[]{:S(2)}) collective-permute-start(bf16[256,896]{1,0:T(8,128)(2,1)} %bitcast.3.own_ref.refs_0_), channel_id=1, source_target_pairs={{0,64},{64,0},{1,65},{65,1},{2,66},{66,2},{3,67},{67,3},{4,68},{68... | collective-permute-start | bytes 1376264 | tf_op jit(solution)/shard_map/ppermute | solution.py:32
  29.9 14.7 %collective-permute-start.3 = (bf16[256,896]{1,0:T(8,128)(2,1)}, bf16[256,896]{1,0:T(8,128)(2,1)}, u32[]{:S(2)}, u32[]{:S(2)}) collective-permute-start(bf16[256,896]{1,0:T(8,128)(2,1)} %bitcast.3.own_ref.refs_0_), channel_id=1, source_target_pairs={{0,1},{1,2},{2,3},{3,0},{4,5},{5,6},{6,7},{7,4},{8,9},{9,10},{10,1... | collective-permute-start | bytes 1376264 | tf_op jit(solution)/shard_map/ppermute | solution.py:32
  31.5 13.1 %collective-permute-start.1 = (bf16[256,896]{1,0:T(8,128)(2,1)}, bf16[256,896]{1,0:T(8,128)(2,1)}, u32[]{:S(2)}, u32[]{:S(2)}) collective-permute-start(bf16[256,896]{1,0:T(8,128)(2,1)} %bitcast.3.own_ref.refs_0_), channel_id=1, source_target_pairs={{0,3},{1,0},{2,1},{3,2},{4,7},{5,4},{6,5},{7,6},{8,11},{9,8},{10,9... | collective-permute-start | bytes 1376264 | tf_op jit(solution)/shard_map/ppermute | solution.py:32
  44.7 9.5 %collective-permute-start.2 = (bf16[256,896]{1,0:T(8,128)(2,1)}, bf16[256,896]{1,0:T(8,128)(2,1)S(1)}, u32[]{:S(2)}, u32[]{:S(2)}) collective-permute-start(bf16[256,896]{1,0:T(8,128)(2,1)} %collective-permute-done.1.own_ref.refs_0_), channel_id=1, source_target_pairs={{0,64},{64,0},{1,65},{65,1},{2,66},{66,2},{3,67},{67,3},{4,68},{68... | collective-permute-start | bytes 1376264 | tf_op jit(solution)/shard_map/ppermute | solution.py:32
  45.1 4.0 %collective-permute-start.5 = (bf16[256,896]{1,0:T(8,128)(2,1)}, bf16[256,896]{1,0:T(8,128)(2,1)S(1)}, u32[]{:S(2)}, u32[]{:S(2)}) collective-permute-start(bf16[256,896]{1,0:T(8,128)(2,1)} %collective-permute-done.3.own_ref.refs_4_), channel_id=1, source_target_pairs={{0,64},{64,0},{1,65},{65,1},{2,66},{66,2},{3,67},{67,3},{4,68},{68... | collective-permute-start | bytes 1376264 | tf_op jit(solution)/shard_map/ppermute | solution.py:32
  46.3 12.9 %collective-permute-start.4 = (bf16[256,896]{1,0:T(8,128)(2,1)S(1)}, bf16[256,896]{1,0:T(8,128)(2,1)S(1)}, u32[]{:S(2)}, u32[]{:S(2)}) collective-permute-start(bf16[256,896]{1,0:T(8,128)(2,1)S(1)} %broadcast_select_fusion), channel_id=1, source_target_pairs={{0,3},{1,0},{2,1},{3,2},{64,65},{65,66},{66,67},{67,64},{4,7},{5,4... | collective-permute-start | bytes 1376264 | tf_op jit(solution)/shard_map/ppermute | solution.py:480
  49.1 10.1 %copy-start.1 = (bf16[256,896]{1,0:T(8,128)(2,1)}, bf16[256,896]{1,0:T(8,128)(2,1)S(1)}, u32[]{:S(2)}) copy-start(bf16[256,896]{1,0:T(8,128)(2,1)S(1)} %collective-permute-done.5.oth_ref.refs_5_) | copy-start | bytes 1376260
  54.1 11.5 %copy-start = (bf16[256,896]{1,0:T(8,128)(2,1)}, bf16[256,896]{1,0:T(8,128)(2,1)S(1)}, u32[]{:S(2)}) copy-start(bf16[256,896]{1,0:T(8,128)(2,1)S(1)} %collective-permute-done.2.oth_ref.refs_1_) | copy-start | bytes 1376260
  59.2 6.4 %copy-start.2 = (bf16[256,896]{1,0:T(8,128)(2,1)}, bf16[256,896]{1,0:T(8,128)(2,1)S(1)}, u32[]{:S(2)}) copy-start(bf16[256,896]{1,0:T(8,128)(2,1)S(1)} %collective-permute-done.4.own_ref.refs_2_) | copy-start | bytes 1376260
  59.2 1.9 %collective-permute-start.6 = (bf16[256,896]{1,0:T(8,128)(2,1)S(1)}, bf16[256,896]{1,0:T(8,128)(2,1)S(1)}, u32[]{:S(2)}, u32[]{:S(2)}) collective-permute-start(bf16[256,896]{1,0:T(8,128)(2,1)S(1)} %collective-permute-done.4.own_ref.refs_2_), channel_id=1, source_target_pairs={{0,64},{64,0},{1,65},{65,1},{2,66},{66,2},{3,67},{67,3},{4,68},{68... | collective-permute-start | bytes 1376264 | tf_op jit(solution)/shard_map/ppermute | solution.py:32
  65.6 1.3 collective-permute-start.7
  66.9 4.9 %collective-permute-start.10 = (f32[4,512]{1,0:T(4,128)S(1)}, f32[4,512]{1,0:T(4,128)S(1)}, u32[]{:S(2)}, u32[]{:S(2)}) collective-permute-start(f32[4,512]{1,0:T(4,128)S(1)} %get-tuple-element.106), channel_id=1, source_target_pairs={{0,1},{1,2},{2,3},{3,0},{4,5},{5,6},{6,7},{7,4},{8,9},{9,10},{10,1... | collective-permute-start | bytes 24584 | tf_op jit(solution)/shard_map/ppermute | solution.py:32
  67.0 5.2 %collective-permute-start.9 = (f32[4,512]{1,0:T(4,128)S(1)}, f32[4,512]{1,0:T(4,128)S(1)}, u32[]{:S(2)}, u32[]{:S(2)}) collective-permute-start(f32[4,512]{1,0:T(4,128)S(1)} %get-tuple-element.106), channel_id=1, source_target_pairs={{0,2},{1,3},{2,0},{3,1},{4,6},{5,7},{6,4},{7,5},{8,10},{9,11},{10,... | collective-permute-start | bytes 24584 | tf_op jit(solution)/shard_map/ppermute | solution.py:32
  69.5 3.7 %collective-permute-start.8 = (f32[4,512]{1,0:T(4,128)S(1)}, f32[4,512]{1,0:T(4,128)S(1)}, u32[]{:S(2)}, u32[]{:S(2)}) collective-permute-start(f32[4,512]{1,0:T(4,128)S(1)} %get-tuple-element.106), channel_id=1, source_target_pairs={{0,3},{1,0},{2,1},{3,2},{4,7},{5,4},{6,5},{7,6},{8,11},{9,8},{10,9... | collective-permute-start | bytes 24584 | tf_op jit(solution)/shard_map/ppermute | solution.py:32
  73.9 13.7 %all-to-all-start.2 = ((f32[16,8,256]{2,1,0:T(8,128)}), f32[16,8,256]{2,1,0:T(8,128)S(1)}, u32[]{:S(2)}, u32[]{:S(2)}) async-start(f32[16,8,256]{2,1,0:T(8,128)} %broadcast_in_dim.16), calls=%async_computation.2 | async-start | bytes 262144 | tf_op jit(solution)/shard_map/all_to_all | solution.py:504
  96.5 2.6 %collective-permute-start.11 = (bf16[512,896]{1,0:T(8,128)(2,1)S(1)}, bf16[512,896]{1,0:T(8,128)(2,1)S(1)}, u32[]{:S(2)}, u32[]{:S(2)}) collective-permute-start(bf16[512,896]{1,0:T(8,128)(2,1)S(1)} %get-tuple-element.80), channel_id=1, source_target_pairs={{0,64},{64,0},{1,65},{65,1},{2,66},{66,2},{3,67},{67,3},{4,68},{68... | collective-permute-start | bytes 2752520 | tf_op jit(solution)/shard_map/ppermute | solution.py:32
  100.2 19.0 %all-to-all-start.3 = ((bf16[4,128,896]{2,1,0:T(8,128)(2,1)}), bf16[4,128,896]{2,1,0:T(8,128)(2,1)}, u32[]{:S(2)}, u32[]{:S(2)}) async-start(bf16[4,128,896]{2,1,0:T(8,128)(2,1)} %bitcast.8), calls=%async_computation.3 | async-start | bytes 1835008 | tf_op jit(solution)/shard_map/all_to_all | solution.py:512
  104.4 7.5 %copy-start.4 = (bf16[512,768]{1,0:T(8,128)(2,1)S(1)}, bf16[512,768]{1,0:T(8,128)(2,1)}, u32[]{:S(2)}) copy-start(bf16[512,768]{1,0:T(8,128)(2,1)} %get-tuple-element.90.refs_8_) | copy-start | bytes 2359300
  104.4 7.5 %copy-start.5 = (bf16[512,768]{1,0:T(8,128)(2,1)S(1)}, bf16[512,768]{1,0:T(8,128)(2,1)}, u32[]{:S(2)}) copy-start(bf16[512,768]{1,0:T(8,128)(2,1)} %get-tuple-element.93.refs_11_) | copy-start | bytes 2359300
  104.4 7.5 %copy-start.6 = (bf16[512,768]{1,0:T(8,128)(2,1)S(1)}, bf16[512,768]{1,0:T(8,128)(2,1)}, u32[]{:S(2)}) copy-start(bf16[512,768]{1,0:T(8,128)(2,1)} %get-tuple-element.91.refs_9_) | copy-start | bytes 2359300
  104.4 7.5 %copy-start.8 = (bf16[512,768]{1,0:T(8,128)(2,1)S(1)}, bf16[512,768]{1,0:T(8,128)(2,1)}, u32[]{:S(2)}) copy-start(bf16[512,768]{1,0:T(8,128)(2,1)} %get-tuple-element.92.refs_10_) | copy-start | bytes 2359300
  121.3 19.4 %all-to-all-start.4 = ((bf16[16,8,896]{2,1,0:T(8,128)(2,1)}), bf16[16,8,896]{2,1,0:T(8,128)(2,1)S(1)}, u32[]{:S(2)}, u32[]{:S(2)}) async-start(bf16[16,8,896]{2,1,0:T(8,128)(2,1)} %bitcast.9), calls=%async_computation.4 | async-start | bytes 458752 | tf_op jit(solution)/shard_map/all_to_all | solution.py:516
  131.2 13.1 %collective-permute-start.12 = (bf16[1024,768]{1,0:T(8,128)(2,1)}, bf16[1024,768]{1,0:T(8,128)(2,1)S(1)}, u32[]{:S(2)}, u32[]{:S(2)}) collective-permute-start(bf16[1024,768]{1,0:T(8,128)(2,1)} %copy-done.10), channel_id=1, source_target_pairs={{0,64},{64,0},{1,65},{65,1},{2,66},{66,2},{3,67},{67,3},{4,68},{68... | collective-permute-start | bytes 4718600 | tf_op jit(solution)/shard_map/ppermute | solution.py:32
  140.6 3.8 %collective-permute-start.13 = (bf16[1024,768]{1,0:T(8,128)(2,1)}, bf16[1024,768]{1,0:T(8,128)(2,1)S(1)}, u32[]{:S(2)}, u32[]{:S(2)}) collective-permute-start(bf16[1024,768]{1,0:T(8,128)(2,1)} %copy-done.11), channel_id=1, source_target_pairs={{0,64},{64,0},{1,65},{65,1},{2,66},{66,2},{3,67},{67,3},{4,68},{68... | collective-permute-start | bytes 4718600 | tf_op jit(solution)/shard_map/ppermute | solution.py:32
  (6 other events, 9.7 us)

commit v8 on v7

--- a/solution.py
+++ b/solution.py
@@ -334,7 +334,7 @@
     kept = () if before is None else (before,)
     return pl.pallas_call(
         class_kernel,
-        out_shape=tuple(jax.ShapeDtypeStruct((n, width), jnp.bfloat16) for n in (2 * labels, each * CLASS)),
+        out_shape=(jax.ShapeDtypeStruct((2 * labels, width), jnp.bfloat16), pltpu.HBM((each * CLASS, width), jnp.bfloat16)),
         grid_spec=pltpu.PrefetchScalarGridSpec(
             num_scalar_prefetch=1,
             grid=(each,),
@@ -514,7 +514,7 @@
     class_grad, one = class_call(core[None], ps, kept, width, 0, None)
     second, v, one = lax.optimization_barrier((ps[0], v, one))
     got = lax.all_to_all(v, ("xl", "z"), 0, 0, tiled=True)
-    class_grad, two = class_call(core[None], (second,) + tuple(ps[1:]), kept, width, 1, class_grad)
+    class_grad, two = class_call(core[None], (second,) + tuple(ps[1:]), in_hbm(kept), width, 1, class_grad)
     two, got = lax.optimization_barrier((two, got))
     sent_parts = [shift(one, "core", 1), shift(two, "core", 1)]
     class_grad = place_call(core[None], sent_parts, class_grad)

time: 148 us -> 144 us (0.973)
  local copies, waits for them, and re-layouts: 5.55 us -> 1.49 us
  starting transfers between devices: 30.4 us -> 28.5 us
  waiting for transfers between devices: 7.89 us -> 9.64 us
  Pallas kernels: 67.5 us -> 69 us
    unnamed x26 -> x18, local copies, waits for them, and re-layouts: 4.78 us -> 0.72 us
    pallas_call x2, Pallas kernels: 12.1 us -> 14 us  [class_call(): pl.pallas_call(class_kernel, out_shape=(jax.ShapeDtypeStruct((2 * labels,...]
    all_to_all x1, starting transfers between devices: 9.92 us -> 8.17 us  [body(): got = lax.all_to_all(v, ('xl', 'z'), 0, 0, tiled=True)]
    all_to_all x1, waiting for transfers between devices: 0.01 us -> 1.65 us  [body(): got = lax.all_to_all(v, ('xl', 'z'), 0, 0, tiled=True)]
  transfers between devices with their start and end apart: 17 -> 17, of which waited for: 7 -> 9; matrix products, arithmetic and copies ran while one was open for 2% -> 2% of each run, Pallas kernels for 35% -> 37%
where the time goes in v8:
time: 144 us; the launch traced here: 142 us
  Pallas kernels  69 us (48%)
  starting transfers between devices  28.5 us (20%)
  blocking collectives  27.8 us (19%)
  waiting for transfers between devices  9.64 us (7%)
  other arithmetic  4.78 us (3%)
  local copies, waits for them, and re-layouts  1.49 us (1%)
    pallas_call x4, Pallas kernels, scores_call(): pl.pallas_call(scores_kernel, out_shape=(pltpu.HBM((labels, 2 * rows), jn...  19.4 us
    pallas_call x2, Pallas kernels, grad_call(): pl.pallas_call(functools.partial(grad_kernel, x), out_shape=p + u, in_spe...  16.3 us
    all_to_all x1, blocking collectives, body(): lax.all_to_all(pack_call(embeddings, positives, counts), 'z', 0, 0, tiled...  15.9 us
    pallas_call x2, Pallas kernels, class_call(): pl.pallas_call(class_kernel, out_shape=(jax.ShapeDtypeStruct((2 * labels,...  14 us
    pallas_call x2, Pallas kernels, hits_call(): pl.pallas_call(hits_kernel, out_shape=(jax.ShapeDtypeStruct((2 * count,),...  12.8 us
    all_to_all x1, blocking collectives, body(): mine = lax.all_to_all(spread(column, 4), ('xh', 'xl'), 0, 0, tiled=True)  11.9 us
    ppermute x13, starting transfers between devices, shift(): return lax.ppermute(x, axis, [(i, (i + step) % n) for i in range(n)])  8.35 us
    all_to_all x1, starting transfers between devices, body(): got = lax.all_to_all(v, ('xl', 'z'), 0, 0, tiled=True)  8.17 us
  transfers between devices with their start and end apart: 17, of which 9 were waited for; matrix products, arithmetic and copies ran while one was open for 2% of the time, Pallas kernels for 37%

profile of v8, /device:TPU:32, one launch (start us, length us, event | category | flops | bytes accessed | tf_op | source)
XLA Modules:
  0.0 142.3 jit_solution(7349627456003604614)
XLA Ops:
  2.1 15.9 %all_to_all.43 = bf16[8,8,896]{2,1,0:T(8,128)(2,1)S(1)} all-to-all(bf16[8,8,896]{2,1,0:T(8,128)(2,1)} %bitcast.14), channel_id=1, replica_groups=mesh['xh'=2,'core'=2,'xl'=2,'z'=8,'y'=4] {'z'}, dimensions={0} | all-to-all | bytes 229376 | tf_op jit(solution)/shard_map/all_to_all | solution.py:476
  18.0 11.9 %all_to_all.44 = bf16[4,64,896]{2,1,0:T(8,128)(2,1)} all-to-all(bf16[4,64,896]{2,1,0:T(8,128)(2,1)S(1)} %broadcast_in_dim.14), channel_id=1, replica_groups=mesh['xh'=2,'core'=2,'xl'=2,'z'=8,'y'=4] {'xh','xl'}, dimensions={0} | all-to-all | bytes 917504 | tf_op jit(solution)/shard_map/all_to_all | solution.py:477
  29.9 1.6 %collective-permute-start.3 = (bf16[256,896]{1,0:T(8,128)(2,1)}, bf16[256,896]{1,0:T(8,128)(2,1)}, u32[]{:S(2)}, u32[]{:S(2)}) collective-permute-start(bf16[256,896]{1,0:T(8,128)(2,1)} %bitcast.3.own_ref.refs_0_), channel_id=1, source_target_pairs={{0,1},{1,2},{2,3},{3,0},{4,5},{5,6},{6,7},{7,4},{8,9},{9,10},{10,1... | collective-permute-start | bytes 1376264 | tf_op jit(solution)/shard_map/ppermute | solution.py:32
  31.5 1.7 %collective-permute-start.1 = (bf16[256,896]{1,0:T(8,128)(2,1)}, bf16[256,896]{1,0:T(8,128)(2,1)}, u32[]{:S(2)}, u32[]{:S(2)}) collective-permute-start(bf16[256,896]{1,0:T(8,128)(2,1)} %bitcast.3.own_ref.refs_0_), channel_id=1, source_target_pairs={{0,3},{1,0},{2,1},{3,2},{4,7},{5,4},{6,5},{7,6},{8,11},{9,8},{10,9... | collective-permute-start | bytes 1376264 | tf_op jit(solution)/shard_map/ppermute | solution.py:32
  33.2 1.9 %take.1.w_ref.refs_2_.refs_6_.refs_0_ = bf16[2048,768]{1,0:T(8,128)(2,1)S(1)} custom-call(s32[1]{0:T(128)} %bitcast.4.core_ref, bf16[4096,768]{1,0:T(8,128)(2,1)} %all_ref.1), custom_call_target="tpu_custom_call" | custom-call | flops 1000 | bytes 1000 | tf_op jit(solution)/shard_map/take/pallas_call | solution.py:427
  35.2 4.9 %scores.4 = (bf16[2048,512]{1,0:T(8,128)(2,1)}, f32[1,512]{1,0:T(1,128)S(1)}, f32[1,512]{1,0:T(1,128)S(1)}, bf16[512,768]{1,0:T(8,128)(2,1)}) custom-call(s32[1]{0:T(128)} %bitcast.xh_ref, bf16[256,896]{1,0:T(8,128)(2,1)} %bitcast.3.own_ref.refs_0_, bf16[256,896]{1,0:T(8,128)(2,1)} %collective-permute-done.oth_ref.refs_1_, ...), custom_call_target="tpu_custom_call" | custom-call | flops 1000 | bytes 1000 | tf_op jit(solution)/shard_map/scores/pallas_call | solution.py:94
  40.0 4.3 %hits.2 = (s32[4]{0:T(128)S(1)}, s32[2560]{0:T(1024)S(1)}, f32[2560]{0:T(1024)S(1)}, f32[2560]{0:T(1024)S(1)}) custom-call(s32[2]{0:T(128)S(1)} %pad_add_fusion.base_ref, bf16[256,896]{1,0:T(8,128)(2,1)} %bitcast.3.own_ref.refs_0_, bf16[256,896]{1,0:T(8,128)(2,1)} %collective-permute-done.oth_ref.refs_1_, bf16[2048,768]{1,0:T(8,128)(2,1)S(1)} %take.1.w_ref.refs_2_.refs_6_.refs_0_), custom_call_target="tpu_custom_call" | custom-call | flops 1000 | bytes 1000 | tf_op jit(solution)/shard_map/hits/pallas_call | solution.py:187
  46.6 2.5 %collective-permute-start.4 = (bf16[256,896]{1,0:T(8,128)(2,1)S(1)}, bf16[256,896]{1,0:T(8,128)(2,1)S(1)}, u32[]{:S(2)}, u32[]{:S(2)}) collective-permute-start(bf16[256,896]{1,0:T(8,128)(2,1)S(1)} %broadcast_select_fusion), channel_id=1, source_target_pairs={{0,3},{1,0},{2,1},{3,2},{64,65},{65,66},{66,67},{67,64},{4,7},{5,4... | collective-permute-start | bytes 1376264 | tf_op jit(solution)/shard_map/ppermute | solution.py:480
  49.1 5.0 %scores.6 = (bf16[2048,512]{1,0:T(8,128)(2,1)}, f32[1,512]{1,0:T(1,128)S(1)}, f32[1,512]{1,0:T(1,128)S(1)}, bf16[512,768]{1,0:T(8,128)(2,1)}) custom-call(s32[1]{0:T(128)} %bitcast.xh_ref, bf16[256,896]{1,0:T(8,128)(2,1)} %collective-permute-done.3.own_ref.refs_4_, bf16[256,896]{1,0:T(8,128)(2,1)S(1)} %collective-permute-done.5.oth_ref.refs_5_, ...), custom_call_target="tpu_custom_call" | custom-call | flops 1000 | bytes 1000 | tf_op jit(solution)/shard_map/scores/pallas_call | solution.py:94
  54.1 5.0 %scores.5 = (bf16[2048,512]{1,0:T(8,128)(2,1)}, f32[1,512]{1,0:T(1,128)S(1)}, f32[1,512]{1,0:T(1,128)S(1)}, bf16[512,768]{1,0:T(8,128)(2,1)}) custom-call(s32[1]{0:T(128)} %bitcast.xh_ref, bf16[256,896]{1,0:T(8,128)(2,1)} %collective-permute-done.1.own_ref.refs_0_, bf16[256,896]{1,0:T(8,128)(2,1)S(1)} %collective-permute-done.2.oth_ref.refs_1_, ...), custom_call_target="tpu_custom_call" | custom-call | flops 1000 | bytes 1000 | tf_op jit(solution)/shard_map/scores/pallas_call | solution.py:94
  59.3 1.8 %collective-permute-done.6.oth_ref.refs_3_ = bf16[256,896]{1,0:T(8,128)(2,1)S(1)} collective-permute-done((bf16[256,896]{1,0:T(8,128)(2,1)S(1)}, bf16[256,896]{1,0:T(8,128)(2,1)S(1)}, u32[]{:S(2)}, u32[]{:S(2)}) %collective-permute-start.6) | collective-permute-done | bytes 458784 | tf_op jit(solution)/shard_map/ppermute | solution.py:32
  61.1 4.4 %scores.7 = (bf16[2048,512]{1,0:T(8,128)(2,1)}, f32[1,512]{1,0:T(1,128)S(1)}, f32[1,512]{1,0:T(1,128)S(1)}, bf16[512,768]{1,0:T(8,128)(2,1)}) custom-call(s32[1]{0:T(128)} %bitcast.xh_ref, bf16[256,896]{1,0:T(8,128)(2,1)S(1)} %collective-permute-done.4.own_ref.refs_2_, bf16[256,896]{1,0:T(8,128)(2,1)S(1)} %collective-permute-done.6.oth_ref.refs_3_, ...), custom_call_target="tpu_custom_call" | custom-call | flops 1000 | bytes 1000 | tf_op jit(solution)/shard_map/scores/pallas_call | solution.py:94
  67.0 2.5 %collective-permute-start.9 = (f32[4,512]{1,0:T(4,128)S(1)}, f32[4,512]{1,0:T(4,128)S(1)}, u32[]{:S(2)}, u32[]{:S(2)}) collective-permute-start(f32[4,512]{1,0:T(4,128)S(1)} %get-tuple-element.106), channel_id=1, source_target_pairs={{0,2},{1,3},{2,0},{3,1},{4,6},{5,7},{6,4},{7,5},{8,10},{9,11},{10,... | collective-permute-start | bytes 24584 | tf_op jit(solution)/shard_map/ppermute | solution.py:32
  73.9 5.1 %all-to-all-start.2 = ((f32[16,8,256]{2,1,0:T(8,128)}), f32[16,8,256]{2,1,0:T(8,128)S(1)}, u32[]{:S(2)}, u32[]{:S(2)}) async-start(f32[16,8,256]{2,1,0:T(8,128)} %broadcast_in_dim.16), calls=%async_computation.2 | async-start | bytes 262144 | tf_op jit(solution)/shard_map/all_to_all | solution.py:504
  79.0 8.5 %hits.3 = (s32[12]{0:T(128)S(1)}, s32[7680]{0:T(1024)S(1)}, f32[7680]{0:T(1024)S(1)}, f32[7680]{0:T(1024)S(1)}) custom-call(s32[2]{0:T(128)S(1)} %pad_add_fusion.base_ref, bf16[256,896]{1,0:T(8,128)(2,1)} %collective-permute-done.1.own_ref.refs_0_, bf16[256,896]{1,0:T(8,128)(2,1)} %copy-done, bf16[256,896]{1,0:T(8,128)(2,1)} %copy-done.2, ...), custom_call_target="tpu_custom_call" | custom-call | flops 1000 | bytes 1000 | tf_op jit(solution)/shard_map/hits/pallas_call | solution.py:187
  87.6 8.8 %query_part.1 = (bf16[2048,256]{1,0:T(8,128)(2,1)}, bf16[2048,256]{1,0:T(8,128)(2,1)}, bf16[2048,256]{1,0:T(8,128)(2,1)}, bf16[2048,256]{1,0:T(8,128)(2,1)}, bf1...) custom-call(s32[1]{0:T(128)} %bitcast.7.at_ref, s32[4]{0:T(128)S(1)} %get-tuple-element.57.na, ...), custom_call_target="tpu_custom_call" | custom-call | flops 8589934592 | bytes 8388608 | tf_op jit(solution)/shard_map/query_part/pallas_call | solution.py:300
  96.5 2.5 %collective-permute-done.11 = bf16[512,896]{1,0:T(8,128)(2,1)S(1)} collective-permute-done((bf16[512,896]{1,0:T(8,128)(2,1)S(1)}, bf16[512,896]{1,0:T(8,128)(2,1)S(1)}, u32[]{:S(2)}, u32[]{:S(2)}) %collective-permute-start.11) | collective-permute-done | bytes 917536 | tf_op jit(solution)/shard_map/ppermute | solution.py:32
  100.2 4.3 %all-to-all-start.3 = ((bf16[4,128,896]{2,1,0:T(8,128)(2,1)}), bf16[4,128,896]{2,1,0:T(8,128)(2,1)S(1)}, u32[]{:S(2)}, u32[]{:S(2)}) async-start(bf16[4,128,896]{2,1,0:T(8,128)(2,1)} %bitcast.8), calls=%async_computation.3 | async-start | bytes 1835008 | tf_op jit(solution)/shard_map/all_to_all | solution.py:512
  104.5 7.4 %rest_part.1 = (bf16[2048,256]{1,0:T(8,128)(2,1)}, bf16[2048,256]{1,0:T(8,128)(2,1)}, bf16[2048,256]{1,0:T(8,128)(2,1)}, bf16[2048,256]{1,0:T(8,128)(2,1)}) custom-call(s32[1]{0:T(128)} %bitcast.7.at_ref, s32[4]{0:T(128)S(1)} %get-tuple-element.57.na, s32[2560]{0:T(1024)S(1)} %get-tuple-element.66.ka, f32[2560]{0:T(1024)S(1)} %get-tuple-element.67.sa, ...), custom_call_target="tpu_custom_call" | custom-call | flops 1000 | bytes 8388608 | tf_op jit(solution)/shard_map/rest_part/pallas_call | solution.py:300
  112.0 6.4 %class_part.2 = (bf16[4096,768]{1,0:T(8,128)(2,1)}, bf16[1024,768]{1,0:T(8,128)(2,1)}) custom-call(s32[1]{0:T(128)} %bitcast.4.core_ref, bf16[2048,256]{1,0:T(8,128)(2,1)} %get-tuple-element.95.refs_0_, bf16[2048,256]{1,0:T(8,128)(2,1)} %get-tuple-element.82.refs_1_, bf16[2048,256]{1,0:T(8,128)(2,1)} %get-tuple-element.83.refs_2_, ...), custom_call_target="tpu_custom_call" | custom-call | flops 3221225472 | bytes 8388608 | tf_op jit(solution)/shard_map/class_part/pallas_call | solution.py:335
  119.4 8.2 %all-to-all-start.4 = ((bf16[16,8,896]{2,1,0:T(8,128)(2,1)}), bf16[16,8,896]{2,1,0:T(8,128)(2,1)S(1)}, u32[]{:S(2)}, u32[]{:S(2)}) async-start(bf16[16,8,896]{2,1,0:T(8,128)(2,1)} %bitcast.9), calls=%async_computation.4 | async-start | bytes 458752 | tf_op jit(solution)/shard_map/all_to_all | solution.py:516
  127.6 7.6 %class_part.3 = (bf16[4096,768]{1,0:T(8,128)(2,1)}, bf16[1024,768]{1,0:T(8,128)(2,1)}) custom-call(s32[1]{0:T(128)} %bitcast.4.core_ref, bf16[2048,256]{1,0:T(8,128)(2,1)} %get-tuple-element.95.refs_0_, bf16[2048,256]{1,0:T(8,128)(2,1)} %get-tuple-element.82.refs_1_, bf16[2048,256]{1,0:T(8,128)(2,1)} %get-tuple-element.83.refs_2_, ...), custom_call_target="tpu_custom_call", output_to_operand_aliasing={{0}: (13, {})} | custom-call | flops 3221225472 | bytes 8388608 | tf_op jit(solution)/shard_map/class_part/pallas_call | solution.py:335
  135.1 1.6 %all-to-all-done.4 = bf16[16,8,896]{2,1,0:T(8,128)(2,1)S(1)} async-done(((bf16[16,8,896]{2,1,0:T(8,128)(2,1)}), bf16[16,8,896]{2,1,0:T(8,128)(2,1)S(1)}, u32[]{:S(2)}, u32[]{:S(2)}) %all-to-all-start.4) | async-done | bytes 229408 | tf_op jit(solution)/shard_map/all_to_all | solution.py:516
  140.4 1.7 %place.1 = bf16[4096,768]{1,0:T(8,128)(2,1)} custom-call(s32[1]{0:T(128)} %bitcast.4.core_ref, bf16[1024,768]{1,0:T(8,128)(2,1)S(1)} %collective-permute-done.12.refs_0_, bf16[1024,768]{1,0:T(8,128)(2,1)S(1)} %collective-permute-done.13.refs_1_, bf16[4096,768]{1,0:T(8,128)(2,1)} %get-tuple-element.104.refs_2_), custom_call_target="tpu_custom_call", output_to_operand_aliasing={{}: (3, {})} | custom-call | flops 1000 | bytes 1000 | tf_op jit(solution)/shard_map/place/pallas_call | solution.py:370
  (73 shorter events, 15.7 us)
Async XLA Ops:
  29.9 5.2 %collective-permute-start = (bf16[256,896]{1,0:T(8,128)(2,1)}, bf16[256,896]{1,0:T(8,128)(2,1)}, u32[]{:S(2)}, u32[]{:S(2)}) collective-permute-start(bf16[256,896]{1,0:T(8,128)(2,1)} %bitcast.3.own_ref.refs_0_), channel_id=1, source_target_pairs={{0,64},{64,0},{1,65},{65,1},{2,66},{66,2},{3,67},{67,3},{4,68},{68... | collective-permute-start | bytes 1376264 | tf_op jit(solution)/shard_map/ppermute | solution.py:32
  29.9 14.5 %collective-permute-start.3 = (bf16[256,896]{1,0:T(8,128)(2,1)}, bf16[256,896]{1,0:T(8,128)(2,1)}, u32[]{:S(2)}, u32[]{:S(2)}) collective-permute-start(bf16[256,896]{1,0:T(8,128)(2,1)} %bitcast.3.own_ref.refs_0_), channel_id=1, source_target_pairs={{0,1},{1,2},{2,3},{3,0},{4,5},{5,6},{6,7},{7,4},{8,9},{9,10},{10,1... | collective-permute-start | bytes 1376264 | tf_op jit(solution)/shard_map/ppermute | solution.py:32
  31.5 13.0 %collective-permute-start.1 = (bf16[256,896]{1,0:T(8,128)(2,1)}, bf16[256,896]{1,0:T(8,128)(2,1)}, u32[]{:S(2)}, u32[]{:S(2)}) collective-permute-start(bf16[256,896]{1,0:T(8,128)(2,1)} %bitcast.3.own_ref.refs_0_), channel_id=1, source_target_pairs={{0,3},{1,0},{2,1},{3,2},{4,7},{5,4},{6,5},{7,6},{8,11},{9,8},{10,9... | collective-permute-start | bytes 1376264 | tf_op jit(solution)/shard_map/ppermute | solution.py:32
  44.5 9.6 %collective-permute-start.2 = (bf16[256,896]{1,0:T(8,128)(2,1)}, bf16[256,896]{1,0:T(8,128)(2,1)S(1)}, u32[]{:S(2)}, u32[]{:S(2)}) collective-permute-start(bf16[256,896]{1,0:T(8,128)(2,1)} %collective-permute-done.1.own_ref.refs_0_), channel_id=1, source_target_pairs={{0,64},{64,0},{1,65},{65,1},{2,66},{66,2},{3,67},{67,3},{4,68},{68... | collective-permute-start | bytes 1376264 | tf_op jit(solution)/shard_map/ppermute | solution.py:32
  45.4 3.7 %collective-permute-start.5 = (bf16[256,896]{1,0:T(8,128)(2,1)}, bf16[256,896]{1,0:T(8,128)(2,1)S(1)}, u32[]{:S(2)}, u32[]{:S(2)}) collective-permute-start(bf16[256,896]{1,0:T(8,128)(2,1)} %collective-permute-done.3.own_ref.refs_4_), channel_id=1, source_target_pairs={{0,64},{64,0},{1,65},{65,1},{2,66},{66,2},{3,67},{67,3},{4,68},{68... | collective-permute-start | bytes 1376264 | tf_op jit(solution)/shard_map/ppermute | solution.py:32
  46.6 12.6 %collective-permute-start.4 = (bf16[256,896]{1,0:T(8,128)(2,1)S(1)}, bf16[256,896]{1,0:T(8,128)(2,1)S(1)}, u32[]{:S(2)}, u32[]{:S(2)}) collective-permute-start(bf16[256,896]{1,0:T(8,128)(2,1)S(1)} %broadcast_select_fusion), channel_id=1, source_target_pairs={{0,3},{1,0},{2,1},{3,2},{64,65},{65,66},{66,67},{67,64},{4,7},{5,4... | collective-permute-start | bytes 1376264 | tf_op jit(solution)/shard_map/ppermute | solution.py:480
  49.1 10.1 %copy-start.1 = (bf16[256,896]{1,0:T(8,128)(2,1)}, bf16[256,896]{1,0:T(8,128)(2,1)S(1)}, u32[]{:S(2)}) copy-start(bf16[256,896]{1,0:T(8,128)(2,1)S(1)} %collective-permute-done.5.oth_ref.refs_5_) | copy-start | bytes 1376260
  54.1 11.4 %copy-start = (bf16[256,896]{1,0:T(8,128)(2,1)}, bf16[256,896]{1,0:T(8,128)(2,1)S(1)}, u32[]{:S(2)}) copy-start(bf16[256,896]{1,0:T(8,128)(2,1)S(1)} %collective-permute-done.2.oth_ref.refs_1_) | copy-start | bytes 1376260
  59.2 6.4 %copy-start.2 = (bf16[256,896]{1,0:T(8,128)(2,1)}, bf16[256,896]{1,0:T(8,128)(2,1)S(1)}, u32[]{:S(2)}) copy-start(bf16[256,896]{1,0:T(8,128)(2,1)S(1)} %collective-permute-done.4.own_ref.refs_2_) | copy-start | bytes 1376260
  59.2 1.9 %collective-permute-start.6 = (bf16[256,896]{1,0:T(8,128)(2,1)S(1)}, bf16[256,896]{1,0:T(8,128)(2,1)S(1)}, u32[]{:S(2)}, u32[]{:S(2)}) collective-permute-start(bf16[256,896]{1,0:T(8,128)(2,1)S(1)} %collective-permute-done.4.own_ref.refs_2_), channel_id=1, source_target_pairs={{0,64},{64,0},{1,65},{65,1},{2,66},{66,2},{3,67},{67,3},{4,68},{68... | collective-permute-start | bytes 1376264 | tf_op jit(solution)/shard_map/ppermute | solution.py:32
  65.6 1.3 collective-permute-start.7
  66.9 4.9 %collective-permute-start.10 = (f32[4,512]{1,0:T(4,128)S(1)}, f32[4,512]{1,0:T(4,128)S(1)}, u32[]{:S(2)}, u32[]{:S(2)}) collective-permute-start(f32[4,512]{1,0:T(4,128)S(1)} %get-tuple-element.106), channel_id=1, source_target_pairs={{0,1},{1,2},{2,3},{3,0},{4,5},{5,6},{6,7},{7,4},{8,9},{9,10},{10,1... | collective-permute-start | bytes 24584 | tf_op jit(solution)/shard_map/ppermute | solution.py:32
  67.0 5.2 %collective-permute-start.9 = (f32[4,512]{1,0:T(4,128)S(1)}, f32[4,512]{1,0:T(4,128)S(1)}, u32[]{:S(2)}, u32[]{:S(2)}) collective-permute-start(f32[4,512]{1,0:T(4,128)S(1)} %get-tuple-element.106), channel_id=1, source_target_pairs={{0,2},{1,3},{2,0},{3,1},{4,6},{5,7},{6,4},{7,5},{8,10},{9,11},{10,... | collective-permute-start | bytes 24584 | tf_op jit(solution)/shard_map/ppermute | solution.py:32
  69.5 3.7 %collective-permute-start.8 = (f32[4,512]{1,0:T(4,128)S(1)}, f32[4,512]{1,0:T(4,128)S(1)}, u32[]{:S(2)}, u32[]{:S(2)}) collective-permute-start(f32[4,512]{1,0:T(4,128)S(1)} %get-tuple-element.106), channel_id=1, source_target_pairs={{0,3},{1,0},{2,1},{3,2},{4,7},{5,4},{6,5},{7,6},{8,11},{9,8},{10,9... | collective-permute-start | bytes 24584 | tf_op jit(solution)/shard_map/ppermute | solution.py:32
  73.9 13.7 %all-to-all-start.2 = ((f32[16,8,256]{2,1,0:T(8,128)}), f32[16,8,256]{2,1,0:T(8,128)S(1)}, u32[]{:S(2)}, u32[]{:S(2)}) async-start(f32[16,8,256]{2,1,0:T(8,128)} %broadcast_in_dim.16), calls=%async_computation.2 | async-start | bytes 262144 | tf_op jit(solution)/shard_map/all_to_all | solution.py:504
  96.4 2.6 %collective-permute-start.11 = (bf16[512,896]{1,0:T(8,128)(2,1)S(1)}, bf16[512,896]{1,0:T(8,128)(2,1)S(1)}, u32[]{:S(2)}, u32[]{:S(2)}) collective-permute-start(bf16[512,896]{1,0:T(8,128)(2,1)S(1)} %get-tuple-element.80), channel_id=1, source_target_pairs={{0,64},{64,0},{1,65},{65,1},{2,66},{66,2},{3,67},{67,3},{4,68},{68... | collective-permute-start | bytes 2752520 | tf_op jit(solution)/shard_map/ppermute | solution.py:32
  100.2 18.3 %all-to-all-start.3 = ((bf16[4,128,896]{2,1,0:T(8,128)(2,1)}), bf16[4,128,896]{2,1,0:T(8,128)(2,1)S(1)}, u32[]{:S(2)}, u32[]{:S(2)}) async-start(bf16[4,128,896]{2,1,0:T(8,128)(2,1)} %bitcast.8), calls=%async_computation.3 | async-start | bytes 1835008 | tf_op jit(solution)/shard_map/all_to_all | solution.py:512
  104.5 7.5 %copy-start.4 = (bf16[512,768]{1,0:T(8,128)(2,1)S(1)}, bf16[512,768]{1,0:T(8,128)(2,1)}, u32[]{:S(2)}) copy-start(bf16[512,768]{1,0:T(8,128)(2,1)} %get-tuple-element.90.refs_8_) | copy-start | bytes 2359300
  104.5 7.5 %copy-start.5 = (bf16[512,768]{1,0:T(8,128)(2,1)S(1)}, bf16[512,768]{1,0:T(8,128)(2,1)}, u32[]{:S(2)}) copy-start(bf16[512,768]{1,0:T(8,128)(2,1)} %get-tuple-element.93.refs_11_) | copy-start | bytes 2359300
  104.5 7.5 %copy-start.6 = (bf16[512,768]{1,0:T(8,128)(2,1)S(1)}, bf16[512,768]{1,0:T(8,128)(2,1)}, u32[]{:S(2)}) copy-start(bf16[512,768]{1,0:T(8,128)(2,1)} %get-tuple-element.91.refs_9_) | copy-start | bytes 2359300
  104.5 7.5 %copy-start.7 = (bf16[512,768]{1,0:T(8,128)(2,1)S(1)}, bf16[512,768]{1,0:T(8,128)(2,1)}, u32[]{:S(2)}) copy-start(bf16[512,768]{1,0:T(8,128)(2,1)} %get-tuple-element.92.refs_10_) | copy-start | bytes 2359300
  119.4 17.4 %all-to-all-start.4 = ((bf16[16,8,896]{2,1,0:T(8,128)(2,1)}), bf16[16,8,896]{2,1,0:T(8,128)(2,1)S(1)}, u32[]{:S(2)}, u32[]{:S(2)}) async-start(bf16[16,8,896]{2,1,0:T(8,128)(2,1)} %bitcast.9), calls=%async_computation.4 | async-start | bytes 458752 | tf_op jit(solution)/shard_map/all_to_all | solution.py:516
  127.6 12.9 %collective-permute-start.12 = (bf16[1024,768]{1,0:T(8,128)(2,1)}, bf16[1024,768]{1,0:T(8,128)(2,1)S(1)}, u32[]{:S(2)}, u32[]{:S(2)}) collective-permute-start(bf16[1024,768]{1,0:T(8,128)(2,1)} %get-tuple-element.102), channel_id=1, source_target_pairs={{0,64},{64,0},{1,65},{65,1},{2,66},{66,2},{3,67},{67,3},{4,68},{68... | collective-permute-start | bytes 4718600 | tf_op jit(solution)/shard_map/ppermute | solution.py:32
  136.8 3.6 %collective-permute-start.13 = (bf16[1024,768]{1,0:T(8,128)(2,1)}, bf16[1024,768]{1,0:T(8,128)(2,1)S(1)}, u32[]{:S(2)}, u32[]{:S(2)}) collective-permute-start(bf16[1024,768]{1,0:T(8,128)(2,1)} %get-tuple-element.103), channel_id=1, source_target_pairs={{0,64},{64,0},{1,65},{65,1},{2,66},{66,2},{3,67},{67,3},{4,68},{68... | collective-permute-start | bytes 4718600 | tf_op jit(solution)/shard_map/ppermute | solution.py:32
  (2 other events, 5.2 us)

commit v9 on v8

--- a/solution.py
+++ b/solution.py
@@ -23,7 +23,6 @@
 EXPO = 128
 SPLIT = (2, 2)
 PARTS = len(SPLIT)
-EARLY = 2
 CLASS = 512
 
 
@@ -201,7 +200,7 @@
     )(base, *in_hbm(blocks), w)
 
 
-def grad_kernel(x, at_ref, na, ka, sa, ta, nb, kb, sb, tb, lse_ref, m_ref, e0, e1, e2, e3, *refs):
+def grad_kernel(x, at_ref, na, ka, sa, ta, nb, kb, sb, tb, nc, kc, sc, tc, lse_ref, m_ref, e0, e1, e2, e3, *refs):
     labels, rows = e0.shape[0], e0.shape[1] // 2
     half = rows // 2
     if x == 0:
@@ -233,7 +232,8 @@
     c1 = lax.broadcasted_iota(jnp.int32, (1, EXTRA), 1)
     lists = []
     for b in range(8):
-        group, spot = ((na, ka, sa, ta), b) if b < EARLY else ((nb, kb, sb, tb), b - EARLY)
+        group = ((na, ka, sa, ta), (nb, kb, sb, tb), (nc, kc, sc, tc), (nb, kb, sb, tb))[b // 2]
+        spot = b if b < 2 else b % 2 + (2 if b >= 6 else 0)
         lists.append(group + (2 * spot + x,))
     most = jnp.int32(0)
     for n_ref, _, _, _, part in lists:
@@ -300,13 +300,13 @@
     res = pl.pallas_call(
         functools.partial(grad_kernel, x),
         out_shape=p + u,
-        in_specs=[SMEM] * 9 + [VMEM] * 2 + [HBM] * 4 + specs,
+        in_specs=[SMEM] * 13 + [VMEM] * 2 + [HBM] * 4 + specs,
         out_specs=(HBM,) * 4 + (VMEM,) * len(u),
         scratch_shapes=pos + held,
         compiler_params=pltpu.CompilerParams(vmem_limit_bytes=20 * 2**20),
         cost_estimate=pl.CostEstimate(flops=4 * labels * rows * 4096 if x == 0 else 1000, bytes_accessed=2**23, transcendentals=0),
         name="rest_part" if x else "query_part",
-    )(at, *hits[0], *hits[1], lse, m, *in_hbm(es), *more)
+    )(at, *hits[0], *hits[1], *hits[2], lse, m, *in_hbm(es), *more)
     return res[:4], res[4:]
 
 
@@ -493,13 +493,16 @@
             hits = [hits_call(jnp.stack([base, xh]), (first, oth[0]), w)]
     es, ms, ls, kept = zip(*parts)
     blocks = [b for pair in zip(own, oth) for b in pair]
-    hits.append(hits_call(jnp.stack([base, xh]), blocks[EARLY:], w))
+    hits.append(hits_call(jnp.stack([base, xh]), blocks[2:4] + blocks[6:], w))
     m = jnp.concatenate(ms, 0)
     stat = jnp.concatenate(ls, 0)
     their, n = shift(stat, "core", 1), rows // 2
     their = jnp.concatenate([their[:, n:2 * n], their[:, :n], their[:, 3 * n:], their[:, 2 * n:3 * n]], 1)
     stat = lse_of([stat, their])
-    stat = lse_of([stat] + [jnp.roll(shift(stat, "y", -d), d, 0) for d in range(1, 4)])
+    at, stat = lax.optimization_barrier((jnp.stack([base, xh]), stat))
+    hits.append(hits_call(at, blocks[4:6], w))
+    others = lax.optimization_barrier((hits[2][0],) + tuple(shift(stat, "y", -d) for d in range(1, 4)))[1:]
+    stat = lse_of([stat] + [jnp.roll(o, d, 0) for d, o in enumerate(others, 1)])
     stat = stat.reshape(8, rows)
     lse = lse_of(lax.all_to_all(jnp.broadcast_to(stat[None], (16, 8, rows)), ("xl", "z"), 0, 0, tiled=True), 0)
 

time: 144 us -> 145 us (level)
  Pallas kernels: 69 us -> 72.4 us
  starting transfers between devices: 28.5 us -> 27 us
    pallas_call x2 -> x3, Pallas kernels: 12.8 us -> 16.1 us  [hits_call(): pl.pallas_call(hits_kernel, out_shape=(jax.ShapeDtypeStruct((2 * count,),...]
    ppermute x13, waiting for transfers between devices: 7.9 us -> 5.32 us  [shift(): return lax.ppermute(x, axis, [(i, (i + step) % n) for i in range(n)])]
    all_to_all x1, waiting for transfers between devices: 0.01 us -> 1.59 us  [body(): lax.all_to_all(jnp.broadcast_to(stat[None], (16, 8, rows)), ('xl', 'z'),...]
  transfers between devices with their start and end apart: 17 -> 17, of which waited for: 9 -> 6; matrix products, arithmetic and copies ran while one was open for 2% -> 2% of each run, Pallas kernels for 37% -> 39%
where the time goes in v9:
time: 145 us; the launch traced here: 144 us
  Pallas kernels  72.4 us (50%)
  blocking collectives  27.8 us (19%)
  starting transfers between devices  27 us (19%)
  waiting for transfers between devices  9.04 us (6%)
  other arithmetic  4.74 us (3%)
  local copies, waits for them, and re-layouts  1.45 us (1%)
    pallas_call x4, Pallas kernels, scores_call(): pl.pallas_call(scores_kernel, out_shape=(pltpu.HBM((labels, 2 * rows), jn...  19.4 us
    pallas_call x2, Pallas kernels, grad_call(): pl.pallas_call(functools.partial(grad_kernel, x), out_shape=p + u, in_spe...  16.3 us
    pallas_call x3, Pallas kernels, hits_call(): pl.pallas_call(hits_kernel, out_shape=(jax.ShapeDtypeStruct((2 * count,),...  16.1 us
    all_to_all x1, blocking collectives, body(): lax.all_to_all(pack_call(embeddings, positives, counts), 'z', 0, 0, tiled...  15.9 us
    pallas_call x2, Pallas kernels, class_call(): pl.pallas_call(class_kernel, out_shape=(jax.ShapeDtypeStruct((2 * labels,...  14 us
    all_to_all x1, blocking collectives, body(): mine = lax.all_to_all(spread(column, 4), ('xh', 'xl'), 0, 0, tiled=True)  11.9 us
    ppermute x13, starting transfers between devices, shift(): return lax.ppermute(x, axis, [(i, (i + step) % n) for i in range(n)])  7.93 us
    all_to_all x1, starting transfers between devices, body(): got = lax.all_to_all(v, ('xl', 'z'), 0, 0, tiled=True)  7.62 us
  transfers between devices with their start and end apart: 17, of which 6 were waited for; matrix products, arithmetic and copies ran while one was open for 2% of the time, Pallas kernels for 39%

profile of v9, /device:TPU:32, one launch (start us, length us, event | category | flops | bytes accessed | tf_op | source)
XLA Modules:
  0.0 143.5 jit_solution(16887829500435003438)
XLA Ops:
  2.1 15.9 %all_to_all.43 = bf16[8,8,896]{2,1,0:T(8,128)(2,1)S(1)} all-to-all(bf16[8,8,896]{2,1,0:T(8,128)(2,1)} %bitcast.14), channel_id=1, replica_groups=mesh['xh'=2,'core'=2,'xl'=2,'z'=8,'y'=4] {'z'}, dimensions={0} | all-to-all | bytes 229376 | tf_op jit(solution)/shard_map/all_to_all | solution.py:476
  18.0 11.9 %all_to_all.44 = bf16[4,64,896]{2,1,0:T(8,128)(2,1)} all-to-all(bf16[4,64,896]{2,1,0:T(8,128)(2,1)S(1)} %broadcast_in_dim.13), channel_id=1, replica_groups=mesh['xh'=2,'core'=2,'xl'=2,'z'=8,'y'=4] {'xh','xl'}, dimensions={0} | all-to-all | bytes 917504 | tf_op jit(solution)/shard_map/all_to_all | solution.py:477
  31.5 1.7 %collective-permute-start.1 = (bf16[256,896]{1,0:T(8,128)(2,1)}, bf16[256,896]{1,0:T(8,128)(2,1)}, u32[]{:S(2)}, u32[]{:S(2)}) collective-permute-start(bf16[256,896]{1,0:T(8,128)(2,1)} %bitcast.4.own_ref.refs_0_), channel_id=1, source_target_pairs={{0,3},{1,0},{2,1},{3,2},{4,7},{5,4},{6,5},{7,6},{8,11},{9,8},{10,9... | collective-permute-start | bytes 1376264 | tf_op jit(solution)/shard_map/ppermute | solution.py:31
  33.2 1.9 %take.1.w_ref.refs_2_.refs_4_.refs_0_ = bf16[2048,768]{1,0:T(8,128)(2,1)S(1)} custom-call(s32[1]{0:T(128)} %bitcast.5.core_ref, bf16[4096,768]{1,0:T(8,128)(2,1)} %all_ref.1), custom_call_target="tpu_custom_call" | custom-call | flops 1000 | bytes 1000 | tf_op jit(solution)/shard_map/take/pallas_call | solution.py:427
  35.2 4.9 %scores.4 = (bf16[2048,512]{1,0:T(8,128)(2,1)}, f32[1,512]{1,0:T(1,128)S(1)}, f32[1,512]{1,0:T(1,128)S(1)}, bf16[512,768]{1,0:T(8,128)(2,1)}) custom-call(s32[1]{0:T(128)} %bitcast.1.xh_ref, bf16[256,896]{1,0:T(8,128)(2,1)} %bitcast.4.own_ref.refs_0_, bf16[256,896]{1,0:T(8,128)(2,1)} %collective-permute-done.oth_ref.refs_1_, ...), custom_call_target="tpu_custom_call" | custom-call | flops 1000 | bytes 1000 | tf_op jit(solution)/shard_map/scores/pallas_call | solution.py:93
  40.0 4.6 %hits.3 = (s32[4]{0:T(128)S(1)}, s32[2560]{0:T(1024)S(1)}, f32[2560]{0:T(1024)S(1)}, f32[2560]{0:T(1024)S(1)}) custom-call(s32[2]{0:T(128)S(1)} %pad_add_fusion.base_ref, bf16[256,896]{1,0:T(8,128)(2,1)} %bitcast.4.own_ref.refs_0_, bf16[256,896]{1,0:T(8,128)(2,1)} %collective-permute-done.oth_ref.refs_1_, bf16[2048,768]{1,0:T(8,128)(2,1)S(1)} %take.1.w_ref.refs_2_.refs_4_.refs_0_), custom_call_target="tpu_custom_call" | custom-call | flops 1000 | bytes 1000 | tf_op jit(solution)/shard_map/hits/pallas_call | solution.py:186
  46.3 2.7 %collective-permute-start.4 = (bf16[256,896]{1,0:T(8,128)(2,1)S(1)}, bf16[256,896]{1,0:T(8,128)(2,1)S(1)}, u32[]{:S(2)}, u32[]{:S(2)}) collective-permute-start(bf16[256,896]{1,0:T(8,128)(2,1)S(1)} %broadcast_select_fusion), channel_id=1, source_target_pairs={{0,3},{1,0},{2,1},{3,2},{64,65},{65,66},{66,67},{67,64},{4,7},{5,4... | collective-permute-start | bytes 1376264 | tf_op jit(solution)/shard_map/ppermute | solution.py:480
  49.1 5.0 %scores.6 = (bf16[2048,512]{1,0:T(8,128)(2,1)}, f32[1,512]{1,0:T(1,128)S(1)}, f32[1,512]{1,0:T(1,128)S(1)}, bf16[512,768]{1,0:T(8,128)(2,1)}) custom-call(s32[1]{0:T(128)} %bitcast.1.xh_ref, bf16[256,896]{1,0:T(8,128)(2,1)} %collective-permute-done.3.own_ref.refs_2_, bf16[256,896]{1,0:T(8,128)(2,1)S(1)} %collective-permute-done.5.oth_ref.refs_3_, ...), custom_call_target="tpu_custom_call" | custom-call | flops 1000 | bytes 1000 | tf_op jit(solution)/shard_map/scores/pallas_call | solution.py:93
  54.1 5.0 %scores.5 = (bf16[2048,512]{1,0:T(8,128)(2,1)}, f32[1,512]{1,0:T(1,128)S(1)}, f32[1,512]{1,0:T(1,128)S(1)}, bf16[512,768]{1,0:T(8,128)(2,1)}) custom-call(s32[1]{0:T(128)} %bitcast.1.xh_ref, bf16[256,896]{1,0:T(8,128)(2,1)} %collective-permute-done.1.own_ref.refs_0_, bf16[256,896]{1,0:T(8,128)(2,1)S(1)} %collective-permute-done.2.oth_ref.refs_1_, ...), custom_call_target="tpu_custom_call" | custom-call | flops 1000 | bytes 1000 | tf_op jit(solution)/shard_map/scores/pallas_call | solution.py:93
  59.3 1.8 %collective-permute-done.6.oth_ref.refs_1_ = bf16[256,896]{1,0:T(8,128)(2,1)S(1)} collective-permute-done((bf16[256,896]{1,0:T(8,128)(2,1)S(1)}, bf16[256,896]{1,0:T(8,128)(2,1)S(1)}, u32[]{:S(2)}, u32[]{:S(2)}) %collective-permute-start.6) | collective-permute-done | bytes 458784 | tf_op jit(solution)/shard_map/ppermute | solution.py:31
  61.1 4.4 %scores.7 = (bf16[2048,512]{1,0:T(8,128)(2,1)}, f32[1,512]{1,0:T(1,128)S(1)}, f32[1,512]{1,0:T(1,128)S(1)}, bf16[512,768]{1,0:T(8,128)(2,1)}) custom-call(s32[1]{0:T(128)} %bitcast.1.xh_ref, bf16[256,896]{1,0:T(8,128)(2,1)S(1)} %collective-permute-done.4.own_ref.refs_0_, bf16[256,896]{1,0:T(8,128)(2,1)S(1)} %collective-permute-done.6.oth_ref.refs_1_, ...), custom_call_target="tpu_custom_call" | custom-call | flops 1000 | bytes 1000 | tf_op jit(solution)/shard_map/scores/pallas_call | solution.py:93
  67.0 2.5 %collective-permute-start.9 = (f32[4,512]{1,0:T(4,128)S(1)}, f32[4,512]{1,0:T(4,128)S(1)}, u32[]{:S(2)}, u32[]{:S(2)}) collective-permute-start(f32[4,512]{1,0:T(4,128)S(1)} %log_add_fusion.2), channel_id=1, source_target_pairs={{0,2},{1,3},{2,0},{3,1},{4,6},{5,7},{6,4},{7,5},{8,10},{9,11},{10,... | collective-permute-start | bytes 24584 | tf_op jit(solution)/shard_map/ppermute | solution.py:31
  70.6 5.1 %hits.4 = (s32[4]{0:T(128)S(1)}, s32[2560]{0:T(1024)S(1)}, f32[2560]{0:T(1024)S(1)}, f32[2560]{0:T(1024)S(1)}) custom-call(s32[2]{0:T(128)S(1)} %pad_add_fusion.base_ref, bf16[256,896]{1,0:T(8,128)(2,1)} %copy-done.2, bf16[256,896]{1,0:T(8,128)(2,1)} %copy-done.3, bf16[2048,768]{1,0:T(8,128)(2,1)S(1)} %take.1.w_ref.refs_2_.refs_4_.refs_0_), custom_call_target="tpu_custom_call" | custom-call | flops 1000 | bytes 1000 | tf_op jit(solution)/shard_map/hits/pallas_call | solution.py:186
  76.5 4.9 %all-to-all-start.2 = ((f32[16,8,256]{2,1,0:T(8,128)}), f32[16,8,256]{2,1,0:T(8,128)S(1)}, u32[]{:S(2)}, u32[]{:S(2)}) async-start(f32[16,8,256]{2,1,0:T(8,128)} %broadcast_in_dim.16), calls=%async_computation.2 | async-start | bytes 262144 | tf_op jit(solution)/shard_map/all_to_all | solution.py:507
  81.4 6.4 %hits.5 = (s32[8]{0:T(128)S(1)}, s32[5120]{0:T(1024)S(1)}, f32[5120]{0:T(1024)S(1)}, f32[5120]{0:T(1024)S(1)}) custom-call(s32[2]{0:T(128)S(1)} %pad_add_fusion.base_ref, bf16[256,896]{1,0:T(8,128)(2,1)} %collective-permute-done.1.own_ref.refs_0_, bf16[256,896]{1,0:T(8,128)(2,1)} %copy-done, bf16[256,896]{1,0:T(8,128)(2,1)} %collective-permute-done.3.own_ref.refs_2_, ...), custom_call_target="tpu_custom_call" | custom-call | flops 1000 | bytes 1000 | tf_op jit(solution)/shard_map/hits/pallas_call | solution.py:186
  89.5 8.9 %query_part.1 = (bf16[2048,256]{1,0:T(8,128)(2,1)}, bf16[2048,256]{1,0:T(8,128)(2,1)}, bf16[2048,256]{1,0:T(8,128)(2,1)}, bf16[2048,256]{1,0:T(8,128)(2,1)}, bf1...) custom-call(s32[1]{0:T(128)} %bitcast.7.at_ref, s32[4]{0:T(128)S(1)} %get-tuple-element.66.na, ...), custom_call_target="tpu_custom_call" | custom-call | flops 8589934592 | bytes 8388608 | tf_op jit(solution)/shard_map/query_part/pallas_call | solution.py:300
  98.6 2.5 %collective-permute-done.11 = bf16[512,896]{1,0:T(8,128)(2,1)S(1)} collective-permute-done((bf16[512,896]{1,0:T(8,128)(2,1)S(1)}, bf16[512,896]{1,0:T(8,128)(2,1)S(1)}, u32[]{:S(2)}, u32[]{:S(2)}) %collective-permute-start.11) | collective-permute-done | bytes 917536 | tf_op jit(solution)/shard_map/ppermute | solution.py:31
  102.2 3.8 %all-to-all-start.3 = ((bf16[4,128,896]{2,1,0:T(8,128)(2,1)}), bf16[4,128,896]{2,1,0:T(8,128)(2,1)S(1)}, u32[]{:S(2)}, u32[]{:S(2)}) async-start(bf16[4,128,896]{2,1,0:T(8,128)(2,1)} %bitcast.8), calls=%async_computation.3 | async-start | bytes 1835008 | tf_op jit(solution)/shard_map/all_to_all | solution.py:515
  106.0 7.4 %rest_part.1 = (bf16[2048,256]{1,0:T(8,128)(2,1)}, bf16[2048,256]{1,0:T(8,128)(2,1)}, bf16[2048,256]{1,0:T(8,128)(2,1)}, bf16[2048,256]{1,0:T(8,128)(2,1)}) custom-call(s32[1]{0:T(128)} %bitcast.7.at_ref, s32[4]{0:T(128)S(1)} %get-tuple-element.66.na, s32[2560]{0:T(1024)S(1)} %get-tuple-element.81.ka, f32[2560]{0:T(1024)S(1)} %get-tuple-element.82.sa, ...), custom_call_target="tpu_custom_call" | custom-call | flops 1000 | bytes 8388608 | tf_op jit(solution)/shard_map/rest_part/pallas_call | solution.py:300
  113.4 6.4 %class_part.2 = (bf16[4096,768]{1,0:T(8,128)(2,1)}, bf16[1024,768]{1,0:T(8,128)(2,1)}) custom-call(s32[1]{0:T(128)} %bitcast.5.core_ref, bf16[2048,256]{1,0:T(8,128)(2,1)} %get-tuple-element.113.refs_0_, bf16[2048,256]{1,0:T(8,128)(2,1)} %get-tuple-element.100.refs_1_, bf16[2048,256]{1,0:T(8,128)(2,1)} %get-tuple-element.101.refs_2_, ...), custom_call_target="tpu_custom_call" | custom-call | flops 3221225472 | bytes 8388608 | tf_op jit(solution)/shard_map/class_part/pallas_call | solution.py:335
  120.8 7.6 %all-to-all-start.4 = ((bf16[16,8,896]{2,1,0:T(8,128)(2,1)}), bf16[16,8,896]{2,1,0:T(8,128)(2,1)S(1)}, u32[]{:S(2)}, u32[]{:S(2)}) async-start(bf16[16,8,896]{2,1,0:T(8,128)(2,1)} %bitcast.9), calls=%async_computation.4 | async-start | bytes 458752 | tf_op jit(solution)/shard_map/all_to_all | solution.py:519
  128.4 7.6 %class_part.3 = (bf16[4096,768]{1,0:T(8,128)(2,1)}, bf16[1024,768]{1,0:T(8,128)(2,1)}) custom-call(s32[1]{0:T(128)} %bitcast.5.core_ref, bf16[2048,256]{1,0:T(8,128)(2,1)} %get-tuple-element.113.refs_0_, bf16[2048,256]{1,0:T(8,128)(2,1)} %get-tuple-element.100.refs_1_, ...), custom_call_target="tpu_custom_call", output_to_operand_aliasing={{0}: (13, {})} | custom-call | flops 3221225472 | bytes 8388608 | tf_op jit(solution)/shard_map/class_part/pallas_call | solution.py:335
  136.0 2.0 %all-to-all-done.4 = bf16[16,8,896]{2,1,0:T(8,128)(2,1)S(1)} async-done(((bf16[16,8,896]{2,1,0:T(8,128)(2,1)}), bf16[16,8,896]{2,1,0:T(8,128)(2,1)S(1)}, u32[]{:S(2)}, u32[]{:S(2)}) %all-to-all-start.4) | async-done | bytes 229408 | tf_op jit(solution)/shard_map/all_to_all | solution.py:519
  141.7 1.7 %place.1 = bf16[4096,768]{1,0:T(8,128)(2,1)} custom-call(s32[1]{0:T(128)} %bitcast.5.core_ref, bf16[1024,768]{1,0:T(8,128)(2,1)S(1)} %collective-permute-done.12.refs_0_, bf16[1024,768]{1,0:T(8,128)(2,1)S(1)} %collective-permute-done.13.refs_1_, bf16[4096,768]{1,0:T(8,128)(2,1)} %get-tuple-element.122.refs_2_), custom_call_target="tpu_custom_call", output_to_operand_aliasing={{}: (3, {})} | custom-call | flops 1000 | bytes 1000 | tf_op jit(solution)/shard_map/place/pallas_call | solution.py:370
  (67 shorter events, 15.8 us)
Async XLA Ops:
  29.9 5.2 %collective-permute-start = (bf16[256,896]{1,0:T(8,128)(2,1)}, bf16[256,896]{1,0:T(8,128)(2,1)}, u32[]{:S(2)}, u32[]{:S(2)}) collective-permute-start(bf16[256,896]{1,0:T(8,128)(2,1)} %bitcast.4.own_ref.refs_0_), channel_id=1, source_target_pairs={{0,64},{64,0},{1,65},{65,1},{2,66},{66,2},{3,67},{67,3},{4,68},{68... | collective-permute-start | bytes 1376264 | tf_op jit(solution)/shard_map/ppermute | solution.py:31
  29.9 14.7 %collective-permute-start.3 = (bf16[256,896]{1,0:T(8,128)(2,1)}, bf16[256,896]{1,0:T(8,128)(2,1)}, u32[]{:S(2)}, u32[]{:S(2)}) collective-permute-start(bf16[256,896]{1,0:T(8,128)(2,1)} %bitcast.4.own_ref.refs_0_), channel_id=1, source_target_pairs={{0,1},{1,2},{2,3},{3,0},{4,5},{5,6},{6,7},{7,4},{8,9},{9,10},{10,1... | collective-permute-start | bytes 1376264 | tf_op jit(solution)/shard_map/ppermute | solution.py:31
  31.5 13.2 %collective-permute-start.1 = (bf16[256,896]{1,0:T(8,128)(2,1)}, bf16[256,896]{1,0:T(8,128)(2,1)}, u32[]{:S(2)}, u32[]{:S(2)}) collective-permute-start(bf16[256,896]{1,0:T(8,128)(2,1)} %bitcast.4.own_ref.refs_0_), channel_id=1, source_target_pairs={{0,3},{1,0},{2,1},{3,2},{4,7},{5,4},{6,5},{7,6},{8,11},{9,8},{10,9... | collective-permute-start | bytes 1376264 | tf_op jit(solution)/shard_map/ppermute | solution.py:31
  44.7 9.5 %collective-permute-start.2 = (bf16[256,896]{1,0:T(8,128)(2,1)}, bf16[256,896]{1,0:T(8,128)(2,1)S(1)}, u32[]{:S(2)}, u32[]{:S(2)}) collective-permute-start(bf16[256,896]{1,0:T(8,128)(2,1)} %collective-permute-done.1.own_ref.refs_0_), channel_id=1, source_target_pairs={{0,64},{64,0},{1,65},{65,1},{2,66},{66,2},{3,67},{67,3},{4,68},{68... | collective-permute-start | bytes 1376264 | tf_op jit(solution)/shard_map/ppermute | solution.py:31
  44.8 4.3 %collective-permute-start.5 = (bf16[256,896]{1,0:T(8,128)(2,1)}, bf16[256,896]{1,0:T(8,128)(2,1)S(1)}, u32[]{:S(2)}, u32[]{:S(2)}) collective-permute-start(bf16[256,896]{1,0:T(8,128)(2,1)} %collective-permute-done.3.own_ref.refs_2_), channel_id=1, source_target_pairs={{0,64},{64,0},{1,65},{65,1},{2,66},{66,2},{3,67},{67,3},{4,68},{68... | collective-permute-start | bytes 1376264 | tf_op jit(solution)/shard_map/ppermute | solution.py:31
  46.3 12.9 %collective-permute-start.4 = (bf16[256,896]{1,0:T(8,128)(2,1)S(1)}, bf16[256,896]{1,0:T(8,128)(2,1)S(1)}, u32[]{:S(2)}, u32[]{:S(2)}) collective-permute-start(bf16[256,896]{1,0:T(8,128)(2,1)S(1)} %broadcast_select_fusion), channel_id=1, source_target_pairs={{0,3},{1,0},{2,1},{3,2},{64,65},{65,66},{66,67},{67,64},{4,7},{5,4... | collective-permute-start | bytes 1376264 | tf_op jit(solution)/shard_map/ppermute | solution.py:480
  49.1 10.1 %copy-start.1 = (bf16[256,896]{1,0:T(8,128)(2,1)}, bf16[256,896]{1,0:T(8,128)(2,1)S(1)}, u32[]{:S(2)}) copy-start(bf16[256,896]{1,0:T(8,128)(2,1)S(1)} %collective-permute-done.5.oth_ref.refs_3_) | copy-start | bytes 1376260
  54.1 11.4 %copy-start = (bf16[256,896]{1,0:T(8,128)(2,1)}, bf16[256,896]{1,0:T(8,128)(2,1)S(1)}, u32[]{:S(2)}) copy-start(bf16[256,896]{1,0:T(8,128)(2,1)S(1)} %collective-permute-done.2.oth_ref.refs_1_) | copy-start | bytes 1376260
  59.2 11.4 %copy-start.2 = (bf16[256,896]{1,0:T(8,128)(2,1)}, bf16[256,896]{1,0:T(8,128)(2,1)S(1)}, u32[]{:S(2)}) copy-start(bf16[256,896]{1,0:T(8,128)(2,1)S(1)} %collective-permute-done.4.own_ref.refs_0_) | copy-start | bytes 1376260
  59.2 1.9 %collective-permute-start.6 = (bf16[256,896]{1,0:T(8,128)(2,1)S(1)}, bf16[256,896]{1,0:T(8,128)(2,1)S(1)}, u32[]{:S(2)}, u32[]{:S(2)}) collective-permute-start(bf16[256,896]{1,0:T(8,128)(2,1)S(1)} %collective-permute-done.4.own_ref.refs_0_), channel_id=1, source_target_pairs={{0,64},{64,0},{1,65},{65,1},{2,66},{66,2},{3,67},{67,3},{4,68},{68... | collective-permute-start | bytes 1376264 | tf_op jit(solution)/shard_map/ppermute | solution.py:31
  61.1 9.5 %copy-start.3 = (bf16[256,896]{1,0:T(8,128)(2,1)}, bf16[256,896]{1,0:T(8,128)(2,1)S(1)}, u32[]{:S(2)}) copy-start(bf16[256,896]{1,0:T(8,128)(2,1)S(1)} %collective-permute-done.6.oth_ref.refs_1_) | copy-start | bytes 1376260
  65.6 1.3 collective-permute-start.7
  66.9 8.8 %collective-permute-start.10 = (f32[4,512]{1,0:T(4,128)S(1)}, f32[4,512]{1,0:T(4,128)S(1)}, u32[]{:S(2)}, u32[]{:S(2)}) collective-permute-start(f32[4,512]{1,0:T(4,128)S(1)} %log_add_fusion.2), channel_id=1, source_target_pairs={{0,1},{1,2},{2,3},{3,0},{4,5},{5,6},{6,7},{7,4},{8,9},{9,10},{10,1... | collective-permute-start | bytes 24584 | tf_op jit(solution)/shard_map/ppermute | solution.py:31
  67.0 8.7 %collective-permute-start.9 = (f32[4,512]{1,0:T(4,128)S(1)}, f32[4,512]{1,0:T(4,128)S(1)}, u32[]{:S(2)}, u32[]{:S(2)}) collective-permute-start(f32[4,512]{1,0:T(4,128)S(1)} %log_add_fusion.2), channel_id=1, source_target_pairs={{0,2},{1,3},{2,0},{3,1},{4,6},{5,7},{6,4},{7,5},{8,10},{9,11},{10,... | collective-permute-start | bytes 24584 | tf_op jit(solution)/shard_map/ppermute | solution.py:31
  69.5 6.3 %collective-permute-start.8 = (f32[4,512]{1,0:T(4,128)S(1)}, f32[4,512]{1,0:T(4,128)S(1)}, u32[]{:S(2)}, u32[]{:S(2)}) collective-permute-start(f32[4,512]{1,0:T(4,128)S(1)} %log_add_fusion.2), channel_id=1, source_target_pairs={{0,3},{1,0},{2,1},{3,2},{4,7},{5,4},{6,5},{7,6},{8,11},{9,8},{10,9... | collective-permute-start | bytes 24584 | tf_op jit(solution)/shard_map/ppermute | solution.py:31
  76.5 13.0 %all-to-all-start.2 = ((f32[16,8,256]{2,1,0:T(8,128)}), f32[16,8,256]{2,1,0:T(8,128)S(1)}, u32[]{:S(2)}, u32[]{:S(2)}) async-start(f32[16,8,256]{2,1,0:T(8,128)} %broadcast_in_dim.16), calls=%async_computation.2 | async-start | bytes 262144 | tf_op jit(solution)/shard_map/all_to_all | solution.py:507
  98.5 2.6 %collective-permute-start.11 = (bf16[512,896]{1,0:T(8,128)(2,1)S(1)}, bf16[512,896]{1,0:T(8,128)(2,1)S(1)}, u32[]{:S(2)}, u32[]{:S(2)}) collective-permute-start(bf16[512,896]{1,0:T(8,128)(2,1)S(1)} %get-tuple-element.98), channel_id=1, source_target_pairs={{0,64},{64,0},{1,65},{65,1},{2,66},{66,2},{3,67},{67,3},{4,68},{68... | collective-permute-start | bytes 2752520 | tf_op jit(solution)/shard_map/ppermute | solution.py:31
  102.2 17.7 %all-to-all-start.3 = ((bf16[4,128,896]{2,1,0:T(8,128)(2,1)}), bf16[4,128,896]{2,1,0:T(8,128)(2,1)S(1)}, u32[]{:S(2)}, u32[]{:S(2)}) async-start(bf16[4,128,896]{2,1,0:T(8,128)(2,1)} %bitcast.8), calls=%async_computation.3 | async-start | bytes 1835008 | tf_op jit(solution)/shard_map/all_to_all | solution.py:515
  105.9 7.4 %copy-start.5 = (bf16[512,768]{1,0:T(8,128)(2,1)S(1)}, bf16[512,768]{1,0:T(8,128)(2,1)}, u32[]{:S(2)}) copy-start(bf16[512,768]{1,0:T(8,128)(2,1)} %get-tuple-element.111.refs_11_) | copy-start | bytes 2359300
  105.9 7.4 %copy-start.6 = (bf16[512,768]{1,0:T(8,128)(2,1)S(1)}, bf16[512,768]{1,0:T(8,128)(2,1)}, u32[]{:S(2)}) copy-start(bf16[512,768]{1,0:T(8,128)(2,1)} %get-tuple-element.109.refs_9_) | copy-start | bytes 2359300
  106.0 7.4 %copy-start.7 = (bf16[512,768]{1,0:T(8,128)(2,1)S(1)}, bf16[512,768]{1,0:T(8,128)(2,1)}, u32[]{:S(2)}) copy-start(bf16[512,768]{1,0:T(8,128)(2,1)} %get-tuple-element.110.refs_10_) | copy-start | bytes 2359300
  120.8 17.2 %all-to-all-start.4 = ((bf16[16,8,896]{2,1,0:T(8,128)(2,1)}), bf16[16,8,896]{2,1,0:T(8,128)(2,1)S(1)}, u32[]{:S(2)}, u32[]{:S(2)}) async-start(bf16[16,8,896]{2,1,0:T(8,128)(2,1)} %bitcast.9), calls=%async_computation.4 | async-start | bytes 458752 | tf_op jit(solution)/shard_map/all_to_all | solution.py:519
  128.4 13.2 %collective-permute-start.12 = (bf16[1024,768]{1,0:T(8,128)(2,1)}, bf16[1024,768]{1,0:T(8,128)(2,1)S(1)}, u32[]{:S(2)}, u32[]{:S(2)}) collective-permute-start(bf16[1024,768]{1,0:T(8,128)(2,1)} %get-tuple-element.120), channel_id=1, source_target_pairs={{0,64},{64,0},{1,65},{65,1},{2,66},{66,2},{3,67},{67,3},{4,68},{68... | collective-permute-start | bytes 4718600 | tf_op jit(solution)/shard_map/ppermute | solution.py:31
  138.0 3.6 %collective-permute-start.13 = (bf16[1024,768]{1,0:T(8,128)(2,1)}, bf16[1024,768]{1,0:T(8,128)(2,1)S(1)}, u32[]{:S(2)}, u32[]{:S(2)}) collective-permute-start(bf16[1024,768]{1,0:T(8,128)(2,1)} %get-tuple-element.121), channel_id=1, source_target_pairs={{0,64},{64,0},{1,65},{65,1},{2,66},{66,2},{3,67},{67,3},{4,68},{68... | collective-permute-start | bytes 4718600 | tf_op jit(solution)/shard_map/ppermute | solution.py:31
  (2 other events, 8.1 us)

commit v10 on v8

--- a/solution.py
+++ b/solution.py
@@ -21,7 +21,7 @@
 LCH = 256
 PROD = 1024
 EXPO = 128
-SPLIT = (2, 2)
+SPLIT = (3, 1)
 PARTS = len(SPLIT)
 EARLY = 2
 CLASS = 512

time: 144 us -> 147 us (1.021)
  waiting for transfers between devices: 9.64 us -> 12.6 us
  Pallas kernels: 69 us -> 71.3 us
    all_to_all x1, waiting for transfers between devices: 1.65 us -> 4.78 us  [body(): got = lax.all_to_all(v, ('xl', 'z'), 0, 0, tiled=True)]
    pallas_call x2, Pallas kernels: 12.8 us -> 14.9 us  [hits_call(): pl.pallas_call(hits_kernel, out_shape=(jax.ShapeDtypeStruct((2 * count,),...]
  transfers between devices with their start and end apart: 17 -> 17, of which waited for: 9 -> 7; matrix products, arithmetic and copies ran while one was open for 2% -> 2% of each run, Pallas kernels for 37% -> 37%
where the time goes in v10:
time: 147 us
  Pallas kernels  71.3 us (49%)
  blocking collectives  27.8 us (19%)
  starting transfers between devices  27.5 us (19%)
  waiting for transfers between devices  12.6 us (9%)
  other arithmetic  4.78 us (3%)
  local copies, waits for them, and re-layouts  1.5 us (1%)
    pallas_call x4, Pallas kernels, scores_call(): pl.pallas_call(scores_kernel, out_shape=(pltpu.HBM((labels, 2 * rows), jn...  19.4 us
    pallas_call x2, Pallas kernels, grad_call(): pl.pallas_call(functools.partial(grad_kernel, x), out_shape=p + u, in_spe...  16.6 us
    all_to_all x1, blocking collectives, body(): lax.all_to_all(pack_call(embeddings, positives, counts), 'z', 0, 0, tiled...  15.9 us
    pallas_call x2, Pallas kernels, hits_call(): pl.pallas_call(hits_kernel, out_shape=(jax.ShapeDtypeStruct((2 * count,),...  14.9 us
    pallas_call x2, Pallas kernels, class_call(): pl.pallas_call(class_kernel, out_shape=(jax.ShapeDtypeStruct((2 * labels,...  13.8 us
    all_to_all x1, blocking collectives, body(): mine = lax.all_to_all(spread(column, 4), ('xh', 'xl'), 0, 0, tiled=True)  11.9 us
    all_to_all x1, starting transfers between devices, body(): got = lax.all_to_all(v, ('xl', 'z'), 0, 0, tiled=True)  8.06 us
    ppermute x13, starting transfers between devices, shift(): return lax.ppermute(x, axis, [(i, (i + step) % n) for i in range(n)])  7.89 us
  transfers between devices with their start and end apart: 17, of which 7 were waited for; matrix products, arithmetic and copies ran while one was open for 2% of the time, Pallas kernels for 37%

profile of v10, /device:TPU:32, one launch (start us, length us, event | category | flops | bytes accessed | tf_op | source)
XLA Modules:
  0.0 146.6 jit_solution(10060854701511643814)
XLA Ops:
  2.1 15.9 %all_to_all.43 = bf16[8,8,896]{2,1,0:T(8,128)(2,1)S(1)} all-to-all(bf16[8,8,896]{2,1,0:T(8,128)(2,1)} %bitcast.14), channel_id=1, replica_groups=mesh['xh'=2,'core'=2,'xl'=2,'z'=8,'y'=4] {'z'}, dimensions={0} | all-to-all | bytes 229376 | tf_op jit(solution)/shard_map/all_to_all | solution.py:476
  18.0 11.9 %all_to_all.44 = bf16[4,64,896]{2,1,0:T(8,128)(2,1)} all-to-all(bf16[4,64,896]{2,1,0:T(8,128)(2,1)S(1)} %broadcast_in_dim.14), channel_id=1, replica_groups=mesh['xh'=2,'core'=2,'xl'=2,'z'=8,'y'=4] {'xh','xl'}, dimensions={0} | all-to-all | bytes 917504 | tf_op jit(solution)/shard_map/all_to_all | solution.py:477
  29.9 1.6 %collective-permute-start.3 = (bf16[256,896]{1,0:T(8,128)(2,1)}, bf16[256,896]{1,0:T(8,128)(2,1)}, u32[]{:S(2)}, u32[]{:S(2)}) collective-permute-start(bf16[256,896]{1,0:T(8,128)(2,1)} %bitcast.3.own_ref.refs_0_), channel_id=1, source_target_pairs={{0,1},{1,2},{2,3},{3,0},{4,5},{5,6},{6,7},{7,4},{8,9},{9,10},{10,1... | collective-permute-start | bytes 1376264 | tf_op jit(solution)/shard_map/ppermute | solution.py:32
  31.5 1.7 %collective-permute-start.1 = (bf16[256,896]{1,0:T(8,128)(2,1)}, bf16[256,896]{1,0:T(8,128)(2,1)}, u32[]{:S(2)}, u32[]{:S(2)}) collective-permute-start(bf16[256,896]{1,0:T(8,128)(2,1)} %bitcast.3.own_ref.refs_0_), channel_id=1, source_target_pairs={{0,3},{1,0},{2,1},{3,2},{4,7},{5,4},{6,5},{7,6},{8,11},{9,8},{10,9... | collective-permute-start | bytes 1376264 | tf_op jit(solution)/shard_map/ppermute | solution.py:32
  33.2 1.9 %take.1.w_ref.refs_2_.refs_6_.refs_0_ = bf16[2048,768]{1,0:T(8,128)(2,1)S(1)} custom-call(s32[1]{0:T(128)} %bitcast.4.core_ref, bf16[4096,768]{1,0:T(8,128)(2,1)} %all_ref.1), custom_call_target="tpu_custom_call" | custom-call | flops 1000 | bytes 1000 | tf_op jit(solution)/shard_map/take/pallas_call | solution.py:427
  35.2 4.9 %scores.4 = (bf16[2048,512]{1,0:T(8,128)(2,1)}, f32[1,512]{1,0:T(1,128)S(1)}, f32[1,512]{1,0:T(1,128)S(1)}, bf16[512,768]{1,0:T(8,128)(2,1)}) custom-call(s32[1]{0:T(128)} %bitcast.xh_ref, bf16[256,896]{1,0:T(8,128)(2,1)} %bitcast.3.own_ref.refs_0_, bf16[256,896]{1,0:T(8,128)(2,1)} %collective-permute-done.oth_ref.refs_1_, ...), custom_call_target="tpu_custom_call" | custom-call | flops 1000 | bytes 1000 | tf_op jit(solution)/shard_map/scores/pallas_call | solution.py:94
  40.0 4.9 %hits.2 = (s32[4]{0:T(128)S(1)}, s32[2560]{0:T(1024)S(1)}, f32[2560]{0:T(1024)S(1)}, f32[2560]{0:T(1024)S(1)}) custom-call(s32[2]{0:T(128)S(1)} %pad_add_fusion.base_ref, bf16[256,896]{1,0:T(8,128)(2,1)} %bitcast.3.own_ref.refs_0_, bf16[256,896]{1,0:T(8,128)(2,1)} %collective-permute-done.oth_ref.refs_1_, bf16[2048,768]{1,0:T(8,128)(2,1)S(1)} %take.1.w_ref.refs_2_.refs_6_.refs_0_), custom_call_target="tpu_custom_call" | custom-call | flops 1000 | bytes 1000 | tf_op jit(solution)/shard_map/hits/pallas_call | solution.py:187
  46.7 2.5 %collective-permute-start.4 = (bf16[256,896]{1,0:T(8,128)(2,1)S(1)}, bf16[256,896]{1,0:T(8,128)(2,1)S(1)}, u32[]{:S(2)}, u32[]{:S(2)}) collective-permute-start(bf16[256,896]{1,0:T(8,128)(2,1)S(1)} %broadcast_select_fusion), channel_id=1, source_target_pairs={{0,3},{1,0},{2,1},{3,2},{64,65},{65,66},{66,67},{67,64},{4,7},{5,4... | collective-permute-start | bytes 1376264 | tf_op jit(solution)/shard_map/ppermute | solution.py:480
  49.2 5.0 %scores.6 = (bf16[2048,512]{1,0:T(8,128)(2,1)}, f32[1,512]{1,0:T(1,128)S(1)}, f32[1,512]{1,0:T(1,128)S(1)}, bf16[512,768]{1,0:T(8,128)(2,1)}) custom-call(s32[1]{0:T(128)} %bitcast.xh_ref, bf16[256,896]{1,0:T(8,128)(2,1)} %collective-permute-done.3.own_ref.refs_4_, bf16[256,896]{1,0:T(8,128)(2,1)S(1)} %collective-permute-done.5.oth_ref.refs_5_, ...), custom_call_target="tpu_custom_call" | custom-call | flops 1000 | bytes 1000 | tf_op jit(solution)/shard_map/scores/pallas_call | solution.py:94
  54.3 5.0 %scores.5 = (bf16[2048,512]{1,0:T(8,128)(2,1)}, f32[1,512]{1,0:T(1,128)S(1)}, f32[1,512]{1,0:T(1,128)S(1)}, bf16[512,768]{1,0:T(8,128)(2,1)}) custom-call(s32[1]{0:T(128)} %bitcast.xh_ref, bf16[256,896]{1,0:T(8,128)(2,1)} %collective-permute-done.1.own_ref.refs_0_, bf16[256,896]{1,0:T(8,128)(2,1)S(1)} %collective-permute-done.2.oth_ref.refs_1_, ...), custom_call_target="tpu_custom_call" | custom-call | flops 1000 | bytes 1000 | tf_op jit(solution)/shard_map/scores/pallas_call | solution.py:94
  59.4 1.8 %collective-permute-done.6.oth_ref.refs_3_ = bf16[256,896]{1,0:T(8,128)(2,1)S(1)} collective-permute-done((bf16[256,896]{1,0:T(8,128)(2,1)S(1)}, bf16[256,896]{1,0:T(8,128)(2,1)S(1)}, u32[]{:S(2)}, u32[]{:S(2)}) %collective-permute-start.6) | collective-permute-done | bytes 458784 | tf_op jit(solution)/shard_map/ppermute | solution.py:32
  61.2 4.4 %scores.7 = (bf16[2048,512]{1,0:T(8,128)(2,1)}, f32[1,512]{1,0:T(1,128)S(1)}, f32[1,512]{1,0:T(1,128)S(1)}, bf16[512,768]{1,0:T(8,128)(2,1)}) custom-call(s32[1]{0:T(128)} %bitcast.xh_ref, bf16[256,896]{1,0:T(8,128)(2,1)S(1)} %collective-permute-done.4.own_ref.refs_2_, bf16[256,896]{1,0:T(8,128)(2,1)S(1)} %collective-permute-done.6.oth_ref.refs_3_, ...), custom_call_target="tpu_custom_call" | custom-call | flops 1000 | bytes 1000 | tf_op jit(solution)/shard_map/scores/pallas_call | solution.py:94
  67.1 2.5 %collective-permute-start.9 = (f32[4,512]{1,0:T(4,128)S(1)}, f32[4,512]{1,0:T(4,128)S(1)}, u32[]{:S(2)}, u32[]{:S(2)}) collective-permute-start(f32[4,512]{1,0:T(4,128)S(1)} %get-tuple-element.106), channel_id=1, source_target_pairs={{0,2},{1,3},{2,0},{3,1},{4,6},{5,7},{6,4},{7,5},{8,10},{9,11},{10,... | collective-permute-start | bytes 24584 | tf_op jit(solution)/shard_map/ppermute | solution.py:32
  74.0 5.5 %all-to-all-start.2 = ((f32[16,8,256]{2,1,0:T(8,128)}), f32[16,8,256]{2,1,0:T(8,128)S(1)}, u32[]{:S(2)}, u32[]{:S(2)}) async-start(f32[16,8,256]{2,1,0:T(8,128)} %broadcast_in_dim.16), calls=%async_computation.2 | async-start | bytes 262144 | tf_op jit(solution)/shard_map/all_to_all | solution.py:504
  79.5 10.0 %hits.3 = (s32[12]{0:T(128)S(1)}, s32[7680]{0:T(1024)S(1)}, f32[7680]{0:T(1024)S(1)}, f32[7680]{0:T(1024)S(1)}) custom-call(s32[2]{0:T(128)S(1)} %pad_add_fusion.base_ref, bf16[256,896]{1,0:T(8,128)(2,1)} %collective-permute-done.1.own_ref.refs_0_, bf16[256,896]{1,0:T(8,128)(2,1)} %copy-done, bf16[256,896]{1,0:T(8,128)(2,1)} %copy-done.2, ...), custom_call_target="tpu_custom_call" | custom-call | flops 1000 | bytes 1000 | tf_op jit(solution)/shard_map/hits/pallas_call | solution.py:187
  89.6 9.0 %query_part.1 = (bf16[2048,256]{1,0:T(8,128)(2,1)}, bf16[2048,256]{1,0:T(8,128)(2,1)}, bf16[2048,256]{1,0:T(8,128)(2,1)}, bf16[2048,256]{1,0:T(8,128)(2,1)}, bf1...) custom-call(s32[1]{0:T(128)} %bitcast.7.at_ref, s32[4]{0:T(128)S(1)} %get-tuple-element.57.na, ...), custom_call_target="tpu_custom_call" | custom-call | flops 8589934592 | bytes 8388608 | tf_op jit(solution)/shard_map/query_part/pallas_call | solution.py:300
  98.7 2.5 %collective-permute-done.11 = bf16[512,896]{1,0:T(8,128)(2,1)S(1)} collective-permute-done((bf16[512,896]{1,0:T(8,128)(2,1)S(1)}, bf16[512,896]{1,0:T(8,128)(2,1)S(1)}, u32[]{:S(2)}, u32[]{:S(2)}) %collective-permute-start.11) | collective-permute-done | bytes 917536 | tf_op jit(solution)/shard_map/ppermute | solution.py:32
  102.3 3.5 %all-to-all-start.3 = ((bf16[4,128,896]{2,1,0:T(8,128)(2,1)}), bf16[4,128,896]{2,1,0:T(8,128)(2,1)S(1)}, u32[]{:S(2)}, u32[]{:S(2)}) async-start(bf16[4,128,896]{2,1,0:T(8,128)(2,1)} %bitcast.8), calls=%async_computation.3 | async-start | bytes 1835008 | tf_op jit(solution)/shard_map/all_to_all | solution.py:512
  105.9 7.6 %rest_part.1 = (bf16[2048,256]{1,0:T(8,128)(2,1)}, bf16[2048,256]{1,0:T(8,128)(2,1)}, bf16[2048,256]{1,0:T(8,128)(2,1)}, bf16[2048,256]{1,0:T(8,128)(2,1)}) custom-call(s32[1]{0:T(128)} %bitcast.7.at_ref, s32[4]{0:T(128)S(1)} %get-tuple-element.57.na, s32[2560]{0:T(1024)S(1)} %get-tuple-element.66.ka, f32[2560]{0:T(1024)S(1)} %get-tuple-element.67.sa, ...), custom_call_target="tpu_custom_call" | custom-call | flops 1000 | bytes 8388608 | tf_op jit(solution)/shard_map/rest_part/pallas_call | solution.py:300
  113.5 8.4 %class_part.2 = (bf16[4096,768]{1,0:T(8,128)(2,1)}, bf16[1536,768]{1,0:T(8,128)(2,1)}) custom-call(s32[1]{0:T(128)} %bitcast.4.core_ref, bf16[2048,256]{1,0:T(8,128)(2,1)} %get-tuple-element.95.refs_0_, bf16[2048,256]{1,0:T(8,128)(2,1)} %get-tuple-element.82.refs_1_, bf16[2048,256]{1,0:T(8,128)(2,1)} %get-tuple-element.83.refs_2_, ...), custom_call_target="tpu_custom_call" | custom-call | flops 4831838208 | bytes 8388608 | tf_op jit(solution)/shard_map/class_part/pallas_call | solution.py:335
  122.8 8.1 %all-to-all-start.4 = ((bf16[16,8,896]{2,1,0:T(8,128)(2,1)}), bf16[16,8,896]{2,1,0:T(8,128)(2,1)S(1)}, u32[]{:S(2)}, u32[]{:S(2)}) async-start(bf16[16,8,896]{2,1,0:T(8,128)(2,1)} %bitcast.9), calls=%async_computation.4 | async-start | bytes 458752 | tf_op jit(solution)/shard_map/all_to_all | solution.py:516
  130.9 5.4 %class_part.3 = (bf16[4096,768]{1,0:T(8,128)(2,1)}, bf16[512,768]{1,0:T(8,128)(2,1)}) custom-call(s32[1]{0:T(128)} %bitcast.4.core_ref, bf16[2048,256]{1,0:T(8,128)(2,1)} %get-tuple-element.95.refs_0_, bf16[2048,256]{1,0:T(8,128)(2,1)} %get-tuple-element.82.refs_1_, bf16[2048,256]{1,0:T(8,128)(2,1)} %get-tuple-element.83.refs_2_, ...), custom_call_target="tpu_custom_call", output_to_operand_aliasing={{0}: (13, {})} | custom-call | flops 1610612736 | bytes 8388608 | tf_op jit(solution)/shard_map/class_part/pallas_call | solution.py:335
  136.3 4.8 %all-to-all-done.4 = bf16[16,8,896]{2,1,0:T(8,128)(2,1)S(1)} async-done(((bf16[16,8,896]{2,1,0:T(8,128)(2,1)}), bf16[16,8,896]{2,1,0:T(8,128)(2,1)S(1)}, u32[]{:S(2)}, u32[]{:S(2)}) %all-to-all-start.4) | async-done | bytes 229408 | tf_op jit(solution)/shard_map/all_to_all | solution.py:516
  144.8 1.7 %place.1 = bf16[4096,768]{1,0:T(8,128)(2,1)} custom-call(s32[1]{0:T(128)} %bitcast.4.core_ref, bf16[1536,768]{1,0:T(8,128)(2,1)S(1)} %collective-permute-done.12.refs_0_, bf16[512,768]{1,0:T(8,128)(2,1)S(1)} %collective-permute-done.13.refs_1_, bf16[4096,768]{1,0:T(8,128)(2,1)} %get-tuple-element.104.refs_2_), custom_call_target="tpu_custom_call", output_to_operand_aliasing={{}: (3, {})} | custom-call | flops 1000 | bytes 1000 | tf_op jit(solution)/shard_map/place/pallas_call | solution.py:370
  (73 shorter events, 15.0 us)
Async XLA Ops:
  29.9 5.2 %collective-permute-start = (bf16[256,896]{1,0:T(8,128)(2,1)}, bf16[256,896]{1,0:T(8,128)(2,1)}, u32[]{:S(2)}, u32[]{:S(2)}) collective-permute-start(bf16[256,896]{1,0:T(8,128)(2,1)} %bitcast.3.own_ref.refs_0_), channel_id=1, source_target_pairs={{0,64},{64,0},{1,65},{65,1},{2,66},{66,2},{3,67},{67,3},{4,68},{68... | collective-permute-start | bytes 1376264 | tf_op jit(solution)/shard_map/ppermute | solution.py:32
  29.9 15.0 %collective-permute-start.3 = (bf16[256,896]{1,0:T(8,128)(2,1)}, bf16[256,896]{1,0:T(8,128)(2,1)}, u32[]{:S(2)}, u32[]{:S(2)}) collective-permute-start(bf16[256,896]{1,0:T(8,128)(2,1)} %bitcast.3.own_ref.refs_0_), channel_id=1, source_target_pairs={{0,1},{1,2},{2,3},{3,0},{4,5},{5,6},{6,7},{7,4},{8,9},{9,10},{10,1... | collective-permute-start | bytes 1376264 | tf_op jit(solution)/shard_map/ppermute | solution.py:32
  31.5 13.5 %collective-permute-start.1 = (bf16[256,896]{1,0:T(8,128)(2,1)}, bf16[256,896]{1,0:T(8,128)(2,1)}, u32[]{:S(2)}, u32[]{:S(2)}) collective-permute-start(bf16[256,896]{1,0:T(8,128)(2,1)} %bitcast.3.own_ref.refs_0_), channel_id=1, source_target_pairs={{0,3},{1,0},{2,1},{3,2},{4,7},{5,4},{6,5},{7,6},{8,11},{9,8},{10,9... | collective-permute-start | bytes 1376264 | tf_op jit(solution)/shard_map/ppermute | solution.py:32
  45.0 9.2 %collective-permute-start.2 = (bf16[256,896]{1,0:T(8,128)(2,1)}, bf16[256,896]{1,0:T(8,128)(2,1)S(1)}, u32[]{:S(2)}, u32[]{:S(2)}) collective-permute-start(bf16[256,896]{1,0:T(8,128)(2,1)} %collective-permute-done.1.own_ref.refs_0_), channel_id=1, source_target_pairs={{0,64},{64,0},{1,65},{65,1},{2,66},{66,2},{3,67},{67,3},{4,68},{68... | collective-permute-start | bytes 1376264 | tf_op jit(solution)/shard_map/ppermute | solution.py:32
  45.4 3.8 %collective-permute-start.5 = (bf16[256,896]{1,0:T(8,128)(2,1)}, bf16[256,896]{1,0:T(8,128)(2,1)S(1)}, u32[]{:S(2)}, u32[]{:S(2)}) collective-permute-start(bf16[256,896]{1,0:T(8,128)(2,1)} %collective-permute-done.3.own_ref.refs_4_), channel_id=1, source_target_pairs={{0,64},{64,0},{1,65},{65,1},{2,66},{66,2},{3,67},{67,3},{4,68},{68... | collective-permute-start | bytes 1376264 | tf_op jit(solution)/shard_map/ppermute | solution.py:32
  46.7 12.7 %collective-permute-start.4 = (bf16[256,896]{1,0:T(8,128)(2,1)S(1)}, bf16[256,896]{1,0:T(8,128)(2,1)S(1)}, u32[]{:S(2)}, u32[]{:S(2)}) collective-permute-start(bf16[256,896]{1,0:T(8,128)(2,1)S(1)} %broadcast_select_fusion), channel_id=1, source_target_pairs={{0,3},{1,0},{2,1},{3,2},{64,65},{65,66},{66,67},{67,64},{4,7},{5,4... | collective-permute-start | bytes 1376264 | tf_op jit(solution)/shard_map/ppermute | solution.py:480
  49.2 10.1 %copy-start.1 = (bf16[256,896]{1,0:T(8,128)(2,1)}, bf16[256,896]{1,0:T(8,128)(2,1)S(1)}, u32[]{:S(2)}) copy-start(bf16[256,896]{1,0:T(8,128)(2,1)S(1)} %collective-permute-done.5.oth_ref.refs_5_) | copy-start | bytes 1376260
  54.2 11.4 %copy-start = (bf16[256,896]{1,0:T(8,128)(2,1)}, bf16[256,896]{1,0:T(8,128)(2,1)S(1)}, u32[]{:S(2)}) copy-start(bf16[256,896]{1,0:T(8,128)(2,1)S(1)} %collective-permute-done.2.oth_ref.refs_1_) | copy-start | bytes 1376260
  59.3 6.4 %copy-start.2 = (bf16[256,896]{1,0:T(8,128)(2,1)}, bf16[256,896]{1,0:T(8,128)(2,1)S(1)}, u32[]{:S(2)}) copy-start(bf16[256,896]{1,0:T(8,128)(2,1)S(1)} %collective-permute-done.4.own_ref.refs_2_) | copy-start | bytes 1376260
  59.3 1.9 %collective-permute-start.6 = (bf16[256,896]{1,0:T(8,128)(2,1)S(1)}, bf16[256,896]{1,0:T(8,128)(2,1)S(1)}, u32[]{:S(2)}, u32[]{:S(2)}) collective-permute-start(bf16[256,896]{1,0:T(8,128)(2,1)S(1)} %collective-permute-done.4.own_ref.refs_2_), channel_id=1, source_target_pairs={{0,64},{64,0},{1,65},{65,1},{2,66},{66,2},{3,67},{67,3},{4,68},{68... | collective-permute-start | bytes 1376264 | tf_op jit(solution)/shard_map/ppermute | solution.py:32
  65.7 1.3 collective-permute-start.7
  67.0 4.9 %collective-permute-start.10 = (f32[4,512]{1,0:T(4,128)S(1)}, f32[4,512]{1,0:T(4,128)S(1)}, u32[]{:S(2)}, u32[]{:S(2)}) collective-permute-start(f32[4,512]{1,0:T(4,128)S(1)} %get-tuple-element.106), channel_id=1, source_target_pairs={{0,1},{1,2},{2,3},{3,0},{4,5},{5,6},{6,7},{7,4},{8,9},{9,10},{10,1... | collective-permute-start | bytes 24584 | tf_op jit(solution)/shard_map/ppermute | solution.py:32
  67.1 5.2 %collective-permute-start.9 = (f32[4,512]{1,0:T(4,128)S(1)}, f32[4,512]{1,0:T(4,128)S(1)}, u32[]{:S(2)}, u32[]{:S(2)}) collective-permute-start(f32[4,512]{1,0:T(4,128)S(1)} %get-tuple-element.106), channel_id=1, source_target_pairs={{0,2},{1,3},{2,0},{3,1},{4,6},{5,7},{6,4},{7,5},{8,10},{9,11},{10,... | collective-permute-start | bytes 24584 | tf_op jit(solution)/shard_map/ppermute | solution.py:32
  69.6 3.7 %collective-permute-start.8 = (f32[4,512]{1,0:T(4,128)S(1)}, f32[4,512]{1,0:T(4,128)S(1)}, u32[]{:S(2)}, u32[]{:S(2)}) collective-permute-start(f32[4,512]{1,0:T(4,128)S(1)} %get-tuple-element.106), channel_id=1, source_target_pairs={{0,3},{1,0},{2,1},{3,2},{4,7},{5,4},{6,5},{7,6},{8,11},{9,8},{10,9... | collective-permute-start | bytes 24584 | tf_op jit(solution)/shard_map/ppermute | solution.py:32
  74.0 15.5 %all-to-all-start.2 = ((f32[16,8,256]{2,1,0:T(8,128)}), f32[16,8,256]{2,1,0:T(8,128)S(1)}, u32[]{:S(2)}, u32[]{:S(2)}) async-start(f32[16,8,256]{2,1,0:T(8,128)} %broadcast_in_dim.16), calls=%async_computation.2 | async-start | bytes 262144 | tf_op jit(solution)/shard_map/all_to_all | solution.py:504
  98.6 2.6 %collective-permute-start.11 = (bf16[512,896]{1,0:T(8,128)(2,1)S(1)}, bf16[512,896]{1,0:T(8,128)(2,1)S(1)}, u32[]{:S(2)}, u32[]{:S(2)}) collective-permute-start(bf16[512,896]{1,0:T(8,128)(2,1)S(1)} %get-tuple-element.80), channel_id=1, source_target_pairs={{0,64},{64,0},{1,65},{65,1},{2,66},{66,2},{3,67},{67,3},{4,68},{68... | collective-permute-start | bytes 2752520 | tf_op jit(solution)/shard_map/ppermute | solution.py:32
  102.3 19.6 %all-to-all-start.3 = ((bf16[4,128,896]{2,1,0:T(8,128)(2,1)}), bf16[4,128,896]{2,1,0:T(8,128)(2,1)S(1)}, u32[]{:S(2)}, u32[]{:S(2)}) async-start(bf16[4,128,896]{2,1,0:T(8,128)(2,1)} %bitcast.8), calls=%async_computation.3 | async-start | bytes 1835008 | tf_op jit(solution)/shard_map/all_to_all | solution.py:512
  105.8 7.7 %copy-start.4 = (bf16[512,768]{1,0:T(8,128)(2,1)S(1)}, bf16[512,768]{1,0:T(8,128)(2,1)}, u32[]{:S(2)}) copy-start(bf16[512,768]{1,0:T(8,128)(2,1)} %get-tuple-element.90.refs_8_) | copy-start | bytes 2359300
  105.8 7.7 %copy-start.5 = (bf16[512,768]{1,0:T(8,128)(2,1)S(1)}, bf16[512,768]{1,0:T(8,128)(2,1)}, u32[]{:S(2)}) copy-start(bf16[512,768]{1,0:T(8,128)(2,1)} %get-tuple-element.93.refs_11_) | copy-start | bytes 2359300
  105.9 7.7 %copy-start.6 = (bf16[512,768]{1,0:T(8,128)(2,1)S(1)}, bf16[512,768]{1,0:T(8,128)(2,1)}, u32[]{:S(2)}) copy-start(bf16[512,768]{1,0:T(8,128)(2,1)} %get-tuple-element.91.refs_9_) | copy-start | bytes 2359300
  105.9 7.7 %copy-start.7 = (bf16[512,768]{1,0:T(8,128)(2,1)S(1)}, bf16[512,768]{1,0:T(8,128)(2,1)}, u32[]{:S(2)}) copy-start(bf16[512,768]{1,0:T(8,128)(2,1)} %get-tuple-element.92.refs_10_) | copy-start | bytes 2359300
  122.8 21.9 %collective-permute-start.12 = (bf16[1536,768]{1,0:T(8,128)(2,1)}, bf16[1536,768]{1,0:T(8,128)(2,1)S(1)}, u32[]{:S(2)}, u32[]{:S(2)}) collective-permute-start(bf16[1536,768]{1,0:T(8,128)(2,1)} %get-tuple-element.102), channel_id=1, source_target_pairs={{0,64},{64,0},{1,65},{65,1},{2,66},{66,2},{3,67},{67,3},{4,68},{68... | collective-permute-start | bytes 7077896 | tf_op jit(solution)/shard_map/ppermute | solution.py:32
  122.8 18.3 %all-to-all-start.4 = ((bf16[16,8,896]{2,1,0:T(8,128)(2,1)}), bf16[16,8,896]{2,1,0:T(8,128)(2,1)S(1)}, u32[]{:S(2)}, u32[]{:S(2)}) async-start(bf16[16,8,896]{2,1,0:T(8,128)(2,1)} %bitcast.9), calls=%async_computation.4 | async-start | bytes 458752 | tf_op jit(solution)/shard_map/all_to_all | solution.py:516
  141.1 3.6 %collective-permute-start.13 = (bf16[512,768]{1,0:T(8,128)(2,1)}, bf16[512,768]{1,0:T(8,128)(2,1)S(1)}, u32[]{:S(2)}, u32[]{:S(2)}) collective-permute-start(bf16[512,768]{1,0:T(8,128)(2,1)} %get-tuple-element.103), channel_id=1, source_target_pairs={{0,64},{64,0},{1,65},{65,1},{2,66},{66,2},{3,67},{67,3},{4,68},{68... | collective-permute-start | bytes 2359304 | tf_op jit(solution)/shard_map/ppermute | solution.py:32
  (2 other events, 5.2 us)
